TPU v7x, 32 devices: a whole 2x2x4 slice. The times are simulated.
32 devices in a mesh: dp: 8 (over z, x), seq: 4 (over y, core).
Axes of the slice: x: 2, y: 2, z: 4, core: 2. Of those that a mesh axis runs over, the one named last changes fastest.
Arguments:
- tokens: bfloat16 [64, 1024, 512], P('dp', 'seq'), may hold values from -6 to 6
- cotangent: bfloat16 [64, 1024, 512], P('dp', 'seq'), may hold values from -6 to 6
- masked: int32 [64, 1024], P('dp', 'seq'), may hold values from 0 to 1, as said below
- omega: float32 [64, 256], replicated, may hold values from -5 to 5
- att_weights: float32 [1050624], P(('dp', 'seq'))
- att_first: float32 [1050624], P(('dp', 'seq'))
- att_second: float32 [1050624], P(('dp', 'seq')), as said below
- ffn_in: float32 [512, 2048], P('dp', 'seq'), may hold values from -0.25 to 0.25
- ffn_out: float32 [2048, 512], P('seq', 'dp'), may hold values from -0.125 to 0.125
- ffn_in_first: float32 [512, 2048], P('dp', 'seq')
- ffn_in_second: float32 [512, 2048], P('dp', 'seq'), as said below
- ffn_out_first: float32 [2048, 512], P('seq', 'dp')
- ffn_out_second: float32 [2048, 512], P('seq', 'dp'), as said below
Outputs:
- block_out: bfloat16 [64, 1024, 512], P('dp', 'seq')
- input_grad: float32 [64, 1024, 512], P('dp', 'seq')
- att_new: float32 [1050624], P(('dp', 'seq'))
- att_first_new: float32 [1050624], P(('dp', 'seq'))
- att_second_new: float32 [1050624], P(('dp', 'seq'))
- att_copy: bfloat16 [1050624], P(('dp', 'seq'))
- ffn_in_new: float32 [512, 2048], P('dp', 'seq')
- ffn_in_first_new: float32 [512, 2048], P('dp', 'seq')
- ffn_in_second_new: float32 [512, 2048], P('dp', 'seq')
- ffn_in_copy: bfloat16 [512, 2048], P('dp', 'seq')
- ffn_out_new: float32 [2048, 512], P('seq', 'dp')
- ffn_out_first_new: float32 [2048, 512], P('seq', 'dp')
- ffn_out_second_new: float32 [2048, 512], P('seq', 'dp')
- ffn_out_copy: bfloat16 [2048, 512], P('seq', 'dp')
Inputs may be any that keep to these rules, and one draw needn't show every extreme that they name: `masked`: each sequence marks a number of positions, from 51 to 256, at random places; some sequence marks exactly 256; the positions of one device are not bounded by that share. `att_second`: positive. `ffn_in_second`: positive. `ffn_out_second`: positive.
All inputs are finite; a program needn't handle non-finite values.
Results may differ from a plain program's by a relative error of at most 0.015.
Values may be sent and summed in bfloat16 or wider, within the bound.
No kernel may reach another device: no remote copies, remote signals or barrier semaphores. Data moves between devices by JAX's collectives and lax.ppermute only.
A program may use at most 320 MiB of HBM per device.

v0:
```python
import jax
import jax.numpy as jnp
from jax import lax
from jax.sharding import PartitionSpec as P

CH = 256
STEP = 10


PRECISE = lax.Precision.HIGHEST
BETA_FIRST = 0.9
BETA_SECOND = 0.999
ADAM_EPS = 1e-08
WEIGHT_DECAY = 0.1
RATE_MATRIX = 0.02
RATE_NORM = 0.3
NORM_EPS = 1e-05


def as_sent(value):

    def short(part):
        return part.astype(jnp.bfloat16) if part.dtype == jnp.float32 else part

    return jax.tree.map(short, value)


def from_behind(value, axis, by):
    size = lax.axis_size(axis)
    pairs = [(i, i + by) for i in range(size) if 0 <= i + by < size]
    return lax.ppermute(value, axis, pairs)


def contract(left, right, left_dim, right_dim):
    return lax.dot_general(
        left, right, (((left_dim,), (right_dim,)), ((), ())), preferred_element_type=jnp.float32
    )


def rounded(value):
    coarse = lax.optimization_barrier(value.astype(jnp.bfloat16)).astype(jnp.float32)
    return value + lax.stop_gradient(coarse - value)


def norm_rows(inputs, gain, offset):
    centre = inputs - jnp.mean(inputs, axis=-1, keepdims=True)
    spread = jnp.mean(centre * centre, axis=-1, keepdims=True)
    return centre * lax.rsqrt(spread + NORM_EPS) * gain + offset


def feature_map(inputs, omega):
    scaled = inputs * omega.shape[0] ** (-0.25)
    projected = jnp.einsum("...e,em->...m", scaled, omega, precision=PRECISE)
    return jnp.exp(
        projected - 0.5 * jnp.sum(scaled * scaled, axis=-1, keepdims=True)
    ) * omega.shape[1] ** (-0.5)


def add_pair(earlier, later):
    return (earlier[0] + later[0], earlier[1] + later[1])


def key_section(key_rows, values, omega):
    seq_count, tok_rows, head_count, head_size = key_rows.shape
    span_count = tok_rows // CH
    features = rounded(feature_map(key_rows, omega))
    features = features.reshape(seq_count, span_count, CH, head_count, features.shape[-1])
    spanned = rounded(values).reshape(seq_count, span_count, CH, head_count, head_size)
    span_state = jnp.einsum("snjhm,snjhe->snhme", features, spanned)
    span_total = jnp.sum(features, axis=2)
    return (features, span_state, span_total)


def exclusive_spans(span_values, carried):
    leading = jnp.zeros_like(span_values)
    running = jnp.cumsum(span_values, axis=1)[:, :-1]
    return jnp.concatenate([leading, running], axis=1) + carried[:, None]


def query_section(
    queries, key_features, values, span_state, span_total, prefix_state, prefix_total, omega
):
    seq_count, span_count, span_len, head_count, feature_count = key_features.shape
    head_size = queries.shape[-1]
    query_features = rounded(feature_map(queries, omega)).reshape(
        seq_count, span_count, span_len, head_count, feature_count
    )
    spanned = rounded(values).reshape(seq_count, span_count, span_len, head_count, head_size)
    state_before = rounded(exclusive_spans(span_state, prefix_state))
    total_before = exclusive_spans(span_total, prefix_total)
    lower = jnp.arange(span_len)[:, None] >= jnp.arange(span_len)[None, :]
    scores = rounded(
        jnp.where(lower, jnp.einsum("snihm,snjhm->snhij", query_features, key_features), 0.0)
    )
    numerator = jnp.einsum("snhij,snjhe->snihe", scores, spanned)
    numerator = numerator + jnp.einsum("snihm,snhme->snihe", query_features, state_before)
    denominator = jnp.einsum("snhij->snih", scores)
    denominator = denominator + jnp.einsum(
        "snihm,snhm->snih", query_features, total_before, precision=PRECISE
    )
    return (numerator / denominator[..., None]).reshape(
        seq_count, span_count * span_len, head_count, head_size
    )


def prefix_chain(pair):
    carried = (jnp.zeros_like(pair[0]), jnp.zeros_like(pair[1]))
    for repeat in range(lax.axis_size("seq") - 1):
        carried = from_behind(as_sent(add_pair(carried, pair)), "seq", 1)
    return carried


def suffix_chain(pair):
    carried = (jnp.zeros_like(pair[0]), jnp.zeros_like(pair[1]))
    for repeat in range(lax.axis_size("seq") - 1):
        carried = from_behind(as_sent(add_pair(carried, pair)), "seq", -1)
    return carried


def adamw(weight, first, second, grad, rate, decay):
    first_new = BETA_FIRST * first + (1.0 - BETA_FIRST) * grad
    second_new = BETA_SECOND * second + (1.0 - BETA_SECOND) * grad * grad
    first_hat = first_new / (1.0 - BETA_FIRST**STEP)
    second_hat = second_new / (1.0 - BETA_SECOND**STEP)
    weight_new = weight - rate * (first_hat / (jnp.sqrt(second_hat) + ADAM_EPS) + decay * weight)
    return (weight_new, first_new, second_new)


def shards(
    tokens,
    cotangent,
    masked,
    omega,
    att_weights,
    att_first,
    att_second,
    ffn_in,
    ffn_out,
    ffn_in_first,
    ffn_in_second,
    ffn_out_first,
    ffn_out_second,
):
    seq_count, tok_rows, model_width = tokens.shape
    head_size = omega.shape[0]
    head_count = model_width // head_size
    square = model_width * model_width
    flat_low = lax.all_gather(att_weights.astype(jnp.bfloat16), ("dp", "seq"), axis=0, tiled=True)
    matrices = flat_low[: 4 * square].reshape(4, model_width, model_width)
    norm_params = flat_low[4 * square :].reshape(4, model_width).astype(jnp.float32)
    first_weight, second_weight = (
        lax.all_gather(ffn_in.astype(jnp.bfloat16), "dp", axis=0, tiled=True),
        lax.all_gather(ffn_out.astype(jnp.bfloat16), "dp", axis=1, tiled=True),
    )
    inputs = tokens.astype(jnp.float32).reshape(seq_count * tok_rows, model_width)
    normed, norm_one_pull = jax.vjp(norm_rows, inputs, norm_params[0], norm_params[1])
    normed_low = normed.astype(jnp.bfloat16)
    head_shape = (seq_count, tok_rows, head_count, head_size)
    queries = jnp.dot(normed_low, matrices[0], preferred_element_type=jnp.float32).reshape(
        head_shape
    )
    key_rows = jnp.dot(normed_low, matrices[1], preferred_element_type=jnp.float32).reshape(
        head_shape
    )
    values = jnp.dot(normed_low, matrices[2], preferred_element_type=jnp.float32).reshape(
        head_shape
    )

    def key_part(key_in, value_in):
        return key_section(key_in, value_in, omega)

    (key_features, span_state, span_total), key_pull = jax.vjp(key_part, key_rows, values)
    local_pair = (jnp.sum(span_state, axis=1), jnp.sum(span_total, axis=1))
    prefix_state, prefix_total = prefix_chain(local_pair)

    def query_part(query_in, feat_in, value_in, state_in, total_in, prefix_in, prefix_sum_in):
        return query_section(
            query_in, feat_in, value_in, state_in, total_in, prefix_in, prefix_sum_in, omega
        )

    mixed, query_pull = jax.vjp(
        query_part,
        queries,
        key_features,
        values,
        span_state,
        span_total,
        prefix_state,
        prefix_total,
    )
    mixed_low = mixed.reshape(seq_count * tok_rows, model_width).astype(jnp.bfloat16)
    middle = inputs + jnp.dot(mixed_low, matrices[3], preferred_element_type=jnp.float32)
    normed_two, norm_two_pull = jax.vjp(norm_rows, middle, norm_params[2], norm_params[3])
    normed_two_low = normed_two.astype(jnp.bfloat16)
    ffn_rows_in = lax.all_gather(
        normed_two_low.reshape(seq_count, tok_rows, model_width), "seq", axis=1, tiled=True
    ).reshape(-1, model_width)
    hidden = jnp.dot(ffn_rows_in, first_weight, preferred_element_type=jnp.float32)
    active, gelu_pull = jax.vjp(jax.nn.gelu, hidden)
    active_low = active.astype(jnp.bfloat16)
    branch = jnp.dot(active_low, second_weight, preferred_element_type=jnp.float32)
    ffn_result = (
        lax.psum_scatter(
            branch.reshape(seq_count, -1, model_width).astype(jnp.bfloat16),
            "seq",
            scatter_dimension=1,
            tiled=True,
        )
        .astype(jnp.float32)
        .reshape(-1, model_width)
    )
    block_out = (middle + ffn_result).reshape(seq_count, tok_rows, model_width).astype(jnp.bfloat16)
    target = (cotangent.astype(jnp.float32) * masked.astype(jnp.float32)[:, :, None]).reshape(
        -1, model_width
    )
    target_low = target.astype(jnp.bfloat16)
    grad_rows = lax.all_gather(
        target_low.reshape(seq_count, tok_rows, model_width), "seq", axis=1, tiled=True
    ).reshape(-1, model_width)
    grad_active = contract(grad_rows, second_weight, 1, 1)
    grad_hidden = gelu_pull(grad_active)[0].astype(jnp.bfloat16)
    grad_second = contract(active_low, grad_rows, 0, 0)
    grad_first = contract(ffn_rows_in, grad_hidden, 0, 0)
    normed_two_part = contract(grad_hidden, first_weight, 1, 1)
    grad_normed_two = (
        lax.psum_scatter(
            normed_two_part.reshape(seq_count, -1, model_width).astype(jnp.bfloat16),
            "seq",
            scatter_dimension=1,
            tiled=True,
        )
        .astype(jnp.float32)
        .reshape(-1, model_width)
    )
    grad_first, grad_second = (
        lax.psum_scatter(grad_first, "dp", scatter_dimension=0, tiled=True),
        lax.psum_scatter(grad_second, "dp", scatter_dimension=1, tiled=True),
    )
    middle_back, gain_two_grad, offset_two_grad = norm_two_pull(grad_normed_two)
    grad_middle = target + middle_back
    grad_middle_low = grad_middle.astype(jnp.bfloat16)
    out_proj_grad = contract(mixed_low, grad_middle_low, 0, 0)
    grad_mixed = contract(grad_middle_low, matrices[3], 1, 1).reshape(head_shape)
    (
        grad_queries,
        grad_features,
        grad_values,
        grad_state,
        grad_total,
        grad_prefix,
        grad_prefix_total,
    ) = query_pull(grad_mixed)
    back_pair = (grad_prefix, grad_prefix_total)
    later_state, later_total = suffix_chain(back_pair)
    grad_keys, extra_values = key_pull(
        (grad_features, grad_state + later_state[:, None], grad_total + later_total[:, None])
    )
    grad_values = grad_values + extra_values
    query_low = grad_queries.reshape(-1, model_width).astype(jnp.bfloat16)
    key_low = grad_keys.reshape(-1, model_width).astype(jnp.bfloat16)
    value_low = grad_values.reshape(-1, model_width).astype(jnp.bfloat16)
    query_proj_grad = contract(normed_low, query_low, 0, 0)
    key_proj_grad = contract(normed_low, key_low, 0, 0)
    value_proj_grad = contract(normed_low, value_low, 0, 0)
    grad_normed = (
        contract(query_low, matrices[0], 1, 1)
        + contract(key_low, matrices[1], 1, 1)
        + contract(value_low, matrices[2], 1, 1)
    )
    input_back, gain_one_grad, offset_one_grad = norm_one_pull(grad_normed)
    input_grad = (grad_middle + input_back).reshape(seq_count, tok_rows, model_width)
    matrix_grads = jnp.stack(
        [query_proj_grad, key_proj_grad, value_proj_grad, out_proj_grad]
    ).reshape(-1)
    norm_grads = jnp.stack(
        [gain_one_grad, offset_one_grad, gain_two_grad, offset_two_grad]
    ).reshape(-1)
    att_grad = lax.psum_scatter(
        jnp.concatenate([matrix_grads, norm_grads]), ("dp", "seq"), scatter_dimension=0, tiled=True
    )
    shard_len = att_weights.shape[0]
    position = lax.axis_index(("dp", "seq")) * shard_len + jnp.arange(shard_len, dtype=jnp.int32)
    is_matrix = position < 4 * square
    rate = jnp.where(is_matrix, RATE_MATRIX, RATE_NORM)
    decay = jnp.where(is_matrix, WEIGHT_DECAY, 0.0)
    att_new, att_first_new, att_second_new = adamw(
        att_weights, att_first, att_second, att_grad, rate, decay
    )
    ffn_in_new, ffn_in_first_new, ffn_in_second_new = adamw(
        ffn_in, ffn_in_first, ffn_in_second, grad_first, RATE_MATRIX, WEIGHT_DECAY
    )
    ffn_out_new, ffn_out_first_new, ffn_out_second_new = adamw(
        ffn_out, ffn_out_first, ffn_out_second, grad_second, RATE_MATRIX, WEIGHT_DECAY
    )
    return (
        block_out,
        input_grad,
        att_new,
        att_first_new,
        att_second_new,
        att_new.astype(jnp.bfloat16),
        ffn_in_new,
        ffn_in_first_new,
        ffn_in_second_new,
        ffn_in_new.astype(jnp.bfloat16),
        ffn_out_new,
        ffn_out_first_new,
        ffn_out_second_new,
        ffn_out_new.astype(jnp.bfloat16),
    )


def solution(mesh):
    in_specs = (
        P("dp", "seq", None),
        P("dp", "seq", None),
        P("dp", "seq"),
        P(),
        P(("dp", "seq")),
        P(("dp", "seq")),
        P(("dp", "seq")),
        P("dp", "seq"),
        P("seq", "dp"),
        P("dp", "seq"),
        P("dp", "seq"),
        P("seq", "dp"),
        P("seq", "dp"),
    )
    out_specs = (
        P("dp", "seq", None),
        P("dp", "seq", None),
        P(("dp", "seq")),
        P(("dp", "seq")),
        P(("dp", "seq")),
        P(("dp", "seq")),
        P("dp", "seq"),
        P("dp", "seq"),
        P("dp", "seq"),
        P("dp", "seq"),
        P("seq", "dp"),
        P("seq", "dp"),
        P("seq", "dp"),
        P("seq", "dp"),
    )
    return jax.shard_map(shards, mesh=mesh, in_specs=in_specs, out_specs=out_specs, check_vma=False)
```

profile of v0, /device:TPU:0, one launch (start us, length us, event | category | flops | bytes accessed | tf_op | source)
XLA Modules:
  0.0 1017.9 jit_solution(16013970723150417375)
XLA Ops:
  11.5 5.0 fusion.81
  19.1 170.2 %all-reduce.5.cloned.1.call-done = bf16[1050624]{0:T(1024)(128)(2,1)} async-done(((bf16[1050624]{0:T(1024)(128)(2,1)}), bf16[1050624]{0:T(1024)(128)(2,1)}) %all-reduce.5.cloned.1.call-update) | async-done | bytes 2101264
  189.3 2.9 fusion.120
  197.6 18.8 %multiply_convert_fusion.2 = (bf16[8,256,8,256]{1,3,2,0:T(8,128)(2,1)}, f32[8,256,8,256]{1,3,2,0:T(8,128)}) fusion(f32[8,256,8]{1,2,0:T(8,128)S(1)} %broadcast_multiply_fusion.1, f32[64,256]{1,0:T(8,128)S(1)} %copy-done, f32[8,256,8,64]{1,3,2,0:T(8,128)S(1)} %get-tuple-element.58), kind=kOutput, calls=%fused_computation.28 | convolution fusion | flops 3234856960 | bytes 29491200 | tf_op jit(solution)/shard_map/jvp(...e,em->...m)/dot_general | solution.py:53
  218.8 3.0 multiply_reduce_fusion.1
  221.9 18.7 %multiply_convert_fusion.1 = (bf16[8,256,8,256]{1,3,2,0:T(8,128)(2,1)}, f32[8,256,8,256]{1,3,2,0:T(8,128)S(1)}) fusion(f32[8,256,8]{1,2,0:T(8,128)S(1)} %broadcast_multiply_fusion, f32[64,256]{1,0:T(8,128)S(1)} %copy-done, f32[8,256,8,64]{1,3,2,0:T(8,128)S(1)} %get-tuple-element.62), kind=kOutput, calls=%fused_computation.27 | convolution fusion | flops 3234856960 | bytes 29491200 | tf_op jit(solution)/shard_map/jvp(...e,em->...m)/dot_general | solution.py:53
  240.6 12.5 %fusion.119 = (f32[8,8,256]{2,1,0:T(8,128)S(1)}, bf16[8,256,8,256]{1,3,2,0:T(8,128)(2,1)}) fusion(bf16[8,256,8,256]{1,3,2,0:T(8,128)(2,1)} %get-tuple-element.63, f32[8,256,8,256]{1,3,2,0:T(8,128)S(1)} %get-tuple-element.64, f32[8,256,8]{1,2,0:T(8,128)S(1)} %broadcast_multiply_fusion), kind=kLoop, calls=%fused_computation.189 | loop fusion | flops 29343744 | bytes 33685504 | tf_op jit(solution)/shard_map/jvp()/reduce_sum | solution.py:70
  253.1 2.2 collective-permute-start.3
  257.6 4.3 fusion.122
  262.0 10.9 %fusion.123 = (bf16[8,8,256,64]{2,3,1,0:T(8,128)(2,1)}, f32[8,8,256,64]{2,3,1,0:T(8,128)}) fusion(bf16[8,256,8,256]{1,3,2,0:T(8,128)(2,1)} %get-tuple-element.34, f32[8,256,8,64]{1,3,2,0:T(8,128)S(1)} %get-tuple-element.66, bf16[8,256,8,64]{1,3,2,0:T(8,128)(2,1)} %get-tuple-element.65), kind=kOutput, calls=%fused_computation.193 | convolution fusion | flops 541065216 | bytes 20971520 | tf_op jit(solution)/shard_map/jvp(snjhm,snjhe->snhme)/dot_general | solution.py:69
  272.9 4.9 collective-permute-start
  277.8 14.4 %subtract_add_fusion.2 = f32[8,256,8,256]{1,3,2,0:T(8,128)} fusion(bf16[8,256,8,256]{1,3,2,0:T(8,128)(2,1)} %get-tuple-element.59, f32[8,256,8,256]{1,3,2,0:T(8,128)} %get-tuple-element.60, f32[8,256,8]{1,2,0:T(8,128)S(1)} %broadcast_multiply_fusion.1), kind=kLoop, calls=%fused_computation.2 | loop fusion | flops 20971520 | bytes 42008576 | tf_op jit(solution)/shard_map/jvp()/add | solution.py:42
  292.2 15.7 %fusion.127 = f32[8,8,256,256]{2,3,1,0:T(8,128)} fusion(f32[8,256,8,256]{1,3,2,0:T(8,128)} %subtract_add_fusion.2, bf16[8,256,8,256]{1,3,2,0:T(8,128)(2,1)} %get-tuple-element.34), kind=kOutput, calls=%fused_computation.197 | convolution fusion | flops 2147483648 | bytes 41943040 | tf_op jit(solution)/shard_map/jvp(snihm,snjhm->snhij)/dot_general | solution.py:93
  307.9 5.0 add_convert_fusion.3
  312.9 2.6 collective-permute-start.1
  315.5 9.6 fusion.16
  326.4 15.5 %fusion.12 = f32[8,8,64,256]{3,2,1,0:T(8,128)} fusion(bf16[8,1,8,256,256]{3,4,2,0,1:T(8,128)(2,1)} %fusion.16, f32[8,8,256,256]{2,3,1,0:T(8,128)} %fusion.127, pred[256,256]{0,1:T(8,128)(4,1)S(1)} %iota_compare_fusion, f32[8,256,8,64]{1,3,2,0:T(8,128)} %copy-done.4, bf16[8,256,8,64]{1,3,2,0:T(8,128)(2,1)} %get-tuple-element.65), kind=kOutput, calls=%fused_computation.20 | convolution fusion | flops 556793856 | bytes 35717120 | tf_op jit(solution)/shard_map/jvp(snhij,snjhe->snihe)/dot_general | solution.py:95
  343.5 5.6 add_convert_fusion.2
  349.1 2.7 collective-permute-start.2
  351.8 8.0 fusion.63
  361.3 10.4 %fusion.95 = f32[8,8,1,256]{3,2,1,0:T(1,128)S(1)} fusion(f32[8,256,8,256]{1,3,2,0:T(8,128)} %subtract_add_fusion.2, bf16[8,8,256,1]{2,1,0,3:T(8,128)(2,1)S(1)} %bitcast.359), kind=kOutput, calls=%fused_computation.150 | convolution fusion | flops 50331648 | bytes 16875520 | tf_op jit(solution)/shard_map/jvp(snihm,snhm->snih)/dot_general | solution.py:98
  371.7 10.8 %fusion.34 = (bf16[8,1,256,8,64]{2,4,3,0,1:T(8,128)(2,1)S(1)}, f32[8,8,64,256]{3,2,1,0:T(8,128)}) fusion(f32[8,256,8]{1,2,0:T(8,128)S(1)} %get-tuple-element.32, f32[8,8,64,256]{3,2,1,0:T(8,128)S(1)} %copy-done.17, f32[8,256,8,256]{1,3,2,0:T(8,128)} %subtract_add_fusion.2, bf16[8,1,8,256,64]{3,4,2,0,1:T(8,128)(2,1)} %bitcast.19, ...), kind=kOutput, calls=%fused_computation.58 | convolution fusion | flops 544210944 | bytes 31522816 | tf_op jit(solution)/shard_map/jvp(snihm,snhme->snihe)/dot_general | solution.py:96
  386.9 1.9 add_convert_fusion.1
  388.9 31.5 %all_gather.18 = bf16[512,512]{0,1:T(8,128)(2,1)S(1)} all-gather(bf16[512,64]{0,1:T(8,128)(2,1)S(1)} %convert_element_type.237), channel_id=1, replica_groups=mesh['dp'=8,'seq'=4] {'dp'}, dimensions={1}, use_global_device_ids=true | all-gather | bytes 589824 | tf_op jit(solution)/shard_map/all_gather | solution.py:153
  420.4 31.7 %all_gather.17 = bf16[512,512]{1,0:T(8,128)(2,1)S(1)} all-gather(bf16[64,512]{1,0:T(8,128)(2,1)S(1)} %convert_element_type.235), channel_id=1, replica_groups=mesh['dp'=8,'seq'=4] {'dp'}, dimensions={0}, use_global_device_ids=true | all-gather | bytes 589824 | tf_op jit(solution)/shard_map/all_gather | solution.py:152
  452.0 11.6 %fusion.128 = f32[8192,512]{1,0:T(8,128)} fusion(bf16[8192,512]{1,0:T(8,128)(2,1)} %bitcast.333, bf16[512,512]{0,1:T(8,128)(2,1)S(1)} %all_gather.18), kind=kOutput, calls=%fused_computation.198 | convolution fusion | flops 4294967296 | bytes 25690112 | tf_op jit(solution)/shard_map/dot_general | solution.py:35
  463.6 20.8 %fusion.6 = (bf16[8192,512]{1,0:T(8,128)(2,1)S(1)}, bf16[8192,512]{1,0:T(8,128)(2,1)}) fusion(f32[8192,512]{1,0:T(8,128)} %fusion.128, bf16[8192,512]{1,0:T(8,128)(2,1)} %bitcast.370, bf16[512,512]{1,0:T(8,128)(2,1)S(1)} %all_gather.17), kind=kOutput, calls=%fused_computation.11 | convolution fusion | flops 4387241984 | bytes 42467328 | tf_op jit(solution)/shard_map/dot_general | solution.py:198
  484.4 6.8 convolution_convert_fusion
  491.3 10.3 %convolution_convert_fusion.1 = bf16[8192,512]{1,0:T(8,128)(2,1)} fusion(bf16[8192,512]{1,0:T(8,128)(2,1)} %get-tuple-element.36, bf16[512,512]{0,1:T(8,128)(2,1)S(1)} %all_gather.18), kind=kOutput, calls=%fused_computation.32 | convolution fusion | flops 4299161600 | bytes 17301504 | tf_op jit(solution)/shard_map/dot_general | solution.py:201
  502.1 14.0 %fusion.131 = f32[512,512]{1,0:T(8,128)} fusion(bf16[8192,512]{1,0:T(8,128)(2,1)} %bitcast.371, bf16[8192,512]{1,0:T(8,128)(2,1)} %copy-done.63), kind=kOutput, calls=%fused_computation.201 | convolution fusion | flops 4294967296 | bytes 17825792 | tf_op jit(solution)/shard_map/dot_general | solution.py:35
  517.3 11.4 %fusion.132 = f32[512,512]{0,1:T(8,128)} fusion(bf16[8192,512]{1,0:T(8,128)(2,1)} %get-tuple-element.36, bf16[8192,512]{1,0:T(8,128)(2,1)} %bitcast.334), kind=kOutput, calls=%fused_computation.202 | convolution fusion | flops 4294967296 | bytes 17825792 | tf_op jit(solution)/shard_map/dot_general | solution.py:35
  528.9 36.2 %reduce-scatter.7.cloned.1.call-done = bf16[8,256,512]{2,1,0:T(8,128)(2,1)} async-done(((bf16[8,1024,512]{2,1,0:T(8,128)(2,1)}), bf16[8,256,512]{2,1,0:T(8,128)(2,1)}) %reduce-scatter.7.cloned.1.call-update) | async-done | bytes 2097168 | tf_op jit(solution)/shard_map/reduce_scatter | solution.py:226
  565.2 4.0 fusion.38
  569.9 2.7 fusion.39
  572.6 66.8 %reduce-scatter.5.cloned.1.call-done = bf16[8,256,512]{2,1,0:T(8,128)(2,1)} async-done(((bf16[8,1024,512]{2,1,0:T(8,128)(2,1)}), bf16[8,256,512]{2,1,0:T(8,128)(2,1)}) %reduce-scatter.5.cloned.1.call-update) | async-done | bytes 2097168 | tf_op jit(solution)/shard_map/reduce_scatter | solution.py:203
  639.4 5.9 bitcast_add_fusion.2
  647.3 4.0 copy.111
  651.3 11.3 %convert_bitcast_fusion = bf16[8,8,256,64]{2,3,1,0:T(8,128)(2,1)} fusion(f32[8,256,8,256]{1,3,2,0:T(8,128)} %subtract_add_fusion.2, f32[8,1,256,8,64]{2,0,4,3,1:T(8,128)} %bitcast.323, f32[8,256,8]{1,2,0:T(8,128)S(1)} %get-tuple-element.32), kind=kOutput, calls=%fused_computation.114 | convolution fusion | flops 537919488 | bytes 23134208 | tf_op jit(solution)/shard_map/transpose(jvp(snihm,snhme->snihe))/dot_general | solution.py:96
  662.6 11.8 %fusion.28 = f32[8,8,256,256]{2,3,1,0:T(8,128)} fusion(f32[8,256,8,64]{1,3,2,0:T(8,128)S(1)} %copy-done.5, bf16[8,256,8,64]{1,3,2,0:T(8,128)(2,1)} %get-tuple-element.65, f32[8,1,256,8,64]{2,0,4,3,1:T(8,128)} %bitcast.324, f32[8,256,8]{1,2,0:T(8,128)S(1)} %get-tuple-element.32), kind=kOutput, calls=%fused_computation.52 | convolution fusion | flops 541065216 | bytes 27328512 | tf_op jit(solution)/shard_map/transpose(jvp(snhij,snjhe->snihe))/dot_general | solution.py:95
  675.9 2.1 fusion.35
  678.0 16.0 %fusion.15 = f32[8,8,256,256]{2,3,1,0:T(8,128)} fusion(bf16[8,256,8,256]{1,3,2,0:T(8,128)(2,1)} %get-tuple-element.34, f32[8,8,256,256]{2,3,1,0:T(8,128)} %fusion.28, f32[8,8,256]{2,1,0:T(8,128)S(1)} %get-tuple-element.46, pred[256,256]{0,1:T(8,128)(4,1)S(1)} %iota_compare_fusion), kind=kOutput, calls=%fused_computation.30 | convolution fusion | flops 2155872256 | bytes 42074112 | tf_op jit(solution)/shard_map/transpose(jvp(snihm,snjhm->snhij))/dot_general | solution.py:93
  694.0 21.6 %fusion.125 = (f32[8,256,8]{1,2,0:T(8,128)S(1)}, f32[8,256,8,256]{1,3,2,0:T(8,128)}) fusion(f32[8,256,8,256]{1,3,2,0:T(8,128)} %get-tuple-element.60, f32[8,256,8]{1,2,0:T(8,128)S(1)} %copy-done.42, f32[8,8,256,256]{2,3,1,0:T(8,128)} %fusion.15, bf16[8,1,8,256,64]{3,4,2,0,1:T(8,128)(2,1)} %bitcast.19, bf16[8,8,256,64]{2,3,1,0:T(8,128)(2,1)} %collective-permute-done.2, ...), kind=kOutput, calls=%fused_computation.195 | convolution fusion | flops 571457536 | bytes 59047936 | tf_op jit(solution)/shard_map/transpose(jvp(snihm,snhme->snihe))/dot_general | solution.py:96
  715.6 15.2 %fusion.10 = f32[8,8,64,256]{3,2,1,0:T(8,128)} fusion(bf16[8,1,8,256,256]{3,4,2,0,1:T(8,128)(2,1)} %fusion.16, f32[8,8,256,256]{2,3,1,0:T(8,128)} %fusion.127, pred[256,256]{0,1:T(8,128)(4,1)S(1)} %iota_compare_fusion, f32[8,1,256,8,64]{2,0,4,3,1:T(8,128)} %bitcast.326, f32[8,256,8]{1,2,0:T(8,128)S(1)} %get-tuple-element.32), kind=kOutput, calls=%fused_computation.18 | convolution fusion | flops 554696704 | bytes 33685504 | tf_op jit(solution)/shard_map/transpose(jvp(snhij,snjhe->snihe))/dot_general | solution.py:95
  730.8 2.5 add.241
  733.3 1.7 collective-permute-start.10
  735.0 14.7 %fusion.55 = bf16[8,256,8,64]{1,3,2,0:T(8,128)(2,1)S(1)} fusion(f32[8,256,8,64]{1,3,2,0:T(8,128)S(1)} %copy-done.21, f32[8,256,8,256]{1,3,2,0:T(8,128)} %get-tuple-element.74, f32[8,256,8]{1,2,0:T(8,128)S(1)} %negate_multiply_fusion.1, f32[64,256]{1,0:T(8,128)S(1)} %copy-done), kind=kOutput, calls=%fused_computation.89 | convolution fusion | flops 3226468352 | bytes 23199744 | tf_op jit(solution)/shard_map/transpose(jvp(...e,em->...m))/dot_general | solution.py:53
  749.7 18.7 %fusion.14 = f32[8,8,256,256]{2,3,1,0:T(8,128)} fusion(f32[8,256,8,256]{1,3,2,0:T(8,128)} %subtract_add_fusion.2, f32[8,8,256,256]{2,3,1,0:T(8,128)} %fusion.28, f32[8,8,256]{2,1,0:T(8,128)S(1)} %get-tuple-element.46, pred[256,256]{0,1:T(8,128)(4,1)S(1)} %iota_compare_fusion), kind=kOutput, calls=%fused_computation.29 | convolution fusion | flops 2155872256 | bytes 50462720 | tf_op jit(solution)/shard_map/transpose(jvp(snihm,snjhm->snhij))/dot_general | solution.py:93
  768.5 2.4 add.242
  772.4 17.1 %fusion.93 = bf16[8,8,1,256]{3,2,1,0:T(2,128)(2,1)S(1)} fusion(f32[8,256,8,256]{1,3,2,0:T(8,128)} %subtract_add_fusion.2, f32[8,8,256,1]{2,1,0,3:T(8,128)S(1)} %get-tuple-element.45), kind=kOutput, calls=%fused_computation.148 | convolution fusion | flops 50331648 | bytes 16875520 | tf_op jit(solution)/shard_map/transpose(jvp(snihm,snhm->snih))/dot_general | solution.py:98
  793.0 2.2 convolution_bitcast_fusion
  795.2 2.3 convolution_bitcast_fusion.3
  799.1 3.3 fusion.129
  805.2 3.4 collective-permute-done.8
  808.8 14.3 %fusion.126 = (f32[8,256,8]{1,2,0:T(8,128)S(1)}, f32[8,256,8,256]{1,3,2,0:T(8,128)}) fusion(f32[8,256,8,256]{1,3,2,0:T(8,128)S(1)} %bitcast.322, f32[8,256,8]{1,2,0:T(8,128)S(1)} %copy-done.38, bf16[8,8,256,64]{2,3,1,0:T(8,128)(2,1)} %collective-permute-done.11, f32[8,256,8,64]{1,3,2,0:T(8,128)} %copy-done.4, bf16[8,256,8,64]{1,3,2,0:T(8,128)(2,1)S(1)} %copy-done.9, ...), kind=kOutput, calls=%fused_computation.196 | convolution fusion | flops 565166080 | bytes 58916864 | tf_op jit(solution)/shard_map/transpose(jvp(snjhm,snjhe->snhme))/dot_general | solution.py:69
  823.1 15.7 %fusion.53 = bf16[8,256,8,64]{1,3,2,0:T(8,128)(2,1)S(1)} fusion(f32[8,256,8,64]{1,3,2,0:T(8,128)} %copy-done.19, f32[8,256,8]{1,2,0:T(8,128)S(1)} %negate_multiply_fusion, f32[8,256,8,256]{1,3,2,0:T(8,128)} %get-tuple-element.76, f32[64,256]{1,0:T(8,128)S(1)} %copy-done), kind=kOutput, calls=%fused_computation.86 | convolution fusion | flops 3226468352 | bytes 23199744 | tf_op jit(solution)/shard_map/transpose(jvp(...e,em->...m))/dot_general | solution.py:53
  845.0 3.1 fusion.77
  852.9 2.9 fusion.49
  855.9 2.4 fusion.51
  860.4 2.8 pad_maximum_fusion
  864.2 1.7 fusion.114
  866.0 1.7 fusion.112
  867.7 5.5 add_add_fusion.2
  873.3 135.2 %all-reduce.7.cloned.1.call-done = f32[1050624]{0:T(1024)} async-done(((f32[1050624]{0:T(1024)}), f32[1050624]{0:T(1024)}) %all-reduce.7.cloned.1.call-update) | async-done | bytes 4202512
  1008.5 1.9 fusion.116
  (243 shorter events, 54.5 us)
Async XLA Ops:
  8.0 189.6 %copy-start = (f32[64,256]{1,0:T(8,128)S(1)}, f32[64,256]{1,0:T(8,128)}, u32[]{:S(2)}) copy-start(f32[64,256]{1,0:T(8,128)} %param.16) | copy-start | bytes 196612
  8.0 3.5 copy-start.62
  8.0 181.3 %all-reduce.5.cloned.1.call-start = ((), (), s32[]{:S(2)}) async-start(), calls=%async_computation.10 | async-start | bytes 4202496
  11.5 440.6 %all-gather.5.cloned.1.call-start = ((), (), s32[]{:S(2)}) async-start(), calls=%async_computation.6 | async-start | bytes 10485760 | tf_op jit(solution)/shard_map/all_gather | solution.py:217
  11.5 5.1 copy-start.7
  16.5 447.1 %all-gather.3.cloned.1.call-start = ((), (), s32[]{:S(2)}) async-start(), calls=%async_computation.4 | async-start | bytes 10485760 | tf_op jit(solution)/shard_map/all_gather | solution.py:195
  193.5 4.0 copy-start.31
  196.2 20.2 %copy-start.26 = (bf16[8,256,512]{2,1,0:T(8,128)(2,1)}, bf16[8,256,512]{2,1,0:T(8,128)(2,1)S(1)}, u32[]{:S(2)}) copy-start(bf16[8,256,512]{2,1,0:T(8,128)(2,1)S(1)} %fusion.48) | copy-start | bytes 6291460
  197.6 18.9 %copy-start.20 = (f32[8,256,8,64]{1,3,2,0:T(8,128)}, f32[8,256,8,64]{1,3,2,0:T(8,128)S(1)}, u32[]{:S(2)}) copy-start(f32[8,256,8,64]{1,3,2,0:T(8,128)S(1)} %get-tuple-element.58) | copy-start | bytes 12582916
  197.6 80.2 %copy-start.41 = (f32[8,256,8]{1,2,0:T(8,128)}, f32[8,256,8]{1,2,0:T(8,128)S(1)}, u32[]{:S(2)}) copy-start(f32[8,256,8]{1,2,0:T(8,128)S(1)} %broadcast_multiply_fusion.1) | copy-start | bytes 196612
  221.8 18.7 %copy-start.19 = (f32[8,256,8,64]{1,3,2,0:T(8,128)}, f32[8,256,8,64]{1,3,2,0:T(8,128)S(1)}, u32[]{:S(2)}) copy-start(f32[8,256,8,64]{1,3,2,0:T(8,128)S(1)} %get-tuple-element.62) | copy-start | bytes 12582916
  221.9 18.7 %copy-start.37 = (f32[8,256,8]{1,2,0:T(8,128)}, f32[8,256,8]{1,2,0:T(8,128)S(1)}, u32[]{:S(2)}) copy-start(f32[8,256,8]{1,2,0:T(8,128)S(1)} %broadcast_multiply_fusion) | copy-start | bytes 196612
  240.6 12.5 %copy-start.1 = (f32[8,256,8,256]{1,3,2,0:T(8,128)}, f32[8,256,8,256]{1,3,2,0:T(8,128)S(1)}, u32[]{:S(2)}) copy-start(f32[8,256,8,256]{1,3,2,0:T(8,128)S(1)} %get-tuple-element.64) | copy-start | bytes 50331652
  253.1 72.0 %collective-permute-start.3 = (bf16[8,8,256]{2,1,0:T(8,128)(2,1)S(1)}, bf16[8,8,256]{2,1,0:T(8,128)(2,1)S(1)}, u32[]{:S(2)}, u32[]{:S(2)}) collective-permute-start(bf16[8,8,256]{2,1,0:T(8,128)(2,1)S(1)} %convert_element_type.227), channel_id=1, source_target_pairs={{0,1},{1,2},{2,3},{4,5},{5,6},{6,7},{8,9},{9,10},{10,11},{12,13},{... | collective-permute-start | bytes 98312 | tf_op jit(solution)/shard_map/ppermute | solution.py:31
  262.0 10.9 %copy-start.4 = (f32[8,256,8,64]{1,3,2,0:T(8,128)}, f32[8,256,8,64]{1,3,2,0:T(8,128)S(1)}, u32[]{:S(2)}) copy-start(f32[8,256,8,64]{1,3,2,0:T(8,128)S(1)} %get-tuple-element.66) | copy-start | bytes 12582916
  272.9 35.1 %collective-permute-start = (bf16[8,8,256,64]{2,3,1,0:T(8,128)(2,1)}, bf16[8,8,256,64]{2,3,1,0:T(8,128)(2,1)}, u32[]{:S(2)}, u32[]{:S(2)}) collective-permute-start(bf16[8,8,256,64]{2,3,1,0:T(8,128)(2,1)} %get-tuple-element.67), channel_id=1, source_target_pairs={{0,1},{1,2},{2,3},{4,5},{5,6},{6,7},{8,9},{9,10},{10,11},{12,13},{... | collective-permute-start | bytes 6291464 | tf_op jit(solution)/shard_map/ppermute | solution.py:31
  312.9 30.6 %collective-permute-start.1 = (bf16[8,8,256,64]{2,3,1,0:T(8,128)(2,1)}, bf16[8,8,256,64]{2,3,1,0:T(8,128)(2,1)}, u32[]{:S(2)}, u32[]{:S(2)}) collective-permute-start(bf16[8,8,256,64]{2,3,1,0:T(8,128)(2,1)} %add_convert_fusion.3), channel_id=1, source_target_pairs={{0,1},{1,2},{2,3},{4,5},{5,6},{6,7},{8,9},{9,10},{10,11},{12,13},{... | collective-permute-start | bytes 6291464 | tf_op jit(solution)/shard_map/ppermute | solution.py:31
  325.1 16.8 %collective-permute-start.4 = (bf16[8,8,256]{2,1,0:T(8,128)(2,1)S(1)}, bf16[8,8,256]{2,1,0:T(8,128)(2,1)S(1)}, u32[]{:S(2)}, u32[]{:S(2)}) collective-permute-start(bf16[8,8,256]{2,1,0:T(8,128)(2,1)S(1)} %add_convert_fusion.5), channel_id=1, source_target_pairs={{0,1},{1,2},{2,3},{4,5},{5,6},{6,7},{8,9},{9,10},{10,11},{12,13},{... | collective-permute-start | bytes 98312 | tf_op jit(solution)/shard_map/ppermute | solution.py:31
  341.9 9.9 copy-start.10
  341.9 19.3 %collective-permute-start.5 = (bf16[8,8,256]{2,1,0:T(8,128)(2,1)S(1)}, bf16[8,8,256]{2,1,0:T(8,128)(2,1)S(1)}, u32[]{:S(2)}, u32[]{:S(2)}) collective-permute-start(bf16[8,8,256]{2,1,0:T(8,128)(2,1)S(1)} %add_convert_fusion.4), channel_id=1, source_target_pairs={{0,1},{1,2},{2,3},{4,5},{5,6},{6,7},{8,9},{9,10},{10,11},{12,13},{... | collective-permute-start | bytes 98312 | tf_op jit(solution)/shard_map/ppermute | solution.py:31
  349.1 22.6 %collective-permute-start.2 = (bf16[8,8,256,64]{2,3,1,0:T(8,128)(2,1)}, bf16[8,8,256,64]{2,3,1,0:T(8,128)(2,1)}, u32[]{:S(2)}, u32[]{:S(2)}) collective-permute-start(bf16[8,8,256,64]{2,3,1,0:T(8,128)(2,1)} %add_convert_fusion.2), channel_id=1, source_target_pairs={{0,1},{1,2},{2,3},{4,5},{5,6},{6,7},{8,9},{9,10},{10,11},{12,13},{... | collective-permute-start | bytes 6291464 | tf_op jit(solution)/shard_map/ppermute | solution.py:31
  361.2 23.3 %copy-start.33 = (bf16[512,512]{1,0:T(8,128)(2,1)}, bf16[512,512]{1,0:T(8,128)(2,1)S(1)}, u32[]{:S(2)}) copy-start(bf16[512,512]{1,0:T(8,128)(2,1)S(1)} %slice.102) | copy-start | bytes 1572868
  361.3 10.4 %copy-start.17 = (f32[8,8,64,256]{3,2,1,0:T(8,128)S(1)}, f32[8,8,64,256]{3,2,1,0:T(8,128)}, u32[]{:S(2)}) copy-start(f32[8,8,64,256]{3,2,1,0:T(8,128)} %fusion.12) | copy-start | bytes 12582916
  388.8 176.4 %reduce-scatter.7.cloned.1.call-start = ((), (), s32[]{:S(2)}) async-start(), calls=%async_computation.7 | async-start | bytes 10485760 | tf_op jit(solution)/shard_map/reduce_scatter | solution.py:226
  484.4 6.8 copy-start.63
  491.2 148.2 %reduce-scatter.5.cloned.1.call-start = ((), (), s32[]{:S(2)}) async-start(), calls=%async_computation.5 | async-start | bytes 10485760 | tf_op jit(solution)/shard_map/reduce_scatter | solution.py:203
  501.6 14.5 %copy-start.58 = (f32[1,2,8,128]{3,2,1,0:T(8,128)S(1)}, f32[1,2,8,128]{3,2,1,0:T(8,128)}, u32[]{:S(2)}) copy-start(f32[1,2,8,128]{3,2,1,0:T(8,128)} %get-tuple-element.51) | copy-start | bytes 24580
  501.6 15.1 %copy-start.59 = (f32[1,2,8,128]{3,2,1,0:T(8,128)S(1)}, f32[1,2,8,128]{3,2,1,0:T(8,128)}, u32[]{:S(2)}) copy-start(f32[1,2,8,128]{3,2,1,0:T(8,128)} %get-tuple-element.49) | copy-start | bytes 24580
  501.6 361.7 %reduce-scatter.9.cloned.1.call-start = ((), (), s32[]{:S(2)}) async-start(), calls=%async_computation.8 | async-start | bytes 1179648 | tf_op jit(solution)/shard_map/reduce_scatter | solution.py:236
  516.1 349.9 %reduce-scatter.11.cloned.1.call-start = ((), (), s32[]{:S(2)}) async-start(), calls=%async_computation.9 | async-start | bytes 1179648 | tf_op jit(solution)/shard_map/reduce_scatter | solution.py:237
  528.7 479.7 %all-reduce.7.cloned.1.call-start = ((), (), s32[]{:S(2)}) async-start(), calls=%async_computation.11 | async-start | bytes 8404992
  565.1 4.0 copy-start.3
  565.1 4.7 copy-start.14
  639.4 5.9 copy-start.34
  651.3 11.3 %copy-start.5 = (f32[8,256,8,64]{1,3,2,0:T(8,128)S(1)}, f32[8,256,8,64]{1,3,2,0:T(8,128)}, u32[]{:S(2)}) copy-start(f32[8,256,8,64]{1,3,2,0:T(8,128)} %copy-done.4) | copy-start | bytes 12582916
  662.6 13.3 %copy-start.6 = (f32[64,8,8,256]{3,2,1,0:T(8,128)S(1)}, f32[64,8,8,256]{3,2,1,0:T(8,128)}, u32[]{:S(2)}) copy-start(f32[64,8,8,256]{3,2,1,0:T(8,128)} %copy.111) | copy-start | bytes 12582916
  662.6 13.3 %copy-start.18 = (f32[8,8,64,256]{3,2,1,0:T(8,128)S(1)}, f32[8,8,64,256]{3,2,1,0:T(8,128)}, u32[]{:S(2)}) copy-start(f32[8,8,64,256]{3,2,1,0:T(8,128)} %get-tuple-element.70) | copy-start | bytes 12582916
  674.3 56.4 %collective-permute-start.9 = (bf16[8,8,256,64]{2,3,1,0:T(8,128)(2,1)}, bf16[8,8,256,64]{2,3,1,0:T(8,128)(2,1)S(1)}, u32[]{:S(2)}, u32[]{:S(2)}) collective-permute-start(bf16[8,8,256,64]{2,3,1,0:T(8,128)(2,1)} %convert_bitcast_fusion), channel_id=1, source_target_pairs={{1,0},{2,1},{3,2},{5,4},{6,5},{7,6},{9,8},{10,9},{11,10},{13,12},{... | collective-permute-start | bytes 6291464 | tf_op jit(solution)/shard_map/ppermute | solution.py:31
  678.0 16.0 %copy-start.42 = (f32[8,256,8]{1,2,0:T(8,128)S(1)}, f32[8,256,8]{1,2,0:T(8,128)}, u32[]{:S(2)}) copy-start(f32[8,256,8]{1,2,0:T(8,128)} %copy-done.41) | copy-start | bytes 196612
  730.7 4.3 copy-start.21
  733.3 35.2 %collective-permute-start.10 = (bf16[8,8,256,64]{2,3,1,0:T(8,128)(2,1)S(1)}, bf16[8,8,256,64]{2,3,1,0:T(8,128)(2,1)S(1)}, u32[]{:S(2)}, u32[]{:S(2)}) collective-permute-start(bf16[8,8,256,64]{2,3,1,0:T(8,128)(2,1)S(1)} %add.241), channel_id=1, source_target_pairs={{1,0},{2,1},{3,2},{5,4},{6,5},{7,6},{9,8},{10,9},{11,10},{13,12},{... | collective-permute-start | bytes 6291464 | tf_op jit(solution)/shard_map/ppermute | solution.py:31
  770.9 37.8 %collective-permute-start.11 = (bf16[8,8,256,64]{2,3,1,0:T(8,128)(2,1)S(1)}, bf16[8,8,256,64]{2,3,1,0:T(8,128)(2,1)}, u32[]{:S(2)}, u32[]{:S(2)}) collective-permute-start(bf16[8,8,256,64]{2,3,1,0:T(8,128)(2,1)S(1)} %add.242), channel_id=1, source_target_pairs={{1,0},{2,1},{3,2},{5,4},{6,5},{7,6},{9,8},{10,9},{11,10},{13,12},{... | collective-permute-start | bytes 6291464 | tf_op jit(solution)/shard_map/ppermute | solution.py:31
  789.5 3.5 copy-start.12
  789.5 3.5 copy-start.23
  791.5 3.7 copy-start.27
  791.5 6.0 collective-permute-start.6
  793.0 15.7 %slice-start.2 = ((s8[16777216]{0:T(1024)(128)(4,1)}), s8[4194304]{0:T(1024)(128)(4,1)S(1)}, s32[]{:S(2)}) async-start(s8[16777216]{0:T(1024)(128)(4,1)} %bitcast.321), calls=%async_computation.14 | async-start | bytes 8388608
  793.0 15.7 %slice-start.3 = ((s8[16777216]{0:T(1024)(128)(4,1)}), s8[4194304]{0:T(1024)(128)(4,1)S(1)}, s32[]{:S(2)}) async-start(s8[16777216]{0:T(1024)(128)(4,1)} %bitcast.321), calls=%async_computation.15 | async-start | bytes 8388608
  795.2 3.9 copy-start.32
  795.2 13.5 %slice-start.4 = ((s8[16777216]{0:T(1024)(128)(4,1)}), s8[4194304]{0:T(1024)(128)(4,1)S(1)}, s32[]{:S(2)}) async-start(s8[16777216]{0:T(1024)(128)(4,1)} %bitcast.321), calls=%async_computation.16 | async-start | bytes 8388608
  797.5 7.4 copy-start.15
  797.5 11.2 %slice-start.5 = ((s8[16777216]{0:T(1024)(128)(4,1)}), s8[4194304]{0:T(1024)(128)(4,1)S(1)}, s32[]{:S(2)}) async-start(s8[16777216]{0:T(1024)(128)(4,1)} %bitcast.321), calls=%async_computation.17 | async-start | bytes 8388608
  797.5 11.2 %copy-start.9 = (bf16[8,256,8,64]{1,3,2,0:T(8,128)(2,1)S(1)}, bf16[8,256,8,64]{1,3,2,0:T(8,128)(2,1)}, u32[]{:S(2)}) copy-start(bf16[8,256,8,64]{1,3,2,0:T(8,128)(2,1)} %get-tuple-element.65) | copy-start | bytes 6291460
  797.5 11.2 %copy-start.38 = (f32[8,256,8]{1,2,0:T(8,128)S(1)}, f32[8,256,8]{1,2,0:T(8,128)}, u32[]{:S(2)}) copy-start(f32[8,256,8]{1,2,0:T(8,128)} %copy-done.37) | copy-start | bytes 196612
  797.5 5.8 collective-permute-start.7
  803.4 5.3 collective-permute-start.8
  838.8 4.9 slice-start
  840.8 2.9 slice-start.1
  852.9 2.9 copy-start.60
  855.8 3.6 copy-start.13
  855.8 3.1 copy-start.40
  867.7 140.8 %copy-start.43 = (f32[32832]{0:T(1024)S(1)}, f32[32832]{0:T(1024)}, u32[]{:S(2)}) copy-start(f32[32832]{0:T(1024)} %param.17) | copy-start | bytes 393988
  867.7 140.8 %copy-start.49 = (f32[32832]{0:T(1024)S(1)}, f32[32832]{0:T(1024)}, u32[]{:S(2)}) copy-start(f32[32832]{0:T(1024)} %param.18) | copy-start | bytes 393988
  867.7 140.8 %copy-start.50 = (f32[32832]{0:T(1024)S(1)}, f32[32832]{0:T(1024)}, u32[]{:S(2)}) copy-start(f32[32832]{0:T(1024)} %param.19) | copy-start | bytes 393988
  (26 other events, 51.6 us)
Sparse Core Ops, SparseCore 0:
  14.4 174.8 all-reduce.4
  863.4 145.0 all-reduce.6
Sparse Core Ops, SparseCore 1:
  16.6 61.2 all-gather.4
  388.8 60.1 all-gather.2
  491.3 73.8 reduce-scatter.6
  567.7 71.6 reduce-scatter.4
  642.8 63.5 reduce-scatter.8
  710.2 62.5 reduce-scatter.10
where the time goes:
time: 1030 us; the launch traced here: 1020 us
  waiting for transfers between devices  413 us (40%)
  matrix products  361 us (35%)
  other arithmetic  104 us (10%)
  blocking collectives  63.2 us (6%)
  local copies, waits for them, and re-layouts  34.1 us (3%)
  starting transfers between devices  25.4 us (2%)
  between operations  16.9 us (2%)
    unnamed x10, waiting for transfers between devices  306 us
    dot_general x4, matrix products, feature_map(): projected = jnp.einsum('...e,em->...m', scaled, omega, precision=PRECISE)  67.9 us
    reduce_scatter x1, waiting for transfers between devices, shards(): lax.psum_scatter(branch.reshape(seq_count, -1, model_width).astype(jnp.bf...  66.8 us
    dot_general x12, matrix products, contract(): lax.dot_general(left, right, (((left_dim,), (right_dim,)), ((), ())), pre...  59.6 us
    dot_general x3, matrix products, query_section(): jnp.einsum('snihm,snjhm->snhij', query_features, key_features)  50.4 us
    dot_general x3, matrix products, query_section(): jnp.einsum('snihm,snhme->snihe', query_features, state_before)  43.7 us
    dot_general x3, matrix products, query_section(): numerator = jnp.einsum('snhij,snjhe->snihe', scores, spanned)  42.4 us
    reduce_scatter x1, waiting for transfers between devices, shards(): lax.psum_scatter(normed_two_part.reshape(seq_count, -1, model_width).asty...  36.2 us
  transfers between devices with their start and end apart: 20, of which 6 were waited for; matrix products, arithmetic and copies ran while one was open for 45% of the time, Pallas kernels for 0%

commit v1 on v0

v1 whole, which is shorter than its diff:
```python
import functools
import math

import jax
import jax.numpy as jnp
from jax import lax
from jax.experimental import pallas as pl
from jax.experimental.pallas import tpu as pltpu
from jax.sharding import PartitionSpec as P

CH = 256
STEP = 10
BETA_FIRST = 0.9
BETA_SECOND = 0.999
ADAM_EPS = 1e-08
WEIGHT_DECAY = 0.1
RATE_MATRIX = 0.02
RATE_NORM = 0.3
NORM_EPS = 1e-05
SPARE = 16
VMEM_LIMIT = 16 * 1024 * 1024
BIG = 1 << 20
LIMITS = {'keys': 14, 'queries': 16, 'mix': 12, 'ffn': 40, 'outer': 14, 'back_query': 24, 'back_key': 34}
F32 = jnp.float32
LOW = jnp.bfloat16


def dot_nn(left, right):
    return lax.dot_general(left, right, (((1,), (0,)), ((), ())), preferred_element_type=F32)


def dot_nt(left, right):
    return lax.dot_general(left, right, (((1,), (1,)), ((), ())), preferred_element_type=F32)


def dot_tn(left, right):
    return lax.dot_general(left, right, (((0,), (0,)), ((), ())), preferred_element_type=F32)


def norm_parts(inputs):
    centre = inputs - jnp.mean(inputs, axis=-1, keepdims=True)
    root = lax.rsqrt(jnp.mean(centre * centre, axis=-1, keepdims=True) + NORM_EPS)
    return centre * root, root


def norm_back(grad, gain, unit, root):
    inner = grad * gain
    mean_inner = jnp.mean(inner, axis=-1, keepdims=True)
    return root * (inner - mean_inner - unit * jnp.mean(inner * unit, axis=-1, keepdims=True))


def causal(length):
    earlier = lax.broadcasted_iota(jnp.int32, (length, length), 0)
    return earlier <= lax.broadcasted_iota(jnp.int32, (length, length), 1)


def put_states(own_out, their_out, core, heads, size, states, copies):
    half = heads // 2
    base = half * size
    first = core[0] == 0
    own_out[0, base:] = jnp.zeros((SPARE, own_out.shape[2]), LOW)
    their_out[0, base:] = jnp.zeros((SPARE, own_out.shape[2]), LOW)
    for index in range(half):
        low, high = states[index], states[index + half]
        total_low, total_high = [
            sum(s[size + i : size + i + 1] for i in range(copies)) for s in (low, high)
        ]
        at = slice(index * size, (index + 1) * size)
        own_out[0, at] = jnp.where(first, low[:size], high[:size]).astype(LOW)
        their_out[0, at] = jnp.where(first, high[:size], low[:size]).astype(LOW)
        row = slice(base + index, base + index + 1)
        own_out[0, row] = jnp.where(first, total_low, total_high).astype(LOW)
        their_out[0, row] = jnp.where(first, total_high, total_low).astype(LOW)


def get_state(core, keep, come, head, heads, size, copies):
    part, index = divmod(head, heads // 2)
    base = heads // 2 * size
    own = core[0] == part
    total = jnp.where(own, keep[0, base : base + SPARE], come[0, base : base + SPARE]).astype(F32)[index : index + 1]
    line = lax.broadcasted_iota(jnp.int32, (SPARE, total.shape[1]), 0)
    spare = jnp.where(line < copies, total, 0.0).astype(LOW)
    rows = slice(index * size, (index + 1) * size)
    return jnp.concatenate([jnp.where(own, keep[0, rows], come[0, rows]), spare], axis=0)


def split_features(rows, scale, shift, high_out, stack, half):
    size = rows.shape[0]
    scaled = rows * scale
    high = scaled.astype(LOW)
    rest = (scaled - high.astype(F32)).astype(LOW)
    high_out[...] = high
    for part, piece in enumerate((high, high, rest, rest)):
        stack[part * size : (part + 1) * size] = piece
    half[...] = 0.5 * jnp.sum(scaled * scaled, axis=0, keepdims=True) + shift


def staged(count, *stages):
    for stage in stages:
        for item in range(count):
            stage(item)


def keys_kernel(
    heads,
    size,
    tok,
    norms,
    weights,
    omega,
    core,
    turned_out,
    uk_out,
    value_out,
    pk_out,
    own_out,
    their_out,
    rows,
    stacks,
    halves,
    states,
):
    width = heads * size
    length = tok.shape[1]
    unit, _ = norm_parts(tok[0].astype(F32))
    turned_out[0] = (unit * norms[0:1] + norms[1:2]).astype(LOW).T
    rows[...] = dot_nn(weights[width:], turned_out[0])
    spare = (lax.broadcasted_iota(jnp.int32, (SPARE, length), 0) < 2).astype(F32).astype(LOW)
    shift = 0.5 * math.log(omega.shape[0])

    def split(head):
        at = slice(head * size, (head + 1) * size)
        split_features(
            rows[at], size ** (-0.25), shift, uk_out.at[0, at], stacks.at[head], halves.at[head : head + 1]
        )
        value_out[0, head, :size] = rows[width + head * size : width + (head + 1) * size].astype(LOW)
        value_out[0, head, size:] = spare

    def feature(head):
        projected = dot_nn(omega[...], stacks[head])
        pk_out[0, head] = jnp.exp(projected - halves[head : head + 1]).astype(LOW)

    def local_state(head):
        states[head] = dot_nt(value_out[0, head], pk_out[0, head])

    staged(heads, split, feature, local_state)
    put_states(own_out, their_out, core, heads, size, states, 1)


def queries_kernel(heads, size, turned, weights, omega, value, pk, uq_out, pq_out, score_out, num_out, rows, stacks, halves):
    width = heads * size
    length = turned.shape[2]
    rows[...] = dot_nn(weights[:width], turned[0])
    shift = 0.5 * math.log(omega.shape[0])
    keep = causal(length)

    def split(head):
        at = slice(head * size, (head + 1) * size)
        split_features(
            rows[at], size ** (-0.25), shift, uq_out.at[0, at], stacks.at[head], halves.at[head : head + 1]
        )

    def feature(head):
        projected = dot_nn(omega[...], stacks[head])
        pq_out[0, head] = jnp.exp(projected - halves[head : head + 1]).astype(LOW)

    def score(head):
        score_out[0, head] = jnp.where(keep, dot_tn(pk[0, head], pq_out[0, head]), 0.0).astype(LOW)

    def numerator(head):
        num_out[0, head] = dot_nn(value[0, head], score_out[0, head])

    staged(heads, split, feature, score, numerator)


def mix_kernel(heads, size, tok, norms, out_weight, num, core, keep, come, pq, mixed_out, recip_out, middle_out, normed_out):
    state = (core, keep, come)
    for head in range(heads):
        at = head * size
        total = num[0, head] + dot_nn(get_state(*state, head, heads, size, 2), pq[0, head])
        recip = 1.0 / total[size : size + 1]
        mixed_out[0, at : at + size] = (total[:size] * recip).astype(LOW)
        recip_out[0, head : head + 1] = recip
    mixed = mixed_out[0]
    middle = tok[0].astype(F32) + dot_tn(mixed, out_weight[...])
    middle_out[0] = middle
    unit, _ = norm_parts(middle)
    normed_out[0] = (unit * norms[2:3] + norms[3:4]).astype(LOW)


def gelu_pair(hidden):
    slope = math.sqrt(2.0 / math.pi)
    square = hidden * hidden
    tanh = jnp.tanh(hidden * (slope + (slope * 0.044715) * square))
    upper = 0.5 + 0.5 * tanh
    inner = (0.5 * slope) + (1.5 * slope * 0.044715) * square
    return hidden * upper, upper + hidden * (1.0 - tanh * tanh) * inner


def ffn_kernel(
    groups, normed, middle, target, norms, pair, core, out, grad_out, leave, stay, norm_grad, first_sum, second_sum
):
    step = pl.program_id(0)
    half = pair.shape[2] // 2
    own = normed[...]
    grads = target[...]
    own_turned = own.T
    grads_turned = grads.T

    @pl.when(step == 0)
    def _():
        first_sum[...] = jnp.zeros_like(first_sum)
        second_sum[...] = jnp.zeros_like(second_sum)
        norm_grad[...] = jnp.zeros_like(norm_grad)

    result = jnp.zeros(own.shape, F32)
    grad_normed = jnp.zeros(own.shape, F32)
    for group in range(groups):
        first = pair[group, :, :half]
        second = pair[group, :, half:]
        active, slope = gelu_pair(dot_nn(own, first))
        active = active.astype(LOW)
        result = result + dot_nt(active, second)
        grad_hidden = (dot_nn(grads, second) * slope).astype(LOW)
        grad_normed = grad_normed + dot_nt(grad_hidden, first)
        first_sum[group] += dot_nn(own_turned, grad_hidden)
        second_sum[group] += dot_nn(grads_turned, active)
    rows = middle[...]
    out[...] = (rows + result).astype(LOW)
    unit, root = norm_parts(rows)
    grad_out[...] = grads.astype(F32) + norm_back(grad_normed, norms[2:3], unit, root)
    norm_grad[0:1] += jnp.sum(grad_normed * unit, axis=0, keepdims=True)
    norm_grad[1:2] += jnp.sum(grad_normed, axis=0, keepdims=True)

    @pl.when(step == pl.num_programs(0) - 1)
    def _():
        mine = core[0]
        for chip in range(groups // 2):
            at = 2 * half * chip
            for side, target_ref in ((mine, stay), (1 - mine, leave)):
                target_ref[:, at : at + half] = first_sum[2 * chip + side].astype(LOW)
                target_ref[:, at + half : at + 2 * half] = second_sum[2 * chip + side].astype(LOW)


def through_omega(flow, scaled, omega_low, size):
    back = dot_nn(omega_low, flow)
    return ((back[:size] - scaled.astype(F32) * back[size : size + 1]) * size ** (-0.25))


def outer_kernel(
    heads, size, grad_middle, out_weight, mixed, recip, pq, core, outer_out, own_out, their_out, out_proj, grad_mixed, states
):
    length = grad_middle.shape[1]

    @pl.when(pl.program_id(0) == 0)
    def _():
        out_proj[...] = jnp.zeros_like(out_proj)

    grad_low = grad_middle[0].astype(LOW)
    grad_mixed[...] = dot_nt(out_weight[...], grad_low)
    out_proj[...] += dot_nn(mixed[0], grad_low)
    line = lax.broadcasted_iota(jnp.int32, (SPARE, length), 0)

    def scale(head):
        at = head * size
        outer = grad_mixed[at : at + size] * recip[0, head : head + 1]
        centre = -jnp.sum(outer * mixed[0, at : at + size].astype(F32), axis=0, keepdims=True)
        rest = centre - centre.astype(LOW).astype(F32)
        outer_out[0, head, :size] = outer.astype(LOW)
        outer_out[0, head, size:] = jnp.where(line == 0, centre, jnp.where(line == 1, rest, 0.0)).astype(LOW)

    def local_state(head):
        states[head] = dot_nt(outer_out[0, head], pq[0, head])

    staged(heads, scale, local_state)
    put_states(own_out, their_out, core, heads, size, states, 2)


def back_query_kernel(
    heads,
    size,
    turned,
    omega_low,
    outers,
    value,
    pq,
    pk,
    scores,
    core,
    keep_state,
    come_state,
    uq,
    uk,
    query_out,
    key_out,
    value_out,
    query_weight,
    befores,
    grad_scores,
    flows,
    key_flows,
):
    @pl.when(pl.program_id(0) == 0)
    def _():
        query_weight[...] = jnp.zeros_like(query_weight)

    keep = causal(turned.shape[2])

    def score(head):
        befores[head] = get_state(core, keep_state, come_state, head, heads, size, 2)
        grad_scores[head] = jnp.where(keep, dot_tn(value[0, head], outers[0, head]), 0.0).astype(LOW)

    def feature(head):
        at = head * size
        grad_feat = dot_nn(pk[0, head], grad_scores[head]) + dot_tn(befores[head], outers[0, head])
        flows[head] = (grad_feat * pq[0, head].astype(F32)).astype(LOW)
        grad_key_feat = dot_nt(pq[0, head], grad_scores[head])
        key_flows[head] = (grad_key_feat * pk[0, head].astype(F32)).astype(LOW)
        value_out[0, at : at + size] = dot_nt(outers[0, head], scores[0, head])[:size].astype(LOW)

    def query(head):
        at = head * size
        query_out[0, at : at + size] = through_omega(flows[head], uq[0, at : at + size], omega_low[...], size).astype(
            LOW
        )
        key_out[0, at : at + size] = through_omega(key_flows[head], uk[0, at : at + size], omega_low[...], size).astype(LOW)

    staged(heads, score, feature, query)
    query_weight[...] += dot_nt(turned[0], query_out[0])


def back_key_kernel(
    heads,
    size,
    layout,
    tok,
    norms,
    grad_middle,
    weights,
    omega_low,
    value,
    pk,
    core,
    keep_state,
    come_state,
    uk,
    query_grad,
    key_part,
    value_part,
    query_weight,
    out_proj,
    norm_two,
    turned,
    input_grad,
    leave,
    stay,
    flat,
    laters,
    flows,
    pair_weight,
    norm_grad,
    whole,
):
    width = heads * size

    @pl.when(pl.program_id(0) == 0)
    def _():
        pair_weight[...] = jnp.zeros_like(pair_weight)
        norm_grad[...] = jnp.zeros_like(norm_grad)

    unit, root = norm_parts(tok[0].astype(F32))
    flat[:width] = query_grad[0]

    def later(head):
        laters[head] = get_state(core, keep_state, come_state, head, heads, size, 1)

    def feature(head):
        at = 2 * width + head * size
        grad_feat = dot_tn(laters[head], value[0, head])
        flows[head] = (grad_feat * pk[0, head].astype(F32)).astype(LOW)
        extra = dot_nn(laters[head], pk[0, head])[:size]
        flat[at : at + size] = (
            value_part[0, head * size : (head + 1) * size].astype(F32) + extra
        ).astype(LOW)

    def key(head):
        at = width + head * size
        part = slice(head * size, (head + 1) * size)
        total = key_part[0, part].astype(F32) + through_omega(flows[head], uk[0, part], omega_low[...], size)
        flat[at : at + size] = total.astype(LOW)

    staged(heads, later, feature, key)
    pair_weight[...] += dot_nt(turned[0], flat[width:])
    grad_normed = dot_tn(flat[...], weights[...])
    input_grad[0] = grad_middle[0] + norm_back(grad_normed, norms[0:1], unit, root)
    norm_grad[0:1] += jnp.sum(grad_normed * unit, axis=0, keepdims=True)
    norm_grad[1:2] += jnp.sum(grad_normed, axis=0, keepdims=True)

    @pl.when(pl.program_id(0) == pl.num_programs(0) - 1)
    def _():
        whole[:width] = query_weight[...]
        whole[width : 2 * width] = pair_weight[:, :width]
        whole[2 * width : 3 * width] = pair_weight[:, width:]
        whole[3 * width : 4 * width] = out_proj[...]
        whole[4 * width : 4 * width + 2] = norm_grad[...]
        whole[4 * width + 2 : 4 * width + 4] = norm_two[...]
        starts, rows, owners = layout
        half = width // 2
        first = core[0] == 0
        leave[...] = jnp.zeros_like(leave)
        stay[...] = jnp.zeros_like(stay)
        for part in range(2):
            count = leave.shape[1]
            columns = slice(part * half, (part + 1) * half)
            for spot in range(count):
                low = starts[owners[part][spot]]
                high = starts[owners[part][spot + count]]
                low = whole[low : low + rows, columns]
                high = whole[high : high + rows, columns]
                stay[part, spot, :rows] = jnp.where(first, low, high)
                leave[part, spot, :rows] = jnp.where(first, high, low).astype(LOW)


def per_seq(shape, offset=0):
    rest = tuple(shape[1:])
    return pl.BlockSpec((1,) + rest, lambda i: (i + offset,) + (0,) * len(rest))


def fixed(shape):
    return pl.BlockSpec(tuple(shape), lambda i: (0,) * len(shape))


def call(kernel, steps, args, in_specs, outs, out_specs, name, flops, scratch=(), aliases=None, after=(), chip=None):
    if chip is not None:
        args = tuple(
            on_chip(a) if i in chip else off_chip(a) if math.prod(a.shape) >= BIG else a for i, a in enumerate(args)
        )
    if after:
        count, body = len(args), kernel
        args = tuple(args) + tuple(after)
        in_specs = list(in_specs) + [pl.BlockSpec(memory_space=pl.ANY)] * len(after)

        def kernel(*refs):
            body(*refs[:count], *refs[count + len(after) :])

    moved = sum(math.prod(a.shape) * jnp.dtype(a.dtype).itemsize for a in list(args) + list(outs))
    return pl.pallas_call(
        kernel,
        grid=(steps,),
        in_specs=in_specs,
        out_specs=out_specs,
        out_shape=outs,
        scratch_shapes=list(scratch),
        name=name,
        input_output_aliases=aliases or {},
        compiler_params=pltpu.CompilerParams(
            dimension_semantics=("arbitrary",), vmem_limit_bytes=LIMITS[name] * 1024 * 1024
        ),
        cost_estimate=pl.CostEstimate(
            flops=flops, bytes_accessed=moved if flops > 1 else 1, transcendentals=0
        ),
    )(*args)


def on_chip(value):
    return pltpu.with_memory_space_constraint(value, pltpu.VMEM)


def off_chip(value):
    return pltpu.with_memory_space_constraint(value, pltpu.HBM)


def array(shape, dtype):
    return pltpu.HBM(tuple(shape), dtype)


def flip(value, axis, bit):
    return lax.ppermute(value, axis, [(i, i ^ (1 << bit)) for i in range(lax.axis_size(axis))])


def bit_of(axis, bit):
    return (lax.axis_index(axis) >> bit) & 1


def send_half(own, their, forward):
    count = lax.axis_size("seq")
    beside = flip(their, "seq", 0)
    mine = (own.astype(F32) + beside.astype(F32)).astype(LOW)
    far = None
    for step in range(1, count // 2):
        hop = 2 * step if forward else -2 * step
        pairs = [(i, i + hop) for i in range(count) if 0 <= i + hop < count]
        come = lax.ppermute(mine, "seq", pairs)
        far = come if far is None else far + come
    return beside, far, mine


def receive_half(own, beside, far, forward):
    core = bit_of("seq", 0)
    giver = (core == 0) if forward else (core == 1)
    give = (far.astype(F32) + jnp.where(giver, own.astype(F32), 0.0)).astype(LOW)
    keep = (far.astype(F32) + jnp.where(giver, 0.0, beside.astype(F32))).astype(LOW)
    return keep, flip(give, "seq", 0)


def axis_bits(axis):
    return lax.axis_size(axis).bit_length() - 1


def gather_orders():
    high = [("dp", bit) for bit in range(1, axis_bits("dp"))]
    seq_high = [("seq", bit) for bit in range(1, axis_bits("seq"))]
    near = [("dp", 0)]
    return [high + near + seq_high + [("seq", 0)], seq_high + high + near + [("seq", 0)]]


def scatter_orders():
    high = [("dp", bit) for bit in range(axis_bits("dp") - 1, 0, -1)]
    seq_high = [("seq", bit) for bit in range(axis_bits("seq") - 1, 0, -1)]
    near = [("dp", 0)]
    return [[("seq", 0)] + seq_high + near + high, [("seq", 0)] + near + high + seq_high]


def place_in(order, index):
    seq_bits = axis_bits("seq")
    spot = 0
    for axis, bit in order:
        shift = bit if axis == "seq" else bit + seq_bits
        spot = 2 * spot + ((index >> shift) & 1)
    return spot


def gather_doubling(value, order, early):
    value = value[None]
    for axis, bit in order:
        come = flip(value, axis, bit)
        early.append(come)
        low = bit_of(axis, bit) == 0
        value = jnp.concatenate([jnp.where(low, value, come), jnp.where(low, come, value)], axis=0)
    return value


def total_of(terms):
    return sum(term.astype(F32) for term in terms)


def scatter_step(terms, axis, bit, leave=None):
    mine = bit_of(axis, bit)
    if leave is None:
        leave = total_of([lax.dynamic_index_in_dim(term, 1 - mine, 0, keepdims=False) for term in terms]).astype(LOW)
    come = flip(leave, axis, bit)
    stay = total_of([lax.dynamic_index_in_dim(term, mine, 0, keepdims=False) for term in terms])
    return [stay, come]


def split_rows(terms, axis, bits, low):
    ways = 1 << len(bits)
    terms = [t.reshape(-1, ways, low, t.shape[1]) for t in terms]
    shift = min(bits)
    mine = (lax.axis_index(axis) >> shift) & (ways - 1)

    def part(which):
        total = total_of([lax.dynamic_index_in_dim(t, which, 1, keepdims=False) for t in terms]).astype(LOW)
        return total.reshape(-1, total.shape[-1])

    leaving = [part(mine ^ other) for other in range(1, ways)]
    size = lax.axis_size(axis)
    come = [
        lax.ppermute(leave, axis, [(i, i ^ (other << shift)) for i in range(size)])
        for other, leave in enumerate(leaving, 1)
    ]
    return leaving, [part(mine)] + come


def scatter_halving(terms, order):
    for axis, bit in order:
        terms = scatter_step([t.reshape((2, t.shape[0] // 2) + t.shape[1:]) for t in terms], axis, bit)
    return total_of(terms)[0]


def adamw(weight, first, second, grad, rate, decay):
    first_new = BETA_FIRST * first + (1.0 - BETA_FIRST) * grad
    second_new = BETA_SECOND * second + (1.0 - BETA_SECOND) * grad * grad
    first_hat = first_new / (1.0 - BETA_FIRST**STEP)
    second_hat = second_new / (1.0 - BETA_SECOND**STEP)
    weight_new = weight - rate * (first_hat / (jnp.sqrt(second_hat) + ADAM_EPS) + decay * weight)
    return (weight_new, first_new, second_new)


def unpack_kernel(starts, spots, rows, left, right, wide_out, out_weight, norms, whole):
    whole[...] = jnp.zeros_like(whole)
    half = left.shape[2]
    for index, start in enumerate(starts):
        whole[start : start + rows, :half] += left[spots[0][index], :rows].astype(F32)
        whole[start : start + rows, half:] += right[spots[1][index], :rows].astype(F32)
    width = out_weight.shape[0]
    for part in range(3):
        wide_out[part * width : (part + 1) * width] = whole[part * width : (part + 1) * width].astype(LOW).T
    out_weight[...] = whole[3 * width : 4 * width].astype(LOW)
    norms[...] = whole[4 * width : 4 * width + 4]


def shards(
    tokens,
    cotangent,
    masked,
    omega,
    att_weights,
    att_first,
    att_second,
    ffn_in,
    ffn_out,
    ffn_in_first,
    ffn_in_second,
    ffn_out_first,
    ffn_out_second,
):
    seqs, length, width = tokens.shape
    size, count = omega.shape
    heads = width // size
    square = width * width
    groups = lax.axis_size("seq")
    devices = lax.axis_size("dp") * groups
    shard_len = att_weights.shape[0]
    place = lax.axis_index(("dp", "seq"))
    starts = [(i * shard_len) // width for i in range(devices)]
    offsets = [(i * shard_len) % width for i in range(devices)]
    rows = -(-(max(offsets) + shard_len) // width)
    held_rows = -(-rows // 8) * 8
    offset = (place * shard_len) % width

    framed = lax.dynamic_update_slice(
        jnp.zeros((held_rows * width,), LOW), att_weights.astype(LOW), (offset,)
    ).reshape(held_rows, width)
    early = []
    halves = [framed[:, : width // 2], framed[:, width // 2 :]]
    gathered = [gather_doubling(half, order, early) for half, order in zip(halves, gather_orders())]
    spots = [[place_in(order[::-1], i) for i in range(devices)] for order in gather_orders()]
    whole_rows = -(-(starts[-1] + rows) // 8) * 8
    group_width = ffn_in.shape[1]
    pair = jnp.concatenate([ffn_in.astype(LOW), ffn_out.astype(LOW).T], axis=1)
    pair, early[0] = lax.optimization_barrier((pair, early[0]))
    pair = lax.all_gather(pair, ("seq", "dp"), axis=0, tiled=True)
    pair = pair.reshape(groups, width, 2 * group_width)

    weights, out_weight, norms = pl.pallas_call(
        functools.partial(unpack_kernel, starts, spots, rows),
        out_shape=[array((3 * width, width), LOW), array((width, width), LOW), array((4, width), F32)],
        scratch_shapes=[pltpu.VMEM((whole_rows, width), F32)],
        name="unpack",
        compiler_params=pltpu.CompilerParams(vmem_limit_bytes=VMEM_LIMIT),
    )(*gathered)

    first_shape = (width, groups * group_width)
    target = (cotangent.astype(F32) * masked.astype(F32)[:, :, None]).astype(LOW)
    omega_high = lax.reduce_precision(omega, 8, 7)
    omega_rest = omega - omega_high
    omega_parts = jnp.concatenate([omega_high, omega_rest, omega_high, omega_rest], axis=0).T.astype(LOW)
    omega_low = jnp.concatenate(
        [omega, jnp.ones((1, count), F32), jnp.zeros((SPARE - 1, count), F32)], axis=0
    ).astype(LOW)

    ext = size + SPARE
    unit = 2 * heads * length * length * length * seqs
    flat = (seqs, width, length)
    feat = (seqs, heads, count, length)
    held = (seqs, heads, ext, length)
    score_shape = (seqs, heads, length, length)
    recip_shape = (seqs, heads, length)
    state_rows = heads // 2 * size + SPARE
    state_shape = (seqs, state_rows, count)
    core = bit_of("seq", 0).astype(jnp.int32).reshape(1)
    in_smem = pl.BlockSpec(memory_space=pltpu.SMEM)

    def spec(value):
        return per_seq(value.shape) if value.shape[0] == seqs else fixed(value.shape)

    def scratch_rows(parts):
        return [
            pltpu.VMEM((parts * width, length), F32),
            pltpu.VMEM((heads, 4 * size, length), LOW),
            pltpu.VMEM((heads, length), F32),
        ]

    tokens, target, omega_low = lax.optimization_barrier((tokens, target, omega_low))
    args = (tokens, norms, weights, omega_parts)
    outs = [array(flat, LOW)] * 2 + [array(held, LOW), pltpu.VMEM(feat, LOW)] + [array(state_shape, LOW)] * 2
    turned, uk, value, pk, own, their = call(
        functools.partial(keys_kernel, heads, size),
        seqs,
        args + (core,),
        [spec(a) for a in args] + [in_smem],
        outs,
        [spec(a) for a in outs],
        "keys",
        1,
        chip=(),
        scratch=scratch_rows(2) + [pltpu.VMEM((heads, ext, count), F32)],
    )
    beside, far, mine = send_half(own, their, True)
    args = (turned, weights, omega_parts, value, pk)
    outs = [array(flat, LOW), pltpu.VMEM(feat, LOW), array(score_shape, LOW), pltpu.VMEM(held, F32)]
    uq, pq, score, num = call(
        functools.partial(queries_kernel, heads, size),
        seqs,
        args,
        [spec(a) for a in args],
        outs,
        [spec(a) for a in outs],
        "queries",
        1,
        scratch_rows(1),
        chip=(4,),
        after=(mine,),
    )
    far, uq = lax.optimization_barrier((far, uq))
    keep, come = receive_half(own, beside, far, True)
    states = [per_seq(keep.shape)] * 2
    outs = [array(flat, LOW), array(recip_shape, F32), array(tokens.shape, F32), array(tokens.shape, LOW)]
    mixed, recip, middle, normed_two = call(
        functools.partial(mix_kernel, heads, size),
        seqs,
        (tokens, norms, out_weight, num, core, keep, come, pq),
        [spec(tokens), spec(norms), spec(out_weight), spec(num), in_smem, *states, spec(pq)],
        outs,
        [spec(a) for a in outs],
        "mix",
        1,
        chip=(3, 7),
    )

    total_rows = seqs * length
    block = 2 * length
    by_block = pl.BlockSpec((block, width), lambda i: (i, 0))
    rows_shape = (total_rows, width)
    block_out, grad_middle, leave, stay, norm_two_grad = call(
        functools.partial(ffn_kernel, groups),
        total_rows // block,
        (*[a.reshape(rows_shape) for a in (normed_two, middle, target)], norms, pair, core),
        [by_block, by_block, by_block, fixed(norms.shape), fixed(pair.shape), in_smem],
        [array(rows_shape, LOW), array(rows_shape, F32)] + [array(first_shape, LOW)] * 2 + [array((2, width), F32)],
        [by_block, by_block, fixed(first_shape), fixed(first_shape), fixed((2, width))],
        "ffn",
        20 * unit,
        chip=(),
        scratch=[pltpu.VMEM((groups, width, group_width), F32)] * 2,
    )
    block_out = block_out.reshape(tokens.shape)
    grad_middle = grad_middle.reshape(tokens.shape)
    come_pair = flip(leave, "seq", 0)

    args = (grad_middle, out_weight, mixed, recip, pq)
    outs = [array(held, LOW)] + [array(state_shape, LOW)] * 2
    outs = outs + [array((width, width), F32)]
    outers, own, their, out_proj = call(
        functools.partial(outer_kernel, heads, size),
        seqs,
        args + (core,),
        [spec(a) for a in args] + [in_smem],
        outs,
        [spec(a) for a in outs],
        "outer",
        1,
        chip=(),
        scratch=[pltpu.VMEM((width, length), F32), pltpu.VMEM((heads, ext, count), F32)],
    )
    their, come_pair = lax.optimization_barrier((their, come_pair))
    dp_rows = width // lax.axis_size("dp")
    near_sent, terms = split_rows([stay, come_pair], "dp", [0], dp_rows)
    beside, far, mine = send_half(own, their, False)
    args = (turned, omega_low, outers, value, pq, pk, score, core, keep, come, uq, uk)
    outs = [array(flat, LOW)] * 3
    query_grad, key_part, value_part, query_weight = call(
        functools.partial(back_query_kernel, heads, size),
        seqs,
        args,
        [spec(a) for a in args[:7]] + [in_smem, *states, spec(uq), spec(uk)],
        outs + [array((width, width), F32)],
        [spec(a) for a in outs] + [fixed((width, width))],
        "back_query",
        1,
        chip=(),
        scratch=[
            pltpu.VMEM((heads, ext, count), LOW),
            pltpu.VMEM(score_shape[1:], LOW),
            pltpu.VMEM(feat[1:], LOW),
            pltpu.VMEM(feat[1:], LOW),
        ],
        after=(mine, *near_sent),
    )
    far, query_grad = lax.optimization_barrier((far, query_grad))
    keep, come = receive_half(own, beside, far, False)
    high = list(range(axis_bits("dp") - 1, 0, -1))
    near_sent, terms = split_rows(terms, "dp", high[:2], dp_rows << max(len(high) - 2, 0))
    orders = scatter_orders()
    owners = [sorted(range(devices), key=lambda i: place_in(order, i)) for order in orders]
    piece_shape = (2, devices // 2, held_rows, width // 2)
    args = (tokens, norms, grad_middle, weights, omega_low, value, pk, core, keep, come)
    more = (uk, query_grad, key_part, value_part, query_weight, out_proj, norm_two_grad, turned)
    input_grad, leave, stay = call(
        functools.partial(back_key_kernel, heads, size, (starts, rows, owners)),
        seqs,
        args + more,
        [spec(a) for a in args[:7]] + [in_smem, *states] + [spec(a) for a in more],
        [array(tokens.shape, F32), array(piece_shape, LOW), array(piece_shape, F32)],
        [per_seq(tokens.shape), fixed(piece_shape), fixed(piece_shape)],
        "back_key",
        7 * unit,
        chip=(),
        scratch=[
            pltpu.VMEM((3 * width, length), LOW),
            pltpu.VMEM((heads, ext, count), LOW),
            pltpu.VMEM(feat[1:], LOW),
            pltpu.VMEM((width, 2 * width), F32),
            pltpu.VMEM((2, width), F32),
            pltpu.VMEM((whole_rows, width), F32),
        ],
        after=tuple(near_sent),
    )
    leave, terms = lax.optimization_barrier((leave, terms))
    come_pieces = flip(leave, "seq", 0)
    for step, bit in enumerate(high[2:]):
        _, terms = split_rows(terms, "dp", [bit], dp_rows << (len(high) - 3 - step))
    terms, come_pieces = lax.optimization_barrier(([total_of(terms)], come_pieces))
    for bit in range(axis_bits("seq") - 1, 0, -1):
        terms = [t.reshape(t.shape[0], 2, -1) for t in terms]
        side = bit_of("seq", bit)
        sent = total_of([lax.dynamic_index_in_dim(t, 1 - side, 1, keepdims=False) for t in terms]).astype(LOW)
        kept = total_of([lax.dynamic_index_in_dim(t, side, 1, keepdims=False) for t in terms])
        terms = [kept, flip(sent, "seq", bit)]
    sums = []
    for index, order in enumerate(orders):
        sums.append(scatter_halving([stay[index], come_pieces[index]], order[1:]))
    own_pair = total_of(terms)
    grad_first = own_pair[:, :group_width]
    grad_second = own_pair[:, group_width:].T
    att_grad = jnp.concatenate(sums, axis=1)
    att_grad = lax.dynamic_slice(att_grad.reshape(-1), (offset,), (shard_len,)).astype(F32)

    position = place * shard_len + jnp.arange(shard_len, dtype=jnp.int32)
    is_matrix = position < 4 * square
    rate = jnp.where(is_matrix, RATE_MATRIX, RATE_NORM)
    decay = jnp.where(is_matrix, WEIGHT_DECAY, 0.0)
    att_new, att_first_new, att_second_new = adamw(
        att_weights, att_first, att_second, att_grad, rate, decay
    )
    ffn_in_new, ffn_in_first_new, ffn_in_second_new = adamw(
        ffn_in, ffn_in_first, ffn_in_second, grad_first, RATE_MATRIX, WEIGHT_DECAY
    )
    ffn_out_new, ffn_out_first_new, ffn_out_second_new = adamw(
        ffn_out, ffn_out_first, ffn_out_second, grad_second, RATE_MATRIX, WEIGHT_DECAY
    )
    return (
        block_out,
        input_grad,
        att_new,
        att_first_new,
        att_second_new,
        att_new.astype(jnp.bfloat16),
        ffn_in_new,
        ffn_in_first_new,
        ffn_in_second_new,
        ffn_in_new.astype(jnp.bfloat16),
        ffn_out_new,
        ffn_out_first_new,
        ffn_out_second_new,
        ffn_out_new.astype(jnp.bfloat16),
    )


def solution(mesh):
    in_specs = (
        P("dp", "seq", None),
        P("dp", "seq", None),
        P("dp", "seq"),
        P(),
        P(("dp", "seq")),
        P(("dp", "seq")),
        P(("dp", "seq")),
        P("dp", "seq"),
        P("seq", "dp"),
        P("dp", "seq"),
        P("dp", "seq"),
        P("seq", "dp"),
        P("seq", "dp"),
    )
    out_specs = (
        P("dp", "seq", None),
        P("dp", "seq", None),
        P(("dp", "seq")),
        P(("dp", "seq")),
        P(("dp", "seq")),
        P(("dp", "seq")),
        P("dp", "seq"),
        P("dp", "seq"),
        P("dp", "seq"),
        P("dp", "seq"),
        P("seq", "dp"),
        P("seq", "dp"),
        P("seq", "dp"),
        P("seq", "dp"),
    )
    return jax.shard_map(shards, mesh=mesh, in_specs=in_specs, out_specs=out_specs, check_vma=False)
```

time: 1030 us -> 286 us (0.28); the launches traced: 1020 us -> 285 us
  matrix products: 361 us -> 0 us
  waiting for transfers between devices: 413 us -> 65.2 us
  Pallas kernels: 0 us -> 131 us
  other arithmetic: 104 us -> 28 us
  blocking collectives: 63.2 us -> 0 us
  local copies, waits for them, and re-layouts: 34.1 us -> 14.4 us
    dot_general x36 -> x0, matrix products: 361 us -> none  [the longest x4 67.9 us: feature_map(): projected = jnp.einsum('...e,em->...m', scaled, omega, precision=PRECISE)]
    unnamed x10 -> x1, waiting for transfers between devices: 306 us -> 0.02 us
    pallas_call x0 -> x8, Pallas kernels: none -> 131 us  [the longest x7 128 us: call(): pl.pallas_call(kernel, grid=(steps,), in_specs=in_specs, out_specs=out_sp...]
    reduce_scatter x4 -> x0, waiting for transfers between devices: 103 us -> none  [the longest x1 66.8 us: shards(): lax.psum_scatter(branch.reshape(seq_count, -1, model_width).astype(jnp.bf...]
    all_gather x2 -> x0, blocking collectives: 63.2 us -> none  [the longest x1 31.7 us: shards(): lax.all_gather(ffn_in.astype(jnp.bfloat16), 'dp', axis=0, tiled=True)]
    ppermute x12 -> x31, waiting for transfers between devices: 4.4 us -> 65.1 us  [the longest x25 51.7 us: flip(): lax.ppermute(value, axis, [(i, i ^ 1 << bit) for i in range(lax.axis_size...]
    reduce_sum x10 -> x0, other arithmetic: 34.3 us -> none  [the longest x1 12.5 us: key_section(): span_total = jnp.sum(features, axis=2)]
    add x7 -> x2, other arithmetic: 30.7 us -> 0.19 us  [total_of(): return sum((term.astype(F32) for term in terms))]
  transfers between devices with their start and end apart: 20 -> 32, of which waited for: 6 -> 19; matrix products, arithmetic and copies ran while one was open for 45% -> 10% of each run, Pallas kernels for 0% -> 32%
where the time goes in v1:
time: 286 us; the launch traced here: 285 us
  Pallas kernels  131 us (46%)
  waiting for transfers between devices  65.2 us (23%)
  starting transfers between devices  32.3 us (11%)
  other arithmetic  28 us (10%)
  between operations  14.7 us (5%)
  local copies, waits for them, and re-layouts  14.4 us (5%)
    pallas_call x7, Pallas kernels, call(): pl.pallas_call(kernel, grid=(steps,), in_specs=in_specs, out_specs=out_sp...  128 us
    ppermute x25, waiting for transfers between devices, flip(): lax.ppermute(value, axis, [(i, i ^ 1 << bit) for i in range(lax.axis_size...  51.7 us
    ppermute x25, starting transfers between devices, flip(): lax.ppermute(value, axis, [(i, i ^ 1 << bit) for i in range(lax.axis_size...  23.3 us
    ppermute x2, waiting for transfers between devices, send_half(): come = lax.ppermute(mine, 'seq', pairs)  13.4 us
    unnamed x73, local copies, waits for them, and re-layouts  9.13 us
  transfers between devices with their start and end apart: 32, of which 19 were waited for; matrix products, arithmetic and copies ran while one was open for 10% of the time, Pallas kernels for 32%

profile of v1, /device:TPU:0, one launch (start us, length us, event | category | flops | bytes accessed | tf_op | source)
XLA Modules:
  0.0 285.1 jit_solution(12986939378475546273)
XLA Ops:
  7.2 0.9 convert_element_type.358
  8.2 0.8 dynamic_update_slice.3
  9.1 3.1 %collective-permute-start = (bf16[1,72,256]{2,1,0:T(8,128)(2,1)S(1)}, bf16[1,72,256]{2,1,0:T(8,128)(2,1)S(1)}, u32[]{:S(2)}, u32[]{:S(2)}) collective-permute-start(bf16[1,72,256]{2,1,0:T(8,128)(2,1)S(1)} %get-tuple-element.177), channel_id=1, source_target_pairs={{0,8},{4,12},{8,0},{12,4},{16,24},{20,28},{24,16},{28,20},{1,9},{5... | collective-permute-start | bytes 110600 | tf_op jit(solution)/shard_map/ppermute | solution.py:478
  12.2 1.5 collective-permute-start.5
  13.7 0.9 convert_bitcast_fusion
  14.6 0.9 convert_element_type.366
  16.2 0.7 convert_element_type.356
  16.9 3.4 %multiply_convert_fusion = bf16[8,256,512]{2,1,0:T(8,128)(2,1)} fusion(bf16[8,256,512]{2,1,0:T(8,128)(2,1)} %param.14, f32[8,256]{1,0:T(8,128)S(1)} %convert_element_type.356), kind=kLoop, calls=%fused_computation | loop fusion | flops 3145728 | bytes 4202496 | tf_op jit(solution)/shard_map/convert_element_type | solution.py:655
  20.4 2.7 collective-permute-start.1
  23.8 2.7 collective-permute-done.1
  26.4 1.0 collective-permute-done.6
  27.5 0.9 collective-permute-start.7
  28.6 1.6 collective-permute-start.2
  30.2 8.0 %collective-permute-done.7 = bf16[4,72,256]{2,1,0:T(8,128)(2,1)S(1)} collective-permute-done((bf16[4,72,256]{2,1,0:T(8,128)(2,1)S(1)}, bf16[4,72,256]{2,1,0:T(8,128)(2,1)S(1)}, u32[]{:S(2)}, u32[]{:S(2)}) %collective-permute-start.7) | collective-permute-done | bytes 147488 | tf_op jit(solution)/shard_map/ppermute | solution.py:478
  38.3 1.6 collective-permute-start.8
  39.9 0.9 collective-permute-start.3
  40.8 7.0 %collective-permute-done.8 = bf16[8,72,256]{2,1,0:T(8,128)(2,1)S(1)} collective-permute-done((bf16[8,72,256]{2,1,0:T(8,128)(2,1)S(1)}, bf16[8,72,256]{2,1,0:T(8,128)(2,1)S(1)}, u32[]{:S(2)}, u32[]{:S(2)}) %collective-permute-start.8) | collective-permute-done | bytes 294944 | tf_op jit(solution)/shard_map/ppermute | solution.py:478
  47.9 2.3 collective-permute-done.3
  50.3 0.9 pad_maximum_fusion.2
  51.6 1.8 collective-permute-done.4
  53.5 2.2 unpack.1
  55.8 1.4 copy-done.2
  57.2 0.7 copy-done.8
  57.9 15.1 %keys.1 = (bf16[8,512,256]{2,1,0:T(8,128)(2,1)}, bf16[8,512,256]{2,1,0:T(8,128)(2,1)}, bf16[8,8,80,256]{3,2,1,0:T(8,128)(2,1)}, bf16[8,8,256,256]{3,2,1,0:T(8,12...) custom-call(bf16[8,256,512]{2,1,0:T(8,128)(2,1)} %refs_0_, f32[4,512]{1,0:T(4,128)S(1)} %copy-done.8, ...), custom_call_target="tpu_custom_call" | custom-call | flops 1 | bytes 1 | tf_op jit(solution)/shard_map/keys/pallas_call | solution.py:447
  73.2 2.9 %collective-permute-done.10 = bf16[8,272,256]{2,1,0:T(8,128)(2,1)S(1)} collective-permute-done((bf16[8,272,256]{2,1,0:T(8,128)(2,1)}, bf16[8,272,256]{2,1,0:T(8,128)(2,1)S(1)}, u32[]{:S(2)}, u32[]{:S(2)}) %collective-permute-start.10) | collective-permute-done | bytes 1114144 | tf_op jit(solution)/shard_map/ppermute | solution.py:478
  76.1 1.9 fusion.refs_5_
  78.0 3.1 %collective-permute-start.11 = (bf16[8,272,256]{2,1,0:T(8,128)(2,1)S(1)}, bf16[8,272,256]{2,1,0:T(8,128)(2,1)S(1)}, u32[]{:S(2)}, u32[]{:S(2)}) collective-permute-start(bf16[8,272,256]{2,1,0:T(8,128)(2,1)S(1)} %fusion.refs_5_), channel_id=1, source_target_pairs={{0,2},{1,3},{4,6},{5,7},{8,10},{9,11},{12,14},{13,15},{16,18},{17,... | collective-permute-start | bytes 3342344 | tf_op jit(solution)/shard_map/ppermute | solution.py:493
  81.1 12.8 %queries.1 = (bf16[8,512,256]{2,1,0:T(8,128)(2,1)}, bf16[8,8,256,256]{3,2,1,0:T(8,128)(2,1)S(1)}, bf16[8,8,256,256]{3,2,1,0:T(8,128)(2,1)}, f32[8,8,80,256]{3,2,1,0:T(8,128)S(1)}) custom-call(bf16[8,512,256]{2,1,0:T(8,128)(2,1)} %get-tuple-element.68.refs_0_.refs_17_, bf16[1536,512]{1,0:T(8,128)(2,1)S(1)} %copy-done.3, ...), custom_call_target="tpu_custom_call" | custom-call | flops 1 | bytes 1 | tf_op jit(solution)/shard_map/queries/pallas_call | solution.py:447
  93.9 11.0 %collective-permute-done.11 = bf16[8,272,256]{2,1,0:T(8,128)(2,1)S(1)} collective-permute-done((bf16[8,272,256]{2,1,0:T(8,128)(2,1)S(1)}, bf16[8,272,256]{2,1,0:T(8,128)(2,1)S(1)}, u32[]{:S(2)}, u32[]{:S(2)}) %collective-permute-start.11) | collective-permute-done | bytes 1114144 | tf_op jit(solution)/shard_map/ppermute | solution.py:493
  105.7 2.7 collective-permute-done.12.come.refs_9_
  108.4 9.1 %mix.1 = (bf16[8,512,256]{2,1,0:T(8,128)(2,1)}, f32[8,8,256]{2,1,0:T(8,128)}, f32[8,256,512]{2,1,0:T(8,128)}, bf16[8,256,512]{2,1,0:T(8,128)(2,1)}) custom-call(bf16[8,256,512]{2,1,0:T(8,128)(2,1)} %refs_0_, f32[4,512]{1,0:T(4,128)S(1)} %copy-done.9, bf16[512,512]{1,0:T(8,128)(2,1)S(1)} %copy-done.6, f32[8,8,80,256]{3,2,1,0:T(8,128)S(1)} %get-tuple-element.73.num, ...), custom_call_target="tpu_custom_call" | custom-call | flops 1 | bytes 1 | tf_op jit(solution)/shard_map/mix/pallas_call | solution.py:447
  117.5 3.3 %copy-done = bf16[8,8,256,256]{3,2,1,0:T(8,128)(2,1)} copy-done((bf16[8,8,256,256]{3,2,1,0:T(8,128)(2,1)}, bf16[8,8,256,256]{3,2,1,0:T(8,128)(2,1)S(1)}, u32[]{:S(2)}) %copy-start) | copy-done | bytes 8388632
  120.8 1.0 copy-done.4
  121.8 39.2 %ffn.1 = (bf16[2048,512]{1,0:T(8,128)(2,1)}, f32[2048,512]{1,0:T(8,128)}, bf16[512,2048]{1,0:T(8,128)(2,1)}, bf16[512,2048]{1,0:T(8,128)(2,1)}, f32[2,512]{1,0:T(2,128)}) custom-call(bf16[2048,512]{1,0:T(8,128)(2,1)} %bitcast.121, f32[2048,512]{1,0:T(8,128)} %bitcast.120, bf16[2048,512]{1,0:T(8,128)(2,1)} %bitcast.108, f32[4,512]{1,0:T(4,128)S(1)} %copy-done.9, ...), custom_call_target="tpu_custom_call" | custom-call | flops 42949672960 | bytes 23080964 | tf_op jit(solution)/shard_map/ffn/pallas_call | solution.py:447
  161.3 11.3 %outer.1 = (bf16[8,8,80,256]{3,2,1,0:T(8,128)(2,1)}, bf16[8,272,256]{2,1,0:T(8,128)(2,1)}, bf16[8,272,256]{2,1,0:T(8,128)(2,1)}, f32[512,512]{1,0:T(8,128)}) custom-call(f32[8,256,512]{2,1,0:T(8,128)} %bitcast.102, bf16[512,512]{1,0:T(8,128)(2,1)S(1)} %copy-done.6, bf16[8,512,256]{2,1,0:T(8,128)(2,1)} %get-tuple-element.84.mixed, ...), custom_call_target="tpu_custom_call" | custom-call | flops 1 | bytes 1 | tf_op jit(solution)/shard_map/outer/pallas_call | solution.py:447
  173.0 2.6 collective-permute-done.14
  175.6 1.0 copy-done.14
  176.6 2.6 fusion.3.refs_12_
  179.2 1.5 collective-permute-start.15
  180.7 4.5 %add_convert_fusion = (bf16[4,1,64,2048]{3,2,1,0:T(8,128)(2,1)}, bf16[4,1,64,2048]{3,2,1,0:T(8,128)(2,1)}) fusion(bf16[4,2,64,2048]{3,2,1,0:T(8,128)(2,1)} %bitcast.110, s32[]{:T(128)S(6)} %select_n.271, bf16[4,2,64,2048]{3,2,1,0:T(8,128)(2,1)} %bitcast.109, s32[]{:T(128)S(6)} %select_n.267), kind=kLoop, calls=%fused_computation.17 | loop fusion | flops 4194304 | bytes 6291464 | tf_op jit(solution)/shard_map/convert_element_type | solution.py:563
  185.2 20.7 %back_query.1 = (bf16[8,512,256]{2,1,0:T(8,128)(2,1)}, bf16[8,512,256]{2,1,0:T(8,128)(2,1)}, bf16[8,512,256]{2,1,0:T(8,128)(2,1)}, f32[512,512]{1,0:T(8,128)}) custom-call(bf16[8,512,256]{2,1,0:T(8,128)(2,1)} %get-tuple-element.68.refs_0_.refs_17_, bf16[80,256]{1,0:T(8,128)(2,1)S(1)} %maximum_maximum_fusion.refs_1_.refs_4_, ...), custom_call_target="tpu_custom_call" | custom-call | flops 1 | bytes 1 | tf_op jit(solution)/shard_map/back_query/pallas_call | solution.py:447
  205.9 2.4 collective-permute-done.15
  208.4 2.9 %fusion.5 = (bf16[8,272,256]{2,1,0:T(8,128)(2,1)}, bf16[8,272,256]{2,1,0:T(8,128)(2,1)S(1)}) fusion(bf16[8,272,256]{2,1,0:T(8,128)(2,1)S(1)} %copy-done.13, bf16[8,272,256]{2,1,0:T(8,128)(2,1)} %collective-permute-done.15, pred[]{:T(512)S(6)} %eq.31, bf16[8,272,256]{2,1,0:T(8,128)(2,1)S(1)} %copy-done.15), kind=kLoop, calls=%fused_computation.16 | loop fusion | flops 5013504 | bytes 5570561 | tf_op jit(solution)/shard_map/convert_element_type | solution.py:501
  211.3 2.8 fusion.11
  214.1 4.4 %collective-permute-start.20 = (bf16[64,2048]{1,0:T(8,128)(2,1)S(1)}, bf16[64,2048]{1,0:T(8,128)(2,1)S(1)}, u32[]{:S(2)}, u32[]{:S(2)}) collective-permute-start(bf16[64,2048]{1,0:T(8,128)(2,1)S(1)} %get-tuple-element.131.refs_20_), channel_id=1, source_target_pairs={{0,24},{4,28},{8,16},{12,20},{16,8},{20,12},{24,0},{28,4},{1,25},{... | collective-permute-start | bytes 786440 | tf_op jit(solution)/shard_map/ppermute | solution.py:569
  218.5 20.1 %back_key.1 = (f32[8,256,512]{2,1,0:T(8,128)}, bf16[2,16,72,256]{3,2,1,0:T(8,128)(2,1)}, f32[2,16,72,256]{3,2,1,0:T(8,128)}) custom-call(bf16[8,256,512]{2,1,0:T(8,128)(2,1)} %refs_0_, f32[4,512]{1,0:T(4,128)S(1)} %copy-done.9, f32[8,256,512]{2,1,0:T(8,128)} %bitcast.103, bf16[1536,512]{1,0:T(8,128)(2,1)S(1)} %copy-done.3, ...), custom_call_target="tpu_custom_call" | custom-call | flops 15032385536 | bytes 42258436 | tf_op jit(solution)/shard_map/back_key/pallas_call | solution.py:447
  240.0 1.9 fusion.32
  242.1 1.1 collective-permute-done.21
  244.0 2.9 %collective-permute-start.30 = (bf16[64,1024]{1,0:T(8,128)(2,1)S(1)}, bf16[64,1024]{1,0:T(8,128)(2,1)S(1)}, u32[]{:S(2)}, u32[]{:S(2)}) collective-permute-start(bf16[64,1024]{1,0:T(8,128)(2,1)S(1)} %bitcast.118), channel_id=1, source_target_pairs={{0,2},{1,3},{2,0},{3,1},{4,6},{5,7},{6,4},{7,5},{8,10},{9,11},{10,... | collective-permute-start | bytes 393224 | tf_op jit(solution)/shard_map/ppermute | solution.py:478
  246.8 1.3 fusion.33
  249.3 1.4 collective-permute-done.30
  250.8 0.8 fusion.26
  251.6 5.6 %collective-permute-done.22 = bf16[8,72,256]{2,1,0:T(8,128)(2,1)S(1)} collective-permute-done((bf16[8,72,256]{2,1,0:T(8,128)(2,1)S(1)}, bf16[8,72,256]{2,1,0:T(8,128)(2,1)S(1)}, u32[]{:S(2)}, u32[]{:S(2)}) %collective-permute-start.22) | collective-permute-done | bytes 294944 | tf_op jit(solution)/shard_map/ppermute | solution.py:478
  257.8 1.7 collective-permute-start.27
  259.5 0.8 fusion.28
  260.3 2.1 collective-permute-done.23
  262.5 0.8 collective-permute-start.24
  263.2 5.5 %collective-permute-done.27 = bf16[4,72,256]{2,1,0:T(8,128)(2,1)S(1)} collective-permute-done((bf16[4,72,256]{2,1,0:T(8,128)(2,1)S(1)}, bf16[4,72,256]{2,1,0:T(8,128)(2,1)S(1)}, u32[]{:S(2)}, u32[]{:S(2)}) %collective-permute-start.27) | collective-permute-done | bytes 147488 | tf_op jit(solution)/shard_map/ppermute | solution.py:478
  268.8 0.8 collective-permute-done.24
  269.6 1.3 collective-permute-start.25
  270.9 2.2 collective-permute-done.28
  273.2 1.9 collective-permute-start.29
  275.1 2.1 collective-permute-done.29
  277.3 0.9 fusion.30
  (145 shorter events, 8.6 us)
Async XLA Ops:
  7.2 114.6 %all-gather.2.cloned.1.call-start = ((), (), s32[]{:S(2)}) async-start(), calls=%async_computation | async-start | bytes 4325376 | tf_op jit(solution)/shard_map/all_gather | solution.py:643
  9.1 7.8 %collective-permute-start = (bf16[1,72,256]{2,1,0:T(8,128)(2,1)S(1)}, bf16[1,72,256]{2,1,0:T(8,128)(2,1)S(1)}, u32[]{:S(2)}, u32[]{:S(2)}) collective-permute-start(bf16[1,72,256]{2,1,0:T(8,128)(2,1)S(1)} %get-tuple-element.177), channel_id=1, source_target_pairs={{0,8},{4,12},{8,0},{12,4},{16,24},{20,28},{24,16},{28,20},{1,9},{5... | collective-permute-start | bytes 110600 | tf_op jit(solution)/shard_map/ppermute | solution.py:478
  12.2 8.2 %collective-permute-start.5 = (bf16[1,72,256]{2,1,0:T(8,128)(2,1)S(1)}, bf16[1,72,256]{2,1,0:T(8,128)(2,1)S(1)}, u32[]{:S(2)}, u32[]{:S(2)}) collective-permute-start(bf16[1,72,256]{2,1,0:T(8,128)(2,1)S(1)} %get-tuple-element.176), channel_id=1, source_target_pairs={{0,2},{1,3},{2,0},{3,1},{4,6},{5,7},{6,4},{7,5},{8,10},{9,11},{10,... | collective-permute-start | bytes 110600 | tf_op jit(solution)/shard_map/ppermute | solution.py:478
  16.9 6.7 %copy-start.22 = (f32[64,256]{1,0:T(8,128)S(1)}, f32[64,256]{1,0:T(8,128)}, u32[]{:S(2)}) copy-start(f32[64,256]{1,0:T(8,128)} %param.16) | copy-start | bytes 196612
  20.4 6.1 %collective-permute-start.1 = (bf16[2,72,256]{2,1,0:T(8,128)(2,1)S(1)}, bf16[2,72,256]{2,1,0:T(8,128)(2,1)S(1)}, u32[]{:S(2)}, u32[]{:S(2)}) collective-permute-start(bf16[2,72,256]{2,1,0:T(8,128)(2,1)S(1)} %pad_maximum_fusion.9), channel_id=1, source_target_pairs={{0,16},{4,20},{8,24},{12,28},{16,0},{20,4},{24,8},{28,12},{1,17},{... | collective-permute-start | bytes 221192 | tf_op jit(solution)/shard_map/ppermute | solution.py:478
  23.1 4.4 %collective-permute-start.6 = (bf16[2,72,256]{2,1,0:T(8,128)(2,1)S(1)}, bf16[2,72,256]{2,1,0:T(8,128)(2,1)S(1)}, u32[]{:S(2)}, u32[]{:S(2)}) collective-permute-start(bf16[2,72,256]{2,1,0:T(8,128)(2,1)S(1)} %pad_maximum_fusion.10), channel_id=1, source_target_pairs={{0,8},{4,12},{8,0},{12,4},{16,24},{20,28},{24,16},{28,20},{1,9},{5... | collective-permute-start | bytes 221192 | tf_op jit(solution)/shard_map/ppermute | solution.py:478
  27.5 10.7 %collective-permute-start.7 = (bf16[4,72,256]{2,1,0:T(8,128)(2,1)S(1)}, bf16[4,72,256]{2,1,0:T(8,128)(2,1)S(1)}, u32[]{:S(2)}, u32[]{:S(2)}) collective-permute-start(bf16[4,72,256]{2,1,0:T(8,128)(2,1)S(1)} %pad_maximum_fusion.7), channel_id=1, source_target_pairs={{0,16},{4,20},{8,24},{12,28},{16,0},{20,4},{24,8},{28,12},{1,17},{... | collective-permute-start | bytes 442376 | tf_op jit(solution)/shard_map/ppermute | solution.py:478
  28.6 11.2 %collective-permute-start.2 = (bf16[4,72,256]{2,1,0:T(8,128)(2,1)S(1)}, bf16[4,72,256]{2,1,0:T(8,128)(2,1)S(1)}, u32[]{:S(2)}, u32[]{:S(2)}) collective-permute-start(bf16[4,72,256]{2,1,0:T(8,128)(2,1)S(1)} %pad_maximum_fusion.6), channel_id=1, source_target_pairs={{0,4},{4,0},{8,12},{12,8},{16,20},{20,16},{24,28},{28,24},{1,5},{5... | collective-permute-start | bytes 442376 | tf_op jit(solution)/shard_map/ppermute | solution.py:478
  38.3 9.5 %collective-permute-start.8 = (bf16[8,72,256]{2,1,0:T(8,128)(2,1)S(1)}, bf16[8,72,256]{2,1,0:T(8,128)(2,1)S(1)}, u32[]{:S(2)}, u32[]{:S(2)}) collective-permute-start(bf16[8,72,256]{2,1,0:T(8,128)(2,1)S(1)} %pad_maximum_fusion.5), channel_id=1, source_target_pairs={{0,4},{4,0},{8,12},{12,8},{16,20},{20,16},{24,28},{28,24},{1,5},{5... | collective-permute-start | bytes 884744 | tf_op jit(solution)/shard_map/ppermute | solution.py:478
  39.9 10.3 %collective-permute-start.3 = (bf16[8,72,256]{2,1,0:T(8,128)(2,1)S(1)}, bf16[8,72,256]{2,1,0:T(8,128)(2,1)S(1)}, u32[]{:S(2)}, u32[]{:S(2)}) collective-permute-start(bf16[8,72,256]{2,1,0:T(8,128)(2,1)S(1)} %pad_maximum_fusion.4), channel_id=1, source_target_pairs={{0,2},{1,3},{2,0},{3,1},{4,6},{5,7},{6,4},{7,5},{8,10},{9,11},{10,... | collective-permute-start | bytes 884744 | tf_op jit(solution)/shard_map/ppermute | solution.py:478
  47.9 3.5 %collective-permute-start.9 = (bf16[16,72,256]{2,1,0:T(8,128)(2,1)S(1)}, bf16[16,72,256]{2,1,0:T(8,128)(2,1)S(1)}, u32[]{:S(2)}, u32[]{:S(2)}) collective-permute-start(bf16[16,72,256]{2,1,0:T(8,128)(2,1)S(1)} %pad_maximum_fusion.3), channel_id=1, source_target_pairs={{0,1},{1,0},{2,3},{3,2},{4,5},{5,4},{6,7},{7,6},{8,9},{9,8},{10,11... | collective-permute-start | bytes 1769480 | tf_op jit(solution)/shard_map/ppermute | solution.py:478
  51.1 2.2 collective-permute-start.4
  55.8 1.4 copy-start.2
  73.0 20.9 %copy-start.1 = (bf16[8,8,256,256]{3,2,1,0:T(8,128)(2,1)}, bf16[8,8,256,256]{3,2,1,0:T(8,128)(2,1)S(1)}, u32[]{:S(2)}) copy-start(bf16[8,8,256,256]{3,2,1,0:T(8,128)(2,1)S(1)} %get-tuple-element.70.refs_4_.refs_5_.refs_6_) | copy-start | bytes 25165828
  73.0 8.0 %copy-start.3 = (bf16[1536,512]{1,0:T(8,128)(2,1)S(1)}, bf16[1536,512]{1,0:T(8,128)(2,1)}, u32[]{:S(2)}) copy-start(bf16[1536,512]{1,0:T(8,128)(2,1)} %get-tuple-element.67.weights.refs_1_.refs_3_) | copy-start | bytes 4718596
  73.0 3.1 %collective-permute-start.10 = (bf16[8,272,256]{2,1,0:T(8,128)(2,1)}, bf16[8,272,256]{2,1,0:T(8,128)(2,1)S(1)}, u32[]{:S(2)}, u32[]{:S(2)}) collective-permute-start(bf16[8,272,256]{2,1,0:T(8,128)(2,1)} %get-tuple-element.72), channel_id=1, source_target_pairs={{0,1},{1,0},{2,3},{3,2},{4,5},{5,4},{6,7},{7,6},{8,9},{9,8},{10,11... | collective-permute-start | bytes 3342344 | tf_op jit(solution)/shard_map/ppermute | solution.py:478
  78.0 26.9 %collective-permute-start.11 = (bf16[8,272,256]{2,1,0:T(8,128)(2,1)S(1)}, bf16[8,272,256]{2,1,0:T(8,128)(2,1)S(1)}, u32[]{:S(2)}, u32[]{:S(2)}) collective-permute-start(bf16[8,272,256]{2,1,0:T(8,128)(2,1)S(1)} %fusion.refs_5_), channel_id=1, source_target_pairs={{0,2},{1,3},{4,6},{5,7},{8,10},{9,11},{12,14},{13,15},{16,18},{17,... | collective-permute-start | bytes 3342344 | tf_op jit(solution)/shard_map/ppermute | solution.py:493
  81.1 23.9 %copy-start.16 = (bf16[8,272,256]{2,1,0:T(8,128)(2,1)S(1)}, bf16[8,272,256]{2,1,0:T(8,128)(2,1)}, u32[]{:S(2)}) copy-start(bf16[8,272,256]{2,1,0:T(8,128)(2,1)} %get-tuple-element.71) | copy-start | bytes 3342340
  104.9 3.5 %copy-start.6 = (bf16[512,512]{1,0:T(8,128)(2,1)S(1)}, bf16[512,512]{1,0:T(8,128)(2,1)}, u32[]{:S(2)}) copy-start(bf16[512,512]{1,0:T(8,128)(2,1)} %get-tuple-element.66.out_weight) | copy-start | bytes 1572868
  104.9 3.5 %copy-start.9 = (f32[4,512]{1,0:T(4,128)S(1)}, f32[4,512]{1,0:T(4,128)}, u32[]{:S(2)}) copy-start(f32[4,512]{1,0:T(4,128)} %get-tuple-element.65.norms.refs_1_) | copy-start | bytes 24580
  105.6 2.8 collective-permute-start.12
  117.5 3.3 %copy-start = (bf16[8,8,256,256]{3,2,1,0:T(8,128)(2,1)}, bf16[8,8,256,256]{3,2,1,0:T(8,128)(2,1)S(1)}, u32[]{:S(2)}) copy-start(bf16[8,8,256,256]{3,2,1,0:T(8,128)(2,1)S(1)} %get-tuple-element.76.pq.refs_4_) | copy-start | bytes 25165828
  120.8 1.0 copy-start.4
  121.8 39.5 %copy-start.7 = (f32[8,8,256]{2,1,0:T(8,128)S(1)}, f32[8,8,256]{2,1,0:T(8,128)}, u32[]{:S(2)}) copy-start(f32[8,8,256]{2,1,0:T(8,128)} %get-tuple-element.85.recip) | copy-start | bytes 196612
  161.1 11.5 %collective-permute-start.13 = (bf16[512,2048]{1,0:T(8,128)(2,1)}, bf16[512,2048]{1,0:T(8,128)(2,1)S(1)}, u32[]{:S(2)}, u32[]{:S(2)}) collective-permute-start(bf16[512,2048]{1,0:T(8,128)(2,1)} %get-tuple-element.88), channel_id=1, source_target_pairs={{0,1},{1,0},{2,3},{3,2},{4,5},{5,4},{6,7},{7,6},{8,9},{9,8},{10,11... | collective-permute-start | bytes 6291464 | tf_op jit(solution)/shard_map/ppermute | solution.py:478
  172.6 6.6 %copy-start.17 = (bf16[512,2048]{1,0:T(8,128)(2,1)}, bf16[512,2048]{1,0:T(8,128)(2,1)S(1)}, u32[]{:S(2)}) copy-start(bf16[512,2048]{1,0:T(8,128)(2,1)S(1)} %collective-permute-done.13) | copy-start | bytes 6291460
  172.6 3.0 %collective-permute-start.14 = (bf16[8,272,256]{2,1,0:T(8,128)(2,1)}, bf16[8,272,256]{2,1,0:T(8,128)(2,1)S(1)}, u32[]{:S(2)}, u32[]{:S(2)}) collective-permute-start(bf16[8,272,256]{2,1,0:T(8,128)(2,1)} %get-tuple-element.89), channel_id=1, source_target_pairs={{0,1},{1,0},{2,3},{3,2},{4,5},{5,4},{6,7},{7,6},{8,9},{9,8},{10,11... | collective-permute-start | bytes 3342344 | tf_op jit(solution)/shard_map/ppermute | solution.py:478
  175.6 1.0 copy-start.14
  179.2 29.2 %collective-permute-start.15 = (bf16[8,272,256]{2,1,0:T(8,128)(2,1)}, bf16[8,272,256]{2,1,0:T(8,128)(2,1)}, u32[]{:S(2)}, u32[]{:S(2)}) collective-permute-start(bf16[8,272,256]{2,1,0:T(8,128)(2,1)} %fusion.3.refs_12_), channel_id=1, source_target_pairs={{2,0},{3,1},{6,4},{7,5},{10,8},{11,9},{14,12},{15,13},{18,16},{19,... | collective-permute-start | bytes 3342344 | tf_op jit(solution)/shard_map/ppermute | solution.py:493
  180.7 4.5 %copy-start.5 = (bf16[8,272,256]{2,1,0:T(8,128)(2,1)S(1)}, bf16[8,272,256]{2,1,0:T(8,128)(2,1)}, u32[]{:S(2)}) copy-start(bf16[8,272,256]{2,1,0:T(8,128)(2,1)} %copy-done.4) | copy-start | bytes 3342340
  185.2 26.1 %collective-permute-start.17 = (bf16[256,2048]{1,0:T(8,128)(2,1)}, bf16[256,2048]{1,0:T(8,128)(2,1)}, u32[]{:S(2)}, u32[]{:S(2)}) collective-permute-start(bf16[256,2048]{1,0:T(8,128)(2,1)} %bitcast.13.refs_13_), channel_id=1, source_target_pairs={{0,4},{4,0},{8,12},{12,8},{16,20},{20,16},{24,28},{28,24},{1,5},{5... | collective-permute-start | bytes 3145736 | tf_op jit(solution)/shard_map/ppermute | solution.py:569
  185.2 23.2 %copy-start.13 = (bf16[8,272,256]{2,1,0:T(8,128)(2,1)S(1)}, bf16[8,272,256]{2,1,0:T(8,128)(2,1)}, u32[]{:S(2)}) copy-start(bf16[8,272,256]{2,1,0:T(8,128)(2,1)} %get-tuple-element.86) | copy-start | bytes 3342340
  185.2 23.2 %copy-start.15 = (bf16[8,272,256]{2,1,0:T(8,128)(2,1)S(1)}, bf16[8,272,256]{2,1,0:T(8,128)(2,1)}, u32[]{:S(2)}) copy-start(bf16[8,272,256]{2,1,0:T(8,128)(2,1)} %copy-done.14) | copy-start | bytes 3342340
  211.3 7.2 %copy-start.12 = (f32[2,512]{1,0:T(2,128)S(1)}, f32[2,512]{1,0:T(2,128)}, u32[]{:S(2)}) copy-start(f32[2,512]{1,0:T(2,128)} %get-tuple-element.103.refs_16_) | copy-start | bytes 12292
  211.3 7.2 %collective-permute-start.16 = (bf16[8,272,256]{2,1,0:T(8,128)(2,1)}, bf16[8,272,256]{2,1,0:T(8,128)(2,1)}, u32[]{:S(2)}, u32[]{:S(2)}) collective-permute-start(bf16[8,272,256]{2,1,0:T(8,128)(2,1)} %get-tuple-element.144), channel_id=1, source_target_pairs={{0,1},{1,0},{2,3},{3,2},{4,5},{5,4},{6,7},{7,6},{8,9},{9,8},{10,11... | collective-permute-start | bytes 3342344 | tf_op jit(solution)/shard_map/ppermute | solution.py:478
  211.3 7.2 %copy-start.10 = (f32[512,512]{1,0:T(8,128)S(1)}, f32[512,512]{1,0:T(8,128)}, u32[]{:S(2)}) copy-start(f32[512,512]{1,0:T(8,128)} %get-tuple-element.102.refs_15_) | copy-start | bytes 3145732
  211.3 7.2 %copy-start.11 = (f32[512,512]{1,0:T(8,128)S(1)}, f32[512,512]{1,0:T(8,128)}, u32[]{:S(2)}) copy-start(f32[512,512]{1,0:T(8,128)} %get-tuple-element.101.refs_14_) | copy-start | bytes 3145732
  214.0 24.6 %collective-permute-start.18 = (bf16[64,2048]{1,0:T(8,128)(2,1)S(1)}, bf16[64,2048]{1,0:T(8,128)(2,1)S(1)}, u32[]{:S(2)}, u32[]{:S(2)}) collective-permute-start(bf16[64,2048]{1,0:T(8,128)(2,1)S(1)} %get-tuple-element.133.refs_18_), channel_id=1, source_target_pairs={{0,8},{4,12},{8,0},{12,4},{16,24},{20,28},{24,16},{28,20},{1,9},{5... | collective-permute-start | bytes 786440 | tf_op jit(solution)/shard_map/ppermute | solution.py:569
  214.1 24.6 %collective-permute-start.19 = (bf16[64,2048]{1,0:T(8,128)(2,1)S(1)}, bf16[64,2048]{1,0:T(8,128)(2,1)S(1)}, u32[]{:S(2)}, u32[]{:S(2)}) collective-permute-start(bf16[64,2048]{1,0:T(8,128)(2,1)S(1)} %get-tuple-element.132.refs_19_), channel_id=1, source_target_pairs={{0,16},{4,20},{8,24},{12,28},{16,0},{20,4},{24,8},{28,12},{1,17},{... | collective-permute-start | bytes 786440 | tf_op jit(solution)/shard_map/ppermute | solution.py:569
  214.1 24.6 %collective-permute-start.20 = (bf16[64,2048]{1,0:T(8,128)(2,1)S(1)}, bf16[64,2048]{1,0:T(8,128)(2,1)S(1)}, u32[]{:S(2)}, u32[]{:S(2)}) collective-permute-start(bf16[64,2048]{1,0:T(8,128)(2,1)S(1)} %get-tuple-element.131.refs_20_), channel_id=1, source_target_pairs={{0,24},{4,28},{8,16},{12,20},{16,8},{20,12},{24,0},{28,4},{1,25},{... | collective-permute-start | bytes 786440 | tf_op jit(solution)/shard_map/ppermute | solution.py:569
  238.6 0.8 copy-start.25
  240.0 3.2 %collective-permute-start.21 = (bf16[2,16,72,256]{3,2,1,0:T(8,128)(2,1)}, bf16[2,16,72,256]{3,2,1,0:T(8,128)(2,1)}, u32[]{:S(2)}, u32[]{:S(2)}) collective-permute-start(bf16[2,16,72,256]{3,2,1,0:T(8,128)(2,1)} %get-tuple-element.111), channel_id=1, source_target_pairs={{0,1},{1,0},{2,3},{3,2},{4,5},{5,4},{6,7},{7,6},{8,9},{9,8},{10,11... | collective-permute-start | bytes 3538952 | tf_op jit(solution)/shard_map/ppermute | solution.py:478
  240.0 1.9 copy-start.18
  240.0 1.9 copy-start.24
  240.0 1.9 copy-start.26
  240.0 1.9 copy-start.28
  244.0 6.7 %collective-permute-start.30 = (bf16[64,1024]{1,0:T(8,128)(2,1)S(1)}, bf16[64,1024]{1,0:T(8,128)(2,1)S(1)}, u32[]{:S(2)}, u32[]{:S(2)}) collective-permute-start(bf16[64,1024]{1,0:T(8,128)(2,1)S(1)} %bitcast.118), channel_id=1, source_target_pairs={{0,2},{1,3},{2,0},{3,1},{4,6},{5,7},{6,4},{7,5},{8,10},{9,11},{10,... | collective-permute-start | bytes 393224 | tf_op jit(solution)/shard_map/ppermute | solution.py:478
  248.3 2.5 copy-start.20
  248.3 2.5 copy-start.31
  248.3 2.5 copy-start.32
  248.3 8.8 %collective-permute-start.22 = (bf16[8,72,256]{2,1,0:T(8,128)(2,1)S(1)}, bf16[8,72,256]{2,1,0:T(8,128)(2,1)S(1)}, u32[]{:S(2)}, u32[]{:S(2)}) collective-permute-start(bf16[8,72,256]{2,1,0:T(8,128)(2,1)S(1)} %get-tuple-element.134), channel_id=1, source_target_pairs={{0,2},{1,3},{2,0},{3,1},{4,6},{5,7},{6,4},{7,5},{8,10},{9,11},{10,... | collective-permute-start | bytes 884744 | tf_op jit(solution)/shard_map/ppermute | solution.py:478
  248.5 9.1 %collective-permute-start.26 = (bf16[8,72,256]{2,1,0:T(8,128)(2,1)S(1)}, bf16[8,72,256]{2,1,0:T(8,128)(2,1)S(1)}, u32[]{:S(2)}, u32[]{:S(2)}) collective-permute-start(bf16[8,72,256]{2,1,0:T(8,128)(2,1)S(1)} %get-tuple-element.136), channel_id=1, source_target_pairs={{0,4},{4,0},{8,12},{12,8},{16,20},{20,16},{24,28},{28,24},{1,5},{5... | collective-permute-start | bytes 884744 | tf_op jit(solution)/shard_map/ppermute | solution.py:478
  249.2 10.3 %copy-start.21 = (f32[64,512]{1,0:T(8,128)S(1)}, f32[64,512]{1,0:T(8,128)}, u32[]{:S(2)}) copy-start(f32[64,512]{1,0:T(8,128)} %param.20) | copy-start | bytes 393220
  249.2 10.2 %copy-start.33 = (f32[64,512]{1,0:T(8,128)S(1)}, f32[64,512]{1,0:T(8,128)}, u32[]{:S(2)}) copy-start(f32[64,512]{1,0:T(8,128)} %param.22) | copy-start | bytes 393220
  249.2 10.2 %copy-start.34 = (f32[64,512]{1,0:T(8,128)S(1)}, f32[64,512]{1,0:T(8,128)}, u32[]{:S(2)}) copy-start(f32[64,512]{1,0:T(8,128)} %param.23) | copy-start | bytes 393220
  257.2 5.2 %collective-permute-start.23 = (bf16[4,72,256]{2,1,0:T(8,128)(2,1)S(1)}, bf16[4,72,256]{2,1,0:T(8,128)(2,1)S(1)}, u32[]{:S(2)}, u32[]{:S(2)}) collective-permute-start(bf16[4,72,256]{2,1,0:T(8,128)(2,1)S(1)} %get-tuple-element.148), channel_id=1, source_target_pairs={{0,4},{4,0},{8,12},{12,8},{16,20},{20,16},{24,28},{28,24},{1,5},{5... | collective-permute-start | bytes 442376 | tf_op jit(solution)/shard_map/ppermute | solution.py:478
  257.7 19.6 %copy-start.19 = (f32[32832]{0:T(1024)S(1)}, f32[32832]{0:T(1024)}, u32[]{:S(2)}) copy-start(f32[32832]{0:T(1024)} %param.17) | copy-start | bytes 393988
  257.7 19.6 %copy-start.29 = (f32[32832]{0:T(1024)S(1)}, f32[32832]{0:T(1024)}, u32[]{:S(2)}) copy-start(f32[32832]{0:T(1024)} %param.18) | copy-start | bytes 393988
  257.8 19.6 %copy-start.30 = (f32[32832]{0:T(1024)S(1)}, f32[32832]{0:T(1024)}, u32[]{:S(2)}) copy-start(f32[32832]{0:T(1024)} %param.19) | copy-start | bytes 393988
  257.8 11.0 %collective-permute-start.27 = (bf16[4,72,256]{2,1,0:T(8,128)(2,1)S(1)}, bf16[4,72,256]{2,1,0:T(8,128)(2,1)S(1)}, u32[]{:S(2)}, u32[]{:S(2)}) collective-permute-start(bf16[4,72,256]{2,1,0:T(8,128)(2,1)S(1)} %get-tuple-element.150), channel_id=1, source_target_pairs={{0,16},{4,20},{8,24},{12,28},{16,0},{20,4},{24,8},{28,12},{1,17},{... | collective-permute-start | bytes 442376 | tf_op jit(solution)/shard_map/ppermute | solution.py:478
  262.5 7.1 %collective-permute-start.24 = (bf16[2,72,256]{2,1,0:T(8,128)(2,1)S(1)}, bf16[2,72,256]{2,1,0:T(8,128)(2,1)S(1)}, u32[]{:S(2)}, u32[]{:S(2)}) collective-permute-start(bf16[2,72,256]{2,1,0:T(8,128)(2,1)S(1)} %get-tuple-element.156), channel_id=1, source_target_pairs={{0,16},{4,20},{8,24},{12,28},{16,0},{20,4},{24,8},{28,12},{1,17},{... | collective-permute-start | bytes 221192 | tf_op jit(solution)/shard_map/ppermute | solution.py:478
  268.8 4.4 %collective-permute-start.28 = (bf16[2,72,256]{2,1,0:T(8,128)(2,1)S(1)}, bf16[2,72,256]{2,1,0:T(8,128)(2,1)S(1)}, u32[]{:S(2)}, u32[]{:S(2)}) collective-permute-start(bf16[2,72,256]{2,1,0:T(8,128)(2,1)S(1)} %get-tuple-element.158), channel_id=1, source_target_pairs={{0,8},{4,12},{8,0},{12,4},{16,24},{20,28},{24,16},{28,20},{1,9},{5... | collective-permute-start | bytes 221192 | tf_op jit(solution)/shard_map/ppermute | solution.py:478
  269.6 5.5 %collective-permute-start.25 = (bf16[1,72,256]{2,1,0:T(8,128)(2,1)S(1)}, bf16[1,72,256]{2,1,0:T(8,128)(2,1)S(1)}, u32[]{:S(2)}, u32[]{:S(2)}) collective-permute-start(bf16[1,72,256]{2,1,0:T(8,128)(2,1)S(1)} %fusion.23), channel_id=1, source_target_pairs={{0,8},{4,12},{8,0},{12,4},{16,24},{20,28},{24,16},{28,20},{1,9},{5... | collective-permute-start | bytes 110600 | tf_op jit(solution)/shard_map/ppermute | solution.py:478
  273.2 4.0 %collective-permute-start.29 = (bf16[1,72,256]{2,1,0:T(8,128)(2,1)S(1)}, bf16[1,72,256]{2,1,0:T(8,128)(2,1)S(1)}, u32[]{:S(2)}, u32[]{:S(2)}) collective-permute-start(bf16[1,72,256]{2,1,0:T(8,128)(2,1)S(1)} %fusion.20), channel_id=1, source_target_pairs={{0,2},{1,3},{2,0},{3,1},{4,6},{5,7},{6,4},{7,5},{8,10},{9,11},{10,... | collective-permute-start | bytes 110600 | tf_op jit(solution)/shard_map/ppermute | solution.py:478
  (3 other events, 2.1 us)
Sparse Core Ops, SparseCore 0:
  17.0 64.7 all-gather.1

commit v2 on v1

--- a/solution.py
+++ b/solution.py
@@ -147,7 +147,7 @@
     put_states(own_out, their_out, core, heads, size, states, 1)
 
 
-def queries_kernel(heads, size, turned, weights, omega, value, pk, uq_out, pq_out, score_out, num_out, rows, stacks, halves):
+def queries_kernel(heads, size, turned, weights, omega, value, pk, uq_out, pq_out, pq_copy, score_out, num_out, rows, stacks, halves):
     width = heads * size
     length = turned.shape[2]
     rows[...] = dot_nn(weights[:width], turned[0])
@@ -162,7 +162,9 @@
 
     def feature(head):
         projected = dot_nn(omega[...], stacks[head])
-        pq_out[0, head] = jnp.exp(projected - halves[head : head + 1]).astype(LOW)
+        feat = jnp.exp(projected - halves[head : head + 1]).astype(LOW)
+        pq_out[0, head] = feat
+        pq_copy[0, head] = feat
 
     def score(head):
         score_out[0, head] = jnp.where(keep, dot_tn(pk[0, head], pq_out[0, head]), 0.0).astype(LOW)
@@ -198,7 +200,7 @@
 
 
 def ffn_kernel(
-    groups, normed, middle, target, norms, pair, core, out, grad_out, leave, stay, norm_grad, first_sum, second_sum
+    groups, devices, normed, middle, target, norms, pair, core, out, grad_out, leave, stay, norm_grad, first_sum, second_sum
 ):
     step = pl.program_id(0)
     half = pair.shape[2] // 2
@@ -235,11 +237,16 @@
     @pl.when(step == pl.num_programs(0) - 1)
     def _():
         mine = core[0]
+        count = normed.shape[1] // devices
         for chip in range(groups // 2):
             at = 2 * half * chip
             for side, target_ref in ((mine, stay), (1 - mine, leave)):
-                target_ref[:, at : at + half] = first_sum[2 * chip + side].astype(LOW)
-                target_ref[:, at + half : at + 2 * half] = second_sum[2 * chip + side].astype(LOW)
+                for place in range(devices):
+                    spot = place // 2 + (place % 2) * (devices // 2)
+                    rows_in = slice(place * count, (place + 1) * count)
+                    rows_out = slice(spot * count, (spot + 1) * count)
+                    target_ref[rows_out, at : at + half] = first_sum[2 * chip + side, rows_in].astype(LOW)
+                    target_ref[rows_out, at + half : at + 2 * half] = second_sum[2 * chip + side, rows_in].astype(LOW)
 
 
 def through_omega(flow, scaled, omega_low, size):
@@ -482,17 +489,18 @@
     return (lax.axis_index(axis) >> bit) & 1
 
 
-def send_half(own, their, forward):
+def send_half(own, their, forward, tie):
     count = lax.axis_size("seq")
     beside = flip(their, "seq", 0)
     mine = (own.astype(F32) + beside.astype(F32)).astype(LOW)
+    mine, tie = lax.optimization_barrier((mine, tie))
     far = None
     for step in range(1, count // 2):
         hop = 2 * step if forward else -2 * step
         pairs = [(i, i + hop) for i in range(count) if 0 <= i + hop < count]
         come = lax.ppermute(mine, "seq", pairs)
         far = come if far is None else far + come
-    return beside, far, mine
+    return beside, far, tie
 
 
 def receive_half(own, beside, far, forward):
@@ -553,7 +561,7 @@
     return [stay, come]
 
 
-def split_rows(terms, axis, bits, low):
+def split_rows(terms, axis, bits, low, tie):
     ways = 1 << len(bits)
     terms = [t.reshape(-1, ways, low, t.shape[1]) for t in terms]
     shift = min(bits)
@@ -564,12 +572,13 @@
         return total.reshape(-1, total.shape[-1])
 
     leaving = [part(mine ^ other) for other in range(1, ways)]
+    leaving, tie = lax.optimization_barrier((leaving, tie))
     size = lax.axis_size(axis)
     come = [
         lax.ppermute(leave, axis, [(i, i ^ (other << shift)) for i in range(size)])
         for other, leave in enumerate(leaving, 1)
     ]
-    return leaving, [part(mine)] + come
+    return tie, [part(mine)] + come
 
 
 def scatter_halving(terms, order):
@@ -645,7 +654,7 @@
 
     weights, out_weight, norms = pl.pallas_call(
         functools.partial(unpack_kernel, starts, spots, rows),
-        out_shape=[array((3 * width, width), LOW), array((width, width), LOW), array((4, width), F32)],
+        out_shape=[pltpu.VMEM((3 * width, width), LOW), pltpu.VMEM((width, width), LOW), array((4, width), F32)],
         scratch_shapes=[pltpu.VMEM((whole_rows, width), F32)],
         name="unpack",
         compiler_params=pltpu.CompilerParams(vmem_limit_bytes=VMEM_LIMIT),
@@ -682,7 +691,6 @@
             pltpu.VMEM((heads, length), F32),
         ]
 
-    tokens, target, omega_low = lax.optimization_barrier((tokens, target, omega_low))
     args = (tokens, norms, weights, omega_parts)
     outs = [array(flat, LOW)] * 2 + [array(held, LOW), pltpu.VMEM(feat, LOW)] + [array(state_shape, LOW)] * 2
     turned, uk, value, pk, own, their = call(
@@ -697,10 +705,10 @@
         chip=(),
         scratch=scratch_rows(2) + [pltpu.VMEM((heads, ext, count), F32)],
     )
-    beside, far, mine = send_half(own, their, True)
-    args = (turned, weights, omega_parts, value, pk)
-    outs = [array(flat, LOW), pltpu.VMEM(feat, LOW), array(score_shape, LOW), pltpu.VMEM(held, F32)]
-    uq, pq, score, num = call(
+    beside, far, omega_tied = send_half(own, their, True, omega_parts)
+    args = (turned, weights, omega_tied, value, pk)
+    outs = [array(flat, LOW), pltpu.VMEM(feat, LOW), array(feat, LOW), array(score_shape, LOW), pltpu.VMEM(held, F32)]
+    uq, pq_near, pq, score, num = call(
         functools.partial(queries_kernel, heads, size),
         seqs,
         args,
@@ -711,17 +719,16 @@
         1,
         scratch_rows(1),
         chip=(4,),
-        after=(mine,),
-    )
-    far, uq = lax.optimization_barrier((far, uq))
+    )
+    far, uq, target = lax.optimization_barrier((far, uq, target))
     keep, come = receive_half(own, beside, far, True)
     states = [per_seq(keep.shape)] * 2
     outs = [array(flat, LOW), array(recip_shape, F32), array(tokens.shape, F32), array(tokens.shape, LOW)]
     mixed, recip, middle, normed_two = call(
         functools.partial(mix_kernel, heads, size),
         seqs,
-        (tokens, norms, out_weight, num, core, keep, come, pq),
-        [spec(tokens), spec(norms), spec(out_weight), spec(num), in_smem, *states, spec(pq)],
+        (tokens, norms, out_weight, num, core, keep, come, pq_near),
+        [spec(tokens), spec(norms), spec(out_weight), spec(num), in_smem, *states, spec(pq_near)],
         outs,
         [spec(a) for a in outs],
         "mix",
@@ -734,7 +741,7 @@
     by_block = pl.BlockSpec((block, width), lambda i: (i, 0))
     rows_shape = (total_rows, width)
     block_out, grad_middle, leave, stay, norm_two_grad = call(
-        functools.partial(ffn_kernel, groups),
+        functools.partial(ffn_kernel, groups, lax.axis_size("dp")),
         total_rows // block,
         (*[a.reshape(rows_shape) for a in (normed_two, middle, target)], norms, pair, core),
         [by_block, by_block, by_block, fixed(norms.shape), fixed(pair.shape), in_smem],
@@ -766,8 +773,8 @@
     )
     their, come_pair = lax.optimization_barrier((their, come_pair))
     dp_rows = width // lax.axis_size("dp")
-    near_sent, terms = split_rows([stay, come_pair], "dp", [0], dp_rows)
-    beside, far, mine = send_half(own, their, False)
+    omega_low, terms = split_rows([stay, come_pair], "dp", [0], width // 2, omega_low)
+    beside, far, omega_low = send_half(own, their, False, omega_low)
     args = (turned, omega_low, outers, value, pq, pk, score, core, keep, come, uq, uk)
     outs = [array(flat, LOW)] * 3
     query_grad, key_part, value_part, query_weight = call(
@@ -786,12 +793,11 @@
             pltpu.VMEM(feat[1:], LOW),
             pltpu.VMEM(feat[1:], LOW),
         ],
-        after=(mine, *near_sent),
     )
     far, query_grad = lax.optimization_barrier((far, query_grad))
     keep, come = receive_half(own, beside, far, False)
     high = list(range(axis_bits("dp") - 1, 0, -1))
-    near_sent, terms = split_rows(terms, "dp", high[:2], dp_rows << max(len(high) - 2, 0))
+    omega_low, terms = split_rows(terms, "dp", high[:2], dp_rows << max(len(high) - 2, 0), omega_low)
     orders = scatter_orders()
     owners = [sorted(range(devices), key=lambda i: place_in(order, i)) for order in orders]
     piece_shape = (2, devices // 2, held_rows, width // 2)
@@ -815,12 +821,11 @@
             pltpu.VMEM((2, width), F32),
             pltpu.VMEM((whole_rows, width), F32),
         ],
-        after=tuple(near_sent),
     )
     leave, terms = lax.optimization_barrier((leave, terms))
     come_pieces = flip(leave, "seq", 0)
     for step, bit in enumerate(high[2:]):
-        _, terms = split_rows(terms, "dp", [bit], dp_rows << (len(high) - 3 - step))
+        omega_low, terms = split_rows(terms, "dp", [bit], dp_rows << (len(high) - 3 - step), omega_low)
     terms, come_pieces = lax.optimization_barrier(([total_of(terms)], come_pieces))
     for bit in range(axis_bits("seq") - 1, 0, -1):
         terms = [t.reshape(t.shape[0], 2, -1) for t in terms]

time: 286 us -> 274 us (0.958)
  waiting for transfers between devices: 65.2 us -> 48.3 us
  starting transfers between devices: 32.3 us -> 38.7 us
    ppermute x25, waiting for transfers between devices: 51.7 us -> 37.9 us  [flip(): lax.ppermute(value, axis, [(i, i ^ 1 << bit) for i in range(lax.axis_size...]
    ppermute x25, starting transfers between devices: 23.3 us -> 28.6 us  [flip(): lax.ppermute(value, axis, [(i, i ^ 1 << bit) for i in range(lax.axis_size...]
    ppermute x2, waiting for transfers between devices: 13.4 us -> 10.3 us  [send_half(): come = lax.ppermute(mine, 'seq', pairs)]
    convert_element_type x1 -> x2, other arithmetic: 4.48 us -> 6.54 us  [part(): total_of([lax.dynamic_index_in_dim(t, which, 1, keepdims=False) for t in...]
    unnamed x73 -> x61, local copies, waits for them, and re-layouts: 9.13 us -> 7.24 us
  transfers between devices with their start and end apart: 32 -> 32, of which waited for: 19 -> 19; matrix products, arithmetic and copies ran while one was open for 10% -> 10% of each run, Pallas kernels for 32% -> 33%
where the time goes in v2:
time: 274 us; the launch traced here: 273 us
  Pallas kernels  131 us (48%)
  waiting for transfers between devices  48.3 us (18%)
  starting transfers between devices  38.7 us (14%)
  other arithmetic  26.7 us (10%)
  between operations  14.7 us (5%)
  local copies, waits for them, and re-layouts  14.2 us (5%)
    pallas_call x7, Pallas kernels, call(): pl.pallas_call(kernel, grid=(steps,), in_specs=in_specs, out_specs=out_sp...  129 us
    ppermute x25, waiting for transfers between devices, flip(): lax.ppermute(value, axis, [(i, i ^ 1 << bit) for i in range(lax.axis_size...  37.9 us
    ppermute x25, starting transfers between devices, flip(): lax.ppermute(value, axis, [(i, i ^ 1 << bit) for i in range(lax.axis_size...  28.6 us
    ppermute x2, waiting for transfers between devices, send_half(): come = lax.ppermute(mine, 'seq', pairs)  10.3 us
    unnamed x61, local copies, waits for them, and re-layouts  7.24 us
    convert_element_type x2, other arithmetic, part(): total_of([lax.dynamic_index_in_dim(t, which, 1, keepdims=False) for t in...  6.54 us
  transfers between devices with their start and end apart: 32, of which 19 were waited for; matrix products, arithmetic and copies ran while one was open for 10% of the time, Pallas kernels for 33%

profile of v2, /device:TPU:0, one launch (start us, length us, event | category | flops | bytes accessed | tf_op | source)
XLA Modules:
  0.0 273.1 jit_solution(14226646987670407014)
XLA Ops:
  7.3 0.9 convert_element_type.374
  8.2 0.8 dynamic_update_slice.3
  9.1 3.1 %collective-permute-start = (bf16[1,72,256]{2,1,0:T(8,128)(2,1)S(1)}, bf16[1,72,256]{2,1,0:T(8,128)(2,1)S(1)}, u32[]{:S(2)}, u32[]{:S(2)}) collective-permute-start(bf16[1,72,256]{2,1,0:T(8,128)(2,1)S(1)} %get-tuple-element.195), channel_id=1, source_target_pairs={{0,8},{4,12},{8,0},{12,4},{16,24},{20,28},{24,16},{28,20},{1,9},{5... | collective-permute-start | bytes 110600 | tf_op jit(solution)/shard_map/ppermute | solution.py:485
  12.2 0.9 convert_bitcast_fusion
  13.1 0.9 convert_element_type.385
  14.7 1.6 collective-permute-start.5
  16.3 2.4 collective-permute-done.5
  18.8 2.7 collective-permute-start.1
  21.4 1.5 collective-permute-start.6
  23.0 1.1 collective-permute-done.1
  24.1 1.8 collective-permute-done.6
  25.9 1.0 collective-permute-start.7
  27.0 0.8 copy.33
  27.8 1.6 collective-permute-start.2
  29.4 4.1 %collective-permute-done.7 = bf16[4,72,256]{2,1,0:T(8,128)(2,1)S(1)} collective-permute-done((bf16[4,72,256]{2,1,0:T(8,128)(2,1)S(1)}, bf16[4,72,256]{2,1,0:T(8,128)(2,1)S(1)}, u32[]{:S(2)}, u32[]{:S(2)}) %collective-permute-start.7) | collective-permute-done | bytes 147488 | tf_op jit(solution)/shard_map/ppermute | solution.py:485
  33.5 3.0 %collective-permute-start.8 = (bf16[8,72,256]{2,1,0:T(8,128)(2,1)S(1)}, bf16[8,72,256]{2,1,0:T(8,128)(2,1)S(1)}, u32[]{:S(2)}, u32[]{:S(2)}) collective-permute-start(bf16[8,72,256]{2,1,0:T(8,128)(2,1)S(1)} %pad_maximum_fusion.5), channel_id=1, source_target_pairs={{0,4},{4,0},{8,12},{12,8},{16,20},{20,16},{24,28},{28,24},{1,5},{5... | collective-permute-start | bytes 884744 | tf_op jit(solution)/shard_map/ppermute | solution.py:485
  36.6 1.7 collective-permute-start.3
  38.3 2.9 %collective-permute-done.8 = bf16[8,72,256]{2,1,0:T(8,128)(2,1)S(1)} collective-permute-done((bf16[8,72,256]{2,1,0:T(8,128)(2,1)S(1)}, bf16[8,72,256]{2,1,0:T(8,128)(2,1)S(1)}, u32[]{:S(2)}, u32[]{:S(2)}) %collective-permute-start.8) | collective-permute-done | bytes 294944 | tf_op jit(solution)/shard_map/ppermute | solution.py:485
  41.4 2.0 collective-permute-done.3
  43.4 0.9 pad_maximum_fusion.2
  44.7 1.8 collective-permute-done.4
  46.7 1.5 unpack.1
  48.2 0.7 copy-done.4
  48.9 15.1 %keys.1 = (bf16[8,512,256]{2,1,0:T(8,128)(2,1)}, bf16[8,512,256]{2,1,0:T(8,128)(2,1)}, bf16[8,8,80,256]{3,2,1,0:T(8,128)(2,1)}, bf16[8,8,256,256]{3,2,1,0:T(8,12...) custom-call(bf16[8,256,512]{2,1,0:T(8,128)(2,1)} %tok.5, f32[4,512]{1,0:T(4,128)S(1)} %copy-done.4, ...), custom_call_target="tpu_custom_call" | custom-call | flops 1 | bytes 1 | tf_op jit(solution)/shard_map/keys/pallas_call | solution.py:454
  64.2 2.8 %collective-permute-done.10 = bf16[8,272,256]{2,1,0:T(8,128)(2,1)S(1)} collective-permute-done((bf16[8,272,256]{2,1,0:T(8,128)(2,1)}, bf16[8,272,256]{2,1,0:T(8,128)(2,1)S(1)}, u32[]{:S(2)}, u32[]{:S(2)}) %collective-permute-start.10) | collective-permute-done | bytes 1114144 | tf_op jit(solution)/shard_map/ppermute | solution.py:485
  67.0 1.6 fusion
  68.6 3.8 %collective-permute-start.11 = (bf16[8,272,256]{2,1,0:T(8,128)(2,1)S(1)}, bf16[8,272,256]{2,1,0:T(8,128)(2,1)S(1)}, u32[]{:S(2)}, u32[]{:S(2)}) collective-permute-start(bf16[8,272,256]{2,1,0:T(8,128)(2,1)S(1)} %fusion), channel_id=1, source_target_pairs={{0,2},{1,3},{4,6},{5,7},{8,10},{9,11},{12,14},{13,15},{16,18},{17,... | collective-permute-start | bytes 3342344 | tf_op jit(solution)/shard_map/ppermute | solution.py:501
  72.4 1.8 multiply_convert_fusion
  74.2 13.6 %queries.1 = (bf16[8,512,256]{2,1,0:T(8,128)(2,1)}, bf16[8,8,256,256]{3,2,1,0:T(8,128)(2,1)S(1)}, bf16[8,8,256,256]{3,2,1,0:T(8,128)(2,1)}, bf16[8,8,256,256]{3,2,1,0:T(8,128)(2,1)}, f32[8,8,80,256]{3,2,1,0:T(8,128)S(1)}) custom-call(bf16[8,512,256]{2,1,0:T(8,128)(2,1)} %get-tuple-element.76.turned, bf16[1536,512]{1,0:T(8,128)(2,1)S(1)} %get-tuple-element.75.weights, ...), custom_call_target="tpu_custom_call" | custom-call | flops 1 | bytes 1 | tf_op jit(solution)/shard_map/queries/pallas_call | solution.py:454
  87.8 3.3 %copy-done = bf16[8,8,256,256]{3,2,1,0:T(8,128)(2,1)} copy-done((bf16[8,8,256,256]{3,2,1,0:T(8,128)(2,1)}, bf16[8,8,256,256]{3,2,1,0:T(8,128)(2,1)S(1)}, u32[]{:S(2)}) %copy-start) | copy-done | bytes 8388632
  91.2 5.1 %collective-permute-done.11 = bf16[8,272,256]{2,1,0:T(8,128)(2,1)S(1)} collective-permute-done((bf16[8,272,256]{2,1,0:T(8,128)(2,1)S(1)}, bf16[8,272,256]{2,1,0:T(8,128)(2,1)S(1)}, u32[]{:S(2)}, u32[]{:S(2)}) %collective-permute-start.11) | collective-permute-done | bytes 1114144 | tf_op jit(solution)/shard_map/ppermute | solution.py:501
  97.0 2.7 %collective-permute-done.12.come.come_state = bf16[8,272,256]{2,1,0:T(8,128)(2,1)S(1)} collective-permute-done((bf16[8,272,256]{2,1,0:T(8,128)(2,1)S(1)}, bf16[8,272,256]{2,1,0:T(8,128)(2,1)S(1)}, u32[]{:S(2)}, u32[]{:S(2)}) %collective-permute-start.12) | collective-permute-done | bytes 1114144 | tf_op jit(solution)/shard_map/ppermute | solution.py:485
  99.8 9.0 %mix.1 = (bf16[8,512,256]{2,1,0:T(8,128)(2,1)}, f32[8,8,256]{2,1,0:T(8,128)}, f32[8,256,512]{2,1,0:T(8,128)}, bf16[8,256,512]{2,1,0:T(8,128)(2,1)}) custom-call(bf16[8,256,512]{2,1,0:T(8,128)(2,1)} %tok.5, f32[4,512]{1,0:T(4,128)S(1)} %copy-done.5, bf16[512,512]{1,0:T(8,128)(2,1)S(1)} %get-tuple-element.74.out_weight, ...), custom_call_target="tpu_custom_call" | custom-call | flops 1 | bytes 1 | tf_op jit(solution)/shard_map/mix/pallas_call | solution.py:454
  108.8 1.0 copy-done.1
  109.8 39.3 %ffn.1 = (bf16[2048,512]{1,0:T(8,128)(2,1)}, f32[2048,512]{1,0:T(8,128)}, bf16[512,2048]{1,0:T(8,128)(2,1)}, bf16[512,2048]{1,0:T(8,128)(2,1)}, f32[2,512]{1,0:T(2,128)}) custom-call(bf16[2048,512]{1,0:T(8,128)(2,1)} %bitcast.123, f32[2048,512]{1,0:T(8,128)} %bitcast.122, bf16[2048,512]{1,0:T(8,128)(2,1)} %bitcast.112, f32[4,512]{1,0:T(4,128)S(1)} %copy-done.5, ...), custom_call_target="tpu_custom_call" | custom-call | flops 42949672960 | bytes 23080964 | tf_op jit(solution)/shard_map/ffn/pallas_call | solution.py:454
  149.3 11.3 %outer.1 = (bf16[8,8,80,256]{3,2,1,0:T(8,128)(2,1)}, bf16[8,272,256]{2,1,0:T(8,128)(2,1)}, bf16[8,272,256]{2,1,0:T(8,128)(2,1)}, f32[512,512]{1,0:T(8,128)}) custom-call(f32[8,256,512]{2,1,0:T(8,128)} %bitcast.104, bf16[512,512]{1,0:T(8,128)(2,1)S(1)} %get-tuple-element.74.out_weight, bf16[8,512,256]{2,1,0:T(8,128)(2,1)} %get-tuple-element.94.mixed, ...), custom_call_target="tpu_custom_call" | custom-call | flops 1 | bytes 1 | tf_op jit(solution)/shard_map/outer/pallas_call | solution.py:454
  161.2 4.5 %add_convert_fusion.1 = (bf16[1,1,256,2048]{3,2,1,0:T(8,128)(2,1)}, bf16[256,2048]{1,0:T(8,128)(2,1)}) fusion(bf16[1,2,256,2048]{3,2,1,0:T(8,128)(2,1)} %bitcast.12, s32[]{:T(128)S(6)} %select_n.267, bf16[1,2,256,2048]{3,2,1,0:T(8,128)(2,1)} %bitcast.111, s32[]{:T(128)S(6)} %select_n.269), kind=kLoop, calls=%fused_computation.18 | loop fusion | flops 4194304 | bytes 6291464 | tf_op jit(solution)/shard_map/convert_element_type | solution.py:571
  165.7 2.6 fusion.3
  168.3 1.3 collective-permute-start.16
  170.1 1.2 copy-done.2
  171.3 20.6 %back_query.1 = (bf16[8,512,256]{2,1,0:T(8,128)(2,1)}, bf16[8,512,256]{2,1,0:T(8,128)(2,1)}, bf16[8,512,256]{2,1,0:T(8,128)(2,1)}, f32[512,512]{1,0:T(8,128)}) custom-call(bf16[8,512,256]{2,1,0:T(8,128)(2,1)} %get-tuple-element.76.turned, bf16[80,256]{1,0:T(8,128)(2,1)S(1)} %maximum_maximum_fusion.omega_low, ...), custom_call_target="tpu_custom_call" | custom-call | flops 1 | bytes 1 | tf_op jit(solution)/shard_map/back_query/pallas_call | solution.py:454
  192.0 5.2 %collective-permute-done.16 = bf16[8,272,256]{2,1,0:T(8,128)(2,1)} collective-permute-done((bf16[8,272,256]{2,1,0:T(8,128)(2,1)}, bf16[8,272,256]{2,1,0:T(8,128)(2,1)}, u32[]{:S(2)}, u32[]{:S(2)}) %collective-permute-start.16) | collective-permute-done | bytes 1114144 | tf_op jit(solution)/shard_map/ppermute | solution.py:501
  197.2 3.2 %fusion.5 = (bf16[8,272,256]{2,1,0:T(8,128)(2,1)}, bf16[8,272,256]{2,1,0:T(8,128)(2,1)S(1)}) fusion(bf16[8,272,256]{2,1,0:T(8,128)(2,1)S(1)} %copy-done.10, bf16[8,272,256]{2,1,0:T(8,128)(2,1)} %collective-permute-done.16, pred[]{:T(512)S(6)} %eq.31, bf16[8,272,256]{2,1,0:T(8,128)(2,1)} %collective-permute-done.15), kind=kLoop, calls=%fused_computation.16 | loop fusion | flops 5013504 | bytes 5570561 | tf_op jit(solution)/shard_map/convert_element_type | solution.py:509
  200.4 2.1 fusion.12
  203.1 1.8 collective-permute-start.19
  204.9 2.0 collective-permute-start.20
  207.0 20.2 %back_key.1 = (f32[8,256,512]{2,1,0:T(8,128)}, bf16[2,16,72,256]{3,2,1,0:T(8,128)(2,1)}, f32[2,16,72,256]{3,2,1,0:T(8,128)}) custom-call(bf16[8,256,512]{2,1,0:T(8,128)(2,1)} %tok.5, f32[4,512]{1,0:T(4,128)S(1)} %copy-done.5, f32[8,256,512]{2,1,0:T(8,128)} %bitcast.105, bf16[1536,512]{1,0:T(8,128)(2,1)S(1)} %get-tuple-element.75.weights, ...), custom_call_target="tpu_custom_call" | custom-call | flops 15032385536 | bytes 41472004 | tf_op jit(solution)/shard_map/back_key/pallas_call | solution.py:454
  228.0 1.9 fusion.32
  229.9 1.9 convert_add_fusion.8
  231.8 1.5 reshape.306
  233.7 1.3 fusion.33
  235.2 2.1 collective-permute-start.22
  238.2 1.8 collective-permute-done.30
  240.2 0.8 fusion.26
  241.0 4.2 %collective-permute-done.22 = bf16[8,72,256]{2,1,0:T(8,128)(2,1)S(1)} collective-permute-done((bf16[8,72,256]{2,1,0:T(8,128)(2,1)S(1)}, bf16[8,72,256]{2,1,0:T(8,128)(2,1)S(1)}, u32[]{:S(2)}, u32[]{:S(2)}) %collective-permute-start.22) | collective-permute-done | bytes 294944 | tf_op jit(solution)/shard_map/ppermute | solution.py:485
  245.9 3.1 %collective-permute-start.27 = (bf16[4,72,256]{2,1,0:T(8,128)(2,1)S(1)}, bf16[4,72,256]{2,1,0:T(8,128)(2,1)S(1)}, u32[]{:S(2)}, u32[]{:S(2)}) collective-permute-start(bf16[4,72,256]{2,1,0:T(8,128)(2,1)S(1)} %get-tuple-element.168), channel_id=1, source_target_pairs={{0,16},{4,20},{8,24},{12,28},{16,0},{20,4},{24,8},{28,12},{1,17},{... | collective-permute-start | bytes 442376 | tf_op jit(solution)/shard_map/ppermute | solution.py:485
  249.1 0.8 fusion.28
  250.5 3.2 %collective-permute-start.24 = (bf16[2,72,256]{2,1,0:T(8,128)(2,1)S(1)}, bf16[2,72,256]{2,1,0:T(8,128)(2,1)S(1)}, u32[]{:S(2)}, u32[]{:S(2)}) collective-permute-start(bf16[2,72,256]{2,1,0:T(8,128)(2,1)S(1)} %get-tuple-element.174), channel_id=1, source_target_pairs={{0,16},{4,20},{8,24},{12,28},{16,0},{20,4},{24,8},{28,12},{1,17},{... | collective-permute-start | bytes 221192 | tf_op jit(solution)/shard_map/ppermute | solution.py:485
  253.7 3.0 %collective-permute-done.27 = bf16[4,72,256]{2,1,0:T(8,128)(2,1)S(1)} collective-permute-done((bf16[4,72,256]{2,1,0:T(8,128)(2,1)S(1)}, bf16[4,72,256]{2,1,0:T(8,128)(2,1)S(1)}, u32[]{:S(2)}, u32[]{:S(2)}) %collective-permute-start.27) | collective-permute-done | bytes 147488 | tf_op jit(solution)/shard_map/ppermute | solution.py:485
  256.8 1.4 collective-permute-start.28
  259.1 2.1 collective-permute-done.28
  261.4 1.4 collective-permute-done.25
  262.9 2.3 collective-permute-done.29
  265.3 0.9 fusion.30
  (133 shorter events, 9.8 us)
Async XLA Ops:
  7.2 19.7 %copy-start.17 = (f32[64,256]{1,0:T(8,128)S(1)}, f32[64,256]{1,0:T(8,128)}, u32[]{:S(2)}) copy-start(f32[64,256]{1,0:T(8,128)} %param.16) | copy-start | bytes 196612
  7.2 102.6 %all-gather.2.cloned.1.call-start = ((), (), s32[]{:S(2)}) async-start(), calls=%async_computation | async-start | bytes 4325376 | tf_op jit(solution)/shard_map/all_gather | solution.py:652
  9.1 5.6 %collective-permute-start = (bf16[1,72,256]{2,1,0:T(8,128)(2,1)S(1)}, bf16[1,72,256]{2,1,0:T(8,128)(2,1)S(1)}, u32[]{:S(2)}, u32[]{:S(2)}) collective-permute-start(bf16[1,72,256]{2,1,0:T(8,128)(2,1)S(1)} %get-tuple-element.195), channel_id=1, source_target_pairs={{0,8},{4,12},{8,0},{12,4},{16,24},{20,28},{24,16},{28,20},{1,9},{5... | collective-permute-start | bytes 110600 | tf_op jit(solution)/shard_map/ppermute | solution.py:485
  14.7 4.0 %collective-permute-start.5 = (bf16[1,72,256]{2,1,0:T(8,128)(2,1)S(1)}, bf16[1,72,256]{2,1,0:T(8,128)(2,1)S(1)}, u32[]{:S(2)}, u32[]{:S(2)}) collective-permute-start(bf16[1,72,256]{2,1,0:T(8,128)(2,1)S(1)} %get-tuple-element.194), channel_id=1, source_target_pairs={{0,2},{1,3},{2,0},{3,1},{4,6},{5,7},{6,4},{7,5},{8,10},{9,11},{10,... | collective-permute-start | bytes 110600 | tf_op jit(solution)/shard_map/ppermute | solution.py:485
  18.8 5.3 %collective-permute-start.1 = (bf16[2,72,256]{2,1,0:T(8,128)(2,1)S(1)}, bf16[2,72,256]{2,1,0:T(8,128)(2,1)S(1)}, u32[]{:S(2)}, u32[]{:S(2)}) collective-permute-start(bf16[2,72,256]{2,1,0:T(8,128)(2,1)S(1)} %pad_maximum_fusion.9), channel_id=1, source_target_pairs={{0,16},{4,20},{8,24},{12,28},{16,0},{20,4},{24,8},{28,12},{1,17},{... | collective-permute-start | bytes 221192 | tf_op jit(solution)/shard_map/ppermute | solution.py:485
  21.4 4.4 %collective-permute-start.6 = (bf16[2,72,256]{2,1,0:T(8,128)(2,1)S(1)}, bf16[2,72,256]{2,1,0:T(8,128)(2,1)S(1)}, u32[]{:S(2)}, u32[]{:S(2)}) collective-permute-start(bf16[2,72,256]{2,1,0:T(8,128)(2,1)S(1)} %pad_maximum_fusion.10), channel_id=1, source_target_pairs={{0,8},{4,12},{8,0},{12,4},{16,24},{20,28},{24,16},{28,20},{1,9},{5... | collective-permute-start | bytes 221192 | tf_op jit(solution)/shard_map/ppermute | solution.py:485
  25.9 7.5 %collective-permute-start.7 = (bf16[4,72,256]{2,1,0:T(8,128)(2,1)S(1)}, bf16[4,72,256]{2,1,0:T(8,128)(2,1)S(1)}, u32[]{:S(2)}, u32[]{:S(2)}) collective-permute-start(bf16[4,72,256]{2,1,0:T(8,128)(2,1)S(1)} %pad_maximum_fusion.7), channel_id=1, source_target_pairs={{0,16},{4,20},{8,24},{12,28},{16,0},{20,4},{24,8},{28,12},{1,17},{... | collective-permute-start | bytes 442376 | tf_op jit(solution)/shard_map/ppermute | solution.py:485
  27.8 8.7 %collective-permute-start.2 = (bf16[4,72,256]{2,1,0:T(8,128)(2,1)S(1)}, bf16[4,72,256]{2,1,0:T(8,128)(2,1)S(1)}, u32[]{:S(2)}, u32[]{:S(2)}) collective-permute-start(bf16[4,72,256]{2,1,0:T(8,128)(2,1)S(1)} %pad_maximum_fusion.6), channel_id=1, source_target_pairs={{0,4},{4,0},{8,12},{12,8},{16,20},{20,16},{24,28},{28,24},{1,5},{5... | collective-permute-start | bytes 442376 | tf_op jit(solution)/shard_map/ppermute | solution.py:485
  33.5 7.7 %collective-permute-start.8 = (bf16[8,72,256]{2,1,0:T(8,128)(2,1)S(1)}, bf16[8,72,256]{2,1,0:T(8,128)(2,1)S(1)}, u32[]{:S(2)}, u32[]{:S(2)}) collective-permute-start(bf16[8,72,256]{2,1,0:T(8,128)(2,1)S(1)} %pad_maximum_fusion.5), channel_id=1, source_target_pairs={{0,4},{4,0},{8,12},{12,8},{16,20},{20,16},{24,28},{28,24},{1,5},{5... | collective-permute-start | bytes 884744 | tf_op jit(solution)/shard_map/ppermute | solution.py:485
  36.6 7.7 %copy-start.16 = (f32[64,256]{0,1:T(8,128)S(1)}, f32[64,256]{0,1:T(8,128)}, u32[]{:S(2)}) copy-start(f32[64,256]{0,1:T(8,128)} %copy.33) | copy-start | bytes 196612
  36.6 6.8 %collective-permute-start.3 = (bf16[8,72,256]{2,1,0:T(8,128)(2,1)S(1)}, bf16[8,72,256]{2,1,0:T(8,128)(2,1)S(1)}, u32[]{:S(2)}, u32[]{:S(2)}) collective-permute-start(bf16[8,72,256]{2,1,0:T(8,128)(2,1)S(1)} %pad_maximum_fusion.4), channel_id=1, source_target_pairs={{0,2},{1,3},{2,0},{3,1},{4,6},{5,7},{6,4},{7,5},{8,10},{9,11},{10,... | collective-permute-start | bytes 884744 | tf_op jit(solution)/shard_map/ppermute | solution.py:485
  41.3 3.1 %collective-permute-start.9 = (bf16[16,72,256]{2,1,0:T(8,128)(2,1)S(1)}, bf16[16,72,256]{2,1,0:T(8,128)(2,1)S(1)}, u32[]{:S(2)}, u32[]{:S(2)}) collective-permute-start(bf16[16,72,256]{2,1,0:T(8,128)(2,1)S(1)} %pad_maximum_fusion.3), channel_id=1, source_target_pairs={{0,1},{1,0},{2,3},{3,2},{4,5},{5,4},{6,7},{7,6},{8,9},{9,8},{10,11... | collective-permute-start | bytes 1769480 | tf_op jit(solution)/shard_map/ppermute | solution.py:485
  44.3 2.2 collective-permute-start.4
  48.2 0.7 copy-start.4
  64.0 8.4 %copy-start.28 = (s32[8,256]{1,0:T(8,128)S(1)}, s32[8,256]{1,0:T(8,128)}, u32[]{:S(2)}) copy-start(s32[8,256]{1,0:T(8,128)} %param.15) | copy-start | bytes 24580
  64.0 8.4 %copy-start.12 = (bf16[8,256,512]{2,1,0:T(8,128)(2,1)S(1)}, bf16[8,256,512]{2,1,0:T(8,128)(2,1)}, u32[]{:S(2)}) copy-start(bf16[8,256,512]{2,1,0:T(8,128)(2,1)} %param.14) | copy-start | bytes 6291460
  64.0 3.0 %collective-permute-start.10 = (bf16[8,272,256]{2,1,0:T(8,128)(2,1)}, bf16[8,272,256]{2,1,0:T(8,128)(2,1)S(1)}, u32[]{:S(2)}, u32[]{:S(2)}) collective-permute-start(bf16[8,272,256]{2,1,0:T(8,128)(2,1)} %get-tuple-element.78), channel_id=1, source_target_pairs={{0,1},{1,0},{2,3},{3,2},{4,5},{5,4},{6,7},{7,6},{8,9},{9,8},{10,11... | collective-permute-start | bytes 3342344 | tf_op jit(solution)/shard_map/ppermute | solution.py:485
  68.6 27.7 %collective-permute-start.11 = (bf16[8,272,256]{2,1,0:T(8,128)(2,1)S(1)}, bf16[8,272,256]{2,1,0:T(8,128)(2,1)S(1)}, u32[]{:S(2)}, u32[]{:S(2)}) collective-permute-start(bf16[8,272,256]{2,1,0:T(8,128)(2,1)S(1)} %fusion), channel_id=1, source_target_pairs={{0,2},{1,3},{4,6},{5,7},{8,10},{9,11},{12,14},{13,15},{16,18},{17,... | collective-permute-start | bytes 3342344 | tf_op jit(solution)/shard_map/ppermute | solution.py:501
  74.2 22.0 %copy-start.11 = (bf16[8,272,256]{2,1,0:T(8,128)(2,1)S(1)}, bf16[8,272,256]{2,1,0:T(8,128)(2,1)}, u32[]{:S(2)}) copy-start(bf16[8,272,256]{2,1,0:T(8,128)(2,1)} %get-tuple-element.77) | copy-start | bytes 3342340
  87.8 3.4 %copy-start = (bf16[8,8,256,256]{3,2,1,0:T(8,128)(2,1)}, bf16[8,8,256,256]{3,2,1,0:T(8,128)(2,1)S(1)}, u32[]{:S(2)}) copy-start(bf16[8,8,256,256]{3,2,1,0:T(8,128)(2,1)S(1)} %get-tuple-element.81.pk) | copy-start | bytes 25165828
  96.2 3.5 %copy-start.5 = (f32[4,512]{1,0:T(4,128)S(1)}, f32[4,512]{1,0:T(4,128)}, u32[]{:S(2)}) copy-start(f32[4,512]{1,0:T(4,128)} %get-tuple-element.73.norms) | copy-start | bytes 24580
  96.9 2.8 %collective-permute-start.12 = (bf16[8,272,256]{2,1,0:T(8,128)(2,1)S(1)}, bf16[8,272,256]{2,1,0:T(8,128)(2,1)S(1)}, u32[]{:S(2)}, u32[]{:S(2)}) collective-permute-start(bf16[8,272,256]{2,1,0:T(8,128)(2,1)S(1)} %get-tuple-element.164), channel_id=1, source_target_pairs={{0,1},{1,0},{2,3},{3,2},{4,5},{5,4},{6,7},{7,6},{8,9},{9,8},{10,11... | collective-permute-start | bytes 3342344 | tf_op jit(solution)/shard_map/ppermute | solution.py:485
  108.8 1.0 copy-start.1
  109.8 39.5 %copy-start.3 = (f32[8,8,256]{2,1,0:T(8,128)S(1)}, f32[8,8,256]{2,1,0:T(8,128)}, u32[]{:S(2)}) copy-start(f32[8,8,256]{2,1,0:T(8,128)} %get-tuple-element.95.recip) | copy-start | bytes 196612
  149.0 11.5 %collective-permute-start.13 = (bf16[512,2048]{1,0:T(8,128)(2,1)}, bf16[512,2048]{1,0:T(8,128)(2,1)}, u32[]{:S(2)}, u32[]{:S(2)}) collective-permute-start(bf16[512,2048]{1,0:T(8,128)(2,1)} %get-tuple-element.98), channel_id=1, source_target_pairs={{0,1},{1,0},{2,3},{3,2},{4,5},{5,4},{6,7},{7,6},{8,9},{9,8},{10,11... | collective-permute-start | bytes 6291464 | tf_op jit(solution)/shard_map/ppermute | solution.py:485
  160.5 5.2 %collective-permute-start.15 = (bf16[8,272,256]{2,1,0:T(8,128)(2,1)}, bf16[8,272,256]{2,1,0:T(8,128)(2,1)}, u32[]{:S(2)}, u32[]{:S(2)}) collective-permute-start(bf16[8,272,256]{2,1,0:T(8,128)(2,1)} %get-tuple-element.102), channel_id=1, source_target_pairs={{0,1},{1,0},{2,3},{3,2},{4,5},{5,4},{6,7},{7,6},{8,9},{9,8},{10,11... | collective-permute-start | bytes 3342344 | tf_op jit(solution)/shard_map/ppermute | solution.py:485
  161.2 4.5 %copy-start.9 = (bf16[8,272,256]{2,1,0:T(8,128)(2,1)S(1)}, bf16[8,272,256]{2,1,0:T(8,128)(2,1)}, u32[]{:S(2)}) copy-start(bf16[8,272,256]{2,1,0:T(8,128)(2,1)} %get-tuple-element.101) | copy-start | bytes 3342340
  168.3 28.9 %collective-permute-start.16 = (bf16[8,272,256]{2,1,0:T(8,128)(2,1)}, bf16[8,272,256]{2,1,0:T(8,128)(2,1)}, u32[]{:S(2)}, u32[]{:S(2)}) collective-permute-start(bf16[8,272,256]{2,1,0:T(8,128)(2,1)} %fusion.3), channel_id=1, source_target_pairs={{2,0},{3,1},{6,4},{7,5},{10,8},{11,9},{14,12},{15,13},{18,16},{19,... | collective-permute-start | bytes 3342344 | tf_op jit(solution)/shard_map/ppermute | solution.py:501
  169.6 30.9 %collective-permute-start.14 = (bf16[256,2048]{1,0:T(8,128)(2,1)}, bf16[256,2048]{1,0:T(8,128)(2,1)}, u32[]{:S(2)}, u32[]{:S(2)}) collective-permute-start(bf16[256,2048]{1,0:T(8,128)(2,1)} %get-tuple-element.100), channel_id=1, source_target_pairs={{0,4},{4,0},{8,12},{12,8},{16,20},{20,16},{24,28},{28,24},{1,5},{5... | collective-permute-start | bytes 3145736 | tf_op jit(solution)/shard_map/ppermute | solution.py:578
  170.1 1.2 copy-start.2
  171.3 25.9 %copy-start.10 = (bf16[8,272,256]{2,1,0:T(8,128)(2,1)S(1)}, bf16[8,272,256]{2,1,0:T(8,128)(2,1)}, u32[]{:S(2)}) copy-start(bf16[8,272,256]{2,1,0:T(8,128)(2,1)} %get-tuple-element.101) | copy-start | bytes 3342340
  200.4 6.6 %copy-start.8 = (f32[2,512]{1,0:T(2,128)S(1)}, f32[2,512]{1,0:T(2,128)}, u32[]{:S(2)}) copy-start(f32[2,512]{1,0:T(2,128)} %get-tuple-element.118.norm_two) | copy-start | bytes 12292
  200.4 6.6 %collective-permute-start.17 = (bf16[8,272,256]{2,1,0:T(8,128)(2,1)}, bf16[8,272,256]{2,1,0:T(8,128)(2,1)}, u32[]{:S(2)}, u32[]{:S(2)}) collective-permute-start(bf16[8,272,256]{2,1,0:T(8,128)(2,1)} %get-tuple-element.162), channel_id=1, source_target_pairs={{0,1},{1,0},{2,3},{3,2},{4,5},{5,4},{6,7},{7,6},{8,9},{9,8},{10,11... | collective-permute-start | bytes 3342344 | tf_op jit(solution)/shard_map/ppermute | solution.py:485
  200.4 6.6 %copy-start.6 = (f32[512,512]{1,0:T(8,128)S(1)}, f32[512,512]{1,0:T(8,128)}, u32[]{:S(2)}) copy-start(f32[512,512]{1,0:T(8,128)} %get-tuple-element.117.out_proj) | copy-start | bytes 3145732
  200.4 6.6 %copy-start.7 = (f32[512,512]{1,0:T(8,128)S(1)}, f32[512,512]{1,0:T(8,128)}, u32[]{:S(2)}) copy-start(f32[512,512]{1,0:T(8,128)} %get-tuple-element.116.query_weight) | copy-start | bytes 3145732
  202.5 24.7 %collective-permute-start.18 = (bf16[64,2048]{1,0:T(8,128)(2,1)S(1)}, bf16[64,2048]{1,0:T(8,128)(2,1)S(1)}, u32[]{:S(2)}, u32[]{:S(2)}) collective-permute-start(bf16[64,2048]{1,0:T(8,128)(2,1)S(1)} %get-tuple-element.122), channel_id=1, source_target_pairs={{0,8},{4,12},{8,0},{12,4},{16,24},{20,28},{24,16},{28,20},{1,9},{5... | collective-permute-start | bytes 786440 | tf_op jit(solution)/shard_map/ppermute | solution.py:578
  203.1 24.1 %collective-permute-start.19 = (bf16[64,2048]{1,0:T(8,128)(2,1)S(1)}, bf16[64,2048]{1,0:T(8,128)(2,1)S(1)}, u32[]{:S(2)}, u32[]{:S(2)}) collective-permute-start(bf16[64,2048]{1,0:T(8,128)(2,1)S(1)} %get-tuple-element.123), channel_id=1, source_target_pairs={{0,16},{4,20},{8,24},{12,28},{16,0},{20,4},{24,8},{28,12},{1,17},{... | collective-permute-start | bytes 786440 | tf_op jit(solution)/shard_map/ppermute | solution.py:578
  204.9 22.3 %collective-permute-start.20 = (bf16[64,2048]{1,0:T(8,128)(2,1)S(1)}, bf16[64,2048]{1,0:T(8,128)(2,1)}, u32[]{:S(2)}, u32[]{:S(2)}) collective-permute-start(bf16[64,2048]{1,0:T(8,128)(2,1)S(1)} %get-tuple-element.124), channel_id=1, source_target_pairs={{0,24},{4,28},{8,16},{12,20},{16,8},{20,12},{24,0},{28,4},{1,25},{... | collective-permute-start | bytes 786440 | tf_op jit(solution)/shard_map/ppermute | solution.py:578
  227.2 0.7 copy-start.18
  227.3 0.8 copy-start.20
  227.3 4.5 %collective-permute-start.21 = (bf16[2,16,72,256]{3,2,1,0:T(8,128)(2,1)}, bf16[2,16,72,256]{3,2,1,0:T(8,128)(2,1)}, u32[]{:S(2)}, u32[]{:S(2)}) collective-permute-start(bf16[2,16,72,256]{3,2,1,0:T(8,128)(2,1)} %get-tuple-element.129), channel_id=1, source_target_pairs={{0,1},{1,0},{2,3},{3,2},{4,5},{5,4},{6,7},{7,6},{8,9},{9,8},{10,11... | collective-permute-start | bytes 3538952 | tf_op jit(solution)/shard_map/ppermute | solution.py:485
  228.0 1.9 copy-start.19
  228.0 1.9 copy-start.21
  233.6 6.5 %collective-permute-start.30 = (bf16[64,1024]{1,0:T(8,128)(2,1)S(1)}, bf16[64,1024]{1,0:T(8,128)(2,1)S(1)}, u32[]{:S(2)}, u32[]{:S(2)}) collective-permute-start(bf16[64,1024]{1,0:T(8,128)(2,1)S(1)} %bitcast.120), channel_id=1, source_target_pairs={{0,2},{1,3},{2,0},{3,1},{4,6},{5,7},{6,4},{7,5},{8,10},{9,11},{10,... | collective-permute-start | bytes 393224 | tf_op jit(solution)/shard_map/ppermute | solution.py:485
  235.2 5.0 %copy-start.14 = (f32[512,64]{0,1:T(8,128)S(1)}, f32[512,64]{0,1:T(8,128)}, u32[]{:S(2)}) copy-start(f32[512,64]{0,1:T(8,128)} %param.21) | copy-start | bytes 393220
  235.2 5.0 %copy-start.24 = (f32[512,64]{0,1:T(8,128)S(1)}, f32[512,64]{0,1:T(8,128)}, u32[]{:S(2)}) copy-start(f32[512,64]{0,1:T(8,128)} %param.24) | copy-start | bytes 393220
  235.2 5.0 %copy-start.25 = (f32[512,64]{0,1:T(8,128)S(1)}, f32[512,64]{0,1:T(8,128)}, u32[]{:S(2)}) copy-start(f32[512,64]{0,1:T(8,128)} %param.25) | copy-start | bytes 393220
  235.2 10.0 %collective-permute-start.22 = (bf16[8,72,256]{2,1,0:T(8,128)(2,1)S(1)}, bf16[8,72,256]{2,1,0:T(8,128)(2,1)S(1)}, u32[]{:S(2)}, u32[]{:S(2)}) collective-permute-start(bf16[8,72,256]{2,1,0:T(8,128)(2,1)S(1)} %get-tuple-element.152), channel_id=1, source_target_pairs={{0,2},{1,3},{2,0},{3,1},{4,6},{5,7},{6,4},{7,5},{8,10},{9,11},{10,... | collective-permute-start | bytes 884744 | tf_op jit(solution)/shard_map/ppermute | solution.py:485
  237.4 8.4 %collective-permute-start.26 = (bf16[8,72,256]{2,1,0:T(8,128)(2,1)S(1)}, bf16[8,72,256]{2,1,0:T(8,128)(2,1)S(1)}, u32[]{:S(2)}, u32[]{:S(2)}) collective-permute-start(bf16[8,72,256]{2,1,0:T(8,128)(2,1)S(1)} %get-tuple-element.154), channel_id=1, source_target_pairs={{0,4},{4,0},{8,12},{12,8},{16,20},{20,16},{24,28},{28,24},{1,5},{5... | collective-permute-start | bytes 884744 | tf_op jit(solution)/shard_map/ppermute | solution.py:485
  238.2 10.9 %copy-start.15 = (f32[64,512]{1,0:T(8,128)S(1)}, f32[64,512]{1,0:T(8,128)}, u32[]{:S(2)}) copy-start(f32[64,512]{1,0:T(8,128)} %param.20) | copy-start | bytes 393220
  238.2 10.9 %copy-start.26 = (f32[64,512]{1,0:T(8,128)S(1)}, f32[64,512]{1,0:T(8,128)}, u32[]{:S(2)}) copy-start(f32[64,512]{1,0:T(8,128)} %param.22) | copy-start | bytes 393220
  238.2 10.8 %copy-start.27 = (f32[64,512]{1,0:T(8,128)S(1)}, f32[64,512]{1,0:T(8,128)}, u32[]{:S(2)}) copy-start(f32[64,512]{1,0:T(8,128)} %param.23) | copy-start | bytes 393220
  245.3 5.2 %collective-permute-start.23 = (bf16[4,72,256]{2,1,0:T(8,128)(2,1)S(1)}, bf16[4,72,256]{2,1,0:T(8,128)(2,1)S(1)}, u32[]{:S(2)}, u32[]{:S(2)}) collective-permute-start(bf16[4,72,256]{2,1,0:T(8,128)(2,1)S(1)} %get-tuple-element.166), channel_id=1, source_target_pairs={{0,4},{4,0},{8,12},{12,8},{16,20},{20,16},{24,28},{28,24},{1,5},{5... | collective-permute-start | bytes 442376 | tf_op jit(solution)/shard_map/ppermute | solution.py:485
  245.9 19.4 %copy-start.13 = (f32[32832]{0:T(1024)S(1)}, f32[32832]{0:T(1024)}, u32[]{:S(2)}) copy-start(f32[32832]{0:T(1024)} %param.17) | copy-start | bytes 393988
  245.9 19.4 %copy-start.22 = (f32[32832]{0:T(1024)S(1)}, f32[32832]{0:T(1024)}, u32[]{:S(2)}) copy-start(f32[32832]{0:T(1024)} %param.18) | copy-start | bytes 393988
  245.9 19.4 %copy-start.23 = (f32[32832]{0:T(1024)S(1)}, f32[32832]{0:T(1024)}, u32[]{:S(2)}) copy-start(f32[32832]{0:T(1024)} %param.19) | copy-start | bytes 393988
  245.9 10.8 %collective-permute-start.27 = (bf16[4,72,256]{2,1,0:T(8,128)(2,1)S(1)}, bf16[4,72,256]{2,1,0:T(8,128)(2,1)S(1)}, u32[]{:S(2)}, u32[]{:S(2)}) collective-permute-start(bf16[4,72,256]{2,1,0:T(8,128)(2,1)S(1)} %get-tuple-element.168), channel_id=1, source_target_pairs={{0,16},{4,20},{8,24},{12,28},{16,0},{20,4},{24,8},{28,12},{1,17},{... | collective-permute-start | bytes 442376 | tf_op jit(solution)/shard_map/ppermute | solution.py:485
  250.5 8.3 %collective-permute-start.24 = (bf16[2,72,256]{2,1,0:T(8,128)(2,1)S(1)}, bf16[2,72,256]{2,1,0:T(8,128)(2,1)S(1)}, u32[]{:S(2)}, u32[]{:S(2)}) collective-permute-start(bf16[2,72,256]{2,1,0:T(8,128)(2,1)S(1)} %get-tuple-element.174), channel_id=1, source_target_pairs={{0,16},{4,20},{8,24},{12,28},{16,0},{20,4},{24,8},{28,12},{1,17},{... | collective-permute-start | bytes 221192 | tf_op jit(solution)/shard_map/ppermute | solution.py:485
  256.8 4.4 %collective-permute-start.28 = (bf16[2,72,256]{2,1,0:T(8,128)(2,1)S(1)}, bf16[2,72,256]{2,1,0:T(8,128)(2,1)S(1)}, u32[]{:S(2)}, u32[]{:S(2)}) collective-permute-start(bf16[2,72,256]{2,1,0:T(8,128)(2,1)S(1)} %get-tuple-element.176), channel_id=1, source_target_pairs={{0,8},{4,12},{8,0},{12,4},{16,24},{20,28},{24,16},{28,20},{1,9},{5... | collective-permute-start | bytes 221192 | tf_op jit(solution)/shard_map/ppermute | solution.py:485
  258.8 4.0 %collective-permute-start.25 = (bf16[1,72,256]{2,1,0:T(8,128)(2,1)S(1)}, bf16[1,72,256]{2,1,0:T(8,128)(2,1)S(1)}, u32[]{:S(2)}, u32[]{:S(2)}) collective-permute-start(bf16[1,72,256]{2,1,0:T(8,128)(2,1)S(1)} %fusion.23), channel_id=1, source_target_pairs={{0,8},{4,12},{8,0},{12,4},{16,24},{20,28},{24,16},{28,20},{1,9},{5... | collective-permute-start | bytes 110600 | tf_op jit(solution)/shard_map/ppermute | solution.py:485
  261.2 4.0 %collective-permute-start.29 = (bf16[1,72,256]{2,1,0:T(8,128)(2,1)S(1)}, bf16[1,72,256]{2,1,0:T(8,128)(2,1)S(1)}, u32[]{:S(2)}, u32[]{:S(2)}) collective-permute-start(bf16[1,72,256]{2,1,0:T(8,128)(2,1)S(1)} %fusion.20), channel_id=1, source_target_pairs={{0,2},{1,3},{2,0},{3,1},{4,6},{5,7},{6,4},{7,5},{8,10},{9,11},{10,... | collective-permute-start | bytes 110600 | tf_op jit(solution)/shard_map/ppermute | solution.py:485
Sparse Core Ops, SparseCore 0:
  14.8 64.7 all-gather.1

commit v3 on v2

--- a/solution.py
+++ b/solution.py
@@ -360,7 +360,8 @@
     turned,
     input_grad,
     leave,
-    stay,
+    stay_left,
+    stay_right,
     flat,
     laters,
     flows,
@@ -415,16 +416,16 @@
         half = width // 2
         first = core[0] == 0
         leave[...] = jnp.zeros_like(leave)
-        stay[...] = jnp.zeros_like(stay)
-        for part in range(2):
+        for part, stay in enumerate((stay_left, stay_right)):
             count = leave.shape[1]
+            stay[...] = jnp.zeros_like(stay)
             columns = slice(part * half, (part + 1) * half)
             for spot in range(count):
                 low = starts[owners[part][spot]]
                 high = starts[owners[part][spot + count]]
                 low = whole[low : low + rows, columns]
                 high = whole[high : high + rows, columns]
-                stay[part, spot, :rows] = jnp.where(first, low, high)
+                stay[spot, :rows] = jnp.where(first, low, high)
                 leave[part, spot, :rows] = jnp.where(first, high, low).astype(LOW)
 
 
@@ -538,27 +539,29 @@
     return spot
 
 
-def gather_doubling(value, order, early):
+def gather_doubling(value, order, late):
     value = value[None]
-    for axis, bit in order:
+    for step, (axis, bit) in enumerate(order):
         come = flip(value, axis, bit)
-        early.append(come)
+        if step == 0:
+            come, late = lax.optimization_barrier((come, late))
         low = bit_of(axis, bit) == 0
         value = jnp.concatenate([jnp.where(low, value, come), jnp.where(low, come, value)], axis=0)
-    return value
+    return value, late
 
 
 def total_of(terms):
     return sum(term.astype(F32) for term in terms)
 
 
-def scatter_step(terms, axis, bit, leave=None):
+def scatter_step(terms, axis, bit, late=None):
     mine = bit_of(axis, bit)
-    if leave is None:
-        leave = total_of([lax.dynamic_index_in_dim(term, 1 - mine, 0, keepdims=False) for term in terms]).astype(LOW)
+    leave = total_of([lax.dynamic_index_in_dim(term, 1 - mine, 0, keepdims=False) for term in terms]).astype(LOW)
+    if late is not None:
+        leave, late = lax.optimization_barrier((leave, late))
     come = flip(leave, axis, bit)
     stay = total_of([lax.dynamic_index_in_dim(term, mine, 0, keepdims=False) for term in terms])
-    return [stay, come]
+    return [stay, come], late
 
 
 def split_rows(terms, axis, bits, low, tie):
@@ -579,12 +582,6 @@
         for other, leave in enumerate(leaving, 1)
     ]
     return tie, [part(mine)] + come
-
-
-def scatter_halving(terms, order):
-    for axis, bit in order:
-        terms = scatter_step([t.reshape((2, t.shape[0] // 2) + t.shape[1:]) for t in terms], axis, bit)
-    return total_of(terms)[0]
 
 
 def adamw(weight, first, second, grad, rate, decay):
@@ -641,20 +638,23 @@
     framed = lax.dynamic_update_slice(
         jnp.zeros((held_rows * width,), LOW), att_weights.astype(LOW), (offset,)
     ).reshape(held_rows, width)
-    early = []
+    group_width = ffn_in.shape[1]
+    ffn_pair = (ffn_in, ffn_out)
     halves = [framed[:, : width // 2], framed[:, width // 2 :]]
-    gathered = [gather_doubling(half, order, early) for half, order in zip(halves, gather_orders())]
+    gathered = []
+    for half, order in zip(halves, gather_orders()):
+        whole, ffn_pair = gather_doubling(half, order, ffn_pair)
+        gathered.append(whole)
     spots = [[place_in(order[::-1], i) for i in range(devices)] for order in gather_orders()]
     whole_rows = -(-(starts[-1] + rows) // 8) * 8
     group_width = ffn_in.shape[1]
-    pair = jnp.concatenate([ffn_in.astype(LOW), ffn_out.astype(LOW).T], axis=1)
-    pair, early[0] = lax.optimization_barrier((pair, early[0]))
+    pair = jnp.concatenate([ffn_pair[0].astype(LOW), ffn_pair[1].astype(LOW).T], axis=1)
     pair = lax.all_gather(pair, ("seq", "dp"), axis=0, tiled=True)
     pair = pair.reshape(groups, width, 2 * group_width)
 
     weights, out_weight, norms = pl.pallas_call(
         functools.partial(unpack_kernel, starts, spots, rows),
-        out_shape=[pltpu.VMEM((3 * width, width), LOW), pltpu.VMEM((width, width), LOW), array((4, width), F32)],
+        out_shape=[pltpu.VMEM((3 * width, width), LOW), pltpu.VMEM((width, width), LOW), pltpu.VMEM((4, width), F32)],
         scratch_shapes=[pltpu.VMEM((whole_rows, width), F32)],
         name="unpack",
         compiler_params=pltpu.CompilerParams(vmem_limit_bytes=VMEM_LIMIT),
@@ -692,7 +692,7 @@
         ]
 
     args = (tokens, norms, weights, omega_parts)
-    outs = [array(flat, LOW)] * 2 + [array(held, LOW), pltpu.VMEM(feat, LOW)] + [array(state_shape, LOW)] * 2
+    outs = [array(flat, LOW)] * 2 + [array(held, LOW), pltpu.VMEM(feat, LOW)] + [pltpu.VMEM(state_shape, LOW)] * 2
     turned, uk, value, pk, own, their = call(
         functools.partial(keys_kernel, heads, size),
         seqs,
@@ -757,7 +757,7 @@
     come_pair = flip(leave, "seq", 0)
 
     args = (grad_middle, out_weight, mixed, recip, pq)
-    outs = [array(held, LOW)] + [array(state_shape, LOW)] * 2
+    outs = [array(held, LOW)] + [pltpu.VMEM(state_shape, LOW)] * 2
     outs = outs + [array((width, width), F32)]
     outers, own, their, out_proj = call(
         functools.partial(outer_kernel, heads, size),
@@ -773,7 +773,13 @@
     )
     their, come_pair = lax.optimization_barrier((their, come_pair))
     dp_rows = width // lax.axis_size("dp")
-    omega_low, terms = split_rows([stay, come_pair], "dp", [0], width // 2, omega_low)
+    columns = stay.shape[1]
+    near = bit_of("dp", 0)
+    sent = total_of(
+        [lax.dynamic_index_in_dim(t.reshape(2, width // 2, columns), 1 - near, 0, keepdims=False) for t in (stay, come_pair)]
+    ).astype(LOW)
+    sent, omega_low = lax.optimization_barrier((sent, omega_low))
+    come_near = flip(sent, "dp", 0)
     beside, far, omega_low = send_half(own, their, False, omega_low)
     args = (turned, omega_low, outers, value, pq, pk, score, core, keep, come, uq, uk)
     outs = [array(flat, LOW)] * 3
@@ -797,19 +803,36 @@
     far, query_grad = lax.optimization_barrier((far, query_grad))
     keep, come = receive_half(own, beside, far, False)
     high = list(range(axis_bits("dp") - 1, 0, -1))
-    omega_low, terms = split_rows(terms, "dp", high[:2], dp_rows << max(len(high) - 2, 0), omega_low)
+    ways = 1 << len(high[:2])
+    low = width // 2 // ways
+    chosen = (lax.axis_index("dp") >> (high[0] + 1 - len(high[:2]))) & (ways - 1)
+
+    def part(which):
+        pieces = [
+            lax.dynamic_slice(t.reshape(2, ways, low, columns), (near, which, 0, 0), (1, 1, low, columns))
+            for t in (stay, come_pair)
+        ]
+        pieces.append(lax.dynamic_index_in_dim(come_near.reshape(ways, low, columns), which, 0))
+        return total_of([p.reshape(low, columns) for p in pieces]).astype(LOW)
+
+    leaving = [part(chosen ^ other) for other in range(1, ways)]
+    leaving, omega_low = lax.optimization_barrier((leaving, omega_low))
+    terms = [part(chosen)]
+    for other, leave_part in enumerate(leaving, 1):
+        jump = other << (high[0] + 1 - len(high[:2]))
+        terms.append(lax.ppermute(leave_part, "dp", [(i, i ^ jump) for i in range(lax.axis_size("dp"))]))
     orders = scatter_orders()
     owners = [sorted(range(devices), key=lambda i: place_in(order, i)) for order in orders]
     piece_shape = (2, devices // 2, held_rows, width // 2)
     args = (tokens, norms, grad_middle, weights, omega_low, value, pk, core, keep, come)
     more = (uk, query_grad, key_part, value_part, query_weight, out_proj, norm_two_grad, turned)
-    input_grad, leave, stay = call(
+    input_grad, leave, *stays = call(
         functools.partial(back_key_kernel, heads, size, (starts, rows, owners)),
         seqs,
         args + more,
         [spec(a) for a in args[:7]] + [in_smem, *states] + [spec(a) for a in more],
-        [array(tokens.shape, F32), array(piece_shape, LOW), array(piece_shape, F32)],
-        [per_seq(tokens.shape), fixed(piece_shape), fixed(piece_shape)],
+        [array(tokens.shape, F32), array(piece_shape, LOW)] + [array(piece_shape[1:], F32)] * 2,
+        [per_seq(tokens.shape), fixed(piece_shape)] + [fixed(piece_shape[1:])] * 2,
         "back_key",
         7 * unit,
         chip=(),
@@ -826,16 +849,23 @@
     come_pieces = flip(leave, "seq", 0)
     for step, bit in enumerate(high[2:]):
         omega_low, terms = split_rows(terms, "dp", [bit], dp_rows << (len(high) - 3 - step), omega_low)
-    terms, come_pieces = lax.optimization_barrier(([total_of(terms)], come_pieces))
+    sums = []
+    for index, (stay, order) in enumerate(zip(stays, orders)):
+        part = [stay, come_pieces[index]]
+        for step, (axis, bit) in enumerate(order[1:]):
+            part = [t.reshape((2, t.shape[0] // 2) + t.shape[1:]) for t in part]
+            if index == 0 and step == 1:
+                part, terms = scatter_step(part, axis, bit, terms)
+            else:
+                part, _ = scatter_step(part, axis, bit)
+        sums.append(total_of(part)[0])
+    terms = [total_of(terms)]
     for bit in range(axis_bits("seq") - 1, 0, -1):
         terms = [t.reshape(t.shape[0], 2, -1) for t in terms]
         side = bit_of("seq", bit)
         sent = total_of([lax.dynamic_index_in_dim(t, 1 - side, 1, keepdims=False) for t in terms]).astype(LOW)
         kept = total_of([lax.dynamic_index_in_dim(t, side, 1, keepdims=False) for t in terms])
         terms = [kept, flip(sent, "seq", bit)]
-    sums = []
-    for index, order in enumerate(orders):
-        sums.append(scatter_halving([stay[index], come_pieces[index]], order[1:]))
     own_pair = total_of(terms)
     grad_first = own_pair[:, :group_width]
     grad_second = own_pair[:, group_width:].T

time: 274 us -> 274 us (level)
  waiting for transfers between devices: 48.3 us -> 52.4 us
  local copies, waits for them, and re-layouts: 14.2 us -> 10.9 us
    ppermute x25 -> x26, starting transfers between devices: 28.6 us -> 30.8 us  [flip(): lax.ppermute(value, axis, [(i, i ^ 1 << bit) for i in range(lax.axis_size...]
    ppermute x25 -> x26, waiting for transfers between devices: 37.9 us -> 39.8 us  [flip(): lax.ppermute(value, axis, [(i, i ^ 1 << bit) for i in range(lax.axis_size...]
    unnamed x61 -> x53, local copies, waits for them, and re-layouts: 7.24 us -> 7.53 us
  transfers between devices with their start and end apart: 32 -> 32, of which waited for: 19 -> 19; matrix products, arithmetic and copies ran while one was open for 10% -> 7% of each run, Pallas kernels for 33% -> 33%
where the time goes in v3:
time: 274 us; the launch traced here: 273 us
  Pallas kernels  130 us (47%)
  waiting for transfers between devices  52.4 us (19%)
  starting transfers between devices  40.3 us (15%)
  other arithmetic  25.4 us (9%)
  between operations  14.7 us (5%)
  local copies, waits for them, and re-layouts  10.9 us (4%)
    pallas_call x7, Pallas kernels, call(): pl.pallas_call(kernel, grid=(steps,), in_specs=in_specs, out_specs=out_sp...  129 us
    ppermute x26, waiting for transfers between devices, flip(): lax.ppermute(value, axis, [(i, i ^ 1 << bit) for i in range(lax.axis_size...  39.8 us
    ppermute x26, starting transfers between devices, flip(): lax.ppermute(value, axis, [(i, i ^ 1 << bit) for i in range(lax.axis_size...  30.8 us
    ppermute x2, waiting for transfers between devices, send_half(): come = lax.ppermute(mine, 'seq', pairs)  12.6 us
    unnamed x53, local copies, waits for them, and re-layouts  7.53 us
  transfers between devices with their start and end apart: 32, of which 19 were waited for; matrix products, arithmetic and copies ran while one was open for 7% of the time, Pallas kernels for 33%

profile of v3, /device:TPU:0, one launch (start us, length us, event | category | flops | bytes accessed | tf_op | source)
XLA Modules:
  0.0 273.3 jit_solution(4685836212705998691)
XLA Ops:
  7.2 0.9 convert_element_type.300
  8.2 0.8 dynamic_update_slice.3
  9.1 3.1 %collective-permute-start = (bf16[1,72,256]{2,1,0:T(8,128)(2,1)S(1)}, bf16[1,72,256]{2,1,0:T(8,128)(2,1)S(1)}, u32[]{:S(2)}, u32[]{:S(2)}) collective-permute-start(bf16[1,72,256]{2,1,0:T(8,128)(2,1)S(1)} %get-tuple-element.209), channel_id=1, source_target_pairs={{0,8},{4,12},{8,0},{12,4},{16,24},{20,28},{24,16},{28,20},{1,9},{5... | collective-permute-start | bytes 110600 | tf_op jit(solution)/shard_map/ppermute | solution.py:486
  12.2 1.5 collective-permute-start.5
  14.1 2.0 collective-permute-done.5
  16.1 0.9 convert_bitcast_fusion
  17.0 0.9 convert_element_type.311
  18.9 3.0 %collective-permute-start.1 = (bf16[2,72,256]{2,1,0:T(8,128)(2,1)S(1)}, bf16[2,72,256]{2,1,0:T(8,128)(2,1)S(1)}, u32[]{:S(2)}, u32[]{:S(2)}) collective-permute-start(bf16[2,72,256]{2,1,0:T(8,128)(2,1)S(1)} %pad_maximum_fusion.9), channel_id=1, source_target_pairs={{0,16},{4,20},{8,24},{12,28},{16,0},{20,4},{24,8},{28,12},{1,17},{... | collective-permute-start | bytes 221192 | tf_op jit(solution)/shard_map/ppermute | solution.py:486
  21.9 1.2 collective-permute-done.6
  23.1 1.2 collective-permute-done.1
  24.4 1.8 collective-permute-start.2
  26.4 2.7 collective-permute-start.7
  29.8 1.6 collective-permute-start.3
  31.5 3.7 %collective-permute-done.7 = bf16[4,72,256]{2,1,0:T(8,128)(2,1)S(1)} collective-permute-done((bf16[4,72,256]{2,1,0:T(8,128)(2,1)S(1)}, bf16[4,72,256]{2,1,0:T(8,128)(2,1)S(1)}, u32[]{:S(2)}, u32[]{:S(2)}) %collective-permute-start.7) | collective-permute-done | bytes 147488 | tf_op jit(solution)/shard_map/ppermute | solution.py:486
  35.3 1.3 collective-permute-done.3
  36.8 5.2 %collective-permute-done.8 = bf16[8,72,256]{2,1,0:T(8,128)(2,1)S(1)} collective-permute-done((bf16[8,72,256]{2,1,0:T(8,128)(2,1)S(1)}, bf16[8,72,256]{2,1,0:T(8,128)(2,1)S(1)}, u32[]{:S(2)}, u32[]{:S(2)}) %collective-permute-start.8) | collective-permute-done | bytes 294944 | tf_op jit(solution)/shard_map/ppermute | solution.py:486
  42.1 0.9 pad_maximum_fusion.3
  43.3 1.8 collective-permute-done.9
  45.3 1.0 unpack.1
  46.3 15.0 %keys.1 = (bf16[8,512,256]{2,1,0:T(8,128)(2,1)}, bf16[8,512,256]{2,1,0:T(8,128)(2,1)}, bf16[8,8,80,256]{3,2,1,0:T(8,128)(2,1)}, bf16[8,8,256,256]{3,2,1,0:T(8,12...) custom-call(bf16[8,256,512]{2,1,0:T(8,128)(2,1)} %tok.5, ...), custom_call_target="tpu_custom_call" | custom-call | flops 1 | bytes 1 | tf_op jit(solution)/shard_map/keys/pallas_call | solution.py:455
  61.4 2.6 collective-permute-done.10
  64.4 3.7 %collective-permute-start.11 = (bf16[8,272,256]{2,1,0:T(8,128)(2,1)S(1)}, bf16[8,272,256]{2,1,0:T(8,128)(2,1)S(1)}, u32[]{:S(2)}, u32[]{:S(2)}) collective-permute-start(bf16[8,272,256]{2,1,0:T(8,128)(2,1)S(1)} %fusion), channel_id=1, source_target_pairs={{0,2},{1,3},{4,6},{5,7},{8,10},{9,11},{12,14},{13,15},{16,18},{17,... | collective-permute-start | bytes 3342344 | tf_op jit(solution)/shard_map/ppermute | solution.py:502
  68.1 1.8 multiply_convert_fusion
  69.9 13.5 %queries.1 = (bf16[8,512,256]{2,1,0:T(8,128)(2,1)}, bf16[8,8,256,256]{3,2,1,0:T(8,128)(2,1)S(1)}, bf16[8,8,256,256]{3,2,1,0:T(8,128)(2,1)}, bf16[8,8,256,256]{3,2,1,0:T(8,128)(2,1)}, f32[8,8,80,256]{3,2,1,0:T(8,128)S(1)}) custom-call(bf16[8,512,256]{2,1,0:T(8,128)(2,1)} %get-tuple-element.89.turned, bf16[1536,512]{1,0:T(8,128)(2,1)S(1)} %get-tuple-element.88.weights, ...), custom_call_target="tpu_custom_call" | custom-call | flops 1 | bytes 1 | tf_op jit(solution)/shard_map/queries/pallas_call | solution.py:455
  83.4 3.2 %copy-done = bf16[8,8,256,256]{3,2,1,0:T(8,128)(2,1)} copy-done((bf16[8,8,256,256]{3,2,1,0:T(8,128)(2,1)}, bf16[8,8,256,256]{3,2,1,0:T(8,128)(2,1)S(1)}, u32[]{:S(2)}) %copy-start) | copy-done | bytes 8388632
  86.6 8.7 %collective-permute-done.11 = bf16[8,272,256]{2,1,0:T(8,128)(2,1)S(1)} collective-permute-done((bf16[8,272,256]{2,1,0:T(8,128)(2,1)S(1)}, bf16[8,272,256]{2,1,0:T(8,128)(2,1)S(1)}, u32[]{:S(2)}, u32[]{:S(2)}) %collective-permute-start.11) | collective-permute-done | bytes 1114144 | tf_op jit(solution)/shard_map/ppermute | solution.py:502
  95.3 0.7 fusion.2
  96.1 2.7 %collective-permute-done.12.come.come_state = bf16[8,272,256]{2,1,0:T(8,128)(2,1)S(1)} collective-permute-done((bf16[8,272,256]{2,1,0:T(8,128)(2,1)S(1)}, bf16[8,272,256]{2,1,0:T(8,128)(2,1)S(1)}, u32[]{:S(2)}, u32[]{:S(2)}) %collective-permute-start.12) | collective-permute-done | bytes 1114144 | tf_op jit(solution)/shard_map/ppermute | solution.py:486
  98.8 9.0 %mix.1 = (bf16[8,512,256]{2,1,0:T(8,128)(2,1)}, f32[8,8,256]{2,1,0:T(8,128)}, f32[8,256,512]{2,1,0:T(8,128)}, bf16[8,256,512]{2,1,0:T(8,128)(2,1)}) custom-call(bf16[8,256,512]{2,1,0:T(8,128)(2,1)} %tok.5, f32[4,512]{1,0:T(4,128)S(1)} %get-tuple-element.86.norms, bf16[512,512]{1,0:T(8,128)(2,1)S(1)} %get-tuple-element.87.out_weight, ...), custom_call_target="tpu_custom_call" | custom-call | flops 1 | bytes 1 | tf_op jit(solution)/shard_map/mix/pallas_call | solution.py:455
  107.8 1.1 copy-done.1
  108.9 39.2 %ffn.1 = (bf16[2048,512]{1,0:T(8,128)(2,1)}, f32[2048,512]{1,0:T(8,128)}, bf16[512,2048]{1,0:T(8,128)(2,1)}, bf16[512,2048]{1,0:T(8,128)(2,1)}, f32[2,512]{1,0:T(2,128)}) custom-call(bf16[2048,512]{1,0:T(8,128)(2,1)} %bitcast.135, f32[2048,512]{1,0:T(8,128)} %bitcast.134, bf16[2048,512]{1,0:T(8,128)(2,1)} %bitcast.121, ...), custom_call_target="tpu_custom_call" | custom-call | flops 42949672960 | bytes 23080964 | tf_op jit(solution)/shard_map/ffn/pallas_call | solution.py:455
  148.4 11.0 %outer.1 = (bf16[8,8,80,256]{3,2,1,0:T(8,128)(2,1)}, bf16[8,272,256]{2,1,0:T(8,128)(2,1)S(1)}, bf16[8,272,256]{2,1,0:T(8,128)(2,1)}, f32[512,512]{1,0:T(8,128)}) custom-call(f32[8,256,512]{2,1,0:T(8,128)} %bitcast.115, bf16[512,512]{1,0:T(8,128)(2,1)S(1)} %get-tuple-element.87.out_weight, bf16[8,512,256]{2,1,0:T(8,128)(2,1)} %get-tuple-element.108.mixed, ...), custom_call_target="tpu_custom_call" | custom-call | flops 1 | bytes 1 | tf_op jit(solution)/shard_map/outer/pallas_call | solution.py:455
  159.3 1.0 copy-done.3
  161.0 3.0 %fusion.6 = bf16[256,2048]{1,0:T(8,128)(2,1)} fusion(bf16[2,256,2048]{2,1,0:T(8,128)(2,1)} %bitcast.15, s32[]{:T(128)S(6)} %select_n.277, bf16[2,256,2048]{2,1,0:T(8,128)(2,1)} %bitcast.122), kind=kLoop, calls=%fused_computation.20 | loop fusion | flops 2097152 | bytes 3145732 | tf_op jit(solution)/shard_map/convert_element_type | solution.py:780
  164.0 2.6 fusion.3
  166.6 1.3 collective-permute-start.16
  167.9 1.8 collective-permute-start.14
  169.6 1.2 copy-done.2
  170.9 20.6 %back_query.1 = (bf16[8,512,256]{2,1,0:T(8,128)(2,1)}, bf16[8,512,256]{2,1,0:T(8,128)(2,1)}, bf16[8,512,256]{2,1,0:T(8,128)(2,1)}, f32[512,512]{1,0:T(8,128)}) custom-call(bf16[8,512,256]{2,1,0:T(8,128)(2,1)} %get-tuple-element.89.turned, bf16[80,256]{1,0:T(8,128)(2,1)S(1)} %maximum_maximum_fusion.omega_low, ...), custom_call_target="tpu_custom_call" | custom-call | flops 1 | bytes 1 | tf_op jit(solution)/shard_map/back_query/pallas_call | solution.py:455
  191.5 4.0 %collective-permute-done.16 = bf16[8,272,256]{2,1,0:T(8,128)(2,1)} collective-permute-done((bf16[8,272,256]{2,1,0:T(8,128)(2,1)}, bf16[8,272,256]{2,1,0:T(8,128)(2,1)}, u32[]{:S(2)}, u32[]{:S(2)}) %collective-permute-start.16) | collective-permute-done | bytes 1114144 | tf_op jit(solution)/shard_map/ppermute | solution.py:502
  195.5 3.2 %fusion.5 = (bf16[8,272,256]{2,1,0:T(8,128)(2,1)}, bf16[8,272,256]{2,1,0:T(8,128)(2,1)S(1)}) fusion(bf16[8,272,256]{2,1,0:T(8,128)(2,1)S(1)} %copy-done.5, bf16[8,272,256]{2,1,0:T(8,128)(2,1)} %collective-permute-done.16, pred[]{:T(512)S(6)} %eq.31, bf16[8,272,256]{2,1,0:T(8,128)(2,1)} %collective-permute-done.15), kind=kLoop, calls=%fused_computation.16 | loop fusion | flops 5013504 | bytes 5570561 | tf_op jit(solution)/shard_map/convert_element_type | solution.py:510
  198.7 2.5 fusion.7
  201.2 1.8 collective-permute-start.18
  203.0 2.4 collective-permute-start.19
  205.7 20.3 %back_key.1 = (f32[8,256,512]{2,1,0:T(8,128)}, bf16[2,16,72,256]{3,2,1,0:T(8,128)(2,1)}, f32[16,72,256]{2,1,0:T(8,128)}, f32[16,72,256]{2,1,0:T(8,128)}) custom-call(bf16[8,256,512]{2,1,0:T(8,128)(2,1)} %tok.5, f32[4,512]{1,0:T(4,128)S(1)} %get-tuple-element.86.norms, f32[8,256,512]{2,1,0:T(8,128)} %bitcast.116, ...), custom_call_target="tpu_custom_call" | custom-call | flops 15032385536 | bytes 41472004 | tf_op jit(solution)/shard_map/back_key/pallas_call | solution.py:455
  226.0 0.7 copy-done.17
  226.7 3.2 %collective-permute-done.21 = bf16[2,16,72,256]{3,2,1,0:T(8,128)(2,1)} collective-permute-done((bf16[2,16,72,256]{3,2,1,0:T(8,128)(2,1)}, bf16[2,16,72,256]{3,2,1,0:T(8,128)(2,1)}, u32[]{:S(2)}, u32[]{:S(2)}) %collective-permute-start.21) | collective-permute-done | bytes 1179680 | tf_op jit(solution)/shard_map/ppermute | solution.py:486
  229.9 1.3 fusion.32
  231.5 0.8 fusion.12
  232.3 1.7 collective-permute-start.26
  234.0 6.6 %collective-permute-done.22 = bf16[8,72,256]{2,1,0:T(8,128)(2,1)} collective-permute-done((bf16[8,72,256]{2,1,0:T(8,128)(2,1)S(1)}, bf16[8,72,256]{2,1,0:T(8,128)(2,1)}, u32[]{:S(2)}, u32[]{:S(2)}) %collective-permute-start.22) | collective-permute-done | bytes 294944 | tf_op jit(solution)/shard_map/ppermute | solution.py:486
  240.6 1.0 fusion.13
  241.7 1.2 convert_add_fusion.12
  244.1 4.8 %collective-permute-start.27 = (bf16[4,72,256]{2,1,0:T(8,128)(2,1)S(1)}, bf16[4,72,256]{2,1,0:T(8,128)(2,1)S(1)}, u32[]{:S(2)}, u32[]{:S(2)}) collective-permute-start(bf16[4,72,256]{2,1,0:T(8,128)(2,1)S(1)} %get-tuple-element.182), channel_id=1, source_target_pairs={{0,16},{4,20},{8,24},{12,28},{16,0},{20,4},{24,8},{28,12},{1,17},{... | collective-permute-start | bytes 442376 | tf_op jit(solution)/shard_map/ppermute | solution.py:486
  248.9 1.5 collective-permute-start.23
  250.7 0.8 fusion.28
  251.6 0.8 fusion.26
  252.4 3.0 %collective-permute-done.27 = bf16[4,72,256]{2,1,0:T(8,128)(2,1)S(1)} collective-permute-done((bf16[4,72,256]{2,1,0:T(8,128)(2,1)S(1)}, bf16[4,72,256]{2,1,0:T(8,128)(2,1)S(1)}, u32[]{:S(2)}, u32[]{:S(2)}) %collective-permute-start.27) | collective-permute-done | bytes 147488 | tf_op jit(solution)/shard_map/ppermute | solution.py:486
  255.6 2.2 collective-permute-start.24
  257.9 2.0 collective-permute-done.28
  259.9 1.5 collective-permute-start.29
  261.4 2.0 collective-permute-start.25
  263.9 1.5 collective-permute-done.25
  265.5 0.9 fusion.30
  (124 shorter events, 7.4 us)
Async XLA Ops:
  7.2 19.0 %copy-start.16 = (f32[64,256]{1,0:T(8,128)S(1)}, f32[64,256]{1,0:T(8,128)}, u32[]{:S(2)}) copy-start(f32[64,256]{1,0:T(8,128)} %param.16) | copy-start | bytes 196612
  7.2 101.7 %all-gather.2.cloned.1.call-start = ((), (), s32[]{:S(2)}) async-start(), calls=%async_computation | async-start | bytes 4325376 | tf_op jit(solution)/shard_map/all_gather | solution.py:652
  9.1 5.0 %collective-permute-start = (bf16[1,72,256]{2,1,0:T(8,128)(2,1)S(1)}, bf16[1,72,256]{2,1,0:T(8,128)(2,1)S(1)}, u32[]{:S(2)}, u32[]{:S(2)}) collective-permute-start(bf16[1,72,256]{2,1,0:T(8,128)(2,1)S(1)} %get-tuple-element.209), channel_id=1, source_target_pairs={{0,8},{4,12},{8,0},{12,4},{16,24},{20,28},{24,16},{28,20},{1,9},{5... | collective-permute-start | bytes 110600 | tf_op jit(solution)/shard_map/ppermute | solution.py:486
  12.2 4.0 %collective-permute-start.5 = (bf16[1,72,256]{2,1,0:T(8,128)(2,1)S(1)}, bf16[1,72,256]{2,1,0:T(8,128)(2,1)S(1)}, u32[]{:S(2)}, u32[]{:S(2)}) collective-permute-start(bf16[1,72,256]{2,1,0:T(8,128)(2,1)S(1)} %get-tuple-element.208), channel_id=1, source_target_pairs={{0,2},{1,3},{2,0},{3,1},{4,6},{5,7},{6,4},{7,5},{8,10},{9,11},{10,... | collective-permute-start | bytes 110600 | tf_op jit(solution)/shard_map/ppermute | solution.py:486
  18.7 4.4 %collective-permute-start.6 = (bf16[2,72,256]{2,1,0:T(8,128)(2,1)S(1)}, bf16[2,72,256]{2,1,0:T(8,128)(2,1)S(1)}, u32[]{:S(2)}, u32[]{:S(2)}) collective-permute-start(bf16[2,72,256]{2,1,0:T(8,128)(2,1)S(1)} %pad_maximum_fusion.10), channel_id=1, source_target_pairs={{0,8},{4,12},{8,0},{12,4},{16,24},{20,28},{24,16},{28,20},{1,9},{5... | collective-permute-start | bytes 221192 | tf_op jit(solution)/shard_map/ppermute | solution.py:486
  18.9 5.4 %collective-permute-start.1 = (bf16[2,72,256]{2,1,0:T(8,128)(2,1)S(1)}, bf16[2,72,256]{2,1,0:T(8,128)(2,1)S(1)}, u32[]{:S(2)}, u32[]{:S(2)}) collective-permute-start(bf16[2,72,256]{2,1,0:T(8,128)(2,1)S(1)} %pad_maximum_fusion.9), channel_id=1, source_target_pairs={{0,16},{4,20},{8,24},{12,28},{16,0},{20,4},{24,8},{28,12},{1,17},{... | collective-permute-start | bytes 221192 | tf_op jit(solution)/shard_map/ppermute | solution.py:486
  24.4 5.4 %collective-permute-start.2 = (bf16[4,72,256]{2,1,0:T(8,128)(2,1)S(1)}, bf16[4,72,256]{2,1,0:T(8,128)(2,1)S(1)}, u32[]{:S(2)}, u32[]{:S(2)}) collective-permute-start(bf16[4,72,256]{2,1,0:T(8,128)(2,1)S(1)} %pad_maximum_fusion.6), channel_id=1, source_target_pairs={{0,4},{4,0},{8,12},{12,8},{16,20},{20,16},{24,28},{28,24},{1,5},{5... | collective-permute-start | bytes 442376 | tf_op jit(solution)/shard_map/ppermute | solution.py:486
  26.4 8.8 %collective-permute-start.7 = (bf16[4,72,256]{2,1,0:T(8,128)(2,1)S(1)}, bf16[4,72,256]{2,1,0:T(8,128)(2,1)S(1)}, u32[]{:S(2)}, u32[]{:S(2)}) collective-permute-start(bf16[4,72,256]{2,1,0:T(8,128)(2,1)S(1)} %pad_maximum_fusion.7), channel_id=1, source_target_pairs={{0,16},{4,20},{8,24},{12,28},{16,0},{20,4},{24,8},{28,12},{1,17},{... | collective-permute-start | bytes 442376 | tf_op jit(solution)/shard_map/ppermute | solution.py:486
  29.8 6.8 %collective-permute-start.3 = (bf16[8,72,256]{2,1,0:T(8,128)(2,1)S(1)}, bf16[8,72,256]{2,1,0:T(8,128)(2,1)S(1)}, u32[]{:S(2)}, u32[]{:S(2)}) collective-permute-start(bf16[8,72,256]{2,1,0:T(8,128)(2,1)S(1)} %pad_maximum_fusion.4), channel_id=1, source_target_pairs={{0,2},{1,3},{2,0},{3,1},{4,6},{5,7},{6,4},{7,5},{8,10},{9,11},{10,... | collective-permute-start | bytes 884744 | tf_op jit(solution)/shard_map/ppermute | solution.py:486
  35.2 6.8 %collective-permute-start.8 = (bf16[8,72,256]{2,1,0:T(8,128)(2,1)S(1)}, bf16[8,72,256]{2,1,0:T(8,128)(2,1)S(1)}, u32[]{:S(2)}, u32[]{:S(2)}) collective-permute-start(bf16[8,72,256]{2,1,0:T(8,128)(2,1)S(1)} %pad_maximum_fusion.5), channel_id=1, source_target_pairs={{0,4},{4,0},{8,12},{12,8},{16,20},{20,16},{24,28},{28,24},{1,5},{5... | collective-permute-start | bytes 884744 | tf_op jit(solution)/shard_map/ppermute | solution.py:486
  36.7 6.4 %collective-permute-start.4 = (bf16[16,72,256]{2,1,0:T(8,128)(2,1)S(1)}, bf16[16,72,256]{2,1,0:T(8,128)(2,1)S(1)}, u32[]{:S(2)}, u32[]{:S(2)}) collective-permute-start(bf16[16,72,256]{2,1,0:T(8,128)(2,1)S(1)} %pad_maximum_fusion.2), channel_id=1, source_target_pairs={{0,1},{1,0},{2,3},{3,2},{4,5},{5,4},{6,7},{7,6},{8,9},{9,8},{10,11... | collective-permute-start | bytes 1769480 | tf_op jit(solution)/shard_map/ppermute | solution.py:486
  42.9 2.2 collective-permute-start.9
  61.3 6.8 %copy-start.24 = (s32[8,256]{1,0:T(8,128)S(1)}, s32[8,256]{1,0:T(8,128)}, u32[]{:S(2)}) copy-start(s32[8,256]{1,0:T(8,128)} %param.15) | copy-start | bytes 24580
  61.3 6.9 %copy-start.10 = (bf16[8,256,512]{2,1,0:T(8,128)(2,1)S(1)}, bf16[8,256,512]{2,1,0:T(8,128)(2,1)}, u32[]{:S(2)}) copy-start(bf16[8,256,512]{2,1,0:T(8,128)(2,1)} %param.14) | copy-start | bytes 6291460
  61.3 2.8 %collective-permute-start.10 = (bf16[8,272,256]{2,1,0:T(8,128)(2,1)S(1)}, bf16[8,272,256]{2,1,0:T(8,128)(2,1)S(1)}, u32[]{:S(2)}, u32[]{:S(2)}) collective-permute-start(bf16[8,272,256]{2,1,0:T(8,128)(2,1)S(1)} %get-tuple-element.91), channel_id=1, source_target_pairs={{0,1},{1,0},{2,3},{3,2},{4,5},{5,4},{6,7},{7,6},{8,9},{9,8},{10,11... | collective-permute-start | bytes 3342344 | tf_op jit(solution)/shard_map/ppermute | solution.py:486
  64.4 30.9 %collective-permute-start.11 = (bf16[8,272,256]{2,1,0:T(8,128)(2,1)S(1)}, bf16[8,272,256]{2,1,0:T(8,128)(2,1)S(1)}, u32[]{:S(2)}, u32[]{:S(2)}) collective-permute-start(bf16[8,272,256]{2,1,0:T(8,128)(2,1)S(1)} %fusion), channel_id=1, source_target_pairs={{0,2},{1,3},{4,6},{5,7},{8,10},{9,11},{12,14},{13,15},{16,18},{17,... | collective-permute-start | bytes 3342344 | tf_op jit(solution)/shard_map/ppermute | solution.py:502
  83.4 3.2 %copy-start = (bf16[8,8,256,256]{3,2,1,0:T(8,128)(2,1)}, bf16[8,8,256,256]{3,2,1,0:T(8,128)(2,1)S(1)}, u32[]{:S(2)}) copy-start(bf16[8,8,256,256]{3,2,1,0:T(8,128)(2,1)S(1)} %get-tuple-element.94.pk) | copy-start | bytes 25165828
  96.0 2.8 %collective-permute-start.12 = (bf16[8,272,256]{2,1,0:T(8,128)(2,1)S(1)}, bf16[8,272,256]{2,1,0:T(8,128)(2,1)S(1)}, u32[]{:S(2)}, u32[]{:S(2)}) collective-permute-start(bf16[8,272,256]{2,1,0:T(8,128)(2,1)S(1)} %get-tuple-element.178), channel_id=1, source_target_pairs={{0,1},{1,0},{2,3},{3,2},{4,5},{5,4},{6,7},{7,6},{8,9},{9,8},{10,11... | collective-permute-start | bytes 3342344 | tf_op jit(solution)/shard_map/ppermute | solution.py:486
  107.8 1.1 copy-start.1
  108.9 39.5 %copy-start.6 = (f32[8,8,256]{2,1,0:T(8,128)S(1)}, f32[8,8,256]{2,1,0:T(8,128)}, u32[]{:S(2)}) copy-start(f32[8,8,256]{2,1,0:T(8,128)} %get-tuple-element.109.recip) | copy-start | bytes 196612
  148.1 12.2 %collective-permute-start.13 = (bf16[512,2048]{1,0:T(8,128)(2,1)}, bf16[512,2048]{1,0:T(8,128)(2,1)}, u32[]{:S(2)}, u32[]{:S(2)}) collective-permute-start(bf16[512,2048]{1,0:T(8,128)(2,1)} %get-tuple-element.112), channel_id=1, source_target_pairs={{0,1},{1,0},{2,3},{3,2},{4,5},{5,4},{6,7},{7,6},{8,9},{9,8},{10,11... | collective-permute-start | bytes 6291464 | tf_op jit(solution)/shard_map/ppermute | solution.py:486
  159.3 1.0 copy-start.3
  160.4 3.6 %collective-permute-start.15 = (bf16[8,272,256]{2,1,0:T(8,128)(2,1)}, bf16[8,272,256]{2,1,0:T(8,128)(2,1)}, u32[]{:S(2)}, u32[]{:S(2)}) collective-permute-start(bf16[8,272,256]{2,1,0:T(8,128)(2,1)} %get-tuple-element.116), channel_id=1, source_target_pairs={{0,1},{1,0},{2,3},{3,2},{4,5},{5,4},{6,7},{7,6},{8,9},{9,8},{10,11... | collective-permute-start | bytes 3342344 | tf_op jit(solution)/shard_map/ppermute | solution.py:486
  160.9 3.1 %copy-start.4 = (bf16[8,272,256]{2,1,0:T(8,128)(2,1)S(1)}, bf16[8,272,256]{2,1,0:T(8,128)(2,1)}, u32[]{:S(2)}) copy-start(bf16[8,272,256]{2,1,0:T(8,128)(2,1)} %copy-done.3) | copy-start | bytes 3342340
  166.6 28.9 %collective-permute-start.16 = (bf16[8,272,256]{2,1,0:T(8,128)(2,1)}, bf16[8,272,256]{2,1,0:T(8,128)(2,1)}, u32[]{:S(2)}, u32[]{:S(2)}) collective-permute-start(bf16[8,272,256]{2,1,0:T(8,128)(2,1)} %fusion.3), channel_id=1, source_target_pairs={{2,0},{3,1},{6,4},{7,5},{10,8},{11,9},{14,12},{15,13},{18,16},{19,... | collective-permute-start | bytes 3342344 | tf_op jit(solution)/shard_map/ppermute | solution.py:502
  167.9 30.8 %collective-permute-start.14 = (bf16[256,2048]{1,0:T(8,128)(2,1)}, bf16[256,2048]{1,0:T(8,128)(2,1)}, u32[]{:S(2)}, u32[]{:S(2)}) collective-permute-start(bf16[256,2048]{1,0:T(8,128)(2,1)} %fusion.6), channel_id=1, source_target_pairs={{0,4},{4,0},{8,12},{12,8},{16,20},{20,16},{24,28},{28,24},{1,5},{5... | collective-permute-start | bytes 3145736 | tf_op jit(solution)/shard_map/ppermute | solution.py:486
  169.6 1.2 copy-start.2
  170.9 24.6 %copy-start.5 = (bf16[8,272,256]{2,1,0:T(8,128)(2,1)S(1)}, bf16[8,272,256]{2,1,0:T(8,128)(2,1)}, u32[]{:S(2)}) copy-start(bf16[8,272,256]{2,1,0:T(8,128)(2,1)} %copy-done.3) | copy-start | bytes 3342340
  198.7 7.0 %collective-permute-start.17 = (bf16[8,272,256]{2,1,0:T(8,128)(2,1)}, bf16[8,272,256]{2,1,0:T(8,128)(2,1)}, u32[]{:S(2)}, u32[]{:S(2)}) collective-permute-start(bf16[8,272,256]{2,1,0:T(8,128)(2,1)} %get-tuple-element.176), channel_id=1, source_target_pairs={{0,1},{1,0},{2,3},{3,2},{4,5},{5,4},{6,7},{7,6},{8,9},{9,8},{10,11... | collective-permute-start | bytes 3342344 | tf_op jit(solution)/shard_map/ppermute | solution.py:486
  198.7 7.0 %copy-start.7 = (f32[512,512]{1,0:T(8,128)S(1)}, f32[512,512]{1,0:T(8,128)}, u32[]{:S(2)}) copy-start(f32[512,512]{1,0:T(8,128)} %get-tuple-element.131.out_proj) | copy-start | bytes 3145732
  198.7 7.0 %copy-start.8 = (f32[512,512]{1,0:T(8,128)S(1)}, f32[512,512]{1,0:T(8,128)}, u32[]{:S(2)}) copy-start(f32[512,512]{1,0:T(8,128)} %get-tuple-element.130.query_weight) | copy-start | bytes 3145732
  198.7 7.0 %copy-start.9 = (f32[2,512]{1,0:T(2,128)S(1)}, f32[2,512]{1,0:T(2,128)}, u32[]{:S(2)}) copy-start(f32[2,512]{1,0:T(2,128)} %get-tuple-element.132.norm_two) | copy-start | bytes 12292
  201.2 24.8 %collective-permute-start.18 = (bf16[64,2048]{1,0:T(8,128)(2,1)S(1)}, bf16[64,2048]{1,0:T(8,128)(2,1)}, u32[]{:S(2)}, u32[]{:S(2)}) collective-permute-start(bf16[64,2048]{1,0:T(8,128)(2,1)S(1)} %get-tuple-element.136), channel_id=1, source_target_pairs={{0,8},{4,12},{8,0},{12,4},{16,24},{20,28},{24,16},{28,20},{1,9},{5... | collective-permute-start | bytes 786440 | tf_op jit(solution)/shard_map/ppermute | solution.py:823
  203.0 23.0 %collective-permute-start.19 = (bf16[64,2048]{1,0:T(8,128)(2,1)S(1)}, bf16[64,2048]{1,0:T(8,128)(2,1)}, u32[]{:S(2)}, u32[]{:S(2)}) collective-permute-start(bf16[64,2048]{1,0:T(8,128)(2,1)S(1)} %get-tuple-element.137), channel_id=1, source_target_pairs={{0,16},{4,20},{8,24},{12,28},{16,0},{20,4},{24,8},{28,12},{1,17},{... | collective-permute-start | bytes 786440 | tf_op jit(solution)/shard_map/ppermute | solution.py:823
  205.4 20.6 %collective-permute-start.20 = (bf16[64,2048]{1,0:T(8,128)(2,1)S(1)}, bf16[64,2048]{1,0:T(8,128)(2,1)S(1)}, u32[]{:S(2)}, u32[]{:S(2)}) collective-permute-start(bf16[64,2048]{1,0:T(8,128)(2,1)S(1)} %get-tuple-element.138), channel_id=1, source_target_pairs={{0,24},{4,28},{8,16},{12,20},{16,8},{20,12},{24,0},{28,4},{1,25},{... | collective-permute-start | bytes 786440 | tf_op jit(solution)/shard_map/ppermute | solution.py:823
  226.0 0.7 copy-start.17
  226.7 3.2 %collective-permute-start.21 = (bf16[2,16,72,256]{3,2,1,0:T(8,128)(2,1)}, bf16[2,16,72,256]{3,2,1,0:T(8,128)(2,1)}, u32[]{:S(2)}, u32[]{:S(2)}) collective-permute-start(bf16[2,16,72,256]{3,2,1,0:T(8,128)(2,1)} %get-tuple-element.139), channel_id=1, source_target_pairs={{0,1},{1,0},{2,3},{3,2},{4,5},{5,4},{6,7},{7,6},{8,9},{9,8},{10,11... | collective-permute-start | bytes 3538952 | tf_op jit(solution)/shard_map/ppermute | solution.py:486
  226.7 4.5 %copy-start.12 = (f32[16,72,256]{2,1,0:T(8,128)S(1)}, f32[16,72,256]{2,1,0:T(8,128)}, u32[]{:S(2)}) copy-start(f32[16,72,256]{2,1,0:T(8,128)} %get-tuple-element.134) | copy-start | bytes 3538948
  226.7 4.7 %copy-start.11 = (f32[16,72,256]{2,1,0:T(8,128)S(1)}, f32[16,72,256]{2,1,0:T(8,128)}, u32[]{:S(2)}) copy-start(f32[16,72,256]{2,1,0:T(8,128)} %get-tuple-element.145) | copy-start | bytes 3538948
  231.4 9.2 %collective-permute-start.22 = (bf16[8,72,256]{2,1,0:T(8,128)(2,1)S(1)}, bf16[8,72,256]{2,1,0:T(8,128)(2,1)}, u32[]{:S(2)}, u32[]{:S(2)}) collective-permute-start(bf16[8,72,256]{2,1,0:T(8,128)(2,1)S(1)} %get-tuple-element.166), channel_id=1, source_target_pairs={{0,2},{1,3},{2,0},{3,1},{4,6},{5,7},{6,4},{7,5},{8,10},{9,11},{10,... | collective-permute-start | bytes 884744 | tf_op jit(solution)/shard_map/ppermute | solution.py:486
  232.3 11.8 %collective-permute-start.26 = (bf16[8,72,256]{2,1,0:T(8,128)(2,1)}, bf16[8,72,256]{2,1,0:T(8,128)(2,1)S(1)}, u32[]{:S(2)}, u32[]{:S(2)}) collective-permute-start(bf16[8,72,256]{2,1,0:T(8,128)(2,1)} %get-tuple-element.168), channel_id=1, source_target_pairs={{0,4},{4,0},{8,12},{12,8},{16,20},{20,16},{24,28},{28,24},{1,5},{5... | collective-permute-start | bytes 884744 | tf_op jit(solution)/shard_map/ppermute | solution.py:486
  242.9 7.8 %copy-start.14 = (f32[64,512]{1,0:T(8,128)S(1)}, f32[64,512]{1,0:T(8,128)}, u32[]{:S(2)}) copy-start(f32[64,512]{1,0:T(8,128)} %param.20) | copy-start | bytes 393220
  242.9 7.8 %copy-start.20 = (f32[64,512]{1,0:T(8,128)S(1)}, f32[64,512]{1,0:T(8,128)}, u32[]{:S(2)}) copy-start(f32[64,512]{1,0:T(8,128)} %param.22) | copy-start | bytes 393220
  242.9 7.8 %copy-start.21 = (f32[64,512]{1,0:T(8,128)S(1)}, f32[64,512]{1,0:T(8,128)}, u32[]{:S(2)}) copy-start(f32[64,512]{1,0:T(8,128)} %param.23) | copy-start | bytes 393220
  243.4 8.2 %copy-start.15 = (f32[512,64]{0,1:T(8,128)S(1)}, f32[512,64]{0,1:T(8,128)}, u32[]{:S(2)}) copy-start(f32[512,64]{0,1:T(8,128)} %param.21) | copy-start | bytes 393220
  243.4 8.2 %copy-start.22 = (f32[512,64]{0,1:T(8,128)S(1)}, f32[512,64]{0,1:T(8,128)}, u32[]{:S(2)}) copy-start(f32[512,64]{0,1:T(8,128)} %param.24) | copy-start | bytes 393220
  243.4 8.2 %copy-start.23 = (f32[512,64]{0,1:T(8,128)S(1)}, f32[512,64]{0,1:T(8,128)}, u32[]{:S(2)}) copy-start(f32[512,64]{0,1:T(8,128)} %param.25) | copy-start | bytes 393220
  243.7 6.9 %collective-permute-start.30 = (bf16[64,1024]{1,0:T(8,128)(2,1)S(1)}, bf16[64,1024]{1,0:T(8,128)(2,1)S(1)}, u32[]{:S(2)}, u32[]{:S(2)}) collective-permute-start(bf16[64,1024]{1,0:T(8,128)(2,1)S(1)} %bitcast.132), channel_id=1, source_target_pairs={{0,2},{1,3},{2,0},{3,1},{4,6},{5,7},{6,4},{7,5},{8,10},{9,11},{10,... | collective-permute-start | bytes 393224 | tf_op jit(solution)/shard_map/ppermute | solution.py:486
  244.1 11.3 %collective-permute-start.27 = (bf16[4,72,256]{2,1,0:T(8,128)(2,1)S(1)}, bf16[4,72,256]{2,1,0:T(8,128)(2,1)S(1)}, u32[]{:S(2)}, u32[]{:S(2)}) collective-permute-start(bf16[4,72,256]{2,1,0:T(8,128)(2,1)S(1)} %get-tuple-element.182), channel_id=1, source_target_pairs={{0,16},{4,20},{8,24},{12,28},{16,0},{20,4},{24,8},{28,12},{1,17},{... | collective-permute-start | bytes 442376 | tf_op jit(solution)/shard_map/ppermute | solution.py:486
  248.9 6.6 %collective-permute-start.23 = (bf16[4,72,256]{2,1,0:T(8,128)(2,1)S(1)}, bf16[4,72,256]{2,1,0:T(8,128)(2,1)S(1)}, u32[]{:S(2)}, u32[]{:S(2)}) collective-permute-start(bf16[4,72,256]{2,1,0:T(8,128)(2,1)S(1)} %get-tuple-element.144), channel_id=1, source_target_pairs={{0,4},{4,0},{8,12},{12,8},{16,20},{20,16},{24,28},{28,24},{1,5},{5... | collective-permute-start | bytes 442376 | tf_op jit(solution)/shard_map/ppermute | solution.py:486
  250.7 14.8 %copy-start.13 = (f32[32832]{0:T(1024)S(1)}, f32[32832]{0:T(1024)}, u32[]{:S(2)}) copy-start(f32[32832]{0:T(1024)} %param.17) | copy-start | bytes 393988
  250.7 14.8 %copy-start.18 = (f32[32832]{0:T(1024)S(1)}, f32[32832]{0:T(1024)}, u32[]{:S(2)}) copy-start(f32[32832]{0:T(1024)} %param.18) | copy-start | bytes 393988
  250.7 14.8 %copy-start.19 = (f32[32832]{0:T(1024)S(1)}, f32[32832]{0:T(1024)}, u32[]{:S(2)}) copy-start(f32[32832]{0:T(1024)} %param.19) | copy-start | bytes 393988
  255.5 4.4 %collective-permute-start.28 = (bf16[2,72,256]{2,1,0:T(8,128)(2,1)S(1)}, bf16[2,72,256]{2,1,0:T(8,128)(2,1)S(1)}, u32[]{:S(2)}, u32[]{:S(2)}) collective-permute-start(bf16[2,72,256]{2,1,0:T(8,128)(2,1)S(1)} %get-tuple-element.190), channel_id=1, source_target_pairs={{0,8},{4,12},{8,0},{12,4},{16,24},{20,28},{24,16},{28,20},{1,9},{5... | collective-permute-start | bytes 221192 | tf_op jit(solution)/shard_map/ppermute | solution.py:486
  255.6 5.8 %collective-permute-start.24 = (bf16[2,72,256]{2,1,0:T(8,128)(2,1)S(1)}, bf16[2,72,256]{2,1,0:T(8,128)(2,1)S(1)}, u32[]{:S(2)}, u32[]{:S(2)}) collective-permute-start(bf16[2,72,256]{2,1,0:T(8,128)(2,1)S(1)} %get-tuple-element.188), channel_id=1, source_target_pairs={{0,16},{4,20},{8,24},{12,28},{16,0},{20,4},{24,8},{28,12},{1,17},{... | collective-permute-start | bytes 221192 | tf_op jit(solution)/shard_map/ppermute | solution.py:486
  259.9 4.0 %collective-permute-start.29 = (bf16[1,72,256]{2,1,0:T(8,128)(2,1)S(1)}, bf16[1,72,256]{2,1,0:T(8,128)(2,1)S(1)}, u32[]{:S(2)}, u32[]{:S(2)}) collective-permute-start(bf16[1,72,256]{2,1,0:T(8,128)(2,1)S(1)} %fusion.20), channel_id=1, source_target_pairs={{0,2},{1,3},{2,0},{3,1},{4,6},{5,7},{6,4},{7,5},{8,10},{9,11},{10,... | collective-permute-start | bytes 110600 | tf_op jit(solution)/shard_map/ppermute | solution.py:486
  261.4 4.0 %collective-permute-start.25 = (bf16[1,72,256]{2,1,0:T(8,128)(2,1)S(1)}, bf16[1,72,256]{2,1,0:T(8,128)(2,1)S(1)}, u32[]{:S(2)}, u32[]{:S(2)}) collective-permute-start(bf16[1,72,256]{2,1,0:T(8,128)(2,1)S(1)} %fusion.23), channel_id=1, source_target_pairs={{0,8},{4,12},{8,0},{12,4},{16,24},{20,28},{24,16},{28,20},{1,9},{5... | collective-permute-start | bytes 110600 | tf_op jit(solution)/shard_map/ppermute | solution.py:486
Sparse Core Ops, SparseCore 0:
  18.8 64.0 all-gather.1

commit v4 on v3

--- a/solution.py
+++ b/solution.py
@@ -20,7 +20,7 @@
 SPARE = 16
 VMEM_LIMIT = 16 * 1024 * 1024
 BIG = 1 << 20
-LIMITS = {'keys': 14, 'queries': 16, 'mix': 12, 'ffn': 40, 'outer': 14, 'back_query': 24, 'back_key': 34}
+LIMITS = {'keys': 14, 'queries': 16, 'mix': 12, 'ffn': 44, 'outer': 14, 'back_query': 24, 'back_key': 34}
 F32 = jnp.float32
 LOW = jnp.bfloat16
 
@@ -200,10 +200,36 @@
 
 
 def ffn_kernel(
-    groups, devices, normed, middle, target, norms, pair, core, out, grad_out, leave, stay, norm_grad, first_sum, second_sum
+    groups,
+    devices,
+    found,
+    normed,
+    middle,
+    target,
+    norms,
+    own_pair,
+    their_pair,
+    core,
+    place,
+    out,
+    grad_out,
+    leave,
+    stay,
+    norm_grad,
+    first_sum,
+    second_sum,
+    pair,
 ):
     step = pl.program_id(0)
-    half = pair.shape[2] // 2
+    half = pair.shape[3] // 2
+    width = normed.shape[1]
+
+    @pl.when(step == 0)
+    def _():
+        for index, (seq_jump, dp_jump) in enumerate(found):
+            pair[place[0] ^ seq_jump, place[1] ^ dp_jump] = own_pair[index]
+            pair[place[0] ^ (seq_jump ^ 1), place[1] ^ dp_jump] = their_pair[index]
+
     own = normed[...]
     grads = target[...]
     own_turned = own.T
@@ -218,8 +244,8 @@
     result = jnp.zeros(own.shape, F32)
     grad_normed = jnp.zeros(own.shape, F32)
     for group in range(groups):
-        first = pair[group, :, :half]
-        second = pair[group, :, half:]
+        first = pair[group, :, :, :half].reshape(width, half)
+        second = pair[group, :, :, half:].reshape(width, half)
         active, slope = gelu_pair(dot_nn(own, first))
         active = active.astype(LOW)
         result = result + dot_nt(active, second)
@@ -539,6 +565,15 @@
     return spot
 
 
+def gather_more(value, found, axis, jumps):
+    size = lax.axis_size(axis)
+    come = [lax.ppermute(value, axis, [(i, i ^ jump) for i in range(size)]) for jump in jumps]
+    more = list(found)
+    for jump in jumps:
+        more += [(a ^ jump, b) if axis == "seq" else (a, b ^ jump) for a, b in found]
+    return jnp.concatenate([value] + come, axis=0), more
+
+
 def gather_doubling(value, order, late):
     value = value[None]
     for step, (axis, bit) in enumerate(order):
@@ -648,9 +683,13 @@
     spots = [[place_in(order[::-1], i) for i in range(devices)] for order in gather_orders()]
     whole_rows = -(-(starts[-1] + rows) // 8) * 8
     group_width = ffn_in.shape[1]
-    pair = jnp.concatenate([ffn_pair[0].astype(LOW), ffn_pair[1].astype(LOW).T], axis=1)
-    pair = lax.all_gather(pair, ("seq", "dp"), axis=0, tiled=True)
-    pair = pair.reshape(groups, width, 2 * group_width)
+    pair = jnp.concatenate([ffn_pair[0].astype(LOW), ffn_pair[1].astype(LOW).T], axis=1)[None]
+    top = lax.axis_size("dp") // 4
+    pair, found = gather_more(pair, [(0, 0)], "dp", [top, 2 * top, 3 * top])
+    for bit in range(axis_bits("dp") - 3, 0, -1):
+        pair, found = gather_more(pair, found, "dp", [1 << bit])
+    pair, gathered = lax.optimization_barrier((pair, gathered))
+
 
     weights, out_weight, norms = pl.pallas_call(
         functools.partial(unpack_kernel, starts, spots, rows),
@@ -679,6 +718,7 @@
     state_rows = heads // 2 * size + SPARE
     state_shape = (seqs, state_rows, count)
     core = bit_of("seq", 0).astype(jnp.int32).reshape(1)
+    place_both = jnp.stack([lax.axis_index("seq"), lax.axis_index("dp")]).astype(jnp.int32)
     in_smem = pl.BlockSpec(memory_space=pltpu.SMEM)
 
     def spec(value):
@@ -691,6 +731,9 @@
             pltpu.VMEM((heads, length), F32),
         ]
 
+    pair, omega_parts = lax.optimization_barrier((pair, omega_parts))
+    for bit in range(1, axis_bits("seq")):
+        pair, found = gather_more(pair, found, "seq", [1 << bit])
     args = (tokens, norms, weights, omega_parts)
     outs = [array(flat, LOW)] * 2 + [array(held, LOW), pltpu.VMEM(feat, LOW)] + [pltpu.VMEM(state_shape, LOW)] * 2
     turned, uk, value, pk, own, their = call(
@@ -705,7 +748,10 @@
         chip=(),
         scratch=scratch_rows(2) + [pltpu.VMEM((heads, ext, count), F32)],
     )
+    their, pair = lax.optimization_barrier((their, pair))
     beside, far, omega_tied = send_half(own, their, True, omega_parts)
+    pair, omega_tied, pk = lax.optimization_barrier((pair, omega_tied, pk))
+    pair, found = gather_more(pair, found, "dp", [1])
     args = (turned, weights, omega_tied, value, pk)
     outs = [array(flat, LOW), pltpu.VMEM(feat, LOW), array(feat, LOW), array(score_shape, LOW), pltpu.VMEM(held, F32)]
     uq, pq_near, pq, score, num = call(
@@ -720,14 +766,16 @@
         scratch_rows(1),
         chip=(4,),
     )
-    far, uq, target = lax.optimization_barrier((far, uq, target))
+    far, uq, target, pair = lax.optimization_barrier((far, uq, target, pair))
+    pair, mix_norms = lax.optimization_barrier((pair, norms))
+    pair_beside = flip(pair, "seq", 0)
     keep, come = receive_half(own, beside, far, True)
     states = [per_seq(keep.shape)] * 2
     outs = [array(flat, LOW), array(recip_shape, F32), array(tokens.shape, F32), array(tokens.shape, LOW)]
     mixed, recip, middle, normed_two = call(
         functools.partial(mix_kernel, heads, size),
         seqs,
-        (tokens, norms, out_weight, num, core, keep, come, pq_near),
+        (tokens, mix_norms, out_weight, num, core, keep, come, pq_near),
         [spec(tokens), spec(norms), spec(out_weight), spec(num), in_smem, *states, spec(pq_near)],
         outs,
         [spec(a) for a in outs],
@@ -741,16 +789,17 @@
     by_block = pl.BlockSpec((block, width), lambda i: (i, 0))
     rows_shape = (total_rows, width)
     block_out, grad_middle, leave, stay, norm_two_grad = call(
-        functools.partial(ffn_kernel, groups, lax.axis_size("dp")),
+        functools.partial(ffn_kernel, groups, lax.axis_size("dp"), found),
         total_rows // block,
-        (*[a.reshape(rows_shape) for a in (normed_two, middle, target)], norms, pair, core),
-        [by_block, by_block, by_block, fixed(norms.shape), fixed(pair.shape), in_smem],
+        (*[a.reshape(rows_shape) for a in (normed_two, middle, target)], norms, pair, pair_beside, core, place_both),
+        [by_block, by_block, by_block, fixed(norms.shape), fixed(pair.shape), fixed(pair.shape), in_smem, in_smem],
         [array(rows_shape, LOW), array(rows_shape, F32)] + [array(first_shape, LOW)] * 2 + [array((2, width), F32)],
         [by_block, by_block, fixed(first_shape), fixed(first_shape), fixed((2, width))],
         "ffn",
         20 * unit,
         chip=(),
-        scratch=[pltpu.VMEM((groups, width, group_width), F32)] * 2,
+        scratch=[pltpu.VMEM((groups, width, group_width), F32)] * 2
+        + [pltpu.VMEM((groups, lax.axis_size("dp"), width // lax.axis_size("dp"), 2 * group_width), LOW)],
     )
     block_out = block_out.reshape(tokens.shape)
     grad_middle = grad_middle.reshape(tokens.shape)

time: 274 us -> 267 us (0.974)
  between operations: 14.7 us -> 1.4 us
  waiting for transfers between devices: 52.4 us -> 56.9 us
    ppermute x2, waiting for transfers between devices: 12.6 us -> 6.36 us  [send_half(): come = lax.ppermute(mine, 'seq', pairs)]
    ppermute x0 -> x5, waiting for transfers between devices: none -> 6.05 us  [gather_more(): lax.ppermute(value, axis, [(i, i ^ jump) for i in range(size)])]
    ppermute x0 -> x5, starting transfers between devices: none -> 5.84 us  [gather_more(): lax.ppermute(value, axis, [(i, i ^ jump) for i in range(size)])]
    ppermute x26 -> x27, waiting for transfers between devices: 39.8 us -> 44.5 us  [flip(): lax.ppermute(value, axis, [(i, i ^ 1 << bit) for i in range(lax.axis_size...]
    ppermute x26 -> x27, starting transfers between devices: 30.8 us -> 27.3 us  [flip(): lax.ppermute(value, axis, [(i, i ^ 1 << bit) for i in range(lax.axis_size...]
    unnamed x53 -> x63, local copies, waits for them, and re-layouts: 7.53 us -> 5.44 us
  transfers between devices with their start and end apart: 32 -> 37, of which waited for: 19 -> 18; matrix products, arithmetic and copies ran while one was open for 7% -> 9% of each run, Pallas kernels for 33% -> 34%
where the time goes in v4:
time: 267 us; the launch traced here: 266 us
  Pallas kernels  130 us (49%)
  waiting for transfers between devices  56.9 us (21%)
  starting transfers between devices  42.2 us (16%)
  other arithmetic  26.6 us (10%)
  local copies, waits for them, and re-layouts  8.8 us (3%)
    pallas_call x7, Pallas kernels, call(): pl.pallas_call(kernel, grid=(steps,), in_specs=in_specs, out_specs=out_sp...  129 us
    ppermute x27, waiting for transfers between devices, flip(): lax.ppermute(value, axis, [(i, i ^ 1 << bit) for i in range(lax.axis_size...  44.5 us
    ppermute x27, starting transfers between devices, flip(): lax.ppermute(value, axis, [(i, i ^ 1 << bit) for i in range(lax.axis_size...  27.3 us
    ppermute x2, waiting for transfers between devices, send_half(): come = lax.ppermute(mine, 'seq', pairs)  6.36 us
    ppermute x5, waiting for transfers between devices, gather_more(): lax.ppermute(value, axis, [(i, i ^ jump) for i in range(size)])  6.05 us
    ppermute x5, starting transfers between devices, gather_more(): lax.ppermute(value, axis, [(i, i ^ jump) for i in range(size)])  5.84 us
    unnamed x63, local copies, waits for them, and re-layouts  5.44 us
  transfers between devices with their start and end apart: 37, of which 18 were waited for; matrix products, arithmetic and copies ran while one was open for 9% of the time, Pallas kernels for 34%

profile of v4, /device:TPU:0, one launch (start us, length us, event | category | flops | bytes accessed | tf_op | source)
XLA Modules:
  0.0 265.9 jit_solution(11554965953184056028)
XLA Ops:
  0.7 1.0 convert_element_type.301
  1.7 0.8 dynamic_update_slice.3
  2.6 3.1 %collective-permute-start.1 = (bf16[1,72,256]{2,1,0:T(8,128)(2,1)S(1)}, bf16[1,72,256]{2,1,0:T(8,128)(2,1)S(1)}, u32[]{:S(2)}, u32[]{:S(2)}) collective-permute-start(bf16[1,72,256]{2,1,0:T(8,128)(2,1)S(1)} %get-tuple-element.234), channel_id=1, source_target_pairs={{0,8},{4,12},{8,0},{12,4},{16,24},{20,28},{24,16},{28,20},{1,9},{5... | collective-permute-start | bytes 110600 | tf_op jit(solution)/shard_map/ppermute | solution.py:512
  5.7 1.5 collective-permute-start
  7.2 1.5 fusion.34
  8.7 0.9 copy.34
  10.5 2.7 collective-permute-start.5
  13.7 2.8 %collective-permute-done.5 = bf16[2,72,256]{2,1,0:T(8,128)(2,1)S(1)} collective-permute-done((bf16[2,72,256]{2,1,0:T(8,128)(2,1)S(1)}, bf16[2,72,256]{2,1,0:T(8,128)(2,1)S(1)}, u32[]{:S(2)}, u32[]{:S(2)}) %collective-permute-start.5) | collective-permute-done | bytes 73760 | tf_op jit(solution)/shard_map/ppermute | solution.py:512
  16.5 1.0 collective-permute-done.9
  17.6 0.9 collective-permute-start.10
  19.3 2.1 collective-permute-start.3
  21.4 1.6 collective-permute-start.4
  23.0 1.6 collective-permute-start.6
  24.5 8.0 %collective-permute-done.10 = bf16[4,72,256]{2,1,0:T(8,128)(2,1)S(1)} collective-permute-done((bf16[4,72,256]{2,1,0:T(8,128)(2,1)S(1)}, bf16[4,72,256]{2,1,0:T(8,128)(2,1)S(1)}, u32[]{:S(2)}, u32[]{:S(2)}) %collective-permute-start.10) | collective-permute-done | bytes 147488 | tf_op jit(solution)/shard_map/ppermute | solution.py:512
  32.6 1.6 collective-permute-start.11
  35.1 4.4 %collective-permute-done.11 = bf16[8,72,256]{2,1,0:T(8,128)(2,1)S(1)} collective-permute-done((bf16[8,72,256]{2,1,0:T(8,128)(2,1)S(1)}, bf16[8,72,256]{2,1,0:T(8,128)(2,1)S(1)}, u32[]{:S(2)}, u32[]{:S(2)}) %collective-permute-start.11) | collective-permute-done | bytes 294944 | tf_op jit(solution)/shard_map/ppermute | solution.py:512
  39.6 1.5 collective-permute-done.7
  41.1 0.9 pad_maximum_fusion.4
  42.1 1.1 pad_maximum_fusion.6
  45.2 0.9 unpack.1
  46.1 15.0 %keys.1 = (bf16[8,512,256]{2,1,0:T(8,128)(2,1)}, bf16[8,512,256]{2,1,0:T(8,128)(2,1)}, bf16[8,8,80,256]{3,2,1,0:T(8,128)(2,1)}, bf16[8,8,256,256]{3,2,1,0:T(8,12...) custom-call(bf16[8,256,512]{2,1,0:T(8,128)(2,1)} %tok.5, ...), custom_call_target="tpu_custom_call" | custom-call | flops 1 | bytes 1 | tf_op jit(solution)/shard_map/keys/pallas_call | solution.py:481
  61.3 2.7 %collective-permute-done.14 = bf16[8,272,256]{2,1,0:T(8,128)(2,1)S(1)} collective-permute-done((bf16[8,272,256]{2,1,0:T(8,128)(2,1)S(1)}, bf16[8,272,256]{2,1,0:T(8,128)(2,1)S(1)}, u32[]{:S(2)}, u32[]{:S(2)}) %collective-permute-start.14) | collective-permute-done | bytes 1114144 | tf_op jit(solution)/shard_map/ppermute | solution.py:512
  64.9 3.3 %collective-permute-start.15 = (bf16[8,272,256]{2,1,0:T(8,128)(2,1)S(1)}, bf16[8,272,256]{2,1,0:T(8,128)(2,1)S(1)}, u32[]{:S(2)}, u32[]{:S(2)}) collective-permute-start(bf16[8,272,256]{2,1,0:T(8,128)(2,1)S(1)} %fusion), channel_id=1, source_target_pairs={{0,2},{1,3},{4,6},{5,7},{8,10},{9,11},{12,14},{13,15},{16,18},{17,... | collective-permute-start | bytes 3342344 | tf_op jit(solution)/shard_map/ppermute | solution.py:528
  68.2 1.8 multiply_convert_fusion
  70.0 13.5 %queries.1 = (bf16[8,512,256]{2,1,0:T(8,128)(2,1)}, bf16[8,8,256,256]{3,2,1,0:T(8,128)(2,1)S(1)}, bf16[8,8,256,256]{3,2,1,0:T(8,128)(2,1)}, bf16[8,8,256,256]{3,2,1,0:T(8,128)(2,1)}, f32[8,8,80,256]{3,2,1,0:T(8,128)S(1)}) custom-call(bf16[8,512,256]{2,1,0:T(8,128)(2,1)} %get-tuple-element.112.turned, bf16[1536,512]{1,0:T(8,128)(2,1)S(1)} %get-tuple-element.104.weights, ...), custom_call_target="tpu_custom_call" | custom-call | flops 1 | bytes 1 | tf_op jit(solution)/shard_map/queries/pallas_call | solution.py:481
  83.5 6.0 %collective-permute-done.16 = bf16[8,64,1024]{2,1,0:T(8,128)(2,1)S(1)} collective-permute-done((bf16[8,64,1024]{2,1,0:T(8,128)(2,1)S(1)}, bf16[8,64,1024]{2,1,0:T(8,128)(2,1)S(1)}, u32[]{:S(2)}, u32[]{:S(2)}) %collective-permute-start.16) | collective-permute-done | bytes 1048608 | tf_op jit(solution)/shard_map/ppermute | solution.py:570
  89.8 2.2 collective-permute-done.15
  93.3 4.4 %collective-permute-done.17.come.come_state = bf16[8,272,256]{2,1,0:T(8,128)(2,1)S(1)} collective-permute-done((bf16[8,272,256]{2,1,0:T(8,128)(2,1)S(1)}, bf16[8,272,256]{2,1,0:T(8,128)(2,1)S(1)}, u32[]{:S(2)}, u32[]{:S(2)}) %collective-permute-start.17) | collective-permute-done | bytes 1114144 | tf_op jit(solution)/shard_map/ppermute | solution.py:512
  97.7 9.2 %mix.1 = (bf16[8,512,256]{2,1,0:T(8,128)(2,1)}, f32[8,8,256]{2,1,0:T(8,128)}, f32[8,256,512]{2,1,0:T(8,128)}, bf16[8,256,512]{2,1,0:T(8,128)(2,1)}) custom-call(bf16[8,256,512]{2,1,0:T(8,128)(2,1)} %tok.5, f32[4,512]{1,0:T(4,128)S(1)} %get-tuple-element.122.norms, bf16[512,512]{1,0:T(8,128)(2,1)S(1)} %get-tuple-element.123.out_weight, ...), custom_call_target="tpu_custom_call" | custom-call | flops 1 | bytes 1 | tf_op jit(solution)/shard_map/mix/pallas_call | solution.py:481
  106.9 1.3 copy-done.29
  108.2 39.6 %ffn.1 = (bf16[2048,512]{1,0:T(8,128)(2,1)}, f32[2048,512]{1,0:T(8,128)}, bf16[512,2048]{1,0:T(8,128)(2,1)}, bf16[512,2048]{1,0:T(8,128)(2,1)}, f32[2,512]{1,0:T(2,128)}) custom-call(bf16[2048,512]{1,0:T(8,128)(2,1)} %bitcast.137, f32[2048,512]{1,0:T(8,128)} %bitcast.136, bf16[2048,512]{1,0:T(8,128)(2,1)} %bitcast.124, ...), custom_call_target="tpu_custom_call" | custom-call | flops 42949672960 | bytes 23080972 | tf_op jit(solution)/shard_map/ffn/pallas_call | solution.py:481
  148.0 11.0 %outer.1 = (bf16[8,8,80,256]{3,2,1,0:T(8,128)(2,1)}, bf16[8,272,256]{2,1,0:T(8,128)(2,1)S(1)}, bf16[8,272,256]{2,1,0:T(8,128)(2,1)}, f32[512,512]{1,0:T(8,128)}) custom-call(f32[8,256,512]{2,1,0:T(8,128)} %bitcast.118, bf16[512,512]{1,0:T(8,128)(2,1)S(1)} %get-tuple-element.123.out_weight, bf16[8,512,256]{2,1,0:T(8,128)(2,1)} %get-tuple-element.134.mixed, ...), custom_call_target="tpu_custom_call" | custom-call | flops 1 | bytes 1 | tf_op jit(solution)/shard_map/outer/pallas_call | solution.py:481
  159.0 1.0 copy-done.3
  160.7 3.0 %fusion.6 = bf16[256,2048]{1,0:T(8,128)(2,1)} fusion(bf16[2,256,2048]{2,1,0:T(8,128)(2,1)} %bitcast.17, s32[]{:T(128)S(6)} %select_n.277, bf16[2,256,2048]{2,1,0:T(8,128)(2,1)} %bitcast.125), kind=kLoop, calls=%fused_computation.21 | loop fusion | flops 2097152 | bytes 3145732 | tf_op jit(solution)/shard_map/convert_element_type | solution.py:829
  163.7 2.6 fusion.3
  166.3 1.3 collective-permute-start.22
  167.6 1.6 collective-permute-start.20
  169.2 1.2 copy-done.2
  170.4 20.6 %back_query.1 = (bf16[8,512,256]{2,1,0:T(8,128)(2,1)}, bf16[8,512,256]{2,1,0:T(8,128)(2,1)}, bf16[8,512,256]{2,1,0:T(8,128)(2,1)}, f32[512,512]{1,0:T(8,128)}) custom-call(bf16[8,512,256]{2,1,0:T(8,128)(2,1)} %get-tuple-element.112.turned, bf16[80,256]{1,0:T(8,128)(2,1)S(1)} %maximum_maximum_fusion.omega_low, ...), custom_call_target="tpu_custom_call" | custom-call | flops 1 | bytes 1 | tf_op jit(solution)/shard_map/back_query/pallas_call | solution.py:481
  191.0 4.2 %collective-permute-done.22 = bf16[8,272,256]{2,1,0:T(8,128)(2,1)} collective-permute-done((bf16[8,272,256]{2,1,0:T(8,128)(2,1)}, bf16[8,272,256]{2,1,0:T(8,128)(2,1)}, u32[]{:S(2)}, u32[]{:S(2)}) %collective-permute-start.22) | collective-permute-done | bytes 1114144 | tf_op jit(solution)/shard_map/ppermute | solution.py:528
  195.2 3.2 %fusion.5 = (bf16[8,272,256]{2,1,0:T(8,128)(2,1)}, bf16[8,272,256]{2,1,0:T(8,128)(2,1)S(1)}) fusion(bf16[8,272,256]{2,1,0:T(8,128)(2,1)S(1)} %copy-done.5, bf16[8,272,256]{2,1,0:T(8,128)(2,1)} %collective-permute-done.22, pred[]{:T(512)S(6)} %eq.31, bf16[8,272,256]{2,1,0:T(8,128)(2,1)} %collective-permute-done.21), kind=kLoop, calls=%fused_computation.16 | loop fusion | flops 5013504 | bytes 5570561 | tf_op jit(solution)/shard_map/convert_element_type | solution.py:536
  198.5 2.5 fusion.7
  201.0 1.1 collective-permute-start.25
  202.2 3.2 %collective-permute-start.26 = (bf16[64,2048]{1,0:T(8,128)(2,1)S(1)}, bf16[64,2048]{1,0:T(8,128)(2,1)S(1)}, u32[]{:S(2)}, u32[]{:S(2)}) collective-permute-start(bf16[64,2048]{1,0:T(8,128)(2,1)S(1)} %get-tuple-element.164), channel_id=1, source_target_pairs={{0,24},{4,28},{8,16},{12,20},{16,8},{20,12},{24,0},{28,4},{1,25},{... | collective-permute-start | bytes 786440 | tf_op jit(solution)/shard_map/ppermute | solution.py:872
  205.4 20.2 %back_key.1 = (f32[8,256,512]{2,1,0:T(8,128)}, bf16[2,16,72,256]{3,2,1,0:T(8,128)(2,1)}, f32[16,72,256]{2,1,0:T(8,128)}, f32[16,72,256]{2,1,0:T(8,128)}) custom-call(bf16[8,256,512]{2,1,0:T(8,128)(2,1)} %tok.5, f32[4,512]{1,0:T(4,128)S(1)} %get-tuple-element.122.norms, f32[8,256,512]{2,1,0:T(8,128)} %bitcast.119, ...), custom_call_target="tpu_custom_call" | custom-call | flops 15032385536 | bytes 41472004 | tf_op jit(solution)/shard_map/back_key/pallas_call | solution.py:481
  226.4 3.2 %collective-permute-done.27 = bf16[2,16,72,256]{3,2,1,0:T(8,128)(2,1)} collective-permute-done((bf16[2,16,72,256]{3,2,1,0:T(8,128)(2,1)}, bf16[2,16,72,256]{3,2,1,0:T(8,128)(2,1)}, u32[]{:S(2)}, u32[]{:S(2)}) %collective-permute-start.27) | collective-permute-done | bytes 1179680 | tf_op jit(solution)/shard_map/ppermute | solution.py:512
  229.6 1.3 fusion.32
  231.1 0.8 fusion.12
  232.0 1.5 collective-permute-start.32
  233.4 6.8 %collective-permute-done.28 = bf16[8,72,256]{2,1,0:T(8,128)(2,1)} collective-permute-done((bf16[8,72,256]{2,1,0:T(8,128)(2,1)S(1)}, bf16[8,72,256]{2,1,0:T(8,128)(2,1)}, u32[]{:S(2)}, u32[]{:S(2)}) %collective-permute-start.28) | collective-permute-done | bytes 294944 | tf_op jit(solution)/shard_map/ppermute | solution.py:512
  240.2 1.0 fusion.13
  241.3 1.2 convert_add_fusion.12
  243.7 1.5 collective-permute-start.29
  245.3 2.5 collective-permute-start.33
  248.5 0.8 fusion.26
  249.4 0.8 fusion.28
  250.2 2.5 collective-permute-start.30
  252.7 3.4 %collective-permute-done.33 = bf16[4,72,256]{2,1,0:T(8,128)(2,1)S(1)} collective-permute-done((bf16[4,72,256]{2,1,0:T(8,128)(2,1)S(1)}, bf16[4,72,256]{2,1,0:T(8,128)(2,1)S(1)}, u32[]{:S(2)}, u32[]{:S(2)}) %collective-permute-start.33) | collective-permute-done | bytes 147488 | tf_op jit(solution)/shard_map/ppermute | solution.py:512
  256.2 1.0 collective-permute-done.30
  257.2 1.2 collective-permute-start.31
  258.5 2.1 collective-permute-done.34
  260.6 2.3 collective-permute-start.35
  262.9 1.9 collective-permute-done.35
  264.9 1.0 fusion.30
  (147 shorter events, 12.0 us)
Async XLA Ops:
  0.6 13.0 %copy-start.17 = (f32[64,512]{1,0:T(8,128)S(1)}, f32[64,512]{1,0:T(8,128)}, u32[]{:S(2)}) copy-start(f32[64,512]{1,0:T(8,128)} %param.20) | copy-start | bytes 393220
  0.7 13.0 %copy-start.15 = (f32[512,64]{0,1:T(8,128)S(1)}, f32[512,64]{0,1:T(8,128)}, u32[]{:S(2)}) copy-start(f32[512,64]{0,1:T(8,128)} %param.21) | copy-start | bytes 393220
  2.6 7.8 %collective-permute-start.1 = (bf16[1,72,256]{2,1,0:T(8,128)(2,1)S(1)}, bf16[1,72,256]{2,1,0:T(8,128)(2,1)S(1)}, u32[]{:S(2)}, u32[]{:S(2)}) collective-permute-start(bf16[1,72,256]{2,1,0:T(8,128)(2,1)S(1)} %get-tuple-element.234), channel_id=1, source_target_pairs={{0,8},{4,12},{8,0},{12,4},{16,24},{20,28},{24,16},{28,20},{1,9},{5... | collective-permute-start | bytes 110600 | tf_op jit(solution)/shard_map/ppermute | solution.py:512
  5.7 4.8 %collective-permute-start = (bf16[1,72,256]{2,1,0:T(8,128)(2,1)S(1)}, bf16[1,72,256]{2,1,0:T(8,128)(2,1)S(1)}, u32[]{:S(2)}, u32[]{:S(2)}) collective-permute-start(bf16[1,72,256]{2,1,0:T(8,128)(2,1)S(1)} %get-tuple-element.235), channel_id=1, source_target_pairs={{0,2},{1,3},{2,0},{3,1},{4,6},{5,7},{6,4},{7,5},{8,10},{9,11},{10,... | collective-permute-start | bytes 110600 | tf_op jit(solution)/shard_map/ppermute | solution.py:512
  10.5 6.1 %collective-permute-start.5 = (bf16[2,72,256]{2,1,0:T(8,128)(2,1)S(1)}, bf16[2,72,256]{2,1,0:T(8,128)(2,1)S(1)}, u32[]{:S(2)}, u32[]{:S(2)}) collective-permute-start(bf16[2,72,256]{2,1,0:T(8,128)(2,1)S(1)} %pad_maximum_fusion.11), channel_id=1, source_target_pairs={{0,16},{4,20},{8,24},{12,28},{16,0},{20,4},{24,8},{28,12},{1,17},{... | collective-permute-start | bytes 221192 | tf_op jit(solution)/shard_map/ppermute | solution.py:512
  13.1 4.4 %collective-permute-start.9 = (bf16[2,72,256]{2,1,0:T(8,128)(2,1)S(1)}, bf16[2,72,256]{2,1,0:T(8,128)(2,1)S(1)}, u32[]{:S(2)}, u32[]{:S(2)}) collective-permute-start(bf16[2,72,256]{2,1,0:T(8,128)(2,1)S(1)} %pad_maximum_fusion.12), channel_id=1, source_target_pairs={{0,8},{4,12},{8,0},{12,4},{16,24},{20,28},{24,16},{28,20},{1,9},{5... | collective-permute-start | bytes 221192 | tf_op jit(solution)/shard_map/ppermute | solution.py:512
  17.6 14.9 %collective-permute-start.10 = (bf16[4,72,256]{2,1,0:T(8,128)(2,1)S(1)}, bf16[4,72,256]{2,1,0:T(8,128)(2,1)S(1)}, u32[]{:S(2)}, u32[]{:S(2)}) collective-permute-start(bf16[4,72,256]{2,1,0:T(8,128)(2,1)S(1)} %pad_maximum_fusion.10), channel_id=1, source_target_pairs={{0,16},{4,20},{8,24},{12,28},{16,0},{20,4},{24,8},{28,12},{1,17},{... | collective-permute-start | bytes 442376 | tf_op jit(solution)/shard_map/ppermute | solution.py:512
  18.5 23.6 %collective-permute-start.2 = (bf16[1,64,1024]{2,1,0:T(8,128)(2,1)S(1)}, bf16[1,64,1024]{2,1,0:T(8,128)(2,1)}, u32[]{:S(2)}, u32[]{:S(2)}) collective-permute-start(bf16[1,64,1024]{2,1,0:T(8,128)(2,1)S(1)} %maximum_bitcast_fusion.1), channel_id=1, source_target_pairs={{0,8},{4,12},{8,0},{12,4},{16,24},{20,28},{24,16},{28,20},{1,9},{5... | collective-permute-start | bytes 393224 | tf_op jit(solution)/shard_map/ppermute | solution.py:570
  19.3 22.8 %collective-permute-start.3 = (bf16[1,64,1024]{2,1,0:T(8,128)(2,1)S(1)}, bf16[1,64,1024]{2,1,0:T(8,128)(2,1)}, u32[]{:S(2)}, u32[]{:S(2)}) collective-permute-start(bf16[1,64,1024]{2,1,0:T(8,128)(2,1)S(1)} %maximum_bitcast_fusion.1), channel_id=1, source_target_pairs={{0,16},{4,20},{8,24},{12,28},{16,0},{20,4},{24,8},{28,12},{1,17},{... | collective-permute-start | bytes 393224 | tf_op jit(solution)/shard_map/ppermute | solution.py:570
  21.4 20.7 %collective-permute-start.4 = (bf16[1,64,1024]{2,1,0:T(8,128)(2,1)S(1)}, bf16[1,64,1024]{2,1,0:T(8,128)(2,1)}, u32[]{:S(2)}, u32[]{:S(2)}) collective-permute-start(bf16[1,64,1024]{2,1,0:T(8,128)(2,1)S(1)} %maximum_bitcast_fusion.1), channel_id=1, source_target_pairs={{0,24},{4,28},{8,16},{12,20},{16,8},{20,12},{24,0},{28,4},{1,25},{... | collective-permute-start | bytes 393224 | tf_op jit(solution)/shard_map/ppermute | solution.py:570
  23.0 11.2 %collective-permute-start.6 = (bf16[4,72,256]{2,1,0:T(8,128)(2,1)S(1)}, bf16[4,72,256]{2,1,0:T(8,128)(2,1)S(1)}, u32[]{:S(2)}, u32[]{:S(2)}) collective-permute-start(bf16[4,72,256]{2,1,0:T(8,128)(2,1)S(1)} %pad_maximum_fusion.9), channel_id=1, source_target_pairs={{0,4},{4,0},{8,12},{12,8},{16,20},{20,16},{24,28},{28,24},{1,5},{5... | collective-permute-start | bytes 442376 | tf_op jit(solution)/shard_map/ppermute | solution.py:512
  32.6 6.8 %collective-permute-start.11 = (bf16[8,72,256]{2,1,0:T(8,128)(2,1)S(1)}, bf16[8,72,256]{2,1,0:T(8,128)(2,1)S(1)}, u32[]{:S(2)}, u32[]{:S(2)}) collective-permute-start(bf16[8,72,256]{2,1,0:T(8,128)(2,1)S(1)} %pad_maximum_fusion.8), channel_id=1, source_target_pairs={{0,4},{4,0},{8,12},{12,8},{16,20},{20,16},{24,28},{28,24},{1,5},{5... | collective-permute-start | bytes 884744 | tf_op jit(solution)/shard_map/ppermute | solution.py:512
  34.2 7.7 %copy-start.20 = (bf16[64,256]{0,1:T(8,128)(2,1)S(1)}, bf16[64,256]{0,1:T(8,128)(2,1)}, u32[]{:S(2)}) copy-start(bf16[64,256]{0,1:T(8,128)(2,1)} %get-tuple-element.227) | copy-start | bytes 98308
  34.3 6.8 %collective-permute-start.7 = (bf16[8,72,256]{2,1,0:T(8,128)(2,1)S(1)}, bf16[8,72,256]{2,1,0:T(8,128)(2,1)S(1)}, u32[]{:S(2)}, u32[]{:S(2)}) collective-permute-start(bf16[8,72,256]{2,1,0:T(8,128)(2,1)S(1)} %pad_maximum_fusion.7), channel_id=1, source_target_pairs={{0,2},{1,3},{2,0},{3,1},{4,6},{5,7},{6,4},{7,5},{8,10},{9,11},{10,... | collective-permute-start | bytes 884744 | tf_op jit(solution)/shard_map/ppermute | solution.py:512
  39.5 3.7 %collective-permute-start.12 = (bf16[16,72,256]{2,1,0:T(8,128)(2,1)S(1)}, bf16[16,72,256]{2,1,0:T(8,128)(2,1)S(1)}, u32[]{:S(2)}, u32[]{:S(2)}) collective-permute-start(bf16[16,72,256]{2,1,0:T(8,128)(2,1)S(1)} %pad_maximum_fusion.5), channel_id=1, source_target_pairs={{0,1},{1,0},{2,3},{3,2},{4,5},{5,4},{6,7},{7,6},{8,9},{9,8},{10,11... | collective-permute-start | bytes 1769480 | tf_op jit(solution)/shard_map/ppermute | solution.py:512
  42.0 2.2 collective-permute-start.8
  44.4 16.7 %collective-permute-start.13 = (bf16[4,64,1024]{2,1,0:T(8,128)(2,1)S(1)}, bf16[4,64,1024]{2,1,0:T(8,128)(2,1)S(1)}, u32[]{:S(2)}, u32[]{:S(2)}) collective-permute-start(bf16[4,64,1024]{2,1,0:T(8,128)(2,1)S(1)} %pad_maximum_fusion.6), channel_id=1, source_target_pairs={{0,2},{1,3},{2,0},{3,1},{4,6},{5,7},{6,4},{7,5},{8,10},{9,11},{10,... | collective-permute-start | bytes 1572872 | tf_op jit(solution)/shard_map/ppermute | solution.py:570
  61.1 9.0 %copy-start = (bf16[8,8,256,256]{3,2,1,0:T(8,128)(2,1)}, bf16[8,8,256,256]{3,2,1,0:T(8,128)(2,1)S(1)}, u32[]{:S(2)}) copy-start(bf16[8,8,256,256]{3,2,1,0:T(8,128)(2,1)S(1)} %get-tuple-element.118.pk) | copy-start | bytes 25165828
  61.2 7.0 %copy-start.28 = (s32[8,256]{1,0:T(8,128)S(1)}, s32[8,256]{1,0:T(8,128)}, u32[]{:S(2)}) copy-start(s32[8,256]{1,0:T(8,128)} %param.15) | copy-start | bytes 24580
  61.2 7.0 %copy-start.10 = (bf16[8,256,512]{2,1,0:T(8,128)(2,1)S(1)}, bf16[8,256,512]{2,1,0:T(8,128)(2,1)}, u32[]{:S(2)}) copy-start(bf16[8,256,512]{2,1,0:T(8,128)(2,1)} %param.14) | copy-start | bytes 6291460
  61.2 2.8 %collective-permute-start.14 = (bf16[8,272,256]{2,1,0:T(8,128)(2,1)S(1)}, bf16[8,272,256]{2,1,0:T(8,128)(2,1)S(1)}, u32[]{:S(2)}, u32[]{:S(2)}) collective-permute-start(bf16[8,272,256]{2,1,0:T(8,128)(2,1)S(1)} %get-tuple-element.110), channel_id=1, source_target_pairs={{0,1},{1,0},{2,3},{3,2},{4,5},{5,4},{6,7},{7,6},{8,9},{9,8},{10,11... | collective-permute-start | bytes 3342344 | tf_op jit(solution)/shard_map/ppermute | solution.py:512
  64.3 25.3 %collective-permute-start.16 = (bf16[8,64,1024]{2,1,0:T(8,128)(2,1)S(1)}, bf16[8,64,1024]{2,1,0:T(8,128)(2,1)S(1)}, u32[]{:S(2)}, u32[]{:S(2)}) collective-permute-start(bf16[8,64,1024]{2,1,0:T(8,128)(2,1)S(1)} %pad_maximum_fusion.3), channel_id=1, source_target_pairs={{0,4},{4,0},{8,12},{12,8},{16,20},{20,16},{24,28},{28,24},{1,5},{5... | collective-permute-start | bytes 3145736 | tf_op jit(solution)/shard_map/ppermute | solution.py:570
  64.9 27.0 %collective-permute-start.15 = (bf16[8,272,256]{2,1,0:T(8,128)(2,1)S(1)}, bf16[8,272,256]{2,1,0:T(8,128)(2,1)S(1)}, u32[]{:S(2)}, u32[]{:S(2)}) collective-permute-start(bf16[8,272,256]{2,1,0:T(8,128)(2,1)S(1)} %fusion), channel_id=1, source_target_pairs={{0,2},{1,3},{4,6},{5,7},{8,10},{9,11},{12,14},{13,15},{16,18},{17,... | collective-permute-start | bytes 3342344 | tf_op jit(solution)/shard_map/ppermute | solution.py:528
  89.8 2.8 %copy-start.11 = (bf16[16,64,1024]{2,1,0:T(8,128)(2,1)}, bf16[16,64,1024]{2,1,0:T(8,128)(2,1)S(1)}, u32[]{:S(2)}) copy-start(bf16[16,64,1024]{2,1,0:T(8,128)(2,1)S(1)} %pad_maximum_fusion.own_pair) | copy-start | bytes 6291460
  92.0 14.9 %collective-permute-start.18 = (bf16[16,64,1024]{2,1,0:T(8,128)(2,1)S(1)}, bf16[16,64,1024]{2,1,0:T(8,128)(2,1)S(1)}, u32[]{:S(2)}, u32[]{:S(2)}) collective-permute-start(bf16[16,64,1024]{2,1,0:T(8,128)(2,1)S(1)} %pad_maximum_fusion.own_pair), channel_id=1, source_target_pairs={{0,1},{1,0},{2,3},{3,2},{4,5},{5,4},{6,7},{7,6},{8,9},{9,8},{10,11... | collective-permute-start | bytes 6291464 | tf_op jit(solution)/shard_map/ppermute | solution.py:512
  92.6 5.1 %collective-permute-start.17 = (bf16[8,272,256]{2,1,0:T(8,128)(2,1)S(1)}, bf16[8,272,256]{2,1,0:T(8,128)(2,1)S(1)}, u32[]{:S(2)}, u32[]{:S(2)}) collective-permute-start(bf16[8,272,256]{2,1,0:T(8,128)(2,1)S(1)} %get-tuple-element.204), channel_id=1, source_target_pairs={{0,1},{1,0},{2,3},{3,2},{4,5},{5,4},{6,7},{7,6},{8,9},{9,8},{10,11... | collective-permute-start | bytes 3342344 | tf_op jit(solution)/shard_map/ppermute | solution.py:512
  97.7 9.2 %copy-start.1 = (bf16[8,272,256]{2,1,0:T(8,128)(2,1)}, bf16[8,272,256]{2,1,0:T(8,128)(2,1)S(1)}, u32[]{:S(2)}) copy-start(bf16[8,272,256]{2,1,0:T(8,128)(2,1)S(1)} %collective-permute-done.17.come.come_state) | copy-start | bytes 3342340
  106.9 1.3 copy-start.29
  108.2 39.8 %copy-start.6 = (f32[8,8,256]{2,1,0:T(8,128)S(1)}, f32[8,8,256]{2,1,0:T(8,128)}, u32[]{:S(2)}) copy-start(f32[8,8,256]{2,1,0:T(8,128)} %get-tuple-element.135.recip) | copy-start | bytes 196612
  147.8 12.2 %collective-permute-start.19 = (bf16[512,2048]{1,0:T(8,128)(2,1)}, bf16[512,2048]{1,0:T(8,128)(2,1)}, u32[]{:S(2)}, u32[]{:S(2)}) collective-permute-start(bf16[512,2048]{1,0:T(8,128)(2,1)} %get-tuple-element.138), channel_id=1, source_target_pairs={{0,1},{1,0},{2,3},{3,2},{4,5},{5,4},{6,7},{7,6},{8,9},{9,8},{10,11... | collective-permute-start | bytes 6291464 | tf_op jit(solution)/shard_map/ppermute | solution.py:512
  148.0 12.6 %copy-start.27 = (bf16[64,256]{1,0:T(8,128)(2,1)S(1)}, bf16[64,256]{1,0:T(8,128)(2,1)}, u32[]{:S(2)}) copy-start(bf16[64,256]{1,0:T(8,128)(2,1)} %get-tuple-element.236) | copy-start | bytes 98308
  160.0 3.6 %collective-permute-start.21 = (bf16[8,272,256]{2,1,0:T(8,128)(2,1)}, bf16[8,272,256]{2,1,0:T(8,128)(2,1)}, u32[]{:S(2)}, u32[]{:S(2)}) collective-permute-start(bf16[8,272,256]{2,1,0:T(8,128)(2,1)} %get-tuple-element.142), channel_id=1, source_target_pairs={{0,1},{1,0},{2,3},{3,2},{4,5},{5,4},{6,7},{7,6},{8,9},{9,8},{10,11... | collective-permute-start | bytes 3342344 | tf_op jit(solution)/shard_map/ppermute | solution.py:512
  160.6 3.1 %copy-start.4 = (bf16[8,272,256]{2,1,0:T(8,128)(2,1)S(1)}, bf16[8,272,256]{2,1,0:T(8,128)(2,1)}, u32[]{:S(2)}) copy-start(bf16[8,272,256]{2,1,0:T(8,128)(2,1)} %copy-done.3) | copy-start | bytes 3342340
  166.3 28.9 %collective-permute-start.22 = (bf16[8,272,256]{2,1,0:T(8,128)(2,1)}, bf16[8,272,256]{2,1,0:T(8,128)(2,1)}, u32[]{:S(2)}, u32[]{:S(2)}) collective-permute-start(bf16[8,272,256]{2,1,0:T(8,128)(2,1)} %fusion.3), channel_id=1, source_target_pairs={{2,0},{3,1},{6,4},{7,5},{10,8},{11,9},{14,12},{15,13},{18,16},{19,... | collective-permute-start | bytes 3342344 | tf_op jit(solution)/shard_map/ppermute | solution.py:528
  167.6 30.8 %collective-permute-start.20 = (bf16[256,2048]{1,0:T(8,128)(2,1)}, bf16[256,2048]{1,0:T(8,128)(2,1)}, u32[]{:S(2)}, u32[]{:S(2)}) collective-permute-start(bf16[256,2048]{1,0:T(8,128)(2,1)} %fusion.6), channel_id=1, source_target_pairs={{0,4},{4,0},{8,12},{12,8},{16,20},{20,16},{24,28},{28,24},{1,5},{5... | collective-permute-start | bytes 3145736 | tf_op jit(solution)/shard_map/ppermute | solution.py:512
  170.4 24.8 %copy-start.5 = (bf16[8,272,256]{2,1,0:T(8,128)(2,1)S(1)}, bf16[8,272,256]{2,1,0:T(8,128)(2,1)}, u32[]{:S(2)}) copy-start(bf16[8,272,256]{2,1,0:T(8,128)(2,1)} %copy-done.3) | copy-start | bytes 3342340
  198.4 7.0 %collective-permute-start.23 = (bf16[8,272,256]{2,1,0:T(8,128)(2,1)}, bf16[8,272,256]{2,1,0:T(8,128)(2,1)}, u32[]{:S(2)}, u32[]{:S(2)}) collective-permute-start(bf16[8,272,256]{2,1,0:T(8,128)(2,1)} %get-tuple-element.202), channel_id=1, source_target_pairs={{0,1},{1,0},{2,3},{3,2},{4,5},{5,4},{6,7},{7,6},{8,9},{9,8},{10,11... | collective-permute-start | bytes 3342344 | tf_op jit(solution)/shard_map/ppermute | solution.py:512
  198.4 7.0 %copy-start.7 = (f32[512,512]{1,0:T(8,128)S(1)}, f32[512,512]{1,0:T(8,128)}, u32[]{:S(2)}) copy-start(f32[512,512]{1,0:T(8,128)} %get-tuple-element.157.out_proj) | copy-start | bytes 3145732
  198.4 7.0 %copy-start.8 = (f32[512,512]{1,0:T(8,128)S(1)}, f32[512,512]{1,0:T(8,128)}, u32[]{:S(2)}) copy-start(f32[512,512]{1,0:T(8,128)} %get-tuple-element.156.query_weight) | copy-start | bytes 3145732
  198.4 7.0 %copy-start.9 = (f32[2,512]{1,0:T(2,128)S(1)}, f32[2,512]{1,0:T(2,128)}, u32[]{:S(2)}) copy-start(f32[2,512]{1,0:T(2,128)} %get-tuple-element.158.norm_two) | copy-start | bytes 12292
  200.9 24.7 %collective-permute-start.24 = (bf16[64,2048]{1,0:T(8,128)(2,1)S(1)}, bf16[64,2048]{1,0:T(8,128)(2,1)}, u32[]{:S(2)}, u32[]{:S(2)}) collective-permute-start(bf16[64,2048]{1,0:T(8,128)(2,1)S(1)} %get-tuple-element.162), channel_id=1, source_target_pairs={{0,8},{4,12},{8,0},{12,4},{16,24},{20,28},{24,16},{28,20},{1,9},{5... | collective-permute-start | bytes 786440 | tf_op jit(solution)/shard_map/ppermute | solution.py:872
  201.0 24.6 %collective-permute-start.25 = (bf16[64,2048]{1,0:T(8,128)(2,1)S(1)}, bf16[64,2048]{1,0:T(8,128)(2,1)}, u32[]{:S(2)}, u32[]{:S(2)}) collective-permute-start(bf16[64,2048]{1,0:T(8,128)(2,1)S(1)} %get-tuple-element.163), channel_id=1, source_target_pairs={{0,16},{4,20},{8,24},{12,28},{16,0},{20,4},{24,8},{28,12},{1,17},{... | collective-permute-start | bytes 786440 | tf_op jit(solution)/shard_map/ppermute | solution.py:872
  202.2 23.5 %collective-permute-start.26 = (bf16[64,2048]{1,0:T(8,128)(2,1)S(1)}, bf16[64,2048]{1,0:T(8,128)(2,1)S(1)}, u32[]{:S(2)}, u32[]{:S(2)}) collective-permute-start(bf16[64,2048]{1,0:T(8,128)(2,1)S(1)} %get-tuple-element.164), channel_id=1, source_target_pairs={{0,24},{4,28},{8,16},{12,20},{16,8},{20,12},{24,0},{28,4},{1,25},{... | collective-permute-start | bytes 786440 | tf_op jit(solution)/shard_map/ppermute | solution.py:872
  226.4 3.2 %collective-permute-start.27 = (bf16[2,16,72,256]{3,2,1,0:T(8,128)(2,1)}, bf16[2,16,72,256]{3,2,1,0:T(8,128)(2,1)}, u32[]{:S(2)}, u32[]{:S(2)}) collective-permute-start(bf16[2,16,72,256]{3,2,1,0:T(8,128)(2,1)} %get-tuple-element.165), channel_id=1, source_target_pairs={{0,1},{1,0},{2,3},{3,2},{4,5},{5,4},{6,7},{7,6},{8,9},{9,8},{10,11... | collective-permute-start | bytes 3538952 | tf_op jit(solution)/shard_map/ppermute | solution.py:512
  226.4 4.5 %copy-start.13 = (f32[16,72,256]{2,1,0:T(8,128)S(1)}, f32[16,72,256]{2,1,0:T(8,128)}, u32[]{:S(2)}) copy-start(f32[16,72,256]{2,1,0:T(8,128)} %get-tuple-element.160) | copy-start | bytes 3538948
  226.4 4.7 %copy-start.12 = (f32[16,72,256]{2,1,0:T(8,128)S(1)}, f32[16,72,256]{2,1,0:T(8,128)}, u32[]{:S(2)}) copy-start(f32[16,72,256]{2,1,0:T(8,128)} %get-tuple-element.171) | copy-start | bytes 3538948
  231.0 9.2 %collective-permute-start.28 = (bf16[8,72,256]{2,1,0:T(8,128)(2,1)S(1)}, bf16[8,72,256]{2,1,0:T(8,128)(2,1)}, u32[]{:S(2)}, u32[]{:S(2)}) collective-permute-start(bf16[8,72,256]{2,1,0:T(8,128)(2,1)S(1)} %get-tuple-element.192), channel_id=1, source_target_pairs={{0,2},{1,3},{2,0},{3,1},{4,6},{5,7},{6,4},{7,5},{8,10},{9,11},{10,... | collective-permute-start | bytes 884744 | tf_op jit(solution)/shard_map/ppermute | solution.py:512
  232.0 13.2 %collective-permute-start.32 = (bf16[8,72,256]{2,1,0:T(8,128)(2,1)}, bf16[8,72,256]{2,1,0:T(8,128)(2,1)S(1)}, u32[]{:S(2)}, u32[]{:S(2)}) collective-permute-start(bf16[8,72,256]{2,1,0:T(8,128)(2,1)} %get-tuple-element.194), channel_id=1, source_target_pairs={{0,4},{4,0},{8,12},{12,8},{16,20},{20,16},{24,28},{28,24},{1,5},{5... | collective-permute-start | bytes 884744 | tf_op jit(solution)/shard_map/ppermute | solution.py:512
  242.5 5.9 %copy-start.16 = (f32[512,64]{0,1:T(8,128)S(1)}, f32[512,64]{0,1:T(8,128)}, u32[]{:S(2)}) copy-start(f32[512,64]{0,1:T(8,128)} %param.21) | copy-start | bytes 393220
  242.5 5.9 %copy-start.23 = (f32[512,64]{0,1:T(8,128)S(1)}, f32[512,64]{0,1:T(8,128)}, u32[]{:S(2)}) copy-start(f32[512,64]{0,1:T(8,128)} %param.24) | copy-start | bytes 393220
  242.6 5.9 %copy-start.24 = (f32[512,64]{0,1:T(8,128)S(1)}, f32[512,64]{0,1:T(8,128)}, u32[]{:S(2)}) copy-start(f32[512,64]{0,1:T(8,128)} %param.25) | copy-start | bytes 393220
  243.0 6.3 %copy-start.18 = (f32[64,512]{1,0:T(8,128)S(1)}, f32[64,512]{1,0:T(8,128)}, u32[]{:S(2)}) copy-start(f32[64,512]{1,0:T(8,128)} %param.20) | copy-start | bytes 393220
  243.0 6.3 %copy-start.25 = (f32[64,512]{1,0:T(8,128)S(1)}, f32[64,512]{1,0:T(8,128)}, u32[]{:S(2)}) copy-start(f32[64,512]{1,0:T(8,128)} %param.22) | copy-start | bytes 393220
  243.0 6.3 %copy-start.26 = (f32[64,512]{1,0:T(8,128)S(1)}, f32[64,512]{1,0:T(8,128)}, u32[]{:S(2)}) copy-start(f32[64,512]{1,0:T(8,128)} %param.23) | copy-start | bytes 393220
  243.4 5.0 %collective-permute-start.36 = (bf16[64,1024]{1,0:T(8,128)(2,1)S(1)}, bf16[64,1024]{1,0:T(8,128)(2,1)S(1)}, u32[]{:S(2)}, u32[]{:S(2)}) collective-permute-start(bf16[64,1024]{1,0:T(8,128)(2,1)S(1)} %bitcast.135), channel_id=1, source_target_pairs={{0,2},{1,3},{2,0},{3,1},{4,6},{5,7},{6,4},{7,5},{8,10},{9,11},{10,... | collective-permute-start | bytes 393224 | tf_op jit(solution)/shard_map/ppermute | solution.py:512
  243.7 6.5 %collective-permute-start.29 = (bf16[4,72,256]{2,1,0:T(8,128)(2,1)S(1)}, bf16[4,72,256]{2,1,0:T(8,128)(2,1)S(1)}, u32[]{:S(2)}, u32[]{:S(2)}) collective-permute-start(bf16[4,72,256]{2,1,0:T(8,128)(2,1)S(1)} %get-tuple-element.170), channel_id=1, source_target_pairs={{0,4},{4,0},{8,12},{12,8},{16,20},{20,16},{24,28},{28,24},{1,5},{5... | collective-permute-start | bytes 442376 | tf_op jit(solution)/shard_map/ppermute | solution.py:512
  245.3 10.8 %collective-permute-start.33 = (bf16[4,72,256]{2,1,0:T(8,128)(2,1)S(1)}, bf16[4,72,256]{2,1,0:T(8,128)(2,1)S(1)}, u32[]{:S(2)}, u32[]{:S(2)}) collective-permute-start(bf16[4,72,256]{2,1,0:T(8,128)(2,1)S(1)} %get-tuple-element.208), channel_id=1, source_target_pairs={{0,16},{4,20},{8,24},{12,28},{16,0},{20,4},{24,8},{28,12},{1,17},{... | collective-permute-start | bytes 442376 | tf_op jit(solution)/shard_map/ppermute | solution.py:512
  248.5 16.4 %copy-start.14 = (f32[32832]{0:T(1024)S(1)}, f32[32832]{0:T(1024)}, u32[]{:S(2)}) copy-start(f32[32832]{0:T(1024)} %param.17) | copy-start | bytes 393988
  248.5 16.4 %copy-start.21 = (f32[32832]{0:T(1024)S(1)}, f32[32832]{0:T(1024)}, u32[]{:S(2)}) copy-start(f32[32832]{0:T(1024)} %param.18) | copy-start | bytes 393988
  248.5 16.4 %copy-start.22 = (f32[32832]{0:T(1024)S(1)}, f32[32832]{0:T(1024)}, u32[]{:S(2)}) copy-start(f32[32832]{0:T(1024)} %param.19) | copy-start | bytes 393988
  250.2 7.0 %collective-permute-start.30 = (bf16[2,72,256]{2,1,0:T(8,128)(2,1)S(1)}, bf16[2,72,256]{2,1,0:T(8,128)(2,1)S(1)}, u32[]{:S(2)}, u32[]{:S(2)}) collective-permute-start(bf16[2,72,256]{2,1,0:T(8,128)(2,1)S(1)} %get-tuple-element.214), channel_id=1, source_target_pairs={{0,16},{4,20},{8,24},{12,28},{16,0},{20,4},{24,8},{28,12},{1,17},{... | collective-permute-start | bytes 221192 | tf_op jit(solution)/shard_map/ppermute | solution.py:512
  256.1 4.4 %collective-permute-start.34 = (bf16[2,72,256]{2,1,0:T(8,128)(2,1)S(1)}, bf16[2,72,256]{2,1,0:T(8,128)(2,1)S(1)}, u32[]{:S(2)}, u32[]{:S(2)}) collective-permute-start(bf16[2,72,256]{2,1,0:T(8,128)(2,1)S(1)} %get-tuple-element.216), channel_id=1, source_target_pairs={{0,8},{4,12},{8,0},{12,4},{16,24},{20,28},{24,16},{28,20},{1,9},{5... | collective-permute-start | bytes 221192 | tf_op jit(solution)/shard_map/ppermute | solution.py:512
  257.2 5.6 %collective-permute-start.31 = (bf16[1,72,256]{2,1,0:T(8,128)(2,1)S(1)}, bf16[1,72,256]{2,1,0:T(8,128)(2,1)S(1)}, u32[]{:S(2)}, u32[]{:S(2)}) collective-permute-start(bf16[1,72,256]{2,1,0:T(8,128)(2,1)S(1)} %fusion.23), channel_id=1, source_target_pairs={{0,8},{4,12},{8,0},{12,4},{16,24},{20,28},{24,16},{28,20},{1,9},{5... | collective-permute-start | bytes 110600 | tf_op jit(solution)/shard_map/ppermute | solution.py:512
  260.6 4.2 %collective-permute-start.35 = (bf16[1,72,256]{2,1,0:T(8,128)(2,1)S(1)}, bf16[1,72,256]{2,1,0:T(8,128)(2,1)S(1)}, u32[]{:S(2)}, u32[]{:S(2)}) collective-permute-start(bf16[1,72,256]{2,1,0:T(8,128)(2,1)S(1)} %fusion.20), channel_id=1, source_target_pairs={{0,2},{1,3},{2,0},{3,1},{4,6},{5,7},{6,4},{7,5},{8,10},{9,11},{10,... | collective-permute-start | bytes 110600 | tf_op jit(solution)/shard_map/ppermute | solution.py:512
  (3 other events, 3.0 us)

commit v5 on v4

--- a/solution.py
+++ b/solution.py
@@ -20,7 +20,7 @@
 SPARE = 16
 VMEM_LIMIT = 16 * 1024 * 1024
 BIG = 1 << 20
-LIMITS = {'keys': 14, 'queries': 16, 'mix': 12, 'ffn': 44, 'outer': 14, 'back_query': 24, 'back_key': 34}
+LIMITS = {'keys': 14, 'queries': 16, 'mix': 12, 'ffn': 44, 'outer': 14, 'back_query': 18, 'back_key': 26}
 F32 = jnp.float32
 LOW = jnp.bfloat16
 
@@ -574,12 +574,15 @@
     return jnp.concatenate([value] + come, axis=0), more
 
 
-def gather_doubling(value, order, late):
+def gather_doubling(value, order, late, prepare=None):
     value = value[None]
     for step, (axis, bit) in enumerate(order):
+        if step == len(order) - 2:
+            value, late = lax.optimization_barrier((value, late))
         come = flip(value, axis, bit)
-        if step == 0:
+        if step == 0 and prepare is not None:
             come, late = lax.optimization_barrier((come, late))
+            late = prepare(late)
         low = bit_of(axis, bit) == 0
         value = jnp.concatenate([jnp.where(low, value, come), jnp.where(low, come, value)], axis=0)
     return value, late
@@ -677,13 +680,17 @@
     ffn_pair = (ffn_in, ffn_out)
     halves = [framed[:, : width // 2], framed[:, width // 2 :]]
     gathered = []
+
+    def beside(shards):
+        return jnp.concatenate([shards[0].astype(LOW), shards[1].astype(LOW).T], axis=1)[None]
+
     for half, order in zip(halves, gather_orders()):
-        whole, ffn_pair = gather_doubling(half, order, ffn_pair)
+        whole, ffn_pair = gather_doubling(half, order, ffn_pair, None if gathered else beside)
         gathered.append(whole)
     spots = [[place_in(order[::-1], i) for i in range(devices)] for order in gather_orders()]
     whole_rows = -(-(starts[-1] + rows) // 8) * 8
     group_width = ffn_in.shape[1]
-    pair = jnp.concatenate([ffn_pair[0].astype(LOW), ffn_pair[1].astype(LOW).T], axis=1)[None]
+    pair = ffn_pair
     top = lax.axis_size("dp") // 4
     pair, found = gather_more(pair, [(0, 0)], "dp", [top, 2 * top, 3 * top])
     for bit in range(axis_bits("dp") - 3, 0, -1):
@@ -806,7 +813,7 @@
     come_pair = flip(leave, "seq", 0)
 
     args = (grad_middle, out_weight, mixed, recip, pq)
-    outs = [array(held, LOW)] + [pltpu.VMEM(state_shape, LOW)] * 2
+    outs = [pltpu.VMEM(held, LOW)] + [pltpu.VMEM(state_shape, LOW)] * 2
     outs = outs + [array((width, width), F32)]
     outers, own, their, out_proj = call(
         functools.partial(outer_kernel, heads, size),
@@ -831,7 +838,7 @@
     come_near = flip(sent, "dp", 0)
     beside, far, omega_low = send_half(own, their, False, omega_low)
     args = (turned, omega_low, outers, value, pq, pk, score, core, keep, come, uq, uk)
-    outs = [array(flat, LOW)] * 3
+    outs = [pltpu.VMEM(flat, LOW)] * 3
     query_grad, key_part, value_part, query_weight = call(
         functools.partial(back_query_kernel, heads, size),
         seqs,
@@ -841,7 +848,7 @@
         [spec(a) for a in outs] + [fixed((width, width))],
         "back_query",
         1,
-        chip=(),
+        chip=(2,),
         scratch=[
             pltpu.VMEM((heads, ext, count), LOW),
             pltpu.VMEM(score_shape[1:], LOW),
@@ -884,7 +891,7 @@
         [per_seq(tokens.shape), fixed(piece_shape)] + [fixed(piece_shape[1:])] * 2,
         "back_key",
         7 * unit,
-        chip=(),
+        chip=(11, 12, 13),
         scratch=[
             pltpu.VMEM((3 * width, length), LOW),
             pltpu.VMEM((heads, ext, count), LOW),

time: 267 us -> 271 us (1.015)
  local copies, waits for them, and re-layouts: 8.8 us -> 16.6 us
  waiting for transfers between devices: 56.9 us -> 50.9 us
  starting transfers between devices: 42.2 us -> 45.1 us
    unnamed x63 -> x73, local copies, waits for them, and re-layouts: 5.44 us -> 13.2 us
    ppermute x27, waiting for transfers between devices: 44.5 us -> 39.6 us  [flip(): lax.ppermute(value, axis, [(i, i ^ 1 << bit) for i in range(lax.axis_size...]
  transfers between devices with their start and end apart: 37 -> 37, of which waited for: 18 -> 18; matrix products, arithmetic and copies ran while one was open for 9% -> 9% of each run, Pallas kernels for 34% -> 33%
where the time goes in v5:
time: 271 us; the launch traced here: 269 us
  Pallas kernels  128 us (47%)
  waiting for transfers between devices  50.9 us (19%)
  starting transfers between devices  45.1 us (17%)
  other arithmetic  26.9 us (10%)
  local copies, waits for them, and re-layouts  16.6 us (6%)
    pallas_call x7, Pallas kernels, call(): pl.pallas_call(kernel, grid=(steps,), in_specs=in_specs, out_specs=out_sp...  127 us
    ppermute x27, waiting for transfers between devices, flip(): lax.ppermute(value, axis, [(i, i ^ 1 << bit) for i in range(lax.axis_size...  39.6 us
    ppermute x27, starting transfers between devices, flip(): lax.ppermute(value, axis, [(i, i ^ 1 << bit) for i in range(lax.axis_size...  28.8 us
    unnamed x73, local copies, waits for them, and re-layouts  13.2 us
    ppermute x5, starting transfers between devices, gather_more(): lax.ppermute(value, axis, [(i, i ^ jump) for i in range(size)])  8.11 us
    ppermute x5, waiting for transfers between devices, gather_more(): lax.ppermute(value, axis, [(i, i ^ jump) for i in range(size)])  5.79 us
    ppermute x2, waiting for transfers between devices, send_half(): come = lax.ppermute(mine, 'seq', pairs)  5.52 us
  transfers between devices with their start and end apart: 37, of which 18 were waited for; matrix products, arithmetic and copies ran while one was open for 9% of the time, Pallas kernels for 33%

profile of v5, /device:TPU:0, one launch (start us, length us, event | category | flops | bytes accessed | tf_op | source)
XLA Modules:
  0.0 269.1 jit_solution(7719303114637159783)
XLA Ops:
  0.7 0.9 convert_element_type.301
  2.5 3.1 %collective-permute-start.3 = (bf16[1,72,256]{2,1,0:T(8,128)(2,1)S(1)}, bf16[1,72,256]{2,1,0:T(8,128)(2,1)S(1)}, u32[]{:S(2)}, u32[]{:S(2)}) collective-permute-start(bf16[1,72,256]{2,1,0:T(8,128)(2,1)S(1)} %get-tuple-element.236), channel_id=1, source_target_pairs={{0,8},{4,12},{8,0},{12,4},{16,24},{20,28},{24,16},{28,20},{1,9},{5... | collective-permute-start | bytes 110600 | tf_op jit(solution)/shard_map/ppermute | solution.py:512
  5.6 1.5 collective-permute-start
  7.5 2.0 collective-permute-done
  9.8 3.0 %collective-permute-start.4 = (bf16[2,72,256]{2,1,0:T(8,128)(2,1)S(1)}, bf16[2,72,256]{2,1,0:T(8,128)(2,1)S(1)}, u32[]{:S(2)}, u32[]{:S(2)}) collective-permute-start(bf16[2,72,256]{2,1,0:T(8,128)(2,1)S(1)} %pad_maximum_fusion.12), channel_id=1, source_target_pairs={{0,16},{4,20},{8,24},{12,28},{16,0},{20,4},{24,8},{28,12},{1,17},{... | collective-permute-start | bytes 221192 | tf_op jit(solution)/shard_map/ppermute | solution.py:512
  12.8 0.9 convert_bitcast_fusion
  13.7 0.9 convert_element_type.302
  15.2 1.8 collective-permute-start.5
  17.7 2.7 %collective-permute-start.2 = (bf16[4,72,256]{2,1,0:T(8,128)(2,1)S(1)}, bf16[4,72,256]{2,1,0:T(8,128)(2,1)S(1)}, u32[]{:S(2)}, u32[]{:S(2)}) collective-permute-start(bf16[4,72,256]{2,1,0:T(8,128)(2,1)S(1)} %pad_maximum_fusion.9), channel_id=1, source_target_pairs={{0,16},{4,20},{8,24},{12,28},{16,0},{20,4},{24,8},{28,12},{1,17},{... | collective-permute-start | bytes 442376 | tf_op jit(solution)/shard_map/ppermute | solution.py:512
  20.5 5.0 %collective-permute-done.2 = bf16[4,72,256]{2,1,0:T(8,128)(2,1)S(1)} collective-permute-done((bf16[4,72,256]{2,1,0:T(8,128)(2,1)S(1)}, bf16[4,72,256]{2,1,0:T(8,128)(2,1)S(1)}, u32[]{:S(2)}, u32[]{:S(2)}) %collective-permute-start.2) | collective-permute-done | bytes 147488 | tf_op jit(solution)/shard_map/ppermute | solution.py:512
  25.9 1.2 collective-permute-start.6
  27.1 3.4 %collective-permute-start.7 = (bf16[1,64,1024]{2,1,0:T(8,128)(2,1)}, bf16[1,64,1024]{2,1,0:T(8,128)(2,1)}, u32[]{:S(2)}, u32[]{:S(2)}) collective-permute-start(bf16[1,64,1024]{2,1,0:T(8,128)(2,1)} %maximum_bitcast_fusion.1), channel_id=1, source_target_pairs={{0,16},{4,20},{8,24},{12,28},{16,0},{20,4},{24,8},{28,12},{1,17},{... | collective-permute-start | bytes 393224 | tf_op jit(solution)/shard_map/ppermute | solution.py:570
  30.5 1.8 collective-permute-start.9
  32.6 4.7 %collective-permute-done.9 = bf16[8,72,256]{2,1,0:T(8,128)(2,1)S(1)} collective-permute-done((bf16[8,72,256]{2,1,0:T(8,128)(2,1)S(1)}, bf16[8,72,256]{2,1,0:T(8,128)(2,1)S(1)}, u32[]{:S(2)}, u32[]{:S(2)}) %collective-permute-start.9) | collective-permute-done | bytes 294944 | tf_op jit(solution)/shard_map/ppermute | solution.py:512
  38.3 1.2 pad_maximum_fusion.6
  40.6 1.8 collective-permute-start.13
  42.4 0.9 unpack.1
  43.4 15.0 %keys.1 = (bf16[8,512,256]{2,1,0:T(8,128)(2,1)}, bf16[8,512,256]{2,1,0:T(8,128)(2,1)}, bf16[8,8,80,256]{3,2,1,0:T(8,128)(2,1)}, bf16[8,8,256,256]{3,2,1,0:T(8,12...) custom-call(bf16[8,256,512]{2,1,0:T(8,128)(2,1)} %tok.5, ...), custom_call_target="tpu_custom_call" | custom-call | flops 1 | bytes 1 | tf_op jit(solution)/shard_map/keys/pallas_call | solution.py:481
  58.6 2.7 %collective-permute-done.14 = bf16[8,272,256]{2,1,0:T(8,128)(2,1)S(1)} collective-permute-done((bf16[8,272,256]{2,1,0:T(8,128)(2,1)S(1)}, bf16[8,272,256]{2,1,0:T(8,128)(2,1)S(1)}, u32[]{:S(2)}, u32[]{:S(2)}) %collective-permute-start.14) | collective-permute-done | bytes 1114144 | tf_op jit(solution)/shard_map/ppermute | solution.py:512
  61.6 1.7 collective-permute-start.16
  63.3 2.5 collective-permute-start.15
  65.8 1.8 multiply_convert_fusion
  67.6 13.5 %queries.1 = (bf16[8,512,256]{2,1,0:T(8,128)(2,1)}, bf16[8,8,256,256]{3,2,1,0:T(8,128)(2,1)S(1)}, bf16[8,8,256,256]{3,2,1,0:T(8,128)(2,1)}, bf16[8,8,256,256]{3,2,1,0:T(8,128)(2,1)}, f32[8,8,80,256]{3,2,1,0:T(8,128)S(1)}) custom-call(bf16[8,512,256]{2,1,0:T(8,128)(2,1)} %get-tuple-element.114.turned, bf16[1536,512]{1,0:T(8,128)(2,1)S(1)} %get-tuple-element.106.weights, ...), custom_call_target="tpu_custom_call" | custom-call | flops 1 | bytes 1 | tf_op jit(solution)/shard_map/queries/pallas_call | solution.py:481
  81.1 5.8 %collective-permute-done.16 = bf16[8,64,1024]{2,1,0:T(8,128)(2,1)S(1)} collective-permute-done((bf16[8,64,1024]{2,1,0:T(8,128)(2,1)S(1)}, bf16[8,64,1024]{2,1,0:T(8,128)(2,1)S(1)}, u32[]{:S(2)}, u32[]{:S(2)}) %collective-permute-start.16) | collective-permute-done | bytes 1048608 | tf_op jit(solution)/shard_map/ppermute | solution.py:570
  87.0 2.4 collective-permute-done.15
  90.8 4.4 %collective-permute-done.17.come.come_state = bf16[8,272,256]{2,1,0:T(8,128)(2,1)S(1)} collective-permute-done((bf16[8,272,256]{2,1,0:T(8,128)(2,1)S(1)}, bf16[8,272,256]{2,1,0:T(8,128)(2,1)S(1)}, u32[]{:S(2)}, u32[]{:S(2)}) %collective-permute-start.17) | collective-permute-done | bytes 1114144 | tf_op jit(solution)/shard_map/ppermute | solution.py:512
  95.2 9.1 %mix.1 = (bf16[8,512,256]{2,1,0:T(8,128)(2,1)}, f32[8,8,256]{2,1,0:T(8,128)}, f32[8,256,512]{2,1,0:T(8,128)}, bf16[8,256,512]{2,1,0:T(8,128)(2,1)}) custom-call(bf16[8,256,512]{2,1,0:T(8,128)(2,1)} %tok.5, f32[4,512]{1,0:T(4,128)S(1)} %get-tuple-element.124.norms, bf16[512,512]{1,0:T(8,128)(2,1)S(1)} %get-tuple-element.125.out_weight, ...), custom_call_target="tpu_custom_call" | custom-call | flops 1 | bytes 1 | tf_op jit(solution)/shard_map/mix/pallas_call | solution.py:481
  104.4 1.4 copy-done.34
  105.8 39.7 %ffn.1 = (bf16[2048,512]{1,0:T(8,128)(2,1)}, f32[2048,512]{1,0:T(8,128)}, bf16[512,2048]{1,0:T(8,128)(2,1)}, bf16[512,2048]{1,0:T(8,128)(2,1)}, f32[2,512]{1,0:T(2,128)}) custom-call(bf16[2048,512]{1,0:T(8,128)(2,1)} %bitcast.137, f32[2048,512]{1,0:T(8,128)} %bitcast.136, bf16[2048,512]{1,0:T(8,128)(2,1)} %bitcast.124, ...), custom_call_target="tpu_custom_call" | custom-call | flops 42949672960 | bytes 23080972 | tf_op jit(solution)/shard_map/ffn/pallas_call | solution.py:481
  145.6 11.0 %outer.1 = (bf16[8,8,80,256]{3,2,1,0:T(8,128)(2,1)S(1)}, bf16[8,272,256]{2,1,0:T(8,128)(2,1)S(1)}, bf16[8,272,256]{2,1,0:T(8,128)(2,1)}, f32[512,512]{1,0:T(8,128)}) custom-call(f32[8,256,512]{2,1,0:T(8,128)} %bitcast.118, bf16[512,512]{1,0:T(8,128)(2,1)S(1)} %get-tuple-element.125.out_weight, bf16[8,512,256]{2,1,0:T(8,128)(2,1)} %get-tuple-element.136.mixed, ...), custom_call_target="tpu_custom_call" | custom-call | flops 1 | bytes 1 | tf_op jit(solution)/shard_map/outer/pallas_call | solution.py:481
  156.6 1.0 copy-done.3
  157.6 1.5 copy-done.6
  159.7 3.0 %fusion.6 = bf16[256,2048]{1,0:T(8,128)(2,1)} fusion(bf16[2,256,2048]{2,1,0:T(8,128)(2,1)} %bitcast.17, s32[]{:T(128)S(6)} %select_n.277, bf16[2,256,2048]{2,1,0:T(8,128)(2,1)} %bitcast.125), kind=kLoop, calls=%fused_computation.21 | loop fusion | flops 2097152 | bytes 3145732 | tf_op jit(solution)/shard_map/convert_element_type | solution.py:836
  162.8 2.6 fusion.3
  165.3 1.3 collective-permute-start.22
  167.0 1.2 copy-done.2
  168.2 1.7 copy-done.7
  170.0 19.9 %back_query.1 = (bf16[8,512,256]{2,1,0:T(8,128)(2,1)S(1)}, bf16[8,512,256]{2,1,0:T(8,128)(2,1)S(1)}, bf16[8,512,256]{2,1,0:T(8,128)(2,1)S(1)}, f32[512,512]{1,0:T(8,128)}) custom-call(bf16[8,512,256]{2,1,0:T(8,128)(2,1)} %get-tuple-element.114.turned, bf16[80,256]{1,0:T(8,128)(2,1)S(1)} %maximum_maximum_fusion.omega_low, ...), custom_call_target="tpu_custom_call" | custom-call | flops 1 | bytes 1 | tf_op jit(solution)/shard_map/back_query/pallas_call | solution.py:481
  189.9 1.3 copy-done.9
  191.2 3.1 %collective-permute-done.22 = bf16[8,272,256]{2,1,0:T(8,128)(2,1)} collective-permute-done((bf16[8,272,256]{2,1,0:T(8,128)(2,1)}, bf16[8,272,256]{2,1,0:T(8,128)(2,1)}, u32[]{:S(2)}, u32[]{:S(2)}) %collective-permute-start.22) | collective-permute-done | bytes 1114144 | tf_op jit(solution)/shard_map/ppermute | solution.py:528
  194.3 3.2 %fusion.5 = (bf16[8,272,256]{2,1,0:T(8,128)(2,1)}, bf16[8,272,256]{2,1,0:T(8,128)(2,1)S(1)}) fusion(bf16[8,272,256]{2,1,0:T(8,128)(2,1)S(1)} %copy-done.5, bf16[8,272,256]{2,1,0:T(8,128)(2,1)} %collective-permute-done.22, pred[]{:T(512)S(6)} %eq.31, bf16[8,272,256]{2,1,0:T(8,128)(2,1)} %collective-permute-done.21), kind=kLoop, calls=%fused_computation.16 | loop fusion | flops 5013504 | bytes 5570561 | tf_op jit(solution)/shard_map/convert_element_type | solution.py:536
  197.6 2.5 fusion.7
  200.4 3.8 %collective-permute-start.25 = (bf16[64,2048]{1,0:T(8,128)(2,1)S(1)}, bf16[64,2048]{1,0:T(8,128)(2,1)}, u32[]{:S(2)}, u32[]{:S(2)}) collective-permute-start(bf16[64,2048]{1,0:T(8,128)(2,1)S(1)} %get-tuple-element.165), channel_id=1, source_target_pairs={{0,16},{4,20},{8,24},{12,28},{16,0},{20,4},{24,8},{28,12},{1,17},{... | collective-permute-start | bytes 786440 | tf_op jit(solution)/shard_map/ppermute | solution.py:879
  204.6 1.6 copy-done.14
  206.1 1.2 copy-done.15
  207.4 1.2 copy-done.16
  208.6 19.1 %back_key.1 = (f32[8,256,512]{2,1,0:T(8,128)}, bf16[2,16,72,256]{3,2,1,0:T(8,128)(2,1)}, f32[16,72,256]{2,1,0:T(8,128)}, f32[16,72,256]{2,1,0:T(8,128)}) custom-call(bf16[8,256,512]{2,1,0:T(8,128)(2,1)} %tok.5, f32[4,512]{1,0:T(4,128)S(1)} %get-tuple-element.124.norms, f32[8,256,512]{2,1,0:T(8,128)} %bitcast.119, ...), custom_call_target="tpu_custom_call" | custom-call | flops 15032385536 | bytes 41472004 | tf_op jit(solution)/shard_map/back_key/pallas_call | solution.py:481
  228.5 3.2 %collective-permute-done.27 = bf16[2,16,72,256]{3,2,1,0:T(8,128)(2,1)} collective-permute-done((bf16[2,16,72,256]{3,2,1,0:T(8,128)(2,1)}, bf16[2,16,72,256]{3,2,1,0:T(8,128)(2,1)}, u32[]{:S(2)}, u32[]{:S(2)}) %collective-permute-start.27) | collective-permute-done | bytes 1179680 | tf_op jit(solution)/shard_map/ppermute | solution.py:512
  231.6 1.3 fusion.32
  233.1 2.1 collective-permute-start.28
  236.1 1.7 collective-permute-start.32
  237.8 4.9 %collective-permute-done.28 = bf16[8,72,256]{2,1,0:T(8,128)(2,1)} collective-permute-done((bf16[8,72,256]{2,1,0:T(8,128)(2,1)S(1)}, bf16[8,72,256]{2,1,0:T(8,128)(2,1)}, u32[]{:S(2)}, u32[]{:S(2)}) %collective-permute-start.28) | collective-permute-done | bytes 294944 | tf_op jit(solution)/shard_map/ppermute | solution.py:512
  242.7 1.0 fusion.13
  243.7 1.2 convert_add_fusion.12
  245.8 1.8 collective-permute-start.36
  247.6 1.7 collective-permute-start.29
  249.3 1.6 collective-permute-start.33
  253.0 1.5 collective-permute-start.30
  254.5 5.1 %collective-permute-done.33 = bf16[4,72,256]{2,1,0:T(8,128)(2,1)S(1)} collective-permute-done((bf16[4,72,256]{2,1,0:T(8,128)(2,1)S(1)}, bf16[4,72,256]{2,1,0:T(8,128)(2,1)S(1)}, u32[]{:S(2)}, u32[]{:S(2)}) %collective-permute-start.33) | collective-permute-done | bytes 147488 | tf_op jit(solution)/shard_map/ppermute | solution.py:512
  260.0 1.2 collective-permute-done.30
  261.8 2.2 collective-permute-done.34
  264.0 1.5 collective-permute-start.35
  265.6 2.5 collective-permute-done.35
  268.2 1.0 fusion.30
  (157 shorter events, 15.0 us)
Async XLA Ops:
  2.5 5.0 %collective-permute-start.3 = (bf16[1,72,256]{2,1,0:T(8,128)(2,1)S(1)}, bf16[1,72,256]{2,1,0:T(8,128)(2,1)S(1)}, u32[]{:S(2)}, u32[]{:S(2)}) collective-permute-start(bf16[1,72,256]{2,1,0:T(8,128)(2,1)S(1)} %get-tuple-element.236), channel_id=1, source_target_pairs={{0,8},{4,12},{8,0},{12,4},{16,24},{20,28},{24,16},{28,20},{1,9},{5... | collective-permute-start | bytes 110600 | tf_op jit(solution)/shard_map/ppermute | solution.py:512
  5.6 4.0 %collective-permute-start = (bf16[1,72,256]{2,1,0:T(8,128)(2,1)S(1)}, bf16[1,72,256]{2,1,0:T(8,128)(2,1)S(1)}, u32[]{:S(2)}, u32[]{:S(2)}) collective-permute-start(bf16[1,72,256]{2,1,0:T(8,128)(2,1)S(1)} %get-tuple-element.237), channel_id=1, source_target_pairs={{0,2},{1,3},{2,0},{3,1},{4,6},{5,7},{6,4},{7,5},{8,10},{9,11},{10,... | collective-permute-start | bytes 110600 | tf_op jit(solution)/shard_map/ppermute | solution.py:512
  9.6 5.0 %collective-permute-start.1 = (bf16[2,72,256]{2,1,0:T(8,128)(2,1)S(1)}, bf16[2,72,256]{2,1,0:T(8,128)(2,1)S(1)}, u32[]{:S(2)}, u32[]{:S(2)}) collective-permute-start(bf16[2,72,256]{2,1,0:T(8,128)(2,1)S(1)} %pad_maximum_fusion.11), channel_id=1, source_target_pairs={{0,8},{4,12},{8,0},{12,4},{16,24},{20,28},{24,16},{28,20},{1,9},{5... | collective-permute-start | bytes 221192 | tf_op jit(solution)/shard_map/ppermute | solution.py:512
  9.7 15.9 %copy-start.25 = (f32[64,256]{1,0:T(8,128)S(1)}, f32[64,256]{1,0:T(8,128)}, u32[]{:S(2)}) copy-start(f32[64,256]{1,0:T(8,128)} %param.16) | copy-start | bytes 196612
  9.8 5.4 %collective-permute-start.4 = (bf16[2,72,256]{2,1,0:T(8,128)(2,1)S(1)}, bf16[2,72,256]{2,1,0:T(8,128)(2,1)S(1)}, u32[]{:S(2)}, u32[]{:S(2)}) collective-permute-start(bf16[2,72,256]{2,1,0:T(8,128)(2,1)S(1)} %pad_maximum_fusion.12), channel_id=1, source_target_pairs={{0,16},{4,20},{8,24},{12,28},{16,0},{20,4},{24,8},{28,12},{1,17},{... | collective-permute-start | bytes 221192 | tf_op jit(solution)/shard_map/ppermute | solution.py:512
  15.2 5.2 %collective-permute-start.5 = (bf16[4,72,256]{2,1,0:T(8,128)(2,1)S(1)}, bf16[4,72,256]{2,1,0:T(8,128)(2,1)S(1)}, u32[]{:S(2)}, u32[]{:S(2)}) collective-permute-start(bf16[4,72,256]{2,1,0:T(8,128)(2,1)S(1)} %pad_maximum_fusion.10), channel_id=1, source_target_pairs={{0,4},{4,0},{8,12},{12,8},{16,20},{20,16},{24,28},{28,24},{1,5},{5... | collective-permute-start | bytes 442376 | tf_op jit(solution)/shard_map/ppermute | solution.py:512
  17.7 7.8 %collective-permute-start.2 = (bf16[4,72,256]{2,1,0:T(8,128)(2,1)S(1)}, bf16[4,72,256]{2,1,0:T(8,128)(2,1)S(1)}, u32[]{:S(2)}, u32[]{:S(2)}) collective-permute-start(bf16[4,72,256]{2,1,0:T(8,128)(2,1)S(1)} %pad_maximum_fusion.9), channel_id=1, source_target_pairs={{0,16},{4,20},{8,24},{12,28},{16,0},{20,4},{24,8},{28,12},{1,17},{... | collective-permute-start | bytes 442376 | tf_op jit(solution)/shard_map/ppermute | solution.py:512
  25.6 6.8 %collective-permute-start.11 = (bf16[8,72,256]{2,1,0:T(8,128)(2,1)S(1)}, bf16[8,72,256]{2,1,0:T(8,128)(2,1)S(1)}, u32[]{:S(2)}, u32[]{:S(2)}) collective-permute-start(bf16[8,72,256]{2,1,0:T(8,128)(2,1)S(1)} %pad_maximum_fusion.7), channel_id=1, source_target_pairs={{0,4},{4,0},{8,12},{12,8},{16,20},{20,16},{24,28},{28,24},{1,5},{5... | collective-permute-start | bytes 884744 | tf_op jit(solution)/shard_map/ppermute | solution.py:512
  25.9 12.4 %collective-permute-start.6 = (bf16[1,64,1024]{2,1,0:T(8,128)(2,1)}, bf16[1,64,1024]{2,1,0:T(8,128)(2,1)}, u32[]{:S(2)}, u32[]{:S(2)}) collective-permute-start(bf16[1,64,1024]{2,1,0:T(8,128)(2,1)} %maximum_bitcast_fusion.1), channel_id=1, source_target_pairs={{0,8},{4,12},{8,0},{12,4},{16,24},{20,28},{24,16},{28,20},{1,9},{5... | collective-permute-start | bytes 393224 | tf_op jit(solution)/shard_map/ppermute | solution.py:570
  27.1 11.2 %collective-permute-start.7 = (bf16[1,64,1024]{2,1,0:T(8,128)(2,1)}, bf16[1,64,1024]{2,1,0:T(8,128)(2,1)}, u32[]{:S(2)}, u32[]{:S(2)}) collective-permute-start(bf16[1,64,1024]{2,1,0:T(8,128)(2,1)} %maximum_bitcast_fusion.1), channel_id=1, source_target_pairs={{0,16},{4,20},{8,24},{12,28},{16,0},{20,4},{24,8},{28,12},{1,17},{... | collective-permute-start | bytes 393224 | tf_op jit(solution)/shard_map/ppermute | solution.py:570
  30.5 7.8 %collective-permute-start.8 = (bf16[1,64,1024]{2,1,0:T(8,128)(2,1)}, bf16[1,64,1024]{2,1,0:T(8,128)(2,1)}, u32[]{:S(2)}, u32[]{:S(2)}) collective-permute-start(bf16[1,64,1024]{2,1,0:T(8,128)(2,1)} %maximum_bitcast_fusion.1), channel_id=1, source_target_pairs={{0,24},{4,28},{8,16},{12,20},{16,8},{20,12},{24,0},{28,4},{1,25},{... | collective-permute-start | bytes 393224 | tf_op jit(solution)/shard_map/ppermute | solution.py:570
  30.5 6.7 %collective-permute-start.9 = (bf16[8,72,256]{2,1,0:T(8,128)(2,1)S(1)}, bf16[8,72,256]{2,1,0:T(8,128)(2,1)S(1)}, u32[]{:S(2)}, u32[]{:S(2)}) collective-permute-start(bf16[8,72,256]{2,1,0:T(8,128)(2,1)S(1)} %pad_maximum_fusion.8), channel_id=1, source_target_pairs={{0,2},{1,3},{2,0},{3,1},{4,6},{5,7},{6,4},{7,5},{8,10},{9,11},{10,... | collective-permute-start | bytes 884744 | tf_op jit(solution)/shard_map/ppermute | solution.py:512
  32.5 7.0 %collective-permute-start.12 = (bf16[16,72,256]{2,1,0:T(8,128)(2,1)S(1)}, bf16[16,72,256]{2,1,0:T(8,128)(2,1)S(1)}, u32[]{:S(2)}, u32[]{:S(2)}) collective-permute-start(bf16[16,72,256]{2,1,0:T(8,128)(2,1)S(1)} %pad_maximum_fusion.5), channel_id=1, source_target_pairs={{0,1},{1,0},{2,3},{3,2},{4,5},{5,4},{6,7},{7,6},{8,9},{9,8},{10,11... | collective-permute-start | bytes 1769480 | tf_op jit(solution)/shard_map/ppermute | solution.py:512
  38.2 2.2 collective-permute-start.10
  40.6 17.8 %collective-permute-start.13 = (bf16[4,64,1024]{2,1,0:T(8,128)(2,1)S(1)}, bf16[4,64,1024]{2,1,0:T(8,128)(2,1)S(1)}, u32[]{:S(2)}, u32[]{:S(2)}) collective-permute-start(bf16[4,64,1024]{2,1,0:T(8,128)(2,1)S(1)} %pad_maximum_fusion.6), channel_id=1, source_target_pairs={{0,2},{1,3},{2,0},{3,1},{4,6},{5,7},{6,4},{7,5},{8,10},{9,11},{10,... | collective-permute-start | bytes 1572872 | tf_op jit(solution)/shard_map/ppermute | solution.py:570
  58.3 9.2 %copy-start = (bf16[8,8,256,256]{3,2,1,0:T(8,128)(2,1)}, bf16[8,8,256,256]{3,2,1,0:T(8,128)(2,1)S(1)}, u32[]{:S(2)}) copy-start(bf16[8,8,256,256]{3,2,1,0:T(8,128)(2,1)S(1)} %get-tuple-element.120.pk) | copy-start | bytes 25165828
  58.5 7.3 %copy-start.33 = (s32[8,256]{1,0:T(8,128)S(1)}, s32[8,256]{1,0:T(8,128)}, u32[]{:S(2)}) copy-start(s32[8,256]{1,0:T(8,128)} %param.15) | copy-start | bytes 24580
  58.5 7.3 %copy-start.18 = (bf16[8,256,512]{2,1,0:T(8,128)(2,1)S(1)}, bf16[8,256,512]{2,1,0:T(8,128)(2,1)}, u32[]{:S(2)}) copy-start(bf16[8,256,512]{2,1,0:T(8,128)(2,1)} %param.14) | copy-start | bytes 6291460
  58.5 2.8 %collective-permute-start.14 = (bf16[8,272,256]{2,1,0:T(8,128)(2,1)S(1)}, bf16[8,272,256]{2,1,0:T(8,128)(2,1)S(1)}, u32[]{:S(2)}, u32[]{:S(2)}) collective-permute-start(bf16[8,272,256]{2,1,0:T(8,128)(2,1)S(1)} %get-tuple-element.112), channel_id=1, source_target_pairs={{0,1},{1,0},{2,3},{3,2},{4,5},{5,4},{6,7},{7,6},{8,9},{9,8},{10,11... | collective-permute-start | bytes 3342344 | tf_op jit(solution)/shard_map/ppermute | solution.py:512
  61.6 25.3 %collective-permute-start.16 = (bf16[8,64,1024]{2,1,0:T(8,128)(2,1)S(1)}, bf16[8,64,1024]{2,1,0:T(8,128)(2,1)S(1)}, u32[]{:S(2)}, u32[]{:S(2)}) collective-permute-start(bf16[8,64,1024]{2,1,0:T(8,128)(2,1)S(1)} %pad_maximum_fusion.3), channel_id=1, source_target_pairs={{0,4},{4,0},{8,12},{12,8},{16,20},{20,16},{24,28},{28,24},{1,5},{5... | collective-permute-start | bytes 3145736 | tf_op jit(solution)/shard_map/ppermute | solution.py:570
  63.3 26.2 %collective-permute-start.15 = (bf16[8,272,256]{2,1,0:T(8,128)(2,1)S(1)}, bf16[8,272,256]{2,1,0:T(8,128)(2,1)S(1)}, u32[]{:S(2)}, u32[]{:S(2)}) collective-permute-start(bf16[8,272,256]{2,1,0:T(8,128)(2,1)S(1)} %fusion), channel_id=1, source_target_pairs={{0,2},{1,3},{4,6},{5,7},{8,10},{9,11},{12,14},{13,15},{16,18},{17,... | collective-permute-start | bytes 3342344 | tf_op jit(solution)/shard_map/ppermute | solution.py:528
  87.0 3.1 %copy-start.19 = (bf16[16,64,1024]{2,1,0:T(8,128)(2,1)}, bf16[16,64,1024]{2,1,0:T(8,128)(2,1)S(1)}, u32[]{:S(2)}) copy-start(bf16[16,64,1024]{2,1,0:T(8,128)(2,1)S(1)} %pad_maximum_fusion.own_pair) | copy-start | bytes 6291460
  89.5 14.9 %collective-permute-start.18 = (bf16[16,64,1024]{2,1,0:T(8,128)(2,1)S(1)}, bf16[16,64,1024]{2,1,0:T(8,128)(2,1)S(1)}, u32[]{:S(2)}, u32[]{:S(2)}) collective-permute-start(bf16[16,64,1024]{2,1,0:T(8,128)(2,1)S(1)} %pad_maximum_fusion.own_pair), channel_id=1, source_target_pairs={{0,1},{1,0},{2,3},{3,2},{4,5},{5,4},{6,7},{7,6},{8,9},{9,8},{10,11... | collective-permute-start | bytes 6291464 | tf_op jit(solution)/shard_map/ppermute | solution.py:512
  90.2 5.1 %collective-permute-start.17 = (bf16[8,272,256]{2,1,0:T(8,128)(2,1)S(1)}, bf16[8,272,256]{2,1,0:T(8,128)(2,1)S(1)}, u32[]{:S(2)}, u32[]{:S(2)}) collective-permute-start(bf16[8,272,256]{2,1,0:T(8,128)(2,1)S(1)} %get-tuple-element.206), channel_id=1, source_target_pairs={{0,1},{1,0},{2,3},{3,2},{4,5},{5,4},{6,7},{7,6},{8,9},{9,8},{10,11... | collective-permute-start | bytes 3342344 | tf_op jit(solution)/shard_map/ppermute | solution.py:512
  95.2 9.1 %copy-start.1 = (bf16[8,272,256]{2,1,0:T(8,128)(2,1)}, bf16[8,272,256]{2,1,0:T(8,128)(2,1)S(1)}, u32[]{:S(2)}) copy-start(bf16[8,272,256]{2,1,0:T(8,128)(2,1)S(1)} %collective-permute-done.17.come.come_state) | copy-start | bytes 3342340
  105.7 39.9 %copy-start.8 = (f32[8,8,256]{2,1,0:T(8,128)S(1)}, f32[8,8,256]{2,1,0:T(8,128)}, u32[]{:S(2)}) copy-start(f32[8,8,256]{2,1,0:T(8,128)} %get-tuple-element.137.recip) | copy-start | bytes 196612
  145.4 13.7 %collective-permute-start.19 = (bf16[512,2048]{1,0:T(8,128)(2,1)}, bf16[512,2048]{1,0:T(8,128)(2,1)}, u32[]{:S(2)}, u32[]{:S(2)}) collective-permute-start(bf16[512,2048]{1,0:T(8,128)(2,1)} %get-tuple-element.140), channel_id=1, source_target_pairs={{0,1},{1,0},{2,3},{3,2},{4,5},{5,4},{6,7},{7,6},{8,9},{9,8},{10,11... | collective-permute-start | bytes 6291464 | tf_op jit(solution)/shard_map/ppermute | solution.py:512
  159.1 3.7 %collective-permute-start.21 = (bf16[8,272,256]{2,1,0:T(8,128)(2,1)}, bf16[8,272,256]{2,1,0:T(8,128)(2,1)}, u32[]{:S(2)}, u32[]{:S(2)}) collective-permute-start(bf16[8,272,256]{2,1,0:T(8,128)(2,1)} %get-tuple-element.144), channel_id=1, source_target_pairs={{0,1},{1,0},{2,3},{3,2},{4,5},{5,4},{6,7},{7,6},{8,9},{9,8},{10,11... | collective-permute-start | bytes 3342344 | tf_op jit(solution)/shard_map/ppermute | solution.py:512
  159.6 3.1 %copy-start.4 = (bf16[8,272,256]{2,1,0:T(8,128)(2,1)S(1)}, bf16[8,272,256]{2,1,0:T(8,128)(2,1)}, u32[]{:S(2)}) copy-start(bf16[8,272,256]{2,1,0:T(8,128)(2,1)} %copy-done.3) | copy-start | bytes 3342340
  165.3 28.9 %collective-permute-start.22 = (bf16[8,272,256]{2,1,0:T(8,128)(2,1)}, bf16[8,272,256]{2,1,0:T(8,128)(2,1)}, u32[]{:S(2)}, u32[]{:S(2)}) collective-permute-start(bf16[8,272,256]{2,1,0:T(8,128)(2,1)} %fusion.3), channel_id=1, source_target_pairs={{2,0},{3,1},{6,4},{7,5},{10,8},{11,9},{14,12},{15,13},{18,16},{19,... | collective-permute-start | bytes 3342344 | tf_op jit(solution)/shard_map/ppermute | solution.py:528
  166.6 30.9 %collective-permute-start.20 = (bf16[256,2048]{1,0:T(8,128)(2,1)}, bf16[256,2048]{1,0:T(8,128)(2,1)}, u32[]{:S(2)}, u32[]{:S(2)}) collective-permute-start(bf16[256,2048]{1,0:T(8,128)(2,1)} %fusion.6), channel_id=1, source_target_pairs={{0,4},{4,0},{8,12},{12,8},{16,20},{20,16},{24,28},{28,24},{1,5},{5... | collective-permute-start | bytes 3145736 | tf_op jit(solution)/shard_map/ppermute | solution.py:512
  168.2 1.7 copy-start.7
  170.0 24.3 %copy-start.5 = (bf16[8,272,256]{2,1,0:T(8,128)(2,1)S(1)}, bf16[8,272,256]{2,1,0:T(8,128)(2,1)}, u32[]{:S(2)}) copy-start(bf16[8,272,256]{2,1,0:T(8,128)(2,1)} %copy-done.3) | copy-start | bytes 3342340
  191.2 6.3 %copy-start.11 = (bf16[8,512,256]{2,1,0:T(8,128)(2,1)}, bf16[8,512,256]{2,1,0:T(8,128)(2,1)S(1)}, u32[]{:S(2)}) copy-start(bf16[8,512,256]{2,1,0:T(8,128)(2,1)S(1)} %get-tuple-element.156.key_part) | copy-start | bytes 6291460
  191.2 6.3 %copy-start.13 = (bf16[8,512,256]{2,1,0:T(8,128)(2,1)}, bf16[8,512,256]{2,1,0:T(8,128)(2,1)S(1)}, u32[]{:S(2)}) copy-start(bf16[8,512,256]{2,1,0:T(8,128)(2,1)S(1)} %get-tuple-element.157.value_part) | copy-start | bytes 6291460
  197.5 7.0 %collective-permute-start.23 = (bf16[8,272,256]{2,1,0:T(8,128)(2,1)}, bf16[8,272,256]{2,1,0:T(8,128)(2,1)}, u32[]{:S(2)}, u32[]{:S(2)}) collective-permute-start(bf16[8,272,256]{2,1,0:T(8,128)(2,1)} %get-tuple-element.204), channel_id=1, source_target_pairs={{0,1},{1,0},{2,3},{3,2},{4,5},{5,4},{6,7},{7,6},{8,9},{9,8},{10,11... | collective-permute-start | bytes 3342344 | tf_op jit(solution)/shard_map/ppermute | solution.py:512
  197.5 7.0 %copy-start.10 = (bf16[8,512,256]{2,1,0:T(8,128)(2,1)S(1)}, bf16[8,512,256]{2,1,0:T(8,128)(2,1)}, u32[]{:S(2)}) copy-start(bf16[8,512,256]{2,1,0:T(8,128)(2,1)} %copy-done.9) | copy-start | bytes 6291460
  197.5 7.0 %copy-start.12 = (bf16[8,512,256]{2,1,0:T(8,128)(2,1)S(1)}, bf16[8,512,256]{2,1,0:T(8,128)(2,1)}, u32[]{:S(2)}) copy-start(bf16[8,512,256]{2,1,0:T(8,128)(2,1)} %copy-done.11) | copy-start | bytes 6291460
  197.6 7.0 %copy-start.17 = (f32[2,512]{1,0:T(2,128)S(1)}, f32[2,512]{1,0:T(2,128)}, u32[]{:S(2)}) copy-start(f32[2,512]{1,0:T(2,128)} %get-tuple-element.160.norm_two) | copy-start | bytes 12292
  200.1 27.6 %collective-permute-start.24 = (bf16[64,2048]{1,0:T(8,128)(2,1)S(1)}, bf16[64,2048]{1,0:T(8,128)(2,1)}, u32[]{:S(2)}, u32[]{:S(2)}) collective-permute-start(bf16[64,2048]{1,0:T(8,128)(2,1)S(1)} %get-tuple-element.164), channel_id=1, source_target_pairs={{0,8},{4,12},{8,0},{12,4},{16,24},{20,28},{24,16},{28,20},{1,9},{5... | collective-permute-start | bytes 786440 | tf_op jit(solution)/shard_map/ppermute | solution.py:879
  200.4 27.4 %collective-permute-start.25 = (bf16[64,2048]{1,0:T(8,128)(2,1)S(1)}, bf16[64,2048]{1,0:T(8,128)(2,1)}, u32[]{:S(2)}, u32[]{:S(2)}) collective-permute-start(bf16[64,2048]{1,0:T(8,128)(2,1)S(1)} %get-tuple-element.165), channel_id=1, source_target_pairs={{0,16},{4,20},{8,24},{12,28},{16,0},{20,4},{24,8},{28,12},{1,17},{... | collective-permute-start | bytes 786440 | tf_op jit(solution)/shard_map/ppermute | solution.py:879
  204.2 23.5 %collective-permute-start.26 = (bf16[64,2048]{1,0:T(8,128)(2,1)S(1)}, bf16[64,2048]{1,0:T(8,128)(2,1)S(1)}, u32[]{:S(2)}, u32[]{:S(2)}) collective-permute-start(bf16[64,2048]{1,0:T(8,128)(2,1)S(1)} %get-tuple-element.166), channel_id=1, source_target_pairs={{0,24},{4,28},{8,16},{12,20},{16,8},{20,12},{24,0},{28,4},{1,25},{... | collective-permute-start | bytes 786440 | tf_op jit(solution)/shard_map/ppermute | solution.py:879
  204.5 1.6 copy-start.14
  228.5 3.2 %collective-permute-start.27 = (bf16[2,16,72,256]{3,2,1,0:T(8,128)(2,1)}, bf16[2,16,72,256]{3,2,1,0:T(8,128)(2,1)}, u32[]{:S(2)}, u32[]{:S(2)}) collective-permute-start(bf16[2,16,72,256]{3,2,1,0:T(8,128)(2,1)} %get-tuple-element.167), channel_id=1, source_target_pairs={{0,1},{1,0},{2,3},{3,2},{4,5},{5,4},{6,7},{7,6},{8,9},{9,8},{10,11... | collective-permute-start | bytes 3538952 | tf_op jit(solution)/shard_map/ppermute | solution.py:512
  228.5 4.5 %copy-start.21 = (f32[16,72,256]{2,1,0:T(8,128)S(1)}, f32[16,72,256]{2,1,0:T(8,128)}, u32[]{:S(2)}) copy-start(f32[16,72,256]{2,1,0:T(8,128)} %get-tuple-element.162) | copy-start | bytes 3538948
  228.5 6.8 %copy-start.20 = (f32[16,72,256]{2,1,0:T(8,128)S(1)}, f32[16,72,256]{2,1,0:T(8,128)}, u32[]{:S(2)}) copy-start(f32[16,72,256]{2,1,0:T(8,128)} %get-tuple-element.173) | copy-start | bytes 3538948
  233.1 9.5 %collective-permute-start.28 = (bf16[8,72,256]{2,1,0:T(8,128)(2,1)S(1)}, bf16[8,72,256]{2,1,0:T(8,128)(2,1)}, u32[]{:S(2)}, u32[]{:S(2)}) collective-permute-start(bf16[8,72,256]{2,1,0:T(8,128)(2,1)S(1)} %get-tuple-element.194), channel_id=1, source_target_pairs={{0,2},{1,3},{2,0},{3,1},{4,6},{5,7},{6,4},{7,5},{8,10},{9,11},{10,... | collective-permute-start | bytes 884744 | tf_op jit(solution)/shard_map/ppermute | solution.py:512
  236.1 13.2 %collective-permute-start.32 = (bf16[8,72,256]{2,1,0:T(8,128)(2,1)}, bf16[8,72,256]{2,1,0:T(8,128)(2,1)S(1)}, u32[]{:S(2)}, u32[]{:S(2)}) collective-permute-start(bf16[8,72,256]{2,1,0:T(8,128)(2,1)} %get-tuple-element.196), channel_id=1, source_target_pairs={{0,4},{4,0},{8,12},{12,8},{16,20},{20,16},{24,28},{28,24},{1,5},{5... | collective-permute-start | bytes 884744 | tf_op jit(solution)/shard_map/ppermute | solution.py:512
  244.9 6.3 %copy-start.23 = (f32[512,64]{0,1:T(8,128)S(1)}, f32[512,64]{0,1:T(8,128)}, u32[]{:S(2)}) copy-start(f32[512,64]{0,1:T(8,128)} %param.21) | copy-start | bytes 393220
  244.9 6.3 %copy-start.29 = (f32[512,64]{0,1:T(8,128)S(1)}, f32[512,64]{0,1:T(8,128)}, u32[]{:S(2)}) copy-start(f32[512,64]{0,1:T(8,128)} %param.24) | copy-start | bytes 393220
  245.0 6.3 %copy-start.30 = (f32[512,64]{0,1:T(8,128)S(1)}, f32[512,64]{0,1:T(8,128)}, u32[]{:S(2)}) copy-start(f32[512,64]{0,1:T(8,128)} %param.25) | copy-start | bytes 393220
  245.4 6.7 %copy-start.24 = (f32[64,512]{1,0:T(8,128)S(1)}, f32[64,512]{1,0:T(8,128)}, u32[]{:S(2)}) copy-start(f32[64,512]{1,0:T(8,128)} %param.20) | copy-start | bytes 393220
  245.4 6.7 %copy-start.31 = (f32[64,512]{1,0:T(8,128)S(1)}, f32[64,512]{1,0:T(8,128)}, u32[]{:S(2)}) copy-start(f32[64,512]{1,0:T(8,128)} %param.22) | copy-start | bytes 393220
  245.4 6.7 %copy-start.32 = (f32[64,512]{1,0:T(8,128)S(1)}, f32[64,512]{1,0:T(8,128)}, u32[]{:S(2)}) copy-start(f32[64,512]{1,0:T(8,128)} %param.23) | copy-start | bytes 393220
  245.8 5.4 %collective-permute-start.36 = (bf16[64,1024]{1,0:T(8,128)(2,1)S(1)}, bf16[64,1024]{1,0:T(8,128)(2,1)S(1)}, u32[]{:S(2)}, u32[]{:S(2)}) collective-permute-start(bf16[64,1024]{1,0:T(8,128)(2,1)S(1)} %bitcast.135), channel_id=1, source_target_pairs={{0,2},{1,3},{2,0},{3,1},{4,6},{5,7},{6,4},{7,5},{8,10},{9,11},{10,... | collective-permute-start | bytes 393224 | tf_op jit(solution)/shard_map/ppermute | solution.py:512
  247.6 5.4 %collective-permute-start.29 = (bf16[4,72,256]{2,1,0:T(8,128)(2,1)S(1)}, bf16[4,72,256]{2,1,0:T(8,128)(2,1)S(1)}, u32[]{:S(2)}, u32[]{:S(2)}) collective-permute-start(bf16[4,72,256]{2,1,0:T(8,128)(2,1)S(1)} %get-tuple-element.172), channel_id=1, source_target_pairs={{0,4},{4,0},{8,12},{12,8},{16,20},{20,16},{24,28},{28,24},{1,5},{5... | collective-permute-start | bytes 442376 | tf_op jit(solution)/shard_map/ppermute | solution.py:512
  249.3 10.2 %collective-permute-start.33 = (bf16[4,72,256]{2,1,0:T(8,128)(2,1)S(1)}, bf16[4,72,256]{2,1,0:T(8,128)(2,1)S(1)}, u32[]{:S(2)}, u32[]{:S(2)}) collective-permute-start(bf16[4,72,256]{2,1,0:T(8,128)(2,1)S(1)} %get-tuple-element.210), channel_id=1, source_target_pairs={{0,16},{4,20},{8,24},{12,28},{16,0},{20,4},{24,8},{28,12},{1,17},{... | collective-permute-start | bytes 442376 | tf_op jit(solution)/shard_map/ppermute | solution.py:512
  251.3 16.9 %copy-start.22 = (f32[32832]{0:T(1024)S(1)}, f32[32832]{0:T(1024)}, u32[]{:S(2)}) copy-start(f32[32832]{0:T(1024)} %param.17) | copy-start | bytes 393988
  251.3 16.9 %copy-start.27 = (f32[32832]{0:T(1024)S(1)}, f32[32832]{0:T(1024)}, u32[]{:S(2)}) copy-start(f32[32832]{0:T(1024)} %param.18) | copy-start | bytes 393988
  251.3 16.9 %copy-start.28 = (f32[32832]{0:T(1024)S(1)}, f32[32832]{0:T(1024)}, u32[]{:S(2)}) copy-start(f32[32832]{0:T(1024)} %param.19) | copy-start | bytes 393988
  253.0 8.2 %collective-permute-start.30 = (bf16[2,72,256]{2,1,0:T(8,128)(2,1)S(1)}, bf16[2,72,256]{2,1,0:T(8,128)(2,1)S(1)}, u32[]{:S(2)}, u32[]{:S(2)}) collective-permute-start(bf16[2,72,256]{2,1,0:T(8,128)(2,1)S(1)} %get-tuple-element.216), channel_id=1, source_target_pairs={{0,16},{4,20},{8,24},{12,28},{16,0},{20,4},{24,8},{28,12},{1,17},{... | collective-permute-start | bytes 221192 | tf_op jit(solution)/shard_map/ppermute | solution.py:512
  259.6 4.4 %collective-permute-start.34 = (bf16[2,72,256]{2,1,0:T(8,128)(2,1)S(1)}, bf16[2,72,256]{2,1,0:T(8,128)(2,1)S(1)}, u32[]{:S(2)}, u32[]{:S(2)}) collective-permute-start(bf16[2,72,256]{2,1,0:T(8,128)(2,1)S(1)} %get-tuple-element.218), channel_id=1, source_target_pairs={{0,8},{4,12},{8,0},{12,4},{16,24},{20,28},{24,16},{28,20},{1,9},{5... | collective-permute-start | bytes 221192 | tf_op jit(solution)/shard_map/ppermute | solution.py:512
  261.3 4.3 %collective-permute-start.31 = (bf16[1,72,256]{2,1,0:T(8,128)(2,1)S(1)}, bf16[1,72,256]{2,1,0:T(8,128)(2,1)S(1)}, u32[]{:S(2)}, u32[]{:S(2)}) collective-permute-start(bf16[1,72,256]{2,1,0:T(8,128)(2,1)S(1)} %fusion.23), channel_id=1, source_target_pairs={{0,8},{4,12},{8,0},{12,4},{16,24},{20,28},{24,16},{28,20},{1,9},{5... | collective-permute-start | bytes 110600 | tf_op jit(solution)/shard_map/ppermute | solution.py:512
  264.0 4.0 %collective-permute-start.35 = (bf16[1,72,256]{2,1,0:T(8,128)(2,1)S(1)}, bf16[1,72,256]{2,1,0:T(8,128)(2,1)S(1)}, u32[]{:S(2)}, u32[]{:S(2)}) collective-permute-start(bf16[1,72,256]{2,1,0:T(8,128)(2,1)S(1)} %fusion.20), channel_id=1, source_target_pairs={{0,2},{1,3},{2,0},{3,1},{4,6},{5,7},{6,4},{7,5},{8,10},{9,11},{10,... | collective-permute-start | bytes 110600 | tf_op jit(solution)/shard_map/ppermute | solution.py:512
  (8 other events, 9.6 us)

commit v6 on v5

--- a/solution.py
+++ b/solution.py
@@ -20,7 +20,7 @@
 SPARE = 16
 VMEM_LIMIT = 16 * 1024 * 1024
 BIG = 1 << 20
-LIMITS = {'keys': 14, 'queries': 16, 'mix': 12, 'ffn': 44, 'outer': 14, 'back_query': 18, 'back_key': 26}
+LIMITS = {'keys': 14, 'queries': 16, 'mix': 12, 'ffn': 44, 'outer': 14, 'back_query': 24, 'back_key': 34}
 F32 = jnp.float32
 LOW = jnp.bfloat16
 
@@ -813,7 +813,7 @@
     come_pair = flip(leave, "seq", 0)
 
     args = (grad_middle, out_weight, mixed, recip, pq)
-    outs = [pltpu.VMEM(held, LOW)] + [pltpu.VMEM(state_shape, LOW)] * 2
+    outs = [array(held, LOW)] + [pltpu.VMEM(state_shape, LOW)] * 2
     outs = outs + [array((width, width), F32)]
     outers, own, their, out_proj = call(
         functools.partial(outer_kernel, heads, size),
@@ -838,7 +838,7 @@
     come_near = flip(sent, "dp", 0)
     beside, far, omega_low = send_half(own, their, False, omega_low)
     args = (turned, omega_low, outers, value, pq, pk, score, core, keep, come, uq, uk)
-    outs = [pltpu.VMEM(flat, LOW)] * 3
+    outs = [array(flat, LOW)] * 3
     query_grad, key_part, value_part, query_weight = call(
         functools.partial(back_query_kernel, heads, size),
         seqs,
@@ -848,7 +848,7 @@
         [spec(a) for a in outs] + [fixed((width, width))],
         "back_query",
         1,
-        chip=(2,),
+        chip=(),
         scratch=[
             pltpu.VMEM((heads, ext, count), LOW),
             pltpu.VMEM(score_shape[1:], LOW),
@@ -891,7 +891,7 @@
         [per_seq(tokens.shape), fixed(piece_shape)] + [fixed(piece_shape[1:])] * 2,
         "back_key",
         7 * unit,
-        chip=(11, 12, 13),
+        chip=(),
         scratch=[
             pltpu.VMEM((3 * width, length), LOW),
             pltpu.VMEM((heads, ext, count), LOW),
@@ -905,16 +905,6 @@
     come_pieces = flip(leave, "seq", 0)
     for step, bit in enumerate(high[2:]):
         omega_low, terms = split_rows(terms, "dp", [bit], dp_rows << (len(high) - 3 - step), omega_low)
-    sums = []
-    for index, (stay, order) in enumerate(zip(stays, orders)):
-        part = [stay, come_pieces[index]]
-        for step, (axis, bit) in enumerate(order[1:]):
-            part = [t.reshape((2, t.shape[0] // 2) + t.shape[1:]) for t in part]
-            if index == 0 and step == 1:
-                part, terms = scatter_step(part, axis, bit, terms)
-            else:
-                part, _ = scatter_step(part, axis, bit)
-        sums.append(total_of(part)[0])
     terms = [total_of(terms)]
     for bit in range(axis_bits("seq") - 1, 0, -1):
         terms = [t.reshape(t.shape[0], 2, -1) for t in terms]
@@ -922,6 +912,16 @@
         sent = total_of([lax.dynamic_index_in_dim(t, 1 - side, 1, keepdims=False) for t in terms]).astype(LOW)
         kept = total_of([lax.dynamic_index_in_dim(t, side, 1, keepdims=False) for t in terms])
         terms = [kept, flip(sent, "seq", bit)]
+    sums = []
+    for index, (stay, order) in enumerate(zip(stays, orders)):
+        part = [stay, come_pieces[index]]
+        for step, (axis, bit) in enumerate(order[1:]):
+            part = [t.reshape((2, t.shape[0] // 2) + t.shape[1:]) for t in part]
+            if index == 0 and step == 2:
+                part, terms = scatter_step(part, axis, bit, terms)
+            else:
+                part, _ = scatter_step(part, axis, bit)
+        sums.append(total_of(part)[0])
     own_pair = total_of(terms)
     grad_first = own_pair[:, :group_width]
     grad_second = own_pair[:, group_width:].T

time: 271 us -> 263 us (0.970)
  local copies, waits for them, and re-layouts: 16.6 us -> 6.98 us
    unnamed x73 -> x64, local copies, waits for them, and re-layouts: 13.2 us -> 4.86 us
  transfers between devices with their start and end apart: 37 -> 37, of which waited for: 18 -> 18; matrix products, arithmetic and copies ran while one was open for 9% -> 8% of each run, Pallas kernels for 33% -> 35%
where the time goes in v6:
time: 263 us; the launch traced here: 262 us
  Pallas kernels  130 us (49%)
  waiting for transfers between devices  51.8 us (20%)
  starting transfers between devices  45.4 us (17%)
  other arithmetic  26.1 us (10%)
  local copies, waits for them, and re-layouts  6.98 us (3%)
    pallas_call x7, Pallas kernels, call(): pl.pallas_call(kernel, grid=(steps,), in_specs=in_specs, out_specs=out_sp...  129 us
    ppermute x27, waiting for transfers between devices, flip(): lax.ppermute(value, axis, [(i, i ^ 1 << bit) for i in range(lax.axis_size...  38.2 us
    ppermute x27, starting transfers between devices, flip(): lax.ppermute(value, axis, [(i, i ^ 1 << bit) for i in range(lax.axis_size...  29.1 us
    ppermute x5, starting transfers between devices, gather_more(): lax.ppermute(value, axis, [(i, i ^ jump) for i in range(size)])  8.11 us
    ppermute x2, waiting for transfers between devices, send_half(): come = lax.ppermute(mine, 'seq', pairs)  7.79 us
    ppermute x5, waiting for transfers between devices, gather_more(): lax.ppermute(value, axis, [(i, i ^ jump) for i in range(size)])  5.78 us
  transfers between devices with their start and end apart: 37, of which 18 were waited for; matrix products, arithmetic and copies ran while one was open for 8% of the time, Pallas kernels for 35%

profile of v6, /device:TPU:0, one launch (start us, length us, event | category | flops | bytes accessed | tf_op | source)
XLA Modules:
  0.0 261.9 jit_solution(8497991458129701072)
XLA Ops:
  0.7 0.9 convert_element_type.301
  1.6 0.8 dynamic_update_slice.3
  2.5 3.1 %collective-permute-start.3 = (bf16[1,72,256]{2,1,0:T(8,128)(2,1)S(1)}, bf16[1,72,256]{2,1,0:T(8,128)(2,1)S(1)}, u32[]{:S(2)}, u32[]{:S(2)}) collective-permute-start(bf16[1,72,256]{2,1,0:T(8,128)(2,1)S(1)} %get-tuple-element.232), channel_id=1, source_target_pairs={{0,8},{4,12},{8,0},{12,4},{16,24},{20,28},{24,16},{28,20},{1,9},{5... | collective-permute-start | bytes 110600 | tf_op jit(solution)/shard_map/ppermute | solution.py:512
  5.6 1.5 collective-permute-start
  7.5 2.0 collective-permute-done
  9.8 3.0 %collective-permute-start.4 = (bf16[2,72,256]{2,1,0:T(8,128)(2,1)S(1)}, bf16[2,72,256]{2,1,0:T(8,128)(2,1)S(1)}, u32[]{:S(2)}, u32[]{:S(2)}) collective-permute-start(bf16[2,72,256]{2,1,0:T(8,128)(2,1)S(1)} %pad_maximum_fusion.12), channel_id=1, source_target_pairs={{0,16},{4,20},{8,24},{12,28},{16,0},{20,4},{24,8},{28,12},{1,17},{... | collective-permute-start | bytes 221192 | tf_op jit(solution)/shard_map/ppermute | solution.py:512
  12.8 0.9 convert_bitcast_fusion
  13.7 0.9 convert_element_type.302
  14.6 0.6 collective-permute-done.4
  15.2 1.8 collective-permute-start.5
  17.1 0.7 maximum_bitcast_fusion.1
  17.7 2.7 %collective-permute-start.2 = (bf16[4,72,256]{2,1,0:T(8,128)(2,1)S(1)}, bf16[4,72,256]{2,1,0:T(8,128)(2,1)S(1)}, u32[]{:S(2)}, u32[]{:S(2)}) collective-permute-start(bf16[4,72,256]{2,1,0:T(8,128)(2,1)S(1)} %pad_maximum_fusion.9), channel_id=1, source_target_pairs={{0,16},{4,20},{8,24},{12,28},{16,0},{20,4},{24,8},{28,12},{1,17},{... | collective-permute-start | bytes 442376 | tf_op jit(solution)/shard_map/ppermute | solution.py:512
  20.5 5.0 %collective-permute-done.2 = bf16[4,72,256]{2,1,0:T(8,128)(2,1)S(1)} collective-permute-done((bf16[4,72,256]{2,1,0:T(8,128)(2,1)S(1)}, bf16[4,72,256]{2,1,0:T(8,128)(2,1)S(1)}, u32[]{:S(2)}, u32[]{:S(2)}) %collective-permute-start.2) | collective-permute-done | bytes 147488 | tf_op jit(solution)/shard_map/ppermute | solution.py:512
  25.9 1.2 collective-permute-start.6
  27.1 3.4 %collective-permute-start.7 = (bf16[1,64,1024]{2,1,0:T(8,128)(2,1)}, bf16[1,64,1024]{2,1,0:T(8,128)(2,1)}, u32[]{:S(2)}, u32[]{:S(2)}) collective-permute-start(bf16[1,64,1024]{2,1,0:T(8,128)(2,1)} %maximum_bitcast_fusion.1), channel_id=1, source_target_pairs={{0,16},{4,20},{8,24},{12,28},{16,0},{20,4},{24,8},{28,12},{1,17},{... | collective-permute-start | bytes 393224 | tf_op jit(solution)/shard_map/ppermute | solution.py:570
  30.5 1.8 collective-permute-start.9
  32.6 4.7 %collective-permute-done.9 = bf16[8,72,256]{2,1,0:T(8,128)(2,1)S(1)} collective-permute-done((bf16[8,72,256]{2,1,0:T(8,128)(2,1)S(1)}, bf16[8,72,256]{2,1,0:T(8,128)(2,1)S(1)}, u32[]{:S(2)}, u32[]{:S(2)}) %collective-permute-start.9) | collective-permute-done | bytes 294944 | tf_op jit(solution)/shard_map/ppermute | solution.py:512
  37.3 0.9 pad_maximum_fusion.4
  38.3 1.2 pad_maximum_fusion.6
  39.7 0.7 collective-permute-done.10
  40.6 1.8 collective-permute-start.13
  42.4 0.9 unpack.1
  43.4 15.0 %keys.1 = (bf16[8,512,256]{2,1,0:T(8,128)(2,1)}, bf16[8,512,256]{2,1,0:T(8,128)(2,1)}, bf16[8,8,80,256]{3,2,1,0:T(8,128)(2,1)}, bf16[8,8,256,256]{3,2,1,0:T(8,12...) custom-call(bf16[8,256,512]{2,1,0:T(8,128)(2,1)} %tok.5, ...), custom_call_target="tpu_custom_call" | custom-call | flops 1 | bytes 1 | tf_op jit(solution)/shard_map/keys/pallas_call | solution.py:481
  58.5 2.7 %collective-permute-done.14 = bf16[8,272,256]{2,1,0:T(8,128)(2,1)S(1)} collective-permute-done((bf16[8,272,256]{2,1,0:T(8,128)(2,1)S(1)}, bf16[8,272,256]{2,1,0:T(8,128)(2,1)S(1)}, u32[]{:S(2)}, u32[]{:S(2)}) %collective-permute-start.14) | collective-permute-done | bytes 1114144 | tf_op jit(solution)/shard_map/ppermute | solution.py:512
  61.6 1.7 collective-permute-start.16
  63.2 2.5 collective-permute-start.15
  65.8 1.8 multiply_convert_fusion
  67.6 13.5 %queries.1 = (bf16[8,512,256]{2,1,0:T(8,128)(2,1)}, bf16[8,8,256,256]{3,2,1,0:T(8,128)(2,1)S(1)}, bf16[8,8,256,256]{3,2,1,0:T(8,128)(2,1)}, bf16[8,8,256,256]{3,2,1,0:T(8,128)(2,1)}, f32[8,8,80,256]{3,2,1,0:T(8,128)S(1)}) custom-call(bf16[8,512,256]{2,1,0:T(8,128)(2,1)} %get-tuple-element.112.turned, bf16[1536,512]{1,0:T(8,128)(2,1)S(1)} %get-tuple-element.104.weights, ...), custom_call_target="tpu_custom_call" | custom-call | flops 1 | bytes 1 | tf_op jit(solution)/shard_map/queries/pallas_call | solution.py:481
  81.1 5.8 %collective-permute-done.16 = bf16[8,64,1024]{2,1,0:T(8,128)(2,1)S(1)} collective-permute-done((bf16[8,64,1024]{2,1,0:T(8,128)(2,1)S(1)}, bf16[8,64,1024]{2,1,0:T(8,128)(2,1)S(1)}, u32[]{:S(2)}, u32[]{:S(2)}) %collective-permute-start.16) | collective-permute-done | bytes 1048608 | tf_op jit(solution)/shard_map/ppermute | solution.py:570
  87.0 2.4 collective-permute-done.15
  89.5 0.7 fusion.2
  90.1 0.6 collective-permute-start.17
  90.8 4.4 %collective-permute-done.17.come.come_state = bf16[8,272,256]{2,1,0:T(8,128)(2,1)S(1)} collective-permute-done((bf16[8,272,256]{2,1,0:T(8,128)(2,1)S(1)}, bf16[8,272,256]{2,1,0:T(8,128)(2,1)S(1)}, u32[]{:S(2)}, u32[]{:S(2)}) %collective-permute-start.17) | collective-permute-done | bytes 1114144 | tf_op jit(solution)/shard_map/ppermute | solution.py:512
  95.2 9.1 %mix.1 = (bf16[8,512,256]{2,1,0:T(8,128)(2,1)}, f32[8,8,256]{2,1,0:T(8,128)}, f32[8,256,512]{2,1,0:T(8,128)}, bf16[8,256,512]{2,1,0:T(8,128)(2,1)}) custom-call(bf16[8,256,512]{2,1,0:T(8,128)(2,1)} %tok.5, f32[4,512]{1,0:T(4,128)S(1)} %get-tuple-element.122.norms, bf16[512,512]{1,0:T(8,128)(2,1)S(1)} %get-tuple-element.123.out_weight, ...), custom_call_target="tpu_custom_call" | custom-call | flops 1 | bytes 1 | tf_op jit(solution)/shard_map/mix/pallas_call | solution.py:481
  104.4 1.3 copy-done.29
  105.7 39.6 %ffn.1 = (bf16[2048,512]{1,0:T(8,128)(2,1)}, f32[2048,512]{1,0:T(8,128)}, bf16[512,2048]{1,0:T(8,128)(2,1)}, bf16[512,2048]{1,0:T(8,128)(2,1)}, f32[2,512]{1,0:T(2,128)}) custom-call(bf16[2048,512]{1,0:T(8,128)(2,1)} %bitcast.138, f32[2048,512]{1,0:T(8,128)} %bitcast.137, bf16[2048,512]{1,0:T(8,128)(2,1)} %bitcast.125, ...), custom_call_target="tpu_custom_call" | custom-call | flops 42949672960 | bytes 23080972 | tf_op jit(solution)/shard_map/ffn/pallas_call | solution.py:481
  145.5 11.0 %outer.1 = (bf16[8,8,80,256]{3,2,1,0:T(8,128)(2,1)}, bf16[8,272,256]{2,1,0:T(8,128)(2,1)S(1)}, bf16[8,272,256]{2,1,0:T(8,128)(2,1)}, f32[512,512]{1,0:T(8,128)}) custom-call(f32[8,256,512]{2,1,0:T(8,128)} %bitcast.119, bf16[512,512]{1,0:T(8,128)(2,1)S(1)} %get-tuple-element.123.out_weight, bf16[8,512,256]{2,1,0:T(8,128)(2,1)} %get-tuple-element.134.mixed, ...), custom_call_target="tpu_custom_call" | custom-call | flops 1 | bytes 1 | tf_op jit(solution)/shard_map/outer/pallas_call | solution.py:481
  156.5 1.0 copy-done.3
  158.1 3.0 %fusion.6 = bf16[256,2048]{1,0:T(8,128)(2,1)} fusion(bf16[2,256,2048]{2,1,0:T(8,128)(2,1)} %bitcast.17, s32[]{:T(128)S(6)} %select_n.277, bf16[2,256,2048]{2,1,0:T(8,128)(2,1)} %bitcast.126), kind=kLoop, calls=%fused_computation.21 | loop fusion | flops 2097152 | bytes 3145732 | tf_op jit(solution)/shard_map/convert_element_type | solution.py:836
  161.1 2.6 %fusion.3 = bf16[8,272,256]{2,1,0:T(8,128)(2,1)} fusion(bf16[8,272,256]{2,1,0:T(8,128)(2,1)} %collective-permute-done.21, bf16[8,272,256]{2,1,0:T(8,128)(2,1)S(1)} %copy-done.4), kind=kLoop, calls=%fused_computation.14 | loop fusion | flops 2228224 | bytes 3342336 | tf_op jit(solution)/shard_map/convert_element_type | solution.py:522
  163.8 1.3 collective-permute-start.22
  165.4 1.2 copy-done.2
  166.7 20.7 %back_query.1 = (bf16[8,512,256]{2,1,0:T(8,128)(2,1)}, bf16[8,512,256]{2,1,0:T(8,128)(2,1)}, bf16[8,512,256]{2,1,0:T(8,128)(2,1)}, f32[512,512]{1,0:T(8,128)}) custom-call(bf16[8,512,256]{2,1,0:T(8,128)(2,1)} %get-tuple-element.112.turned, bf16[80,256]{1,0:T(8,128)(2,1)S(1)} %maximum_maximum_fusion.omega_low, ...), custom_call_target="tpu_custom_call" | custom-call | flops 1 | bytes 1 | tf_op jit(solution)/shard_map/back_query/pallas_call | solution.py:481
  187.3 5.4 %collective-permute-done.22 = bf16[8,272,256]{2,1,0:T(8,128)(2,1)} collective-permute-done((bf16[8,272,256]{2,1,0:T(8,128)(2,1)}, bf16[8,272,256]{2,1,0:T(8,128)(2,1)}, u32[]{:S(2)}, u32[]{:S(2)}) %collective-permute-start.22) | collective-permute-done | bytes 1114144 | tf_op jit(solution)/shard_map/ppermute | solution.py:528
  192.7 3.2 %fusion.5 = (bf16[8,272,256]{2,1,0:T(8,128)(2,1)}, bf16[8,272,256]{2,1,0:T(8,128)(2,1)S(1)}) fusion(bf16[8,272,256]{2,1,0:T(8,128)(2,1)S(1)} %copy-done.5, bf16[8,272,256]{2,1,0:T(8,128)(2,1)} %collective-permute-done.22, pred[]{:T(512)S(6)} %eq.31, bf16[8,272,256]{2,1,0:T(8,128)(2,1)} %collective-permute-done.21), kind=kLoop, calls=%fused_computation.16 | loop fusion | flops 5013504 | bytes 5570561 | tf_op jit(solution)/shard_map/convert_element_type | solution.py:536
  195.9 2.5 fusion.7
  198.7 3.8 %collective-permute-start.25 = (bf16[64,2048]{1,0:T(8,128)(2,1)S(1)}, bf16[64,2048]{1,0:T(8,128)(2,1)S(1)}, u32[]{:S(2)}, u32[]{:S(2)}) collective-permute-start(bf16[64,2048]{1,0:T(8,128)(2,1)S(1)} %get-tuple-element.163), channel_id=1, source_target_pairs={{0,16},{4,20},{8,24},{12,28},{16,0},{20,4},{24,8},{28,12},{1,17},{... | collective-permute-start | bytes 786440 | tf_op jit(solution)/shard_map/ppermute | solution.py:879
  202.9 20.3 %back_key.1 = (f32[8,256,512]{2,1,0:T(8,128)}, bf16[2,16,72,256]{3,2,1,0:T(8,128)(2,1)}, f32[16,72,256]{2,1,0:T(8,128)}, f32[16,72,256]{2,1,0:T(8,128)}) custom-call(bf16[8,256,512]{2,1,0:T(8,128)(2,1)} %tok.5, f32[4,512]{1,0:T(4,128)S(1)} %get-tuple-element.122.norms, f32[8,256,512]{2,1,0:T(8,128)} %bitcast.120, ...), custom_call_target="tpu_custom_call" | custom-call | flops 15032385536 | bytes 41472004 | tf_op jit(solution)/shard_map/back_key/pallas_call | solution.py:481
  223.2 0.7 copy-done.20
  223.9 3.1 %collective-permute-done.27 = bf16[2,16,72,256]{3,2,1,0:T(8,128)(2,1)S(1)} collective-permute-done((bf16[2,16,72,256]{3,2,1,0:T(8,128)(2,1)}, bf16[2,16,72,256]{3,2,1,0:T(8,128)(2,1)S(1)}, u32[]{:S(2)}, u32[]{:S(2)}) %collective-permute-start.27) | collective-permute-done | bytes 1179680 | tf_op jit(solution)/shard_map/ppermute | solution.py:512
  229.0 1.8 collective-permute-start.30
  230.8 6.5 %collective-permute-done.28 = bf16[8,72,256]{2,1,0:T(8,128)(2,1)} collective-permute-done((bf16[8,72,256]{2,1,0:T(8,128)(2,1)S(1)}, bf16[8,72,256]{2,1,0:T(8,128)(2,1)}, u32[]{:S(2)}, u32[]{:S(2)}) %collective-permute-start.28) | collective-permute-done | bytes 294944 | tf_op jit(solution)/shard_map/ppermute | solution.py:512
  237.2 1.0 fusion.13
  238.7 1.1 fusion.14
  239.8 4.7 %collective-permute-start.34 = (bf16[4,72,256]{2,1,0:T(8,128)(2,1)S(1)}, bf16[4,72,256]{2,1,0:T(8,128)(2,1)S(1)}, u32[]{:S(2)}, u32[]{:S(2)}) collective-permute-start(bf16[4,72,256]{2,1,0:T(8,128)(2,1)S(1)} %get-tuple-element.206), channel_id=1, source_target_pairs={{0,16},{4,20},{8,24},{12,28},{16,0},{20,4},{24,8},{28,12},{1,17},{... | collective-permute-start | bytes 442376 | tf_op jit(solution)/shard_map/ppermute | solution.py:512
  244.9 3.2 %collective-permute-start.31 = (bf16[2,72,256]{2,1,0:T(8,128)(2,1)S(1)}, bf16[2,72,256]{2,1,0:T(8,128)(2,1)S(1)}, u32[]{:S(2)}, u32[]{:S(2)}) collective-permute-start(bf16[2,72,256]{2,1,0:T(8,128)(2,1)S(1)} %get-tuple-element.170), channel_id=1, source_target_pairs={{0,16},{4,20},{8,24},{12,28},{16,0},{20,4},{24,8},{28,12},{1,17},{... | collective-permute-start | bytes 221192 | tf_op jit(solution)/shard_map/ppermute | solution.py:512
  248.0 4.2 %collective-permute-done.34 = bf16[4,72,256]{2,1,0:T(8,128)(2,1)S(1)} collective-permute-done((bf16[4,72,256]{2,1,0:T(8,128)(2,1)S(1)}, bf16[4,72,256]{2,1,0:T(8,128)(2,1)S(1)}, u32[]{:S(2)}, u32[]{:S(2)}) %collective-permute-start.34) | collective-permute-done | bytes 147488 | tf_op jit(solution)/shard_map/ppermute | solution.py:512
  252.5 0.8 fusion.26
  253.3 0.8 fusion.28
  254.2 2.1 collective-permute-start.32
  256.8 0.7 collective-permute-start.36
  257.4 0.7 collective-permute-done.32
  258.2 2.6 collective-permute-done.36
  260.9 0.9 fusion.30
  (148 shorter events, 8.0 us)
Async XLA Ops:
  2.5 5.0 %collective-permute-start.3 = (bf16[1,72,256]{2,1,0:T(8,128)(2,1)S(1)}, bf16[1,72,256]{2,1,0:T(8,128)(2,1)S(1)}, u32[]{:S(2)}, u32[]{:S(2)}) collective-permute-start(bf16[1,72,256]{2,1,0:T(8,128)(2,1)S(1)} %get-tuple-element.232), channel_id=1, source_target_pairs={{0,8},{4,12},{8,0},{12,4},{16,24},{20,28},{24,16},{28,20},{1,9},{5... | collective-permute-start | bytes 110600 | tf_op jit(solution)/shard_map/ppermute | solution.py:512
  5.6 4.0 %collective-permute-start = (bf16[1,72,256]{2,1,0:T(8,128)(2,1)S(1)}, bf16[1,72,256]{2,1,0:T(8,128)(2,1)S(1)}, u32[]{:S(2)}, u32[]{:S(2)}) collective-permute-start(bf16[1,72,256]{2,1,0:T(8,128)(2,1)S(1)} %get-tuple-element.233), channel_id=1, source_target_pairs={{0,2},{1,3},{2,0},{3,1},{4,6},{5,7},{6,4},{7,5},{8,10},{9,11},{10,... | collective-permute-start | bytes 110600 | tf_op jit(solution)/shard_map/ppermute | solution.py:512
  9.6 5.0 %collective-permute-start.1 = (bf16[2,72,256]{2,1,0:T(8,128)(2,1)S(1)}, bf16[2,72,256]{2,1,0:T(8,128)(2,1)S(1)}, u32[]{:S(2)}, u32[]{:S(2)}) collective-permute-start(bf16[2,72,256]{2,1,0:T(8,128)(2,1)S(1)} %pad_maximum_fusion.11), channel_id=1, source_target_pairs={{0,8},{4,12},{8,0},{12,4},{16,24},{20,28},{24,16},{28,20},{1,9},{5... | collective-permute-start | bytes 221192 | tf_op jit(solution)/shard_map/ppermute | solution.py:512
  9.7 15.9 %copy-start.17 = (f32[64,256]{1,0:T(8,128)S(1)}, f32[64,256]{1,0:T(8,128)}, u32[]{:S(2)}) copy-start(f32[64,256]{1,0:T(8,128)} %param.16) | copy-start | bytes 196612
  9.8 5.4 %collective-permute-start.4 = (bf16[2,72,256]{2,1,0:T(8,128)(2,1)S(1)}, bf16[2,72,256]{2,1,0:T(8,128)(2,1)S(1)}, u32[]{:S(2)}, u32[]{:S(2)}) collective-permute-start(bf16[2,72,256]{2,1,0:T(8,128)(2,1)S(1)} %pad_maximum_fusion.12), channel_id=1, source_target_pairs={{0,16},{4,20},{8,24},{12,28},{16,0},{20,4},{24,8},{28,12},{1,17},{... | collective-permute-start | bytes 221192 | tf_op jit(solution)/shard_map/ppermute | solution.py:512
  15.2 5.2 %collective-permute-start.5 = (bf16[4,72,256]{2,1,0:T(8,128)(2,1)S(1)}, bf16[4,72,256]{2,1,0:T(8,128)(2,1)S(1)}, u32[]{:S(2)}, u32[]{:S(2)}) collective-permute-start(bf16[4,72,256]{2,1,0:T(8,128)(2,1)S(1)} %pad_maximum_fusion.10), channel_id=1, source_target_pairs={{0,4},{4,0},{8,12},{12,8},{16,20},{20,16},{24,28},{28,24},{1,5},{5... | collective-permute-start | bytes 442376 | tf_op jit(solution)/shard_map/ppermute | solution.py:512
  17.7 7.8 %collective-permute-start.2 = (bf16[4,72,256]{2,1,0:T(8,128)(2,1)S(1)}, bf16[4,72,256]{2,1,0:T(8,128)(2,1)S(1)}, u32[]{:S(2)}, u32[]{:S(2)}) collective-permute-start(bf16[4,72,256]{2,1,0:T(8,128)(2,1)S(1)} %pad_maximum_fusion.9), channel_id=1, source_target_pairs={{0,16},{4,20},{8,24},{12,28},{16,0},{20,4},{24,8},{28,12},{1,17},{... | collective-permute-start | bytes 442376 | tf_op jit(solution)/shard_map/ppermute | solution.py:512
  25.6 6.8 %collective-permute-start.11 = (bf16[8,72,256]{2,1,0:T(8,128)(2,1)S(1)}, bf16[8,72,256]{2,1,0:T(8,128)(2,1)S(1)}, u32[]{:S(2)}, u32[]{:S(2)}) collective-permute-start(bf16[8,72,256]{2,1,0:T(8,128)(2,1)S(1)} %pad_maximum_fusion.7), channel_id=1, source_target_pairs={{0,4},{4,0},{8,12},{12,8},{16,20},{20,16},{24,28},{28,24},{1,5},{5... | collective-permute-start | bytes 884744 | tf_op jit(solution)/shard_map/ppermute | solution.py:512
  25.9 12.4 %collective-permute-start.6 = (bf16[1,64,1024]{2,1,0:T(8,128)(2,1)}, bf16[1,64,1024]{2,1,0:T(8,128)(2,1)}, u32[]{:S(2)}, u32[]{:S(2)}) collective-permute-start(bf16[1,64,1024]{2,1,0:T(8,128)(2,1)} %maximum_bitcast_fusion.1), channel_id=1, source_target_pairs={{0,8},{4,12},{8,0},{12,4},{16,24},{20,28},{24,16},{28,20},{1,9},{5... | collective-permute-start | bytes 393224 | tf_op jit(solution)/shard_map/ppermute | solution.py:570
  27.1 11.2 %collective-permute-start.7 = (bf16[1,64,1024]{2,1,0:T(8,128)(2,1)}, bf16[1,64,1024]{2,1,0:T(8,128)(2,1)}, u32[]{:S(2)}, u32[]{:S(2)}) collective-permute-start(bf16[1,64,1024]{2,1,0:T(8,128)(2,1)} %maximum_bitcast_fusion.1), channel_id=1, source_target_pairs={{0,16},{4,20},{8,24},{12,28},{16,0},{20,4},{24,8},{28,12},{1,17},{... | collective-permute-start | bytes 393224 | tf_op jit(solution)/shard_map/ppermute | solution.py:570
  30.5 7.8 %collective-permute-start.8 = (bf16[1,64,1024]{2,1,0:T(8,128)(2,1)}, bf16[1,64,1024]{2,1,0:T(8,128)(2,1)}, u32[]{:S(2)}, u32[]{:S(2)}) collective-permute-start(bf16[1,64,1024]{2,1,0:T(8,128)(2,1)} %maximum_bitcast_fusion.1), channel_id=1, source_target_pairs={{0,24},{4,28},{8,16},{12,20},{16,8},{20,12},{24,0},{28,4},{1,25},{... | collective-permute-start | bytes 393224 | tf_op jit(solution)/shard_map/ppermute | solution.py:570
  30.5 6.7 %collective-permute-start.9 = (bf16[8,72,256]{2,1,0:T(8,128)(2,1)S(1)}, bf16[8,72,256]{2,1,0:T(8,128)(2,1)S(1)}, u32[]{:S(2)}, u32[]{:S(2)}) collective-permute-start(bf16[8,72,256]{2,1,0:T(8,128)(2,1)S(1)} %pad_maximum_fusion.8), channel_id=1, source_target_pairs={{0,2},{1,3},{2,0},{3,1},{4,6},{5,7},{6,4},{7,5},{8,10},{9,11},{10,... | collective-permute-start | bytes 884744 | tf_op jit(solution)/shard_map/ppermute | solution.py:512
  32.5 7.0 %collective-permute-start.12 = (bf16[16,72,256]{2,1,0:T(8,128)(2,1)S(1)}, bf16[16,72,256]{2,1,0:T(8,128)(2,1)S(1)}, u32[]{:S(2)}, u32[]{:S(2)}) collective-permute-start(bf16[16,72,256]{2,1,0:T(8,128)(2,1)S(1)} %pad_maximum_fusion.5), channel_id=1, source_target_pairs={{0,1},{1,0},{2,3},{3,2},{4,5},{5,4},{6,7},{7,6},{8,9},{9,8},{10,11... | collective-permute-start | bytes 1769480 | tf_op jit(solution)/shard_map/ppermute | solution.py:512
  38.2 2.2 collective-permute-start.10
  40.6 17.8 %collective-permute-start.13 = (bf16[4,64,1024]{2,1,0:T(8,128)(2,1)S(1)}, bf16[4,64,1024]{2,1,0:T(8,128)(2,1)S(1)}, u32[]{:S(2)}, u32[]{:S(2)}) collective-permute-start(bf16[4,64,1024]{2,1,0:T(8,128)(2,1)S(1)} %pad_maximum_fusion.6), channel_id=1, source_target_pairs={{0,2},{1,3},{2,0},{3,1},{4,6},{5,7},{6,4},{7,5},{8,10},{9,11},{10,... | collective-permute-start | bytes 1572872 | tf_op jit(solution)/shard_map/ppermute | solution.py:570
  58.3 9.2 %copy-start = (bf16[8,8,256,256]{3,2,1,0:T(8,128)(2,1)}, bf16[8,8,256,256]{3,2,1,0:T(8,128)(2,1)S(1)}, u32[]{:S(2)}) copy-start(bf16[8,8,256,256]{3,2,1,0:T(8,128)(2,1)S(1)} %get-tuple-element.118.pk) | copy-start | bytes 25165828
  58.4 7.3 %copy-start.28 = (s32[8,256]{1,0:T(8,128)S(1)}, s32[8,256]{1,0:T(8,128)}, u32[]{:S(2)}) copy-start(s32[8,256]{1,0:T(8,128)} %param.15) | copy-start | bytes 24580
  58.5 7.3 %copy-start.10 = (bf16[8,256,512]{2,1,0:T(8,128)(2,1)S(1)}, bf16[8,256,512]{2,1,0:T(8,128)(2,1)}, u32[]{:S(2)}) copy-start(bf16[8,256,512]{2,1,0:T(8,128)(2,1)} %param.14) | copy-start | bytes 6291460
  58.5 2.8 %collective-permute-start.14 = (bf16[8,272,256]{2,1,0:T(8,128)(2,1)S(1)}, bf16[8,272,256]{2,1,0:T(8,128)(2,1)S(1)}, u32[]{:S(2)}, u32[]{:S(2)}) collective-permute-start(bf16[8,272,256]{2,1,0:T(8,128)(2,1)S(1)} %get-tuple-element.110), channel_id=1, source_target_pairs={{0,1},{1,0},{2,3},{3,2},{4,5},{5,4},{6,7},{7,6},{8,9},{9,8},{10,11... | collective-permute-start | bytes 3342344 | tf_op jit(solution)/shard_map/ppermute | solution.py:512
  61.6 25.3 %collective-permute-start.16 = (bf16[8,64,1024]{2,1,0:T(8,128)(2,1)S(1)}, bf16[8,64,1024]{2,1,0:T(8,128)(2,1)S(1)}, u32[]{:S(2)}, u32[]{:S(2)}) collective-permute-start(bf16[8,64,1024]{2,1,0:T(8,128)(2,1)S(1)} %pad_maximum_fusion.3), channel_id=1, source_target_pairs={{0,4},{4,0},{8,12},{12,8},{16,20},{20,16},{24,28},{28,24},{1,5},{5... | collective-permute-start | bytes 3145736 | tf_op jit(solution)/shard_map/ppermute | solution.py:570
  63.2 26.2 %collective-permute-start.15 = (bf16[8,272,256]{2,1,0:T(8,128)(2,1)S(1)}, bf16[8,272,256]{2,1,0:T(8,128)(2,1)S(1)}, u32[]{:S(2)}, u32[]{:S(2)}) collective-permute-start(bf16[8,272,256]{2,1,0:T(8,128)(2,1)S(1)} %fusion), channel_id=1, source_target_pairs={{0,2},{1,3},{4,6},{5,7},{8,10},{9,11},{12,14},{13,15},{16,18},{17,... | collective-permute-start | bytes 3342344 | tf_op jit(solution)/shard_map/ppermute | solution.py:528
  87.0 3.1 %copy-start.11 = (bf16[16,64,1024]{2,1,0:T(8,128)(2,1)}, bf16[16,64,1024]{2,1,0:T(8,128)(2,1)S(1)}, u32[]{:S(2)}) copy-start(bf16[16,64,1024]{2,1,0:T(8,128)(2,1)S(1)} %pad_maximum_fusion.own_pair) | copy-start | bytes 6291460
  89.5 14.9 %collective-permute-start.18 = (bf16[16,64,1024]{2,1,0:T(8,128)(2,1)S(1)}, bf16[16,64,1024]{2,1,0:T(8,128)(2,1)S(1)}, u32[]{:S(2)}, u32[]{:S(2)}) collective-permute-start(bf16[16,64,1024]{2,1,0:T(8,128)(2,1)S(1)} %pad_maximum_fusion.own_pair), channel_id=1, source_target_pairs={{0,1},{1,0},{2,3},{3,2},{4,5},{5,4},{6,7},{7,6},{8,9},{9,8},{10,11... | collective-permute-start | bytes 6291464 | tf_op jit(solution)/shard_map/ppermute | solution.py:512
  90.1 5.1 %collective-permute-start.17 = (bf16[8,272,256]{2,1,0:T(8,128)(2,1)S(1)}, bf16[8,272,256]{2,1,0:T(8,128)(2,1)S(1)}, u32[]{:S(2)}, u32[]{:S(2)}) collective-permute-start(bf16[8,272,256]{2,1,0:T(8,128)(2,1)S(1)} %get-tuple-element.202), channel_id=1, source_target_pairs={{0,1},{1,0},{2,3},{3,2},{4,5},{5,4},{6,7},{7,6},{8,9},{9,8},{10,11... | collective-permute-start | bytes 3342344 | tf_op jit(solution)/shard_map/ppermute | solution.py:512
  95.2 9.2 %copy-start.1 = (bf16[8,272,256]{2,1,0:T(8,128)(2,1)}, bf16[8,272,256]{2,1,0:T(8,128)(2,1)S(1)}, u32[]{:S(2)}) copy-start(bf16[8,272,256]{2,1,0:T(8,128)(2,1)S(1)} %collective-permute-done.17.come.come_state) | copy-start | bytes 3342340
  104.4 1.3 copy-start.29
  105.7 39.8 %copy-start.6 = (f32[8,8,256]{2,1,0:T(8,128)S(1)}, f32[8,8,256]{2,1,0:T(8,128)}, u32[]{:S(2)}) copy-start(f32[8,8,256]{2,1,0:T(8,128)} %get-tuple-element.135.recip) | copy-start | bytes 196612
  145.3 12.2 %collective-permute-start.19 = (bf16[512,2048]{1,0:T(8,128)(2,1)}, bf16[512,2048]{1,0:T(8,128)(2,1)}, u32[]{:S(2)}, u32[]{:S(2)}) collective-permute-start(bf16[512,2048]{1,0:T(8,128)(2,1)} %get-tuple-element.138), channel_id=1, source_target_pairs={{0,1},{1,0},{2,3},{3,2},{4,5},{5,4},{6,7},{7,6},{8,9},{9,8},{10,11... | collective-permute-start | bytes 6291464 | tf_op jit(solution)/shard_map/ppermute | solution.py:512
  157.5 3.6 %collective-permute-start.21 = (bf16[8,272,256]{2,1,0:T(8,128)(2,1)}, bf16[8,272,256]{2,1,0:T(8,128)(2,1)}, u32[]{:S(2)}, u32[]{:S(2)}) collective-permute-start(bf16[8,272,256]{2,1,0:T(8,128)(2,1)} %get-tuple-element.142), channel_id=1, source_target_pairs={{0,1},{1,0},{2,3},{3,2},{4,5},{5,4},{6,7},{7,6},{8,9},{9,8},{10,11... | collective-permute-start | bytes 3342344 | tf_op jit(solution)/shard_map/ppermute | solution.py:512
  158.0 3.1 %copy-start.4 = (bf16[8,272,256]{2,1,0:T(8,128)(2,1)S(1)}, bf16[8,272,256]{2,1,0:T(8,128)(2,1)}, u32[]{:S(2)}) copy-start(bf16[8,272,256]{2,1,0:T(8,128)(2,1)} %copy-done.3) | copy-start | bytes 3342340
  163.8 28.9 %collective-permute-start.22 = (bf16[8,272,256]{2,1,0:T(8,128)(2,1)}, bf16[8,272,256]{2,1,0:T(8,128)(2,1)}, u32[]{:S(2)}, u32[]{:S(2)}) collective-permute-start(bf16[8,272,256]{2,1,0:T(8,128)(2,1)} %fusion.3), channel_id=1, source_target_pairs={{2,0},{3,1},{6,4},{7,5},{10,8},{11,9},{14,12},{15,13},{18,16},{19,... | collective-permute-start | bytes 3342344 | tf_op jit(solution)/shard_map/ppermute | solution.py:528
  165.0 30.8 %collective-permute-start.20 = (bf16[256,2048]{1,0:T(8,128)(2,1)}, bf16[256,2048]{1,0:T(8,128)(2,1)}, u32[]{:S(2)}, u32[]{:S(2)}) collective-permute-start(bf16[256,2048]{1,0:T(8,128)(2,1)} %fusion.6), channel_id=1, source_target_pairs={{0,4},{4,0},{8,12},{12,8},{16,20},{20,16},{24,28},{28,24},{1,5},{5... | collective-permute-start | bytes 3145736 | tf_op jit(solution)/shard_map/ppermute | solution.py:512
  165.4 1.2 copy-start.2
  166.7 26.0 %copy-start.5 = (bf16[8,272,256]{2,1,0:T(8,128)(2,1)S(1)}, bf16[8,272,256]{2,1,0:T(8,128)(2,1)}, u32[]{:S(2)}) copy-start(bf16[8,272,256]{2,1,0:T(8,128)(2,1)} %copy-done.3) | copy-start | bytes 3342340
  195.9 7.0 %collective-permute-start.23 = (bf16[8,272,256]{2,1,0:T(8,128)(2,1)}, bf16[8,272,256]{2,1,0:T(8,128)(2,1)}, u32[]{:S(2)}, u32[]{:S(2)}) collective-permute-start(bf16[8,272,256]{2,1,0:T(8,128)(2,1)} %get-tuple-element.200), channel_id=1, source_target_pairs={{0,1},{1,0},{2,3},{3,2},{4,5},{5,4},{6,7},{7,6},{8,9},{9,8},{10,11... | collective-permute-start | bytes 3342344 | tf_op jit(solution)/shard_map/ppermute | solution.py:512
  195.9 7.0 %copy-start.7 = (f32[512,512]{1,0:T(8,128)S(1)}, f32[512,512]{1,0:T(8,128)}, u32[]{:S(2)}) copy-start(f32[512,512]{1,0:T(8,128)} %get-tuple-element.157.out_proj) | copy-start | bytes 3145732
  195.9 7.0 %copy-start.8 = (f32[512,512]{1,0:T(8,128)S(1)}, f32[512,512]{1,0:T(8,128)}, u32[]{:S(2)}) copy-start(f32[512,512]{1,0:T(8,128)} %get-tuple-element.156.query_weight) | copy-start | bytes 3145732
  195.9 7.0 %copy-start.9 = (f32[2,512]{1,0:T(2,128)S(1)}, f32[2,512]{1,0:T(2,128)}, u32[]{:S(2)}) copy-start(f32[2,512]{1,0:T(2,128)} %get-tuple-element.158.norm_two) | copy-start | bytes 12292
  198.4 24.8 %collective-permute-start.24 = (bf16[64,2048]{1,0:T(8,128)(2,1)S(1)}, bf16[64,2048]{1,0:T(8,128)(2,1)S(1)}, u32[]{:S(2)}, u32[]{:S(2)}) collective-permute-start(bf16[64,2048]{1,0:T(8,128)(2,1)S(1)} %get-tuple-element.162), channel_id=1, source_target_pairs={{0,8},{4,12},{8,0},{12,4},{16,24},{20,28},{24,16},{28,20},{1,9},{5... | collective-permute-start | bytes 786440 | tf_op jit(solution)/shard_map/ppermute | solution.py:879
  198.7 24.5 %collective-permute-start.25 = (bf16[64,2048]{1,0:T(8,128)(2,1)S(1)}, bf16[64,2048]{1,0:T(8,128)(2,1)S(1)}, u32[]{:S(2)}, u32[]{:S(2)}) collective-permute-start(bf16[64,2048]{1,0:T(8,128)(2,1)S(1)} %get-tuple-element.163), channel_id=1, source_target_pairs={{0,16},{4,20},{8,24},{12,28},{16,0},{20,4},{24,8},{28,12},{1,17},{... | collective-permute-start | bytes 786440 | tf_op jit(solution)/shard_map/ppermute | solution.py:879
  202.5 20.7 %collective-permute-start.26 = (bf16[64,2048]{1,0:T(8,128)(2,1)S(1)}, bf16[64,2048]{1,0:T(8,128)(2,1)S(1)}, u32[]{:S(2)}, u32[]{:S(2)}) collective-permute-start(bf16[64,2048]{1,0:T(8,128)(2,1)S(1)} %get-tuple-element.164), channel_id=1, source_target_pairs={{0,24},{4,28},{8,16},{12,20},{16,8},{20,12},{24,0},{28,4},{1,25},{... | collective-permute-start | bytes 786440 | tf_op jit(solution)/shard_map/ppermute | solution.py:879
  223.2 3.9 %copy-start.13 = (f32[16,72,256]{2,1,0:T(8,128)S(1)}, f32[16,72,256]{2,1,0:T(8,128)}, u32[]{:S(2)}) copy-start(f32[16,72,256]{2,1,0:T(8,128)} %get-tuple-element.160) | copy-start | bytes 3538948
  223.2 3.9 %copy-start.18 = (bf16[64,2048]{1,0:T(8,128)(2,1)}, bf16[64,2048]{1,0:T(8,128)(2,1)S(1)}, u32[]{:S(2)}) copy-start(bf16[64,2048]{1,0:T(8,128)(2,1)S(1)} %collective-permute-done.25) | copy-start | bytes 786436
  223.9 3.1 %collective-permute-start.27 = (bf16[2,16,72,256]{3,2,1,0:T(8,128)(2,1)}, bf16[2,16,72,256]{3,2,1,0:T(8,128)(2,1)S(1)}, u32[]{:S(2)}, u32[]{:S(2)}) collective-permute-start(bf16[2,16,72,256]{3,2,1,0:T(8,128)(2,1)} %get-tuple-element.165), channel_id=1, source_target_pairs={{0,1},{1,0},{2,3},{3,2},{4,5},{5,4},{6,7},{7,6},{8,9},{9,8},{10,11... | collective-permute-start | bytes 3538952 | tf_op jit(solution)/shard_map/ppermute | solution.py:512
  223.9 3.4 %copy-start.12 = (f32[16,72,256]{2,1,0:T(8,128)S(1)}, f32[16,72,256]{2,1,0:T(8,128)}, u32[]{:S(2)}) copy-start(f32[16,72,256]{2,1,0:T(8,128)} %get-tuple-element.171) | copy-start | bytes 3538948
  227.1 1.0 copy-start.21
  227.2 10.0 %collective-permute-start.28 = (bf16[8,72,256]{2,1,0:T(8,128)(2,1)S(1)}, bf16[8,72,256]{2,1,0:T(8,128)(2,1)}, u32[]{:S(2)}, u32[]{:S(2)}) collective-permute-start(bf16[8,72,256]{2,1,0:T(8,128)(2,1)S(1)} %get-tuple-element.190), channel_id=1, source_target_pairs={{0,2},{1,3},{2,0},{3,1},{4,6},{5,7},{6,4},{7,5},{8,10},{9,11},{10,... | collective-permute-start | bytes 884744 | tf_op jit(solution)/shard_map/ppermute | solution.py:512
  227.4 11.2 %collective-permute-start.33 = (bf16[8,72,256]{2,1,0:T(8,128)(2,1)S(1)}, bf16[8,72,256]{2,1,0:T(8,128)(2,1)}, u32[]{:S(2)}, u32[]{:S(2)}) collective-permute-start(bf16[8,72,256]{2,1,0:T(8,128)(2,1)S(1)} %get-tuple-element.192), channel_id=1, source_target_pairs={{0,4},{4,0},{8,12},{12,8},{16,20},{20,16},{24,28},{28,24},{1,5},{5... | collective-permute-start | bytes 884744 | tf_op jit(solution)/shard_map/ppermute | solution.py:512
  229.0 15.9 %collective-permute-start.30 = (bf16[64,1024]{1,0:T(8,128)(2,1)S(1)}, bf16[64,1024]{1,0:T(8,128)(2,1)S(1)}, u32[]{:S(2)}, u32[]{:S(2)}) collective-permute-start(bf16[64,1024]{1,0:T(8,128)(2,1)S(1)} %bitcast.136), channel_id=1, source_target_pairs={{0,2},{1,3},{2,0},{3,1},{4,6},{5,7},{6,4},{7,5},{8,10},{9,11},{10,... | collective-permute-start | bytes 393224 | tf_op jit(solution)/shard_map/ppermute | solution.py:512
  238.3 6.5 %collective-permute-start.29 = (bf16[4,72,256]{2,1,0:T(8,128)(2,1)S(1)}, bf16[4,72,256]{2,1,0:T(8,128)(2,1)S(1)}, u32[]{:S(2)}, u32[]{:S(2)}) collective-permute-start(bf16[4,72,256]{2,1,0:T(8,128)(2,1)S(1)} %get-tuple-element.204), channel_id=1, source_target_pairs={{0,4},{4,0},{8,12},{12,8},{16,20},{20,16},{24,28},{28,24},{1,5},{5... | collective-permute-start | bytes 442376 | tf_op jit(solution)/shard_map/ppermute | solution.py:512
  238.7 13.8 %copy-start.15 = (f32[512,64]{0,1:T(8,128)S(1)}, f32[512,64]{0,1:T(8,128)}, u32[]{:S(2)}) copy-start(f32[512,64]{0,1:T(8,128)} %param.21) | copy-start | bytes 393220
  238.7 13.8 %copy-start.24 = (f32[512,64]{0,1:T(8,128)S(1)}, f32[512,64]{0,1:T(8,128)}, u32[]{:S(2)}) copy-start(f32[512,64]{0,1:T(8,128)} %param.24) | copy-start | bytes 393220
  238.7 13.8 %copy-start.25 = (f32[512,64]{0,1:T(8,128)S(1)}, f32[512,64]{0,1:T(8,128)}, u32[]{:S(2)}) copy-start(f32[512,64]{0,1:T(8,128)} %param.25) | copy-start | bytes 393220
  239.8 13.5 %copy-start.16 = (f32[64,512]{1,0:T(8,128)S(1)}, f32[64,512]{1,0:T(8,128)}, u32[]{:S(2)}) copy-start(f32[64,512]{1,0:T(8,128)} %param.20) | copy-start | bytes 393220
  239.8 13.5 %copy-start.26 = (f32[64,512]{1,0:T(8,128)S(1)}, f32[64,512]{1,0:T(8,128)}, u32[]{:S(2)}) copy-start(f32[64,512]{1,0:T(8,128)} %param.22) | copy-start | bytes 393220
  239.8 13.5 %copy-start.27 = (f32[64,512]{1,0:T(8,128)S(1)}, f32[64,512]{1,0:T(8,128)}, u32[]{:S(2)}) copy-start(f32[64,512]{1,0:T(8,128)} %param.23) | copy-start | bytes 393220
  239.8 12.5 %collective-permute-start.34 = (bf16[4,72,256]{2,1,0:T(8,128)(2,1)S(1)}, bf16[4,72,256]{2,1,0:T(8,128)(2,1)S(1)}, u32[]{:S(2)}, u32[]{:S(2)}) collective-permute-start(bf16[4,72,256]{2,1,0:T(8,128)(2,1)S(1)} %get-tuple-element.206), channel_id=1, source_target_pairs={{0,16},{4,20},{8,24},{12,28},{16,0},{20,4},{24,8},{28,12},{1,17},{... | collective-permute-start | bytes 442376 | tf_op jit(solution)/shard_map/ppermute | solution.py:512
  244.9 9.3 %collective-permute-start.31 = (bf16[2,72,256]{2,1,0:T(8,128)(2,1)S(1)}, bf16[2,72,256]{2,1,0:T(8,128)(2,1)S(1)}, u32[]{:S(2)}, u32[]{:S(2)}) collective-permute-start(bf16[2,72,256]{2,1,0:T(8,128)(2,1)S(1)} %get-tuple-element.170), channel_id=1, source_target_pairs={{0,16},{4,20},{8,24},{12,28},{16,0},{20,4},{24,8},{28,12},{1,17},{... | collective-permute-start | bytes 221192 | tf_op jit(solution)/shard_map/ppermute | solution.py:512
  252.3 8.6 %copy-start.14 = (f32[32832]{0:T(1024)S(1)}, f32[32832]{0:T(1024)}, u32[]{:S(2)}) copy-start(f32[32832]{0:T(1024)} %param.17) | copy-start | bytes 393988
  252.3 8.6 %copy-start.22 = (f32[32832]{0:T(1024)S(1)}, f32[32832]{0:T(1024)}, u32[]{:S(2)}) copy-start(f32[32832]{0:T(1024)} %param.18) | copy-start | bytes 393988
  252.3 8.6 %copy-start.23 = (f32[32832]{0:T(1024)S(1)}, f32[32832]{0:T(1024)}, u32[]{:S(2)}) copy-start(f32[32832]{0:T(1024)} %param.19) | copy-start | bytes 393988
  252.3 4.4 %collective-permute-start.35 = (bf16[2,72,256]{2,1,0:T(8,128)(2,1)S(1)}, bf16[2,72,256]{2,1,0:T(8,128)(2,1)S(1)}, u32[]{:S(2)}, u32[]{:S(2)}) collective-permute-start(bf16[2,72,256]{2,1,0:T(8,128)(2,1)S(1)} %get-tuple-element.214), channel_id=1, source_target_pairs={{0,8},{4,12},{8,0},{12,4},{16,24},{20,28},{24,16},{28,20},{1,9},{5... | collective-permute-start | bytes 221192 | tf_op jit(solution)/shard_map/ppermute | solution.py:512
  254.2 4.0 %collective-permute-start.32 = (bf16[1,72,256]{2,1,0:T(8,128)(2,1)S(1)}, bf16[1,72,256]{2,1,0:T(8,128)(2,1)S(1)}, u32[]{:S(2)}, u32[]{:S(2)}) collective-permute-start(bf16[1,72,256]{2,1,0:T(8,128)(2,1)S(1)} %fusion.23), channel_id=1, source_target_pairs={{0,8},{4,12},{8,0},{12,4},{16,24},{20,28},{24,16},{28,20},{1,9},{5... | collective-permute-start | bytes 110600 | tf_op jit(solution)/shard_map/ppermute | solution.py:512
  256.8 4.0 %collective-permute-start.36 = (bf16[1,72,256]{2,1,0:T(8,128)(2,1)S(1)}, bf16[1,72,256]{2,1,0:T(8,128)(2,1)S(1)}, u32[]{:S(2)}, u32[]{:S(2)}) collective-permute-start(bf16[1,72,256]{2,1,0:T(8,128)(2,1)S(1)} %fusion.20), channel_id=1, source_target_pairs={{0,2},{1,3},{2,0},{3,1},{4,6},{5,7},{6,4},{7,5},{8,10},{9,11},{10,... | collective-permute-start | bytes 110600 | tf_op jit(solution)/shard_map/ppermute | solution.py:512
  (3 other events, 2.6 us)

commit v7 on v6

--- a/solution.py
+++ b/solution.py
@@ -774,9 +774,9 @@
         chip=(4,),
     )
     far, uq, target, pair = lax.optimization_barrier((far, uq, target, pair))
-    pair, mix_norms = lax.optimization_barrier((pair, norms))
+    keep, come = receive_half(own, beside, far, True)
+    pair, come, mix_norms = lax.optimization_barrier((pair, come, norms))
     pair_beside = flip(pair, "seq", 0)
-    keep, come = receive_half(own, beside, far, True)
     states = [per_seq(keep.shape)] * 2
     outs = [array(flat, LOW), array(recip_shape, F32), array(tokens.shape, F32), array(tokens.shape, LOW)]
     mixed, recip, middle, normed_two = call(
@@ -813,7 +813,7 @@
     come_pair = flip(leave, "seq", 0)
 
     args = (grad_middle, out_weight, mixed, recip, pq)
-    outs = [array(held, LOW)] + [pltpu.VMEM(state_shape, LOW)] * 2
+    outs = [array(held, LOW)] + [array(state_shape, LOW)] * 2
     outs = outs + [array((width, width), F32)]
     outers, own, their, out_proj = call(
         functools.partial(outer_kernel, heads, size),

time: 263 us -> 260 us (0.989)
  no operation moved by 1% of the time
where the time goes in v7:
time: 260 us; the launch traced here: 259 us
  Pallas kernels  130 us (50%)
  waiting for transfers between devices  50.2 us (19%)
  starting transfers between devices  45.1 us (17%)
  other arithmetic  26.1 us (10%)
  local copies, waits for them, and re-layouts  5.99 us (2%)
    pallas_call x7, Pallas kernels, call(): pl.pallas_call(kernel, grid=(steps,), in_specs=in_specs, out_specs=out_sp...  129 us
    ppermute x27, waiting for transfers between devices, flip(): lax.ppermute(value, axis, [(i, i ^ 1 << bit) for i in range(lax.axis_size...  36.5 us
    ppermute x27, starting transfers between devices, flip(): lax.ppermute(value, axis, [(i, i ^ 1 << bit) for i in range(lax.axis_size...  28.8 us
    ppermute x5, starting transfers between devices, gather_more(): lax.ppermute(value, axis, [(i, i ^ jump) for i in range(size)])  8.11 us
    ppermute x2, waiting for transfers between devices, send_half(): come = lax.ppermute(mine, 'seq', pairs)  7.87 us
    ppermute x5, waiting for transfers between devices, gather_more(): lax.ppermute(value, axis, [(i, i ^ jump) for i in range(size)])  5.78 us
  transfers between devices with their start and end apart: 37, of which 18 were waited for; matrix products, arithmetic and copies ran while one was open for 8% of the time, Pallas kernels for 35%

profile of v7, /device:TPU:0, one launch (start us, length us, event | category | flops | bytes accessed | tf_op | source)
XLA Modules:
  0.0 259.3 jit_solution(5178445370649166901)
XLA Ops:
  0.7 0.9 convert_element_type.301
  1.6 0.8 dynamic_update_slice.3
  2.5 3.1 %collective-permute-start.3 = (bf16[1,72,256]{2,1,0:T(8,128)(2,1)S(1)}, bf16[1,72,256]{2,1,0:T(8,128)(2,1)S(1)}, u32[]{:S(2)}, u32[]{:S(2)}) collective-permute-start(bf16[1,72,256]{2,1,0:T(8,128)(2,1)S(1)} %get-tuple-element.234), channel_id=1, source_target_pairs={{0,8},{4,12},{8,0},{12,4},{16,24},{20,28},{24,16},{28,20},{1,9},{5... | collective-permute-start | bytes 110600 | tf_op jit(solution)/shard_map/ppermute | solution.py:512
  5.6 1.5 collective-permute-start
  7.5 2.0 collective-permute-done
  9.8 3.0 %collective-permute-start.4 = (bf16[2,72,256]{2,1,0:T(8,128)(2,1)S(1)}, bf16[2,72,256]{2,1,0:T(8,128)(2,1)S(1)}, u32[]{:S(2)}, u32[]{:S(2)}) collective-permute-start(bf16[2,72,256]{2,1,0:T(8,128)(2,1)S(1)} %pad_maximum_fusion.12), channel_id=1, source_target_pairs={{0,16},{4,20},{8,24},{12,28},{16,0},{20,4},{24,8},{28,12},{1,17},{... | collective-permute-start | bytes 221192 | tf_op jit(solution)/shard_map/ppermute | solution.py:512
  12.8 0.9 convert_bitcast_fusion
  13.7 0.9 convert_element_type.302
  14.6 0.6 collective-permute-done.4
  15.2 1.8 collective-permute-start.5
  17.1 0.7 maximum_bitcast_fusion.1
  17.7 2.7 %collective-permute-start.2 = (bf16[4,72,256]{2,1,0:T(8,128)(2,1)S(1)}, bf16[4,72,256]{2,1,0:T(8,128)(2,1)S(1)}, u32[]{:S(2)}, u32[]{:S(2)}) collective-permute-start(bf16[4,72,256]{2,1,0:T(8,128)(2,1)S(1)} %pad_maximum_fusion.9), channel_id=1, source_target_pairs={{0,16},{4,20},{8,24},{12,28},{16,0},{20,4},{24,8},{28,12},{1,17},{... | collective-permute-start | bytes 442376 | tf_op jit(solution)/shard_map/ppermute | solution.py:512
  20.5 5.0 %collective-permute-done.2 = bf16[4,72,256]{2,1,0:T(8,128)(2,1)S(1)} collective-permute-done((bf16[4,72,256]{2,1,0:T(8,128)(2,1)S(1)}, bf16[4,72,256]{2,1,0:T(8,128)(2,1)S(1)}, u32[]{:S(2)}, u32[]{:S(2)}) %collective-permute-start.2) | collective-permute-done | bytes 147488 | tf_op jit(solution)/shard_map/ppermute | solution.py:512
  25.9 1.2 collective-permute-start.6
  27.1 3.4 %collective-permute-start.7 = (bf16[1,64,1024]{2,1,0:T(8,128)(2,1)}, bf16[1,64,1024]{2,1,0:T(8,128)(2,1)}, u32[]{:S(2)}, u32[]{:S(2)}) collective-permute-start(bf16[1,64,1024]{2,1,0:T(8,128)(2,1)} %maximum_bitcast_fusion.1), channel_id=1, source_target_pairs={{0,16},{4,20},{8,24},{12,28},{16,0},{20,4},{24,8},{28,12},{1,17},{... | collective-permute-start | bytes 393224 | tf_op jit(solution)/shard_map/ppermute | solution.py:570
  30.5 1.8 collective-permute-start.9
  32.6 4.7 %collective-permute-done.9 = bf16[8,72,256]{2,1,0:T(8,128)(2,1)S(1)} collective-permute-done((bf16[8,72,256]{2,1,0:T(8,128)(2,1)S(1)}, bf16[8,72,256]{2,1,0:T(8,128)(2,1)S(1)}, u32[]{:S(2)}, u32[]{:S(2)}) %collective-permute-start.9) | collective-permute-done | bytes 294944 | tf_op jit(solution)/shard_map/ppermute | solution.py:512
  37.3 0.9 pad_maximum_fusion.4
  38.3 1.2 pad_maximum_fusion.6
  39.7 0.7 collective-permute-done.10
  40.6 1.8 collective-permute-start.13
  42.4 0.9 unpack.1
  43.4 15.0 %keys.1 = (bf16[8,512,256]{2,1,0:T(8,128)(2,1)}, bf16[8,512,256]{2,1,0:T(8,128)(2,1)}, bf16[8,8,80,256]{3,2,1,0:T(8,128)(2,1)}, bf16[8,8,256,256]{3,2,1,0:T(8,12...) custom-call(bf16[8,256,512]{2,1,0:T(8,128)(2,1)} %tok.5, ...), custom_call_target="tpu_custom_call" | custom-call | flops 1 | bytes 1 | tf_op jit(solution)/shard_map/keys/pallas_call | solution.py:481
  58.6 2.7 %collective-permute-done.14 = bf16[8,272,256]{2,1,0:T(8,128)(2,1)S(1)} collective-permute-done((bf16[8,272,256]{2,1,0:T(8,128)(2,1)S(1)}, bf16[8,272,256]{2,1,0:T(8,128)(2,1)S(1)}, u32[]{:S(2)}, u32[]{:S(2)}) %collective-permute-start.14) | collective-permute-done | bytes 1114144 | tf_op jit(solution)/shard_map/ppermute | solution.py:512
  61.6 1.7 collective-permute-start.16
  63.3 2.5 collective-permute-start.15
  65.8 1.8 multiply_convert_fusion
  67.6 13.5 %queries.1 = (bf16[8,512,256]{2,1,0:T(8,128)(2,1)}, bf16[8,8,256,256]{3,2,1,0:T(8,128)(2,1)S(1)}, bf16[8,8,256,256]{3,2,1,0:T(8,128)(2,1)}, bf16[8,8,256,256]{3,2,1,0:T(8,128)(2,1)}, f32[8,8,80,256]{3,2,1,0:T(8,128)S(1)}) custom-call(bf16[8,512,256]{2,1,0:T(8,128)(2,1)} %get-tuple-element.113.turned, bf16[1536,512]{1,0:T(8,128)(2,1)S(1)} %get-tuple-element.105.weights, ...), custom_call_target="tpu_custom_call" | custom-call | flops 1 | bytes 1 | tf_op jit(solution)/shard_map/queries/pallas_call | solution.py:481
  81.1 5.8 %collective-permute-done.16 = bf16[8,64,1024]{2,1,0:T(8,128)(2,1)S(1)} collective-permute-done((bf16[8,64,1024]{2,1,0:T(8,128)(2,1)S(1)}, bf16[8,64,1024]{2,1,0:T(8,128)(2,1)S(1)}, u32[]{:S(2)}, u32[]{:S(2)}) %collective-permute-start.16) | collective-permute-done | bytes 1048608 | tf_op jit(solution)/shard_map/ppermute | solution.py:570
  87.0 2.4 collective-permute-done.15
  89.5 0.7 fusion.2
  90.2 2.7 %collective-permute-done.17.come.come_state = bf16[8,272,256]{2,1,0:T(8,128)(2,1)S(1)} collective-permute-done((bf16[8,272,256]{2,1,0:T(8,128)(2,1)S(1)}, bf16[8,272,256]{2,1,0:T(8,128)(2,1)S(1)}, u32[]{:S(2)}, u32[]{:S(2)}) %collective-permute-start.17) | collective-permute-done | bytes 1114144 | tf_op jit(solution)/shard_map/ppermute | solution.py:512
  93.2 9.2 %mix.1 = (bf16[8,512,256]{2,1,0:T(8,128)(2,1)}, f32[8,8,256]{2,1,0:T(8,128)}, f32[8,256,512]{2,1,0:T(8,128)}, bf16[8,256,512]{2,1,0:T(8,128)(2,1)}) custom-call(bf16[8,256,512]{2,1,0:T(8,128)(2,1)} %tok.5, f32[4,512]{1,0:T(4,128)S(1)} %get-tuple-element.124.norms, bf16[512,512]{1,0:T(8,128)(2,1)S(1)} %get-tuple-element.125.out_weight, ...), custom_call_target="tpu_custom_call" | custom-call | flops 1 | bytes 1 | tf_op jit(solution)/shard_map/mix/pallas_call | solution.py:481
  102.4 1.3 copy-done.28
  103.7 39.6 %ffn.1 = (bf16[2048,512]{1,0:T(8,128)(2,1)}, f32[2048,512]{1,0:T(8,128)}, bf16[512,2048]{1,0:T(8,128)(2,1)}, bf16[512,2048]{1,0:T(8,128)(2,1)}, f32[2,512]{1,0:T(2,128)}) custom-call(bf16[2048,512]{1,0:T(8,128)(2,1)} %bitcast.138, f32[2048,512]{1,0:T(8,128)} %bitcast.137, bf16[2048,512]{1,0:T(8,128)(2,1)} %bitcast.125, ...), custom_call_target="tpu_custom_call" | custom-call | flops 42949672960 | bytes 23080972 | tf_op jit(solution)/shard_map/ffn/pallas_call | solution.py:481
  143.5 11.3 %outer.1 = (bf16[8,8,80,256]{3,2,1,0:T(8,128)(2,1)}, bf16[8,272,256]{2,1,0:T(8,128)(2,1)}, bf16[8,272,256]{2,1,0:T(8,128)(2,1)}, f32[512,512]{1,0:T(8,128)}) custom-call(f32[8,256,512]{2,1,0:T(8,128)} %bitcast.119, bf16[512,512]{1,0:T(8,128)(2,1)S(1)} %get-tuple-element.125.out_weight, bf16[8,512,256]{2,1,0:T(8,128)(2,1)} %get-tuple-element.136.mixed, ...), custom_call_target="tpu_custom_call" | custom-call | flops 1 | bytes 1 | tf_op jit(solution)/shard_map/outer/pallas_call | solution.py:481
  155.4 3.0 %fusion.6 = bf16[256,2048]{1,0:T(8,128)(2,1)} fusion(bf16[2,256,2048]{2,1,0:T(8,128)(2,1)} %bitcast.17, s32[]{:T(128)S(6)} %select_n.277, bf16[2,256,2048]{2,1,0:T(8,128)(2,1)} %bitcast.126), kind=kLoop, calls=%fused_computation.21 | loop fusion | flops 2097152 | bytes 3145732 | tf_op jit(solution)/shard_map/convert_element_type | solution.py:836
  158.4 2.6 %fusion.3 = bf16[8,272,256]{2,1,0:T(8,128)(2,1)} fusion(bf16[8,272,256]{2,1,0:T(8,128)(2,1)} %collective-permute-done.21, bf16[8,272,256]{2,1,0:T(8,128)(2,1)S(1)} %copy-done.7), kind=kLoop, calls=%fused_computation.14 | loop fusion | flops 2228224 | bytes 3342336 | tf_op jit(solution)/shard_map/convert_element_type | solution.py:522
  161.1 1.3 collective-permute-start.22
  162.7 1.2 copy-done.2
  164.0 20.7 %back_query.1 = (bf16[8,512,256]{2,1,0:T(8,128)(2,1)}, bf16[8,512,256]{2,1,0:T(8,128)(2,1)}, bf16[8,512,256]{2,1,0:T(8,128)(2,1)}, f32[512,512]{1,0:T(8,128)}) custom-call(bf16[8,512,256]{2,1,0:T(8,128)(2,1)} %get-tuple-element.113.turned, bf16[80,256]{1,0:T(8,128)(2,1)S(1)} %maximum_maximum_fusion.omega_low, ...), custom_call_target="tpu_custom_call" | custom-call | flops 1 | bytes 1 | tf_op jit(solution)/shard_map/back_query/pallas_call | solution.py:481
  184.6 5.4 %collective-permute-done.22 = bf16[8,272,256]{2,1,0:T(8,128)(2,1)} collective-permute-done((bf16[8,272,256]{2,1,0:T(8,128)(2,1)}, bf16[8,272,256]{2,1,0:T(8,128)(2,1)}, u32[]{:S(2)}, u32[]{:S(2)}) %collective-permute-start.22) | collective-permute-done | bytes 1114144 | tf_op jit(solution)/shard_map/ppermute | solution.py:528
  190.1 3.2 %fusion.5 = (bf16[8,272,256]{2,1,0:T(8,128)(2,1)}, bf16[8,272,256]{2,1,0:T(8,128)(2,1)S(1)}) fusion(bf16[8,272,256]{2,1,0:T(8,128)(2,1)S(1)} %copy-done.8, bf16[8,272,256]{2,1,0:T(8,128)(2,1)} %collective-permute-done.22, pred[]{:T(512)S(6)} %eq.31, bf16[8,272,256]{2,1,0:T(8,128)(2,1)} %collective-permute-done.21), kind=kLoop, calls=%fused_computation.16 | loop fusion | flops 5013504 | bytes 5570561 | tf_op jit(solution)/shard_map/convert_element_type | solution.py:536
  193.3 2.5 fusion.7
  196.1 3.8 %collective-permute-start.25 = (bf16[64,2048]{1,0:T(8,128)(2,1)S(1)}, bf16[64,2048]{1,0:T(8,128)(2,1)S(1)}, u32[]{:S(2)}, u32[]{:S(2)}) collective-permute-start(bf16[64,2048]{1,0:T(8,128)(2,1)S(1)} %get-tuple-element.165), channel_id=1, source_target_pairs={{0,16},{4,20},{8,24},{12,28},{16,0},{20,4},{24,8},{28,12},{1,17},{... | collective-permute-start | bytes 786440 | tf_op jit(solution)/shard_map/ppermute | solution.py:879
  200.3 20.3 %back_key.1 = (f32[8,256,512]{2,1,0:T(8,128)}, bf16[2,16,72,256]{3,2,1,0:T(8,128)(2,1)}, f32[16,72,256]{2,1,0:T(8,128)}, f32[16,72,256]{2,1,0:T(8,128)}) custom-call(bf16[8,256,512]{2,1,0:T(8,128)(2,1)} %tok.5, f32[4,512]{1,0:T(4,128)S(1)} %get-tuple-element.124.norms, f32[8,256,512]{2,1,0:T(8,128)} %bitcast.120, ...), custom_call_target="tpu_custom_call" | custom-call | flops 15032385536 | bytes 41472004 | tf_op jit(solution)/shard_map/back_key/pallas_call | solution.py:481
  220.6 0.7 copy-done.19
  221.3 3.1 %collective-permute-done.27 = bf16[2,16,72,256]{3,2,1,0:T(8,128)(2,1)S(1)} collective-permute-done((bf16[2,16,72,256]{3,2,1,0:T(8,128)(2,1)}, bf16[2,16,72,256]{3,2,1,0:T(8,128)(2,1)S(1)}, u32[]{:S(2)}, u32[]{:S(2)}) %collective-permute-start.27) | collective-permute-done | bytes 1179680 | tf_op jit(solution)/shard_map/ppermute | solution.py:512
  225.6 0.4 reshape.243
  226.3 1.8 collective-permute-start.30
  228.1 6.5 %collective-permute-done.28 = bf16[8,72,256]{2,1,0:T(8,128)(2,1)} collective-permute-done((bf16[8,72,256]{2,1,0:T(8,128)(2,1)S(1)}, bf16[8,72,256]{2,1,0:T(8,128)(2,1)}, u32[]{:S(2)}, u32[]{:S(2)}) %collective-permute-start.28) | collective-permute-done | bytes 294944 | tf_op jit(solution)/shard_map/ppermute | solution.py:512
  234.6 1.0 fusion.13
  236.0 1.1 fusion.14
  237.2 4.7 %collective-permute-start.34 = (bf16[4,72,256]{2,1,0:T(8,128)(2,1)S(1)}, bf16[4,72,256]{2,1,0:T(8,128)(2,1)S(1)}, u32[]{:S(2)}, u32[]{:S(2)}) collective-permute-start(bf16[4,72,256]{2,1,0:T(8,128)(2,1)S(1)} %get-tuple-element.208), channel_id=1, source_target_pairs={{0,16},{4,20},{8,24},{12,28},{16,0},{20,4},{24,8},{28,12},{1,17},{... | collective-permute-start | bytes 442376 | tf_op jit(solution)/shard_map/ppermute | solution.py:512
  242.3 3.2 %collective-permute-start.31 = (bf16[2,72,256]{2,1,0:T(8,128)(2,1)S(1)}, bf16[2,72,256]{2,1,0:T(8,128)(2,1)S(1)}, u32[]{:S(2)}, u32[]{:S(2)}) collective-permute-start(bf16[2,72,256]{2,1,0:T(8,128)(2,1)S(1)} %get-tuple-element.172), channel_id=1, source_target_pairs={{0,16},{4,20},{8,24},{12,28},{16,0},{20,4},{24,8},{28,12},{1,17},{... | collective-permute-start | bytes 221192 | tf_op jit(solution)/shard_map/ppermute | solution.py:512
  245.4 4.2 %collective-permute-done.34 = bf16[4,72,256]{2,1,0:T(8,128)(2,1)S(1)} collective-permute-done((bf16[4,72,256]{2,1,0:T(8,128)(2,1)S(1)}, bf16[4,72,256]{2,1,0:T(8,128)(2,1)S(1)}, u32[]{:S(2)}, u32[]{:S(2)}) %collective-permute-start.34) | collective-permute-done | bytes 147488 | tf_op jit(solution)/shard_map/ppermute | solution.py:512
  249.9 0.8 fusion.26
  250.7 0.8 fusion.28
  251.6 2.1 collective-permute-start.32
  253.6 0.5 collective-permute-done.35
  254.2 0.7 collective-permute-start.36
  254.8 0.7 collective-permute-done.32
  255.6 2.6 collective-permute-done.36
  258.3 0.9 fusion.30
  (146 shorter events, 7.3 us)
Async XLA Ops:
  2.5 5.0 %collective-permute-start.3 = (bf16[1,72,256]{2,1,0:T(8,128)(2,1)S(1)}, bf16[1,72,256]{2,1,0:T(8,128)(2,1)S(1)}, u32[]{:S(2)}, u32[]{:S(2)}) collective-permute-start(bf16[1,72,256]{2,1,0:T(8,128)(2,1)S(1)} %get-tuple-element.234), channel_id=1, source_target_pairs={{0,8},{4,12},{8,0},{12,4},{16,24},{20,28},{24,16},{28,20},{1,9},{5... | collective-permute-start | bytes 110600 | tf_op jit(solution)/shard_map/ppermute | solution.py:512
  5.6 4.0 %collective-permute-start = (bf16[1,72,256]{2,1,0:T(8,128)(2,1)S(1)}, bf16[1,72,256]{2,1,0:T(8,128)(2,1)S(1)}, u32[]{:S(2)}, u32[]{:S(2)}) collective-permute-start(bf16[1,72,256]{2,1,0:T(8,128)(2,1)S(1)} %get-tuple-element.235), channel_id=1, source_target_pairs={{0,2},{1,3},{2,0},{3,1},{4,6},{5,7},{6,4},{7,5},{8,10},{9,11},{10,... | collective-permute-start | bytes 110600 | tf_op jit(solution)/shard_map/ppermute | solution.py:512
  9.6 5.0 %collective-permute-start.1 = (bf16[2,72,256]{2,1,0:T(8,128)(2,1)S(1)}, bf16[2,72,256]{2,1,0:T(8,128)(2,1)S(1)}, u32[]{:S(2)}, u32[]{:S(2)}) collective-permute-start(bf16[2,72,256]{2,1,0:T(8,128)(2,1)S(1)} %pad_maximum_fusion.11), channel_id=1, source_target_pairs={{0,8},{4,12},{8,0},{12,4},{16,24},{20,28},{24,16},{28,20},{1,9},{5... | collective-permute-start | bytes 221192 | tf_op jit(solution)/shard_map/ppermute | solution.py:512
  9.7 15.9 %copy-start.16 = (f32[64,256]{1,0:T(8,128)S(1)}, f32[64,256]{1,0:T(8,128)}, u32[]{:S(2)}) copy-start(f32[64,256]{1,0:T(8,128)} %param.16) | copy-start | bytes 196612
  9.8 5.4 %collective-permute-start.4 = (bf16[2,72,256]{2,1,0:T(8,128)(2,1)S(1)}, bf16[2,72,256]{2,1,0:T(8,128)(2,1)S(1)}, u32[]{:S(2)}, u32[]{:S(2)}) collective-permute-start(bf16[2,72,256]{2,1,0:T(8,128)(2,1)S(1)} %pad_maximum_fusion.12), channel_id=1, source_target_pairs={{0,16},{4,20},{8,24},{12,28},{16,0},{20,4},{24,8},{28,12},{1,17},{... | collective-permute-start | bytes 221192 | tf_op jit(solution)/shard_map/ppermute | solution.py:512
  15.2 5.2 %collective-permute-start.5 = (bf16[4,72,256]{2,1,0:T(8,128)(2,1)S(1)}, bf16[4,72,256]{2,1,0:T(8,128)(2,1)S(1)}, u32[]{:S(2)}, u32[]{:S(2)}) collective-permute-start(bf16[4,72,256]{2,1,0:T(8,128)(2,1)S(1)} %pad_maximum_fusion.10), channel_id=1, source_target_pairs={{0,4},{4,0},{8,12},{12,8},{16,20},{20,16},{24,28},{28,24},{1,5},{5... | collective-permute-start | bytes 442376 | tf_op jit(solution)/shard_map/ppermute | solution.py:512
  17.7 7.8 %collective-permute-start.2 = (bf16[4,72,256]{2,1,0:T(8,128)(2,1)S(1)}, bf16[4,72,256]{2,1,0:T(8,128)(2,1)S(1)}, u32[]{:S(2)}, u32[]{:S(2)}) collective-permute-start(bf16[4,72,256]{2,1,0:T(8,128)(2,1)S(1)} %pad_maximum_fusion.9), channel_id=1, source_target_pairs={{0,16},{4,20},{8,24},{12,28},{16,0},{20,4},{24,8},{28,12},{1,17},{... | collective-permute-start | bytes 442376 | tf_op jit(solution)/shard_map/ppermute | solution.py:512
  25.6 6.8 %collective-permute-start.11 = (bf16[8,72,256]{2,1,0:T(8,128)(2,1)S(1)}, bf16[8,72,256]{2,1,0:T(8,128)(2,1)S(1)}, u32[]{:S(2)}, u32[]{:S(2)}) collective-permute-start(bf16[8,72,256]{2,1,0:T(8,128)(2,1)S(1)} %pad_maximum_fusion.7), channel_id=1, source_target_pairs={{0,4},{4,0},{8,12},{12,8},{16,20},{20,16},{24,28},{28,24},{1,5},{5... | collective-permute-start | bytes 884744 | tf_op jit(solution)/shard_map/ppermute | solution.py:512
  25.9 12.4 %collective-permute-start.6 = (bf16[1,64,1024]{2,1,0:T(8,128)(2,1)}, bf16[1,64,1024]{2,1,0:T(8,128)(2,1)}, u32[]{:S(2)}, u32[]{:S(2)}) collective-permute-start(bf16[1,64,1024]{2,1,0:T(8,128)(2,1)} %maximum_bitcast_fusion.1), channel_id=1, source_target_pairs={{0,8},{4,12},{8,0},{12,4},{16,24},{20,28},{24,16},{28,20},{1,9},{5... | collective-permute-start | bytes 393224 | tf_op jit(solution)/shard_map/ppermute | solution.py:570
  27.1 11.2 %collective-permute-start.7 = (bf16[1,64,1024]{2,1,0:T(8,128)(2,1)}, bf16[1,64,1024]{2,1,0:T(8,128)(2,1)}, u32[]{:S(2)}, u32[]{:S(2)}) collective-permute-start(bf16[1,64,1024]{2,1,0:T(8,128)(2,1)} %maximum_bitcast_fusion.1), channel_id=1, source_target_pairs={{0,16},{4,20},{8,24},{12,28},{16,0},{20,4},{24,8},{28,12},{1,17},{... | collective-permute-start | bytes 393224 | tf_op jit(solution)/shard_map/ppermute | solution.py:570
  30.5 7.8 %collective-permute-start.8 = (bf16[1,64,1024]{2,1,0:T(8,128)(2,1)}, bf16[1,64,1024]{2,1,0:T(8,128)(2,1)}, u32[]{:S(2)}, u32[]{:S(2)}) collective-permute-start(bf16[1,64,1024]{2,1,0:T(8,128)(2,1)} %maximum_bitcast_fusion.1), channel_id=1, source_target_pairs={{0,24},{4,28},{8,16},{12,20},{16,8},{20,12},{24,0},{28,4},{1,25},{... | collective-permute-start | bytes 393224 | tf_op jit(solution)/shard_map/ppermute | solution.py:570
  30.5 6.7 %collective-permute-start.9 = (bf16[8,72,256]{2,1,0:T(8,128)(2,1)S(1)}, bf16[8,72,256]{2,1,0:T(8,128)(2,1)S(1)}, u32[]{:S(2)}, u32[]{:S(2)}) collective-permute-start(bf16[8,72,256]{2,1,0:T(8,128)(2,1)S(1)} %pad_maximum_fusion.8), channel_id=1, source_target_pairs={{0,2},{1,3},{2,0},{3,1},{4,6},{5,7},{6,4},{7,5},{8,10},{9,11},{10,... | collective-permute-start | bytes 884744 | tf_op jit(solution)/shard_map/ppermute | solution.py:512
  32.5 7.0 %collective-permute-start.12 = (bf16[16,72,256]{2,1,0:T(8,128)(2,1)S(1)}, bf16[16,72,256]{2,1,0:T(8,128)(2,1)S(1)}, u32[]{:S(2)}, u32[]{:S(2)}) collective-permute-start(bf16[16,72,256]{2,1,0:T(8,128)(2,1)S(1)} %pad_maximum_fusion.5), channel_id=1, source_target_pairs={{0,1},{1,0},{2,3},{3,2},{4,5},{5,4},{6,7},{7,6},{8,9},{9,8},{10,11... | collective-permute-start | bytes 1769480 | tf_op jit(solution)/shard_map/ppermute | solution.py:512
  38.2 2.2 collective-permute-start.10
  40.6 17.8 %collective-permute-start.13 = (bf16[4,64,1024]{2,1,0:T(8,128)(2,1)S(1)}, bf16[4,64,1024]{2,1,0:T(8,128)(2,1)S(1)}, u32[]{:S(2)}, u32[]{:S(2)}) collective-permute-start(bf16[4,64,1024]{2,1,0:T(8,128)(2,1)S(1)} %pad_maximum_fusion.6), channel_id=1, source_target_pairs={{0,2},{1,3},{2,0},{3,1},{4,6},{5,7},{6,4},{7,5},{8,10},{9,11},{10,... | collective-permute-start | bytes 1572872 | tf_op jit(solution)/shard_map/ppermute | solution.py:570
  58.3 9.2 %copy-start = (bf16[8,8,256,256]{3,2,1,0:T(8,128)(2,1)}, bf16[8,8,256,256]{3,2,1,0:T(8,128)(2,1)S(1)}, u32[]{:S(2)}) copy-start(bf16[8,8,256,256]{3,2,1,0:T(8,128)(2,1)S(1)} %get-tuple-element.119.pk) | copy-start | bytes 25165828
  58.5 7.3 %copy-start.27 = (s32[8,256]{1,0:T(8,128)S(1)}, s32[8,256]{1,0:T(8,128)}, u32[]{:S(2)}) copy-start(s32[8,256]{1,0:T(8,128)} %param.15) | copy-start | bytes 24580
  58.5 7.3 %copy-start.9 = (bf16[8,256,512]{2,1,0:T(8,128)(2,1)S(1)}, bf16[8,256,512]{2,1,0:T(8,128)(2,1)}, u32[]{:S(2)}) copy-start(bf16[8,256,512]{2,1,0:T(8,128)(2,1)} %param.14) | copy-start | bytes 6291460
  58.5 2.8 %collective-permute-start.14 = (bf16[8,272,256]{2,1,0:T(8,128)(2,1)S(1)}, bf16[8,272,256]{2,1,0:T(8,128)(2,1)S(1)}, u32[]{:S(2)}, u32[]{:S(2)}) collective-permute-start(bf16[8,272,256]{2,1,0:T(8,128)(2,1)S(1)} %get-tuple-element.111), channel_id=1, source_target_pairs={{0,1},{1,0},{2,3},{3,2},{4,5},{5,4},{6,7},{7,6},{8,9},{9,8},{10,11... | collective-permute-start | bytes 3342344 | tf_op jit(solution)/shard_map/ppermute | solution.py:512
  61.6 25.3 %collective-permute-start.16 = (bf16[8,64,1024]{2,1,0:T(8,128)(2,1)S(1)}, bf16[8,64,1024]{2,1,0:T(8,128)(2,1)S(1)}, u32[]{:S(2)}, u32[]{:S(2)}) collective-permute-start(bf16[8,64,1024]{2,1,0:T(8,128)(2,1)S(1)} %pad_maximum_fusion.3), channel_id=1, source_target_pairs={{0,4},{4,0},{8,12},{12,8},{16,20},{20,16},{24,28},{28,24},{1,5},{5... | collective-permute-start | bytes 3145736 | tf_op jit(solution)/shard_map/ppermute | solution.py:570
  63.3 26.2 %collective-permute-start.15 = (bf16[8,272,256]{2,1,0:T(8,128)(2,1)S(1)}, bf16[8,272,256]{2,1,0:T(8,128)(2,1)S(1)}, u32[]{:S(2)}, u32[]{:S(2)}) collective-permute-start(bf16[8,272,256]{2,1,0:T(8,128)(2,1)S(1)} %fusion), channel_id=1, source_target_pairs={{0,2},{1,3},{4,6},{5,7},{8,10},{9,11},{12,14},{13,15},{16,18},{17,... | collective-permute-start | bytes 3342344 | tf_op jit(solution)/shard_map/ppermute | solution.py:528
  87.0 5.9 %copy-start.10 = (bf16[16,64,1024]{2,1,0:T(8,128)(2,1)}, bf16[16,64,1024]{2,1,0:T(8,128)(2,1)S(1)}, u32[]{:S(2)}) copy-start(bf16[16,64,1024]{2,1,0:T(8,128)(2,1)S(1)} %pad_maximum_fusion.own_pair) | copy-start | bytes 6291460
  90.1 2.8 %collective-permute-start.17 = (bf16[8,272,256]{2,1,0:T(8,128)(2,1)S(1)}, bf16[8,272,256]{2,1,0:T(8,128)(2,1)S(1)}, u32[]{:S(2)}, u32[]{:S(2)}) collective-permute-start(bf16[8,272,256]{2,1,0:T(8,128)(2,1)S(1)} %get-tuple-element.205), channel_id=1, source_target_pairs={{0,1},{1,0},{2,3},{3,2},{4,5},{5,4},{6,7},{7,6},{8,9},{9,8},{10,11... | collective-permute-start | bytes 3342344 | tf_op jit(solution)/shard_map/ppermute | solution.py:512
  93.0 9.4 %copy-start.1 = (bf16[8,272,256]{2,1,0:T(8,128)(2,1)}, bf16[8,272,256]{2,1,0:T(8,128)(2,1)S(1)}, u32[]{:S(2)}) copy-start(bf16[8,272,256]{2,1,0:T(8,128)(2,1)S(1)} %collective-permute-done.17.come.come_state) | copy-start | bytes 3342340
  93.0 9.4 %collective-permute-start.18 = (bf16[16,64,1024]{2,1,0:T(8,128)(2,1)S(1)}, bf16[16,64,1024]{2,1,0:T(8,128)(2,1)S(1)}, u32[]{:S(2)}, u32[]{:S(2)}) collective-permute-start(bf16[16,64,1024]{2,1,0:T(8,128)(2,1)S(1)} %pad_maximum_fusion.own_pair), channel_id=1, source_target_pairs={{0,1},{1,0},{2,3},{3,2},{4,5},{5,4},{6,7},{7,6},{8,9},{9,8},{10,11... | collective-permute-start | bytes 6291464 | tf_op jit(solution)/shard_map/ppermute | solution.py:512
  102.4 1.3 copy-start.28
  103.7 39.9 %copy-start.3 = (f32[8,8,256]{2,1,0:T(8,128)S(1)}, f32[8,8,256]{2,1,0:T(8,128)}, u32[]{:S(2)}) copy-start(f32[8,8,256]{2,1,0:T(8,128)} %get-tuple-element.137.recip) | copy-start | bytes 196612
  143.3 11.6 %collective-permute-start.19 = (bf16[512,2048]{1,0:T(8,128)(2,1)}, bf16[512,2048]{1,0:T(8,128)(2,1)}, u32[]{:S(2)}, u32[]{:S(2)}) collective-permute-start(bf16[512,2048]{1,0:T(8,128)(2,1)} %get-tuple-element.140), channel_id=1, source_target_pairs={{0,1},{1,0},{2,3},{3,2},{4,5},{5,4},{6,7},{7,6},{8,9},{9,8},{10,11... | collective-permute-start | bytes 6291464 | tf_op jit(solution)/shard_map/ppermute | solution.py:512
  154.8 3.6 %collective-permute-start.21 = (bf16[8,272,256]{2,1,0:T(8,128)(2,1)}, bf16[8,272,256]{2,1,0:T(8,128)(2,1)}, u32[]{:S(2)}, u32[]{:S(2)}) collective-permute-start(bf16[8,272,256]{2,1,0:T(8,128)(2,1)} %get-tuple-element.144), channel_id=1, source_target_pairs={{0,1},{1,0},{2,3},{3,2},{4,5},{5,4},{6,7},{7,6},{8,9},{9,8},{10,11... | collective-permute-start | bytes 3342344 | tf_op jit(solution)/shard_map/ppermute | solution.py:512
  155.3 3.1 %copy-start.7 = (bf16[8,272,256]{2,1,0:T(8,128)(2,1)S(1)}, bf16[8,272,256]{2,1,0:T(8,128)(2,1)}, u32[]{:S(2)}) copy-start(bf16[8,272,256]{2,1,0:T(8,128)(2,1)} %get-tuple-element.143) | copy-start | bytes 3342340
  161.1 29.0 %collective-permute-start.22 = (bf16[8,272,256]{2,1,0:T(8,128)(2,1)}, bf16[8,272,256]{2,1,0:T(8,128)(2,1)}, u32[]{:S(2)}, u32[]{:S(2)}) collective-permute-start(bf16[8,272,256]{2,1,0:T(8,128)(2,1)} %fusion.3), channel_id=1, source_target_pairs={{2,0},{3,1},{6,4},{7,5},{10,8},{11,9},{14,12},{15,13},{18,16},{19,... | collective-permute-start | bytes 3342344 | tf_op jit(solution)/shard_map/ppermute | solution.py:528
  162.4 30.9 %collective-permute-start.20 = (bf16[256,2048]{1,0:T(8,128)(2,1)}, bf16[256,2048]{1,0:T(8,128)(2,1)}, u32[]{:S(2)}, u32[]{:S(2)}) collective-permute-start(bf16[256,2048]{1,0:T(8,128)(2,1)} %fusion.6), channel_id=1, source_target_pairs={{0,4},{4,0},{8,12},{12,8},{16,20},{20,16},{24,28},{28,24},{1,5},{5... | collective-permute-start | bytes 3145736 | tf_op jit(solution)/shard_map/ppermute | solution.py:512
  162.7 1.2 copy-start.2
  164.0 26.1 %copy-start.8 = (bf16[8,272,256]{2,1,0:T(8,128)(2,1)S(1)}, bf16[8,272,256]{2,1,0:T(8,128)(2,1)}, u32[]{:S(2)}) copy-start(bf16[8,272,256]{2,1,0:T(8,128)(2,1)} %get-tuple-element.143) | copy-start | bytes 3342340
  193.3 7.0 %collective-permute-start.23 = (bf16[8,272,256]{2,1,0:T(8,128)(2,1)}, bf16[8,272,256]{2,1,0:T(8,128)(2,1)}, u32[]{:S(2)}, u32[]{:S(2)}) collective-permute-start(bf16[8,272,256]{2,1,0:T(8,128)(2,1)} %get-tuple-element.202), channel_id=1, source_target_pairs={{0,1},{1,0},{2,3},{3,2},{4,5},{5,4},{6,7},{7,6},{8,9},{9,8},{10,11... | collective-permute-start | bytes 3342344 | tf_op jit(solution)/shard_map/ppermute | solution.py:512
  193.3 7.0 %copy-start.4 = (f32[512,512]{1,0:T(8,128)S(1)}, f32[512,512]{1,0:T(8,128)}, u32[]{:S(2)}) copy-start(f32[512,512]{1,0:T(8,128)} %get-tuple-element.159.out_proj) | copy-start | bytes 3145732
  193.3 7.0 %copy-start.5 = (f32[512,512]{1,0:T(8,128)S(1)}, f32[512,512]{1,0:T(8,128)}, u32[]{:S(2)}) copy-start(f32[512,512]{1,0:T(8,128)} %get-tuple-element.158.query_weight) | copy-start | bytes 3145732
  193.3 7.0 %copy-start.6 = (f32[2,512]{1,0:T(2,128)S(1)}, f32[2,512]{1,0:T(2,128)}, u32[]{:S(2)}) copy-start(f32[2,512]{1,0:T(2,128)} %get-tuple-element.160.norm_two) | copy-start | bytes 12292
  195.8 24.7 %collective-permute-start.24 = (bf16[64,2048]{1,0:T(8,128)(2,1)S(1)}, bf16[64,2048]{1,0:T(8,128)(2,1)S(1)}, u32[]{:S(2)}, u32[]{:S(2)}) collective-permute-start(bf16[64,2048]{1,0:T(8,128)(2,1)S(1)} %get-tuple-element.164), channel_id=1, source_target_pairs={{0,8},{4,12},{8,0},{12,4},{16,24},{20,28},{24,16},{28,20},{1,9},{5... | collective-permute-start | bytes 786440 | tf_op jit(solution)/shard_map/ppermute | solution.py:879
  196.1 24.5 %collective-permute-start.25 = (bf16[64,2048]{1,0:T(8,128)(2,1)S(1)}, bf16[64,2048]{1,0:T(8,128)(2,1)S(1)}, u32[]{:S(2)}, u32[]{:S(2)}) collective-permute-start(bf16[64,2048]{1,0:T(8,128)(2,1)S(1)} %get-tuple-element.165), channel_id=1, source_target_pairs={{0,16},{4,20},{8,24},{12,28},{16,0},{20,4},{24,8},{28,12},{1,17},{... | collective-permute-start | bytes 786440 | tf_op jit(solution)/shard_map/ppermute | solution.py:879
  199.9 20.7 %collective-permute-start.26 = (bf16[64,2048]{1,0:T(8,128)(2,1)S(1)}, bf16[64,2048]{1,0:T(8,128)(2,1)S(1)}, u32[]{:S(2)}, u32[]{:S(2)}) collective-permute-start(bf16[64,2048]{1,0:T(8,128)(2,1)S(1)} %get-tuple-element.166), channel_id=1, source_target_pairs={{0,24},{4,28},{8,16},{12,20},{16,8},{20,12},{24,0},{28,4},{1,25},{... | collective-permute-start | bytes 786440 | tf_op jit(solution)/shard_map/ppermute | solution.py:879
  220.5 3.9 %copy-start.12 = (f32[16,72,256]{2,1,0:T(8,128)S(1)}, f32[16,72,256]{2,1,0:T(8,128)}, u32[]{:S(2)}) copy-start(f32[16,72,256]{2,1,0:T(8,128)} %get-tuple-element.162) | copy-start | bytes 3538948
  220.6 3.9 %copy-start.17 = (bf16[64,2048]{1,0:T(8,128)(2,1)}, bf16[64,2048]{1,0:T(8,128)(2,1)S(1)}, u32[]{:S(2)}) copy-start(bf16[64,2048]{1,0:T(8,128)(2,1)S(1)} %collective-permute-done.25) | copy-start | bytes 786436
  221.3 3.1 %collective-permute-start.27 = (bf16[2,16,72,256]{3,2,1,0:T(8,128)(2,1)}, bf16[2,16,72,256]{3,2,1,0:T(8,128)(2,1)S(1)}, u32[]{:S(2)}, u32[]{:S(2)}) collective-permute-start(bf16[2,16,72,256]{3,2,1,0:T(8,128)(2,1)} %get-tuple-element.167), channel_id=1, source_target_pairs={{0,1},{1,0},{2,3},{3,2},{4,5},{5,4},{6,7},{7,6},{8,9},{9,8},{10,11... | collective-permute-start | bytes 3538952 | tf_op jit(solution)/shard_map/ppermute | solution.py:512
  221.3 3.4 %copy-start.11 = (f32[16,72,256]{2,1,0:T(8,128)S(1)}, f32[16,72,256]{2,1,0:T(8,128)}, u32[]{:S(2)}) copy-start(f32[16,72,256]{2,1,0:T(8,128)} %get-tuple-element.173) | copy-start | bytes 3538948
  224.4 1.0 copy-start.20
  224.6 10.0 %collective-permute-start.28 = (bf16[8,72,256]{2,1,0:T(8,128)(2,1)S(1)}, bf16[8,72,256]{2,1,0:T(8,128)(2,1)}, u32[]{:S(2)}, u32[]{:S(2)}) collective-permute-start(bf16[8,72,256]{2,1,0:T(8,128)(2,1)S(1)} %get-tuple-element.192), channel_id=1, source_target_pairs={{0,2},{1,3},{2,0},{3,1},{4,6},{5,7},{6,4},{7,5},{8,10},{9,11},{10,... | collective-permute-start | bytes 884744 | tf_op jit(solution)/shard_map/ppermute | solution.py:512
  224.8 11.2 %collective-permute-start.33 = (bf16[8,72,256]{2,1,0:T(8,128)(2,1)S(1)}, bf16[8,72,256]{2,1,0:T(8,128)(2,1)}, u32[]{:S(2)}, u32[]{:S(2)}) collective-permute-start(bf16[8,72,256]{2,1,0:T(8,128)(2,1)S(1)} %get-tuple-element.194), channel_id=1, source_target_pairs={{0,4},{4,0},{8,12},{12,8},{16,20},{20,16},{24,28},{28,24},{1,5},{5... | collective-permute-start | bytes 884744 | tf_op jit(solution)/shard_map/ppermute | solution.py:512
  226.3 15.9 %collective-permute-start.30 = (bf16[64,1024]{1,0:T(8,128)(2,1)S(1)}, bf16[64,1024]{1,0:T(8,128)(2,1)S(1)}, u32[]{:S(2)}, u32[]{:S(2)}) collective-permute-start(bf16[64,1024]{1,0:T(8,128)(2,1)S(1)} %bitcast.136), channel_id=1, source_target_pairs={{0,2},{1,3},{2,0},{3,1},{4,6},{5,7},{6,4},{7,5},{8,10},{9,11},{10,... | collective-permute-start | bytes 393224 | tf_op jit(solution)/shard_map/ppermute | solution.py:512
  235.7 6.5 %collective-permute-start.29 = (bf16[4,72,256]{2,1,0:T(8,128)(2,1)S(1)}, bf16[4,72,256]{2,1,0:T(8,128)(2,1)S(1)}, u32[]{:S(2)}, u32[]{:S(2)}) collective-permute-start(bf16[4,72,256]{2,1,0:T(8,128)(2,1)S(1)} %get-tuple-element.206), channel_id=1, source_target_pairs={{0,4},{4,0},{8,12},{12,8},{16,20},{20,16},{24,28},{28,24},{1,5},{5... | collective-permute-start | bytes 442376 | tf_op jit(solution)/shard_map/ppermute | solution.py:512
  236.0 13.8 %copy-start.14 = (f32[512,64]{0,1:T(8,128)S(1)}, f32[512,64]{0,1:T(8,128)}, u32[]{:S(2)}) copy-start(f32[512,64]{0,1:T(8,128)} %param.21) | copy-start | bytes 393220
  236.0 13.8 %copy-start.23 = (f32[512,64]{0,1:T(8,128)S(1)}, f32[512,64]{0,1:T(8,128)}, u32[]{:S(2)}) copy-start(f32[512,64]{0,1:T(8,128)} %param.24) | copy-start | bytes 393220
  236.0 13.8 %copy-start.24 = (f32[512,64]{0,1:T(8,128)S(1)}, f32[512,64]{0,1:T(8,128)}, u32[]{:S(2)}) copy-start(f32[512,64]{0,1:T(8,128)} %param.25) | copy-start | bytes 393220
  237.1 13.6 %copy-start.15 = (f32[64,512]{1,0:T(8,128)S(1)}, f32[64,512]{1,0:T(8,128)}, u32[]{:S(2)}) copy-start(f32[64,512]{1,0:T(8,128)} %param.20) | copy-start | bytes 393220
  237.2 13.6 %copy-start.25 = (f32[64,512]{1,0:T(8,128)S(1)}, f32[64,512]{1,0:T(8,128)}, u32[]{:S(2)}) copy-start(f32[64,512]{1,0:T(8,128)} %param.22) | copy-start | bytes 393220
  237.2 13.5 %copy-start.26 = (f32[64,512]{1,0:T(8,128)S(1)}, f32[64,512]{1,0:T(8,128)}, u32[]{:S(2)}) copy-start(f32[64,512]{1,0:T(8,128)} %param.23) | copy-start | bytes 393220
  237.2 12.5 %collective-permute-start.34 = (bf16[4,72,256]{2,1,0:T(8,128)(2,1)S(1)}, bf16[4,72,256]{2,1,0:T(8,128)(2,1)S(1)}, u32[]{:S(2)}, u32[]{:S(2)}) collective-permute-start(bf16[4,72,256]{2,1,0:T(8,128)(2,1)S(1)} %get-tuple-element.208), channel_id=1, source_target_pairs={{0,16},{4,20},{8,24},{12,28},{16,0},{20,4},{24,8},{28,12},{1,17},{... | collective-permute-start | bytes 442376 | tf_op jit(solution)/shard_map/ppermute | solution.py:512
  242.3 9.3 %collective-permute-start.31 = (bf16[2,72,256]{2,1,0:T(8,128)(2,1)S(1)}, bf16[2,72,256]{2,1,0:T(8,128)(2,1)S(1)}, u32[]{:S(2)}, u32[]{:S(2)}) collective-permute-start(bf16[2,72,256]{2,1,0:T(8,128)(2,1)S(1)} %get-tuple-element.172), channel_id=1, source_target_pairs={{0,16},{4,20},{8,24},{12,28},{16,0},{20,4},{24,8},{28,12},{1,17},{... | collective-permute-start | bytes 221192 | tf_op jit(solution)/shard_map/ppermute | solution.py:512
  249.7 8.6 %copy-start.13 = (f32[32832]{0:T(1024)S(1)}, f32[32832]{0:T(1024)}, u32[]{:S(2)}) copy-start(f32[32832]{0:T(1024)} %param.17) | copy-start | bytes 393988
  249.7 8.6 %copy-start.21 = (f32[32832]{0:T(1024)S(1)}, f32[32832]{0:T(1024)}, u32[]{:S(2)}) copy-start(f32[32832]{0:T(1024)} %param.18) | copy-start | bytes 393988
  249.7 8.6 %copy-start.22 = (f32[32832]{0:T(1024)S(1)}, f32[32832]{0:T(1024)}, u32[]{:S(2)}) copy-start(f32[32832]{0:T(1024)} %param.19) | copy-start | bytes 393988
  249.7 4.4 %collective-permute-start.35 = (bf16[2,72,256]{2,1,0:T(8,128)(2,1)S(1)}, bf16[2,72,256]{2,1,0:T(8,128)(2,1)S(1)}, u32[]{:S(2)}, u32[]{:S(2)}) collective-permute-start(bf16[2,72,256]{2,1,0:T(8,128)(2,1)S(1)} %get-tuple-element.216), channel_id=1, source_target_pairs={{0,8},{4,12},{8,0},{12,4},{16,24},{20,28},{24,16},{28,20},{1,9},{5... | collective-permute-start | bytes 221192 | tf_op jit(solution)/shard_map/ppermute | solution.py:512
  251.6 4.0 %collective-permute-start.32 = (bf16[1,72,256]{2,1,0:T(8,128)(2,1)S(1)}, bf16[1,72,256]{2,1,0:T(8,128)(2,1)S(1)}, u32[]{:S(2)}, u32[]{:S(2)}) collective-permute-start(bf16[1,72,256]{2,1,0:T(8,128)(2,1)S(1)} %fusion.23), channel_id=1, source_target_pairs={{0,8},{4,12},{8,0},{12,4},{16,24},{20,28},{24,16},{28,20},{1,9},{5... | collective-permute-start | bytes 110600 | tf_op jit(solution)/shard_map/ppermute | solution.py:512
  254.2 4.0 %collective-permute-start.36 = (bf16[1,72,256]{2,1,0:T(8,128)(2,1)S(1)}, bf16[1,72,256]{2,1,0:T(8,128)(2,1)S(1)}, u32[]{:S(2)}, u32[]{:S(2)}) collective-permute-start(bf16[1,72,256]{2,1,0:T(8,128)(2,1)S(1)} %fusion.20), channel_id=1, source_target_pairs={{0,2},{1,3},{2,0},{3,1},{4,6},{5,7},{6,4},{7,5},{8,10},{9,11},{10,... | collective-permute-start | bytes 110600 | tf_op jit(solution)/shard_map/ppermute | solution.py:512
  (2 other events, 1.7 us)

commit v8 on v7

--- a/solution.py
+++ b/solution.py
@@ -20,7 +20,7 @@
 SPARE = 16
 VMEM_LIMIT = 16 * 1024 * 1024
 BIG = 1 << 20
-LIMITS = {'keys': 14, 'queries': 16, 'mix': 12, 'ffn': 44, 'outer': 14, 'back_query': 24, 'back_key': 34}
+LIMITS = {'keys': 14, 'queries': 16, 'mix': 12, 'ffn': 40, 'outer': 14, 'back_query': 24, 'back_key': 34}
 F32 = jnp.float32
 LOW = jnp.bfloat16
 
@@ -804,7 +804,7 @@
         [by_block, by_block, fixed(first_shape), fixed(first_shape), fixed((2, width))],
         "ffn",
         20 * unit,
-        chip=(),
+        chip=(4, 5),
         scratch=[pltpu.VMEM((groups, width, group_width), F32)] * 2
         + [pltpu.VMEM((groups, lax.axis_size("dp"), width // lax.axis_size("dp"), 2 * group_width), LOW)],
     )

time: 260 us -> 257 us (0.988)
  no operation moved by 1% of the time
where the time goes in v8:
time: 257 us; the launch traced here: 256 us
  Pallas kernels  129 us (50%)
  waiting for transfers between devices  50.2 us (20%)
  starting transfers between devices  45.1 us (18%)
  other arithmetic  26.2 us (10%)
  local copies, waits for them, and re-layouts  4.69 us (2%)
    pallas_call x7, Pallas kernels, call(): pl.pallas_call(kernel, grid=(steps,), in_specs=in_specs, out_specs=out_sp...  128 us
    ppermute x27, waiting for transfers between devices, flip(): lax.ppermute(value, axis, [(i, i ^ 1 << bit) for i in range(lax.axis_size...  36.5 us
    ppermute x27, starting transfers between devices, flip(): lax.ppermute(value, axis, [(i, i ^ 1 << bit) for i in range(lax.axis_size...  28.8 us
    ppermute x5, starting transfers between devices, gather_more(): lax.ppermute(value, axis, [(i, i ^ jump) for i in range(size)])  8.11 us
    ppermute x2, waiting for transfers between devices, send_half(): come = lax.ppermute(mine, 'seq', pairs)  7.89 us
    ppermute x5, waiting for transfers between devices, gather_more(): lax.ppermute(value, axis, [(i, i ^ jump) for i in range(size)])  5.8 us
  transfers between devices with their start and end apart: 37, of which 18 were waited for; matrix products, arithmetic and copies ran while one was open for 8% of the time, Pallas kernels for 35%

profile of v8, /device:TPU:0, one launch (start us, length us, event | category | flops | bytes accessed | tf_op | source)
XLA Modules:
  0.0 256.4 jit_solution(8085550786201444629)
XLA Ops:
  0.7 0.9 convert_element_type.301
  1.6 0.8 dynamic_update_slice.3
  2.5 3.1 %collective-permute-start.3 = (bf16[1,72,256]{2,1,0:T(8,128)(2,1)S(1)}, bf16[1,72,256]{2,1,0:T(8,128)(2,1)S(1)}, u32[]{:S(2)}, u32[]{:S(2)}) collective-permute-start(bf16[1,72,256]{2,1,0:T(8,128)(2,1)S(1)} %get-tuple-element.234), channel_id=1, source_target_pairs={{0,8},{4,12},{8,0},{12,4},{16,24},{20,28},{24,16},{28,20},{1,9},{5... | collective-permute-start | bytes 110600 | tf_op jit(solution)/shard_map/ppermute | solution.py:512
  5.6 1.5 collective-permute-start
  7.1 0.4 collective-permute-done.3
  7.5 2.0 collective-permute-done
  9.8 3.0 %collective-permute-start.4 = (bf16[2,72,256]{2,1,0:T(8,128)(2,1)S(1)}, bf16[2,72,256]{2,1,0:T(8,128)(2,1)S(1)}, u32[]{:S(2)}, u32[]{:S(2)}) collective-permute-start(bf16[2,72,256]{2,1,0:T(8,128)(2,1)S(1)} %pad_maximum_fusion.12), channel_id=1, source_target_pairs={{0,16},{4,20},{8,24},{12,28},{16,0},{20,4},{24,8},{28,12},{1,17},{... | collective-permute-start | bytes 221192 | tf_op jit(solution)/shard_map/ppermute | solution.py:512
  12.8 0.9 convert_bitcast_fusion
  13.7 0.9 convert_element_type.302
  14.6 0.6 collective-permute-done.4
  15.2 1.8 collective-permute-start.5
  17.1 0.7 maximum_bitcast_fusion.1
  17.7 2.7 %collective-permute-start.2 = (bf16[4,72,256]{2,1,0:T(8,128)(2,1)S(1)}, bf16[4,72,256]{2,1,0:T(8,128)(2,1)S(1)}, u32[]{:S(2)}, u32[]{:S(2)}) collective-permute-start(bf16[4,72,256]{2,1,0:T(8,128)(2,1)S(1)} %pad_maximum_fusion.9), channel_id=1, source_target_pairs={{0,16},{4,20},{8,24},{12,28},{16,0},{20,4},{24,8},{28,12},{1,17},{... | collective-permute-start | bytes 442376 | tf_op jit(solution)/shard_map/ppermute | solution.py:512
  20.5 5.0 %collective-permute-done.2 = bf16[4,72,256]{2,1,0:T(8,128)(2,1)S(1)} collective-permute-done((bf16[4,72,256]{2,1,0:T(8,128)(2,1)S(1)}, bf16[4,72,256]{2,1,0:T(8,128)(2,1)S(1)}, u32[]{:S(2)}, u32[]{:S(2)}) %collective-permute-start.2) | collective-permute-done | bytes 147488 | tf_op jit(solution)/shard_map/ppermute | solution.py:512
  25.9 1.2 collective-permute-start.6
  27.1 3.4 %collective-permute-start.7 = (bf16[1,64,1024]{2,1,0:T(8,128)(2,1)}, bf16[1,64,1024]{2,1,0:T(8,128)(2,1)}, u32[]{:S(2)}, u32[]{:S(2)}) collective-permute-start(bf16[1,64,1024]{2,1,0:T(8,128)(2,1)} %maximum_bitcast_fusion.1), channel_id=1, source_target_pairs={{0,16},{4,20},{8,24},{12,28},{16,0},{20,4},{24,8},{28,12},{1,17},{... | collective-permute-start | bytes 393224 | tf_op jit(solution)/shard_map/ppermute | solution.py:570
  30.5 1.8 collective-permute-start.9
  32.6 4.7 %collective-permute-done.9 = bf16[8,72,256]{2,1,0:T(8,128)(2,1)S(1)} collective-permute-done((bf16[8,72,256]{2,1,0:T(8,128)(2,1)S(1)}, bf16[8,72,256]{2,1,0:T(8,128)(2,1)S(1)}, u32[]{:S(2)}, u32[]{:S(2)}) %collective-permute-start.9) | collective-permute-done | bytes 294944 | tf_op jit(solution)/shard_map/ppermute | solution.py:512
  37.3 0.9 pad_maximum_fusion.4
  38.3 1.2 pad_maximum_fusion.6
  39.7 0.7 collective-permute-done.10
  40.6 1.8 collective-permute-start.13
  42.4 0.9 unpack.1
  43.4 15.0 %keys.1 = (bf16[8,512,256]{2,1,0:T(8,128)(2,1)}, bf16[8,512,256]{2,1,0:T(8,128)(2,1)}, bf16[8,8,80,256]{3,2,1,0:T(8,128)(2,1)}, bf16[8,8,256,256]{3,2,1,0:T(8,12...) custom-call(bf16[8,256,512]{2,1,0:T(8,128)(2,1)} %tok.5, ...), custom_call_target="tpu_custom_call" | custom-call | flops 1 | bytes 1 | tf_op jit(solution)/shard_map/keys/pallas_call | solution.py:481
  58.6 2.7 %collective-permute-done.14 = bf16[8,272,256]{2,1,0:T(8,128)(2,1)S(1)} collective-permute-done((bf16[8,272,256]{2,1,0:T(8,128)(2,1)S(1)}, bf16[8,272,256]{2,1,0:T(8,128)(2,1)S(1)}, u32[]{:S(2)}, u32[]{:S(2)}) %collective-permute-start.14) | collective-permute-done | bytes 1114144 | tf_op jit(solution)/shard_map/ppermute | solution.py:512
  61.6 1.7 collective-permute-start.16
  63.3 2.5 collective-permute-start.15
  65.8 1.8 multiply_convert_fusion
  67.6 13.5 %queries.1 = (bf16[8,512,256]{2,1,0:T(8,128)(2,1)}, bf16[8,8,256,256]{3,2,1,0:T(8,128)(2,1)S(1)}, bf16[8,8,256,256]{3,2,1,0:T(8,128)(2,1)}, bf16[8,8,256,256]{3,2,1,0:T(8,128)(2,1)}, f32[8,8,80,256]{3,2,1,0:T(8,128)S(1)}) custom-call(bf16[8,512,256]{2,1,0:T(8,128)(2,1)} %get-tuple-element.113.turned, bf16[1536,512]{1,0:T(8,128)(2,1)S(1)} %get-tuple-element.105.weights, ...), custom_call_target="tpu_custom_call" | custom-call | flops 1 | bytes 1 | tf_op jit(solution)/shard_map/queries/pallas_call | solution.py:481
  81.1 5.8 %collective-permute-done.16 = bf16[8,64,1024]{2,1,0:T(8,128)(2,1)S(1)} collective-permute-done((bf16[8,64,1024]{2,1,0:T(8,128)(2,1)S(1)}, bf16[8,64,1024]{2,1,0:T(8,128)(2,1)S(1)}, u32[]{:S(2)}, u32[]{:S(2)}) %collective-permute-start.16) | collective-permute-done | bytes 1048608 | tf_op jit(solution)/shard_map/ppermute | solution.py:570
  87.1 2.4 collective-permute-done.15
  89.5 0.7 fusion.2
  90.3 2.7 %collective-permute-done.17.come.come_state = bf16[8,272,256]{2,1,0:T(8,128)(2,1)S(1)} collective-permute-done((bf16[8,272,256]{2,1,0:T(8,128)(2,1)S(1)}, bf16[8,272,256]{2,1,0:T(8,128)(2,1)S(1)}, u32[]{:S(2)}, u32[]{:S(2)}) %collective-permute-start.17) | collective-permute-done | bytes 1114144 | tf_op jit(solution)/shard_map/ppermute | solution.py:512
  93.2 9.2 %mix.1 = (bf16[8,512,256]{2,1,0:T(8,128)(2,1)}, f32[8,8,256]{2,1,0:T(8,128)}, f32[8,256,512]{2,1,0:T(8,128)}, bf16[8,256,512]{2,1,0:T(8,128)(2,1)}) custom-call(bf16[8,256,512]{2,1,0:T(8,128)(2,1)} %tok.5, f32[4,512]{1,0:T(4,128)S(1)} %get-tuple-element.124.norms, bf16[512,512]{1,0:T(8,128)(2,1)S(1)} %get-tuple-element.125.out_weight, ...), custom_call_target="tpu_custom_call" | custom-call | flops 1 | bytes 1 | tf_op jit(solution)/shard_map/mix/pallas_call | solution.py:481
  102.5 37.9 %ffn.1 = (bf16[2048,512]{1,0:T(8,128)(2,1)}, f32[2048,512]{1,0:T(8,128)}, bf16[512,2048]{1,0:T(8,128)(2,1)}, bf16[512,2048]{1,0:T(8,128)(2,1)}, f32[2,512]{1,0:T(2,128)}) custom-call(bf16[2048,512]{1,0:T(8,128)(2,1)} %bitcast.138, f32[2048,512]{1,0:T(8,128)} %bitcast.137, bf16[2048,512]{1,0:T(8,128)(2,1)} %bitcast.125, ...), custom_call_target="tpu_custom_call" | custom-call | flops 42949672960 | bytes 23080972 | tf_op jit(solution)/shard_map/ffn/pallas_call | solution.py:481
  140.7 11.3 %outer.1 = (bf16[8,8,80,256]{3,2,1,0:T(8,128)(2,1)}, bf16[8,272,256]{2,1,0:T(8,128)(2,1)}, bf16[8,272,256]{2,1,0:T(8,128)(2,1)}, f32[512,512]{1,0:T(8,128)}) custom-call(f32[8,256,512]{2,1,0:T(8,128)} %bitcast.119, bf16[512,512]{1,0:T(8,128)(2,1)S(1)} %get-tuple-element.125.out_weight, bf16[8,512,256]{2,1,0:T(8,128)(2,1)} %get-tuple-element.136.mixed, ...), custom_call_target="tpu_custom_call" | custom-call | flops 1 | bytes 1 | tf_op jit(solution)/shard_map/outer/pallas_call | solution.py:481
  152.6 3.0 %fusion.6 = bf16[256,2048]{1,0:T(8,128)(2,1)} fusion(bf16[2,256,2048]{2,1,0:T(8,128)(2,1)} %bitcast.17, s32[]{:T(128)S(6)} %select_n.277, bf16[2,256,2048]{2,1,0:T(8,128)(2,1)} %bitcast.126), kind=kLoop, calls=%fused_computation.21 | loop fusion | flops 2097152 | bytes 3145732 | tf_op jit(solution)/shard_map/convert_element_type | solution.py:836
  155.6 2.6 %fusion.3 = bf16[8,272,256]{2,1,0:T(8,128)(2,1)} fusion(bf16[8,272,256]{2,1,0:T(8,128)(2,1)} %collective-permute-done.21, bf16[8,272,256]{2,1,0:T(8,128)(2,1)S(1)} %copy-done.7), kind=kLoop, calls=%fused_computation.14 | loop fusion | flops 2228224 | bytes 3342336 | tf_op jit(solution)/shard_map/convert_element_type | solution.py:522
  158.2 1.3 collective-permute-start.22
  159.8 1.2 copy-done.2
  161.1 20.7 %back_query.1 = (bf16[8,512,256]{2,1,0:T(8,128)(2,1)}, bf16[8,512,256]{2,1,0:T(8,128)(2,1)}, bf16[8,512,256]{2,1,0:T(8,128)(2,1)}, f32[512,512]{1,0:T(8,128)}) custom-call(bf16[8,512,256]{2,1,0:T(8,128)(2,1)} %get-tuple-element.113.turned, bf16[80,256]{1,0:T(8,128)(2,1)S(1)} %maximum_maximum_fusion.omega_low, ...), custom_call_target="tpu_custom_call" | custom-call | flops 1 | bytes 1 | tf_op jit(solution)/shard_map/back_query/pallas_call | solution.py:481
  181.7 5.4 %collective-permute-done.22 = bf16[8,272,256]{2,1,0:T(8,128)(2,1)} collective-permute-done((bf16[8,272,256]{2,1,0:T(8,128)(2,1)}, bf16[8,272,256]{2,1,0:T(8,128)(2,1)}, u32[]{:S(2)}, u32[]{:S(2)}) %collective-permute-start.22) | collective-permute-done | bytes 1114144 | tf_op jit(solution)/shard_map/ppermute | solution.py:528
  187.2 3.2 %fusion.5 = (bf16[8,272,256]{2,1,0:T(8,128)(2,1)}, bf16[8,272,256]{2,1,0:T(8,128)(2,1)S(1)}) fusion(bf16[8,272,256]{2,1,0:T(8,128)(2,1)S(1)} %copy-done.8, bf16[8,272,256]{2,1,0:T(8,128)(2,1)} %collective-permute-done.22, pred[]{:T(512)S(6)} %eq.31, bf16[8,272,256]{2,1,0:T(8,128)(2,1)} %collective-permute-done.21), kind=kLoop, calls=%fused_computation.16 | loop fusion | flops 5013504 | bytes 5570561 | tf_op jit(solution)/shard_map/convert_element_type | solution.py:536
  190.4 2.5 fusion.7
  193.2 3.8 %collective-permute-start.25 = (bf16[64,2048]{1,0:T(8,128)(2,1)S(1)}, bf16[64,2048]{1,0:T(8,128)(2,1)S(1)}, u32[]{:S(2)}, u32[]{:S(2)}) collective-permute-start(bf16[64,2048]{1,0:T(8,128)(2,1)S(1)} %get-tuple-element.165), channel_id=1, source_target_pairs={{0,16},{4,20},{8,24},{12,28},{16,0},{20,4},{24,8},{28,12},{1,17},{... | collective-permute-start | bytes 786440 | tf_op jit(solution)/shard_map/ppermute | solution.py:879
  197.4 20.2 %back_key.1 = (f32[8,256,512]{2,1,0:T(8,128)}, bf16[2,16,72,256]{3,2,1,0:T(8,128)(2,1)}, f32[16,72,256]{2,1,0:T(8,128)}, f32[16,72,256]{2,1,0:T(8,128)}) custom-call(bf16[8,256,512]{2,1,0:T(8,128)(2,1)} %tok.5, f32[4,512]{1,0:T(4,128)S(1)} %get-tuple-element.124.norms, f32[8,256,512]{2,1,0:T(8,128)} %bitcast.120, ...), custom_call_target="tpu_custom_call" | custom-call | flops 15032385536 | bytes 41472004 | tf_op jit(solution)/shard_map/back_key/pallas_call | solution.py:481
  217.7 0.7 copy-done.18
  218.4 3.1 %collective-permute-done.27 = bf16[2,16,72,256]{3,2,1,0:T(8,128)(2,1)S(1)} collective-permute-done((bf16[2,16,72,256]{3,2,1,0:T(8,128)(2,1)}, bf16[2,16,72,256]{3,2,1,0:T(8,128)(2,1)S(1)}, u32[]{:S(2)}, u32[]{:S(2)}) %collective-permute-start.27) | collective-permute-done | bytes 1179680 | tf_op jit(solution)/shard_map/ppermute | solution.py:512
  222.7 0.4 reshape.243
  223.4 1.8 collective-permute-start.30
  225.2 6.5 %collective-permute-done.28 = bf16[8,72,256]{2,1,0:T(8,128)(2,1)} collective-permute-done((bf16[8,72,256]{2,1,0:T(8,128)(2,1)S(1)}, bf16[8,72,256]{2,1,0:T(8,128)(2,1)}, u32[]{:S(2)}, u32[]{:S(2)}) %collective-permute-start.28) | collective-permute-done | bytes 294944 | tf_op jit(solution)/shard_map/ppermute | solution.py:512
  231.7 1.0 fusion.13
  233.1 1.1 fusion.14
  234.3 4.7 %collective-permute-start.34 = (bf16[4,72,256]{2,1,0:T(8,128)(2,1)S(1)}, bf16[4,72,256]{2,1,0:T(8,128)(2,1)S(1)}, u32[]{:S(2)}, u32[]{:S(2)}) collective-permute-start(bf16[4,72,256]{2,1,0:T(8,128)(2,1)S(1)} %get-tuple-element.208), channel_id=1, source_target_pairs={{0,16},{4,20},{8,24},{12,28},{16,0},{20,4},{24,8},{28,12},{1,17},{... | collective-permute-start | bytes 442376 | tf_op jit(solution)/shard_map/ppermute | solution.py:512
  239.4 3.2 %collective-permute-start.31 = (bf16[2,72,256]{2,1,0:T(8,128)(2,1)S(1)}, bf16[2,72,256]{2,1,0:T(8,128)(2,1)S(1)}, u32[]{:S(2)}, u32[]{:S(2)}) collective-permute-start(bf16[2,72,256]{2,1,0:T(8,128)(2,1)S(1)} %get-tuple-element.172), channel_id=1, source_target_pairs={{0,16},{4,20},{8,24},{12,28},{16,0},{20,4},{24,8},{28,12},{1,17},{... | collective-permute-start | bytes 221192 | tf_op jit(solution)/shard_map/ppermute | solution.py:512
  242.5 4.2 %collective-permute-done.34 = bf16[4,72,256]{2,1,0:T(8,128)(2,1)S(1)} collective-permute-done((bf16[4,72,256]{2,1,0:T(8,128)(2,1)S(1)}, bf16[4,72,256]{2,1,0:T(8,128)(2,1)S(1)}, u32[]{:S(2)}, u32[]{:S(2)}) %collective-permute-start.34) | collective-permute-done | bytes 147488 | tf_op jit(solution)/shard_map/ppermute | solution.py:512
  247.0 0.8 fusion.26
  247.8 0.8 fusion.28
  248.7 2.1 collective-permute-start.32
  250.7 0.5 collective-permute-done.35
  251.3 0.7 collective-permute-start.36
  251.9 0.7 collective-permute-done.32
  252.7 2.6 %collective-permute-done.36 = bf16[1,72,256]{2,1,0:T(8,128)(2,1)S(1)} collective-permute-done((bf16[1,72,256]{2,1,0:T(8,128)(2,1)S(1)}, bf16[1,72,256]{2,1,0:T(8,128)(2,1)S(1)}, u32[]{:S(2)}, u32[]{:S(2)}) %collective-permute-start.36) | collective-permute-done | bytes 36896 | tf_op jit(solution)/shard_map/ppermute | solution.py:512
  255.4 0.9 fusion.30
  (142 shorter events, 6.9 us)
Async XLA Ops:
  2.5 5.0 %collective-permute-start.3 = (bf16[1,72,256]{2,1,0:T(8,128)(2,1)S(1)}, bf16[1,72,256]{2,1,0:T(8,128)(2,1)S(1)}, u32[]{:S(2)}, u32[]{:S(2)}) collective-permute-start(bf16[1,72,256]{2,1,0:T(8,128)(2,1)S(1)} %get-tuple-element.234), channel_id=1, source_target_pairs={{0,8},{4,12},{8,0},{12,4},{16,24},{20,28},{24,16},{28,20},{1,9},{5... | collective-permute-start | bytes 110600 | tf_op jit(solution)/shard_map/ppermute | solution.py:512
  5.6 4.0 %collective-permute-start = (bf16[1,72,256]{2,1,0:T(8,128)(2,1)S(1)}, bf16[1,72,256]{2,1,0:T(8,128)(2,1)S(1)}, u32[]{:S(2)}, u32[]{:S(2)}) collective-permute-start(bf16[1,72,256]{2,1,0:T(8,128)(2,1)S(1)} %get-tuple-element.235), channel_id=1, source_target_pairs={{0,2},{1,3},{2,0},{3,1},{4,6},{5,7},{6,4},{7,5},{8,10},{9,11},{10,... | collective-permute-start | bytes 110600 | tf_op jit(solution)/shard_map/ppermute | solution.py:512
  9.6 5.0 %collective-permute-start.1 = (bf16[2,72,256]{2,1,0:T(8,128)(2,1)S(1)}, bf16[2,72,256]{2,1,0:T(8,128)(2,1)S(1)}, u32[]{:S(2)}, u32[]{:S(2)}) collective-permute-start(bf16[2,72,256]{2,1,0:T(8,128)(2,1)S(1)} %pad_maximum_fusion.11), channel_id=1, source_target_pairs={{0,8},{4,12},{8,0},{12,4},{16,24},{20,28},{24,16},{28,20},{1,9},{5... | collective-permute-start | bytes 221192 | tf_op jit(solution)/shard_map/ppermute | solution.py:512
  9.7 15.9 %copy-start.15 = (f32[64,256]{1,0:T(8,128)S(1)}, f32[64,256]{1,0:T(8,128)}, u32[]{:S(2)}) copy-start(f32[64,256]{1,0:T(8,128)} %param.16) | copy-start | bytes 196612
  9.8 5.4 %collective-permute-start.4 = (bf16[2,72,256]{2,1,0:T(8,128)(2,1)S(1)}, bf16[2,72,256]{2,1,0:T(8,128)(2,1)S(1)}, u32[]{:S(2)}, u32[]{:S(2)}) collective-permute-start(bf16[2,72,256]{2,1,0:T(8,128)(2,1)S(1)} %pad_maximum_fusion.12), channel_id=1, source_target_pairs={{0,16},{4,20},{8,24},{12,28},{16,0},{20,4},{24,8},{28,12},{1,17},{... | collective-permute-start | bytes 221192 | tf_op jit(solution)/shard_map/ppermute | solution.py:512
  15.2 5.2 %collective-permute-start.5 = (bf16[4,72,256]{2,1,0:T(8,128)(2,1)S(1)}, bf16[4,72,256]{2,1,0:T(8,128)(2,1)S(1)}, u32[]{:S(2)}, u32[]{:S(2)}) collective-permute-start(bf16[4,72,256]{2,1,0:T(8,128)(2,1)S(1)} %pad_maximum_fusion.10), channel_id=1, source_target_pairs={{0,4},{4,0},{8,12},{12,8},{16,20},{20,16},{24,28},{28,24},{1,5},{5... | collective-permute-start | bytes 442376 | tf_op jit(solution)/shard_map/ppermute | solution.py:512
  17.7 7.8 %collective-permute-start.2 = (bf16[4,72,256]{2,1,0:T(8,128)(2,1)S(1)}, bf16[4,72,256]{2,1,0:T(8,128)(2,1)S(1)}, u32[]{:S(2)}, u32[]{:S(2)}) collective-permute-start(bf16[4,72,256]{2,1,0:T(8,128)(2,1)S(1)} %pad_maximum_fusion.9), channel_id=1, source_target_pairs={{0,16},{4,20},{8,24},{12,28},{16,0},{20,4},{24,8},{28,12},{1,17},{... | collective-permute-start | bytes 442376 | tf_op jit(solution)/shard_map/ppermute | solution.py:512
  25.6 6.8 %collective-permute-start.11 = (bf16[8,72,256]{2,1,0:T(8,128)(2,1)S(1)}, bf16[8,72,256]{2,1,0:T(8,128)(2,1)S(1)}, u32[]{:S(2)}, u32[]{:S(2)}) collective-permute-start(bf16[8,72,256]{2,1,0:T(8,128)(2,1)S(1)} %pad_maximum_fusion.7), channel_id=1, source_target_pairs={{0,4},{4,0},{8,12},{12,8},{16,20},{20,16},{24,28},{28,24},{1,5},{5... | collective-permute-start | bytes 884744 | tf_op jit(solution)/shard_map/ppermute | solution.py:512
  25.9 12.4 %collective-permute-start.6 = (bf16[1,64,1024]{2,1,0:T(8,128)(2,1)}, bf16[1,64,1024]{2,1,0:T(8,128)(2,1)}, u32[]{:S(2)}, u32[]{:S(2)}) collective-permute-start(bf16[1,64,1024]{2,1,0:T(8,128)(2,1)} %maximum_bitcast_fusion.1), channel_id=1, source_target_pairs={{0,8},{4,12},{8,0},{12,4},{16,24},{20,28},{24,16},{28,20},{1,9},{5... | collective-permute-start | bytes 393224 | tf_op jit(solution)/shard_map/ppermute | solution.py:570
  27.1 11.2 %collective-permute-start.7 = (bf16[1,64,1024]{2,1,0:T(8,128)(2,1)}, bf16[1,64,1024]{2,1,0:T(8,128)(2,1)}, u32[]{:S(2)}, u32[]{:S(2)}) collective-permute-start(bf16[1,64,1024]{2,1,0:T(8,128)(2,1)} %maximum_bitcast_fusion.1), channel_id=1, source_target_pairs={{0,16},{4,20},{8,24},{12,28},{16,0},{20,4},{24,8},{28,12},{1,17},{... | collective-permute-start | bytes 393224 | tf_op jit(solution)/shard_map/ppermute | solution.py:570
  30.5 7.8 %collective-permute-start.8 = (bf16[1,64,1024]{2,1,0:T(8,128)(2,1)}, bf16[1,64,1024]{2,1,0:T(8,128)(2,1)}, u32[]{:S(2)}, u32[]{:S(2)}) collective-permute-start(bf16[1,64,1024]{2,1,0:T(8,128)(2,1)} %maximum_bitcast_fusion.1), channel_id=1, source_target_pairs={{0,24},{4,28},{8,16},{12,20},{16,8},{20,12},{24,0},{28,4},{1,25},{... | collective-permute-start | bytes 393224 | tf_op jit(solution)/shard_map/ppermute | solution.py:570
  30.5 6.7 %collective-permute-start.9 = (bf16[8,72,256]{2,1,0:T(8,128)(2,1)S(1)}, bf16[8,72,256]{2,1,0:T(8,128)(2,1)S(1)}, u32[]{:S(2)}, u32[]{:S(2)}) collective-permute-start(bf16[8,72,256]{2,1,0:T(8,128)(2,1)S(1)} %pad_maximum_fusion.8), channel_id=1, source_target_pairs={{0,2},{1,3},{2,0},{3,1},{4,6},{5,7},{6,4},{7,5},{8,10},{9,11},{10,... | collective-permute-start | bytes 884744 | tf_op jit(solution)/shard_map/ppermute | solution.py:512
  32.5 7.0 %collective-permute-start.12 = (bf16[16,72,256]{2,1,0:T(8,128)(2,1)S(1)}, bf16[16,72,256]{2,1,0:T(8,128)(2,1)S(1)}, u32[]{:S(2)}, u32[]{:S(2)}) collective-permute-start(bf16[16,72,256]{2,1,0:T(8,128)(2,1)S(1)} %pad_maximum_fusion.5), channel_id=1, source_target_pairs={{0,1},{1,0},{2,3},{3,2},{4,5},{5,4},{6,7},{7,6},{8,9},{9,8},{10,11... | collective-permute-start | bytes 1769480 | tf_op jit(solution)/shard_map/ppermute | solution.py:512
  38.2 2.2 collective-permute-start.10
  40.6 17.8 %collective-permute-start.13 = (bf16[4,64,1024]{2,1,0:T(8,128)(2,1)S(1)}, bf16[4,64,1024]{2,1,0:T(8,128)(2,1)S(1)}, u32[]{:S(2)}, u32[]{:S(2)}) collective-permute-start(bf16[4,64,1024]{2,1,0:T(8,128)(2,1)S(1)} %pad_maximum_fusion.6), channel_id=1, source_target_pairs={{0,2},{1,3},{2,0},{3,1},{4,6},{5,7},{6,4},{7,5},{8,10},{9,11},{10,... | collective-permute-start | bytes 1572872 | tf_op jit(solution)/shard_map/ppermute | solution.py:570
  58.3 9.3 %copy-start = (bf16[8,8,256,256]{3,2,1,0:T(8,128)(2,1)}, bf16[8,8,256,256]{3,2,1,0:T(8,128)(2,1)S(1)}, u32[]{:S(2)}) copy-start(bf16[8,8,256,256]{3,2,1,0:T(8,128)(2,1)S(1)} %get-tuple-element.119.pk) | copy-start | bytes 25165828
  58.4 7.3 %copy-start.26 = (s32[8,256]{1,0:T(8,128)S(1)}, s32[8,256]{1,0:T(8,128)}, u32[]{:S(2)}) copy-start(s32[8,256]{1,0:T(8,128)} %param.15) | copy-start | bytes 24580
  58.5 7.3 %copy-start.9 = (bf16[8,256,512]{2,1,0:T(8,128)(2,1)S(1)}, bf16[8,256,512]{2,1,0:T(8,128)(2,1)}, u32[]{:S(2)}) copy-start(bf16[8,256,512]{2,1,0:T(8,128)(2,1)} %param.14) | copy-start | bytes 6291460
  58.5 2.8 %collective-permute-start.14 = (bf16[8,272,256]{2,1,0:T(8,128)(2,1)S(1)}, bf16[8,272,256]{2,1,0:T(8,128)(2,1)S(1)}, u32[]{:S(2)}, u32[]{:S(2)}) collective-permute-start(bf16[8,272,256]{2,1,0:T(8,128)(2,1)S(1)} %get-tuple-element.111), channel_id=1, source_target_pairs={{0,1},{1,0},{2,3},{3,2},{4,5},{5,4},{6,7},{7,6},{8,9},{9,8},{10,11... | collective-permute-start | bytes 3342344 | tf_op jit(solution)/shard_map/ppermute | solution.py:512
  61.6 25.3 %collective-permute-start.16 = (bf16[8,64,1024]{2,1,0:T(8,128)(2,1)S(1)}, bf16[8,64,1024]{2,1,0:T(8,128)(2,1)S(1)}, u32[]{:S(2)}, u32[]{:S(2)}) collective-permute-start(bf16[8,64,1024]{2,1,0:T(8,128)(2,1)S(1)} %pad_maximum_fusion.3), channel_id=1, source_target_pairs={{0,4},{4,0},{8,12},{12,8},{16,20},{20,16},{24,28},{28,24},{1,5},{5... | collective-permute-start | bytes 3145736 | tf_op jit(solution)/shard_map/ppermute | solution.py:570
  63.3 26.2 %collective-permute-start.15 = (bf16[8,272,256]{2,1,0:T(8,128)(2,1)S(1)}, bf16[8,272,256]{2,1,0:T(8,128)(2,1)S(1)}, u32[]{:S(2)}, u32[]{:S(2)}) collective-permute-start(bf16[8,272,256]{2,1,0:T(8,128)(2,1)S(1)} %fusion), channel_id=1, source_target_pairs={{0,2},{1,3},{4,6},{5,7},{8,10},{9,11},{12,14},{13,15},{16,18},{17,... | collective-permute-start | bytes 3342344 | tf_op jit(solution)/shard_map/ppermute | solution.py:528
  90.2 2.8 %collective-permute-start.17 = (bf16[8,272,256]{2,1,0:T(8,128)(2,1)S(1)}, bf16[8,272,256]{2,1,0:T(8,128)(2,1)S(1)}, u32[]{:S(2)}, u32[]{:S(2)}) collective-permute-start(bf16[8,272,256]{2,1,0:T(8,128)(2,1)S(1)} %get-tuple-element.205), channel_id=1, source_target_pairs={{0,1},{1,0},{2,3},{3,2},{4,5},{5,4},{6,7},{7,6},{8,9},{9,8},{10,11... | collective-permute-start | bytes 3342344 | tf_op jit(solution)/shard_map/ppermute | solution.py:512
  93.0 9.4 %copy-start.1 = (bf16[8,272,256]{2,1,0:T(8,128)(2,1)}, bf16[8,272,256]{2,1,0:T(8,128)(2,1)S(1)}, u32[]{:S(2)}) copy-start(bf16[8,272,256]{2,1,0:T(8,128)(2,1)S(1)} %collective-permute-done.17.come.come_state) | copy-start | bytes 3342340
  93.0 9.4 %collective-permute-start.18 = (bf16[16,64,1024]{2,1,0:T(8,128)(2,1)S(1)}, bf16[16,64,1024]{2,1,0:T(8,128)(2,1)S(1)}, u32[]{:S(2)}, u32[]{:S(2)}) collective-permute-start(bf16[16,64,1024]{2,1,0:T(8,128)(2,1)S(1)} %pad_maximum_fusion.own_pair), channel_id=1, source_target_pairs={{0,1},{1,0},{2,3},{3,2},{4,5},{5,4},{6,7},{7,6},{8,9},{9,8},{10,11... | collective-permute-start | bytes 6291464 | tf_op jit(solution)/shard_map/ppermute | solution.py:512
  102.5 38.2 %copy-start.3 = (f32[8,8,256]{2,1,0:T(8,128)S(1)}, f32[8,8,256]{2,1,0:T(8,128)}, u32[]{:S(2)}) copy-start(f32[8,8,256]{2,1,0:T(8,128)} %get-tuple-element.137.recip) | copy-start | bytes 196612
  140.4 11.6 %collective-permute-start.19 = (bf16[512,2048]{1,0:T(8,128)(2,1)}, bf16[512,2048]{1,0:T(8,128)(2,1)}, u32[]{:S(2)}, u32[]{:S(2)}) collective-permute-start(bf16[512,2048]{1,0:T(8,128)(2,1)} %get-tuple-element.140), channel_id=1, source_target_pairs={{0,1},{1,0},{2,3},{3,2},{4,5},{5,4},{6,7},{7,6},{8,9},{9,8},{10,11... | collective-permute-start | bytes 6291464 | tf_op jit(solution)/shard_map/ppermute | solution.py:512
  151.9 3.6 %collective-permute-start.21 = (bf16[8,272,256]{2,1,0:T(8,128)(2,1)}, bf16[8,272,256]{2,1,0:T(8,128)(2,1)}, u32[]{:S(2)}, u32[]{:S(2)}) collective-permute-start(bf16[8,272,256]{2,1,0:T(8,128)(2,1)} %get-tuple-element.144), channel_id=1, source_target_pairs={{0,1},{1,0},{2,3},{3,2},{4,5},{5,4},{6,7},{7,6},{8,9},{9,8},{10,11... | collective-permute-start | bytes 3342344 | tf_op jit(solution)/shard_map/ppermute | solution.py:512
  152.5 3.1 %copy-start.7 = (bf16[8,272,256]{2,1,0:T(8,128)(2,1)S(1)}, bf16[8,272,256]{2,1,0:T(8,128)(2,1)}, u32[]{:S(2)}) copy-start(bf16[8,272,256]{2,1,0:T(8,128)(2,1)} %get-tuple-element.143) | copy-start | bytes 3342340
  158.2 29.0 %collective-permute-start.22 = (bf16[8,272,256]{2,1,0:T(8,128)(2,1)}, bf16[8,272,256]{2,1,0:T(8,128)(2,1)}, u32[]{:S(2)}, u32[]{:S(2)}) collective-permute-start(bf16[8,272,256]{2,1,0:T(8,128)(2,1)} %fusion.3), channel_id=1, source_target_pairs={{2,0},{3,1},{6,4},{7,5},{10,8},{11,9},{14,12},{15,13},{18,16},{19,... | collective-permute-start | bytes 3342344 | tf_op jit(solution)/shard_map/ppermute | solution.py:528
  159.5 30.9 %collective-permute-start.20 = (bf16[256,2048]{1,0:T(8,128)(2,1)}, bf16[256,2048]{1,0:T(8,128)(2,1)}, u32[]{:S(2)}, u32[]{:S(2)}) collective-permute-start(bf16[256,2048]{1,0:T(8,128)(2,1)} %fusion.6), channel_id=1, source_target_pairs={{0,4},{4,0},{8,12},{12,8},{16,20},{20,16},{24,28},{28,24},{1,5},{5... | collective-permute-start | bytes 3145736 | tf_op jit(solution)/shard_map/ppermute | solution.py:512
  159.8 1.2 copy-start.2
  161.1 26.1 %copy-start.8 = (bf16[8,272,256]{2,1,0:T(8,128)(2,1)S(1)}, bf16[8,272,256]{2,1,0:T(8,128)(2,1)}, u32[]{:S(2)}) copy-start(bf16[8,272,256]{2,1,0:T(8,128)(2,1)} %get-tuple-element.143) | copy-start | bytes 3342340
  190.4 7.0 %collective-permute-start.23 = (bf16[8,272,256]{2,1,0:T(8,128)(2,1)}, bf16[8,272,256]{2,1,0:T(8,128)(2,1)}, u32[]{:S(2)}, u32[]{:S(2)}) collective-permute-start(bf16[8,272,256]{2,1,0:T(8,128)(2,1)} %get-tuple-element.202), channel_id=1, source_target_pairs={{0,1},{1,0},{2,3},{3,2},{4,5},{5,4},{6,7},{7,6},{8,9},{9,8},{10,11... | collective-permute-start | bytes 3342344 | tf_op jit(solution)/shard_map/ppermute | solution.py:512
  190.4 7.0 %copy-start.4 = (f32[512,512]{1,0:T(8,128)S(1)}, f32[512,512]{1,0:T(8,128)}, u32[]{:S(2)}) copy-start(f32[512,512]{1,0:T(8,128)} %get-tuple-element.159.out_proj) | copy-start | bytes 3145732
  190.4 7.0 %copy-start.5 = (f32[512,512]{1,0:T(8,128)S(1)}, f32[512,512]{1,0:T(8,128)}, u32[]{:S(2)}) copy-start(f32[512,512]{1,0:T(8,128)} %get-tuple-element.158.query_weight) | copy-start | bytes 3145732
  190.4 7.0 %copy-start.6 = (f32[2,512]{1,0:T(2,128)S(1)}, f32[2,512]{1,0:T(2,128)}, u32[]{:S(2)}) copy-start(f32[2,512]{1,0:T(2,128)} %get-tuple-element.160.norm_two) | copy-start | bytes 12292
  192.9 24.7 %collective-permute-start.24 = (bf16[64,2048]{1,0:T(8,128)(2,1)S(1)}, bf16[64,2048]{1,0:T(8,128)(2,1)S(1)}, u32[]{:S(2)}, u32[]{:S(2)}) collective-permute-start(bf16[64,2048]{1,0:T(8,128)(2,1)S(1)} %get-tuple-element.164), channel_id=1, source_target_pairs={{0,8},{4,12},{8,0},{12,4},{16,24},{20,28},{24,16},{28,20},{1,9},{5... | collective-permute-start | bytes 786440 | tf_op jit(solution)/shard_map/ppermute | solution.py:879
  193.2 24.4 %collective-permute-start.25 = (bf16[64,2048]{1,0:T(8,128)(2,1)S(1)}, bf16[64,2048]{1,0:T(8,128)(2,1)S(1)}, u32[]{:S(2)}, u32[]{:S(2)}) collective-permute-start(bf16[64,2048]{1,0:T(8,128)(2,1)S(1)} %get-tuple-element.165), channel_id=1, source_target_pairs={{0,16},{4,20},{8,24},{12,28},{16,0},{20,4},{24,8},{28,12},{1,17},{... | collective-permute-start | bytes 786440 | tf_op jit(solution)/shard_map/ppermute | solution.py:879
  197.0 20.6 %collective-permute-start.26 = (bf16[64,2048]{1,0:T(8,128)(2,1)S(1)}, bf16[64,2048]{1,0:T(8,128)(2,1)S(1)}, u32[]{:S(2)}, u32[]{:S(2)}) collective-permute-start(bf16[64,2048]{1,0:T(8,128)(2,1)S(1)} %get-tuple-element.166), channel_id=1, source_target_pairs={{0,24},{4,28},{8,16},{12,20},{16,8},{20,12},{24,0},{28,4},{1,25},{... | collective-permute-start | bytes 786440 | tf_op jit(solution)/shard_map/ppermute | solution.py:879
  217.6 3.9 %copy-start.11 = (f32[16,72,256]{2,1,0:T(8,128)S(1)}, f32[16,72,256]{2,1,0:T(8,128)}, u32[]{:S(2)}) copy-start(f32[16,72,256]{2,1,0:T(8,128)} %get-tuple-element.162) | copy-start | bytes 3538948
  217.6 3.9 %copy-start.16 = (bf16[64,2048]{1,0:T(8,128)(2,1)}, bf16[64,2048]{1,0:T(8,128)(2,1)S(1)}, u32[]{:S(2)}) copy-start(bf16[64,2048]{1,0:T(8,128)(2,1)S(1)} %collective-permute-done.25) | copy-start | bytes 786436
  217.7 0.7 copy-start.18
  218.4 3.1 %collective-permute-start.27 = (bf16[2,16,72,256]{3,2,1,0:T(8,128)(2,1)}, bf16[2,16,72,256]{3,2,1,0:T(8,128)(2,1)S(1)}, u32[]{:S(2)}, u32[]{:S(2)}) collective-permute-start(bf16[2,16,72,256]{3,2,1,0:T(8,128)(2,1)} %get-tuple-element.167), channel_id=1, source_target_pairs={{0,1},{1,0},{2,3},{3,2},{4,5},{5,4},{6,7},{7,6},{8,9},{9,8},{10,11... | collective-permute-start | bytes 3538952 | tf_op jit(solution)/shard_map/ppermute | solution.py:512
  218.4 3.4 %copy-start.10 = (f32[16,72,256]{2,1,0:T(8,128)S(1)}, f32[16,72,256]{2,1,0:T(8,128)}, u32[]{:S(2)}) copy-start(f32[16,72,256]{2,1,0:T(8,128)} %get-tuple-element.173) | copy-start | bytes 3538948
  221.5 1.0 copy-start.17
  221.5 1.0 copy-start.19
  221.7 10.0 %collective-permute-start.28 = (bf16[8,72,256]{2,1,0:T(8,128)(2,1)S(1)}, bf16[8,72,256]{2,1,0:T(8,128)(2,1)}, u32[]{:S(2)}, u32[]{:S(2)}) collective-permute-start(bf16[8,72,256]{2,1,0:T(8,128)(2,1)S(1)} %get-tuple-element.192), channel_id=1, source_target_pairs={{0,2},{1,3},{2,0},{3,1},{4,6},{5,7},{6,4},{7,5},{8,10},{9,11},{10,... | collective-permute-start | bytes 884744 | tf_op jit(solution)/shard_map/ppermute | solution.py:512
  221.9 11.2 %collective-permute-start.33 = (bf16[8,72,256]{2,1,0:T(8,128)(2,1)S(1)}, bf16[8,72,256]{2,1,0:T(8,128)(2,1)}, u32[]{:S(2)}, u32[]{:S(2)}) collective-permute-start(bf16[8,72,256]{2,1,0:T(8,128)(2,1)S(1)} %get-tuple-element.194), channel_id=1, source_target_pairs={{0,4},{4,0},{8,12},{12,8},{16,20},{20,16},{24,28},{28,24},{1,5},{5... | collective-permute-start | bytes 884744 | tf_op jit(solution)/shard_map/ppermute | solution.py:512
  223.4 15.9 %collective-permute-start.30 = (bf16[64,1024]{1,0:T(8,128)(2,1)S(1)}, bf16[64,1024]{1,0:T(8,128)(2,1)S(1)}, u32[]{:S(2)}, u32[]{:S(2)}) collective-permute-start(bf16[64,1024]{1,0:T(8,128)(2,1)S(1)} %bitcast.136), channel_id=1, source_target_pairs={{0,2},{1,3},{2,0},{3,1},{4,6},{5,7},{6,4},{7,5},{8,10},{9,11},{10,... | collective-permute-start | bytes 393224 | tf_op jit(solution)/shard_map/ppermute | solution.py:512
  232.7 6.6 %collective-permute-start.29 = (bf16[4,72,256]{2,1,0:T(8,128)(2,1)S(1)}, bf16[4,72,256]{2,1,0:T(8,128)(2,1)S(1)}, u32[]{:S(2)}, u32[]{:S(2)}) collective-permute-start(bf16[4,72,256]{2,1,0:T(8,128)(2,1)S(1)} %get-tuple-element.206), channel_id=1, source_target_pairs={{0,4},{4,0},{8,12},{12,8},{16,20},{20,16},{24,28},{28,24},{1,5},{5... | collective-permute-start | bytes 442376 | tf_op jit(solution)/shard_map/ppermute | solution.py:512
  233.1 13.8 %copy-start.13 = (f32[512,64]{0,1:T(8,128)S(1)}, f32[512,64]{0,1:T(8,128)}, u32[]{:S(2)}) copy-start(f32[512,64]{0,1:T(8,128)} %param.21) | copy-start | bytes 393220
  233.1 13.9 %copy-start.22 = (f32[512,64]{0,1:T(8,128)S(1)}, f32[512,64]{0,1:T(8,128)}, u32[]{:S(2)}) copy-start(f32[512,64]{0,1:T(8,128)} %param.24) | copy-start | bytes 393220
  233.1 13.9 %copy-start.23 = (f32[512,64]{0,1:T(8,128)S(1)}, f32[512,64]{0,1:T(8,128)}, u32[]{:S(2)}) copy-start(f32[512,64]{0,1:T(8,128)} %param.25) | copy-start | bytes 393220
  234.2 13.6 %copy-start.14 = (f32[64,512]{1,0:T(8,128)S(1)}, f32[64,512]{1,0:T(8,128)}, u32[]{:S(2)}) copy-start(f32[64,512]{1,0:T(8,128)} %param.20) | copy-start | bytes 393220
  234.2 13.6 %copy-start.24 = (f32[64,512]{1,0:T(8,128)S(1)}, f32[64,512]{1,0:T(8,128)}, u32[]{:S(2)}) copy-start(f32[64,512]{1,0:T(8,128)} %param.22) | copy-start | bytes 393220
  234.2 13.6 %copy-start.25 = (f32[64,512]{1,0:T(8,128)S(1)}, f32[64,512]{1,0:T(8,128)}, u32[]{:S(2)}) copy-start(f32[64,512]{1,0:T(8,128)} %param.23) | copy-start | bytes 393220
  234.3 12.5 %collective-permute-start.34 = (bf16[4,72,256]{2,1,0:T(8,128)(2,1)S(1)}, bf16[4,72,256]{2,1,0:T(8,128)(2,1)S(1)}, u32[]{:S(2)}, u32[]{:S(2)}) collective-permute-start(bf16[4,72,256]{2,1,0:T(8,128)(2,1)S(1)} %get-tuple-element.208), channel_id=1, source_target_pairs={{0,16},{4,20},{8,24},{12,28},{16,0},{20,4},{24,8},{28,12},{1,17},{... | collective-permute-start | bytes 442376 | tf_op jit(solution)/shard_map/ppermute | solution.py:512
  239.4 9.3 %collective-permute-start.31 = (bf16[2,72,256]{2,1,0:T(8,128)(2,1)S(1)}, bf16[2,72,256]{2,1,0:T(8,128)(2,1)S(1)}, u32[]{:S(2)}, u32[]{:S(2)}) collective-permute-start(bf16[2,72,256]{2,1,0:T(8,128)(2,1)S(1)} %get-tuple-element.172), channel_id=1, source_target_pairs={{0,16},{4,20},{8,24},{12,28},{16,0},{20,4},{24,8},{28,12},{1,17},{... | collective-permute-start | bytes 221192 | tf_op jit(solution)/shard_map/ppermute | solution.py:512
  246.8 8.6 %copy-start.12 = (f32[32832]{0:T(1024)S(1)}, f32[32832]{0:T(1024)}, u32[]{:S(2)}) copy-start(f32[32832]{0:T(1024)} %param.17) | copy-start | bytes 393988
  246.8 8.6 %copy-start.20 = (f32[32832]{0:T(1024)S(1)}, f32[32832]{0:T(1024)}, u32[]{:S(2)}) copy-start(f32[32832]{0:T(1024)} %param.18) | copy-start | bytes 393988
  246.8 8.6 %copy-start.21 = (f32[32832]{0:T(1024)S(1)}, f32[32832]{0:T(1024)}, u32[]{:S(2)}) copy-start(f32[32832]{0:T(1024)} %param.19) | copy-start | bytes 393988
  246.8 4.4 %collective-permute-start.35 = (bf16[2,72,256]{2,1,0:T(8,128)(2,1)S(1)}, bf16[2,72,256]{2,1,0:T(8,128)(2,1)S(1)}, u32[]{:S(2)}, u32[]{:S(2)}) collective-permute-start(bf16[2,72,256]{2,1,0:T(8,128)(2,1)S(1)} %get-tuple-element.216), channel_id=1, source_target_pairs={{0,8},{4,12},{8,0},{12,4},{16,24},{20,28},{24,16},{28,20},{1,9},{5... | collective-permute-start | bytes 221192 | tf_op jit(solution)/shard_map/ppermute | solution.py:512
  248.7 4.0 %collective-permute-start.32 = (bf16[1,72,256]{2,1,0:T(8,128)(2,1)S(1)}, bf16[1,72,256]{2,1,0:T(8,128)(2,1)S(1)}, u32[]{:S(2)}, u32[]{:S(2)}) collective-permute-start(bf16[1,72,256]{2,1,0:T(8,128)(2,1)S(1)} %fusion.23), channel_id=1, source_target_pairs={{0,8},{4,12},{8,0},{12,4},{16,24},{20,28},{24,16},{28,20},{1,9},{5... | collective-permute-start | bytes 110600 | tf_op jit(solution)/shard_map/ppermute | solution.py:512
  251.3 4.0 %collective-permute-start.36 = (bf16[1,72,256]{2,1,0:T(8,128)(2,1)S(1)}, bf16[1,72,256]{2,1,0:T(8,128)(2,1)S(1)}, u32[]{:S(2)}, u32[]{:S(2)}) collective-permute-start(bf16[1,72,256]{2,1,0:T(8,128)(2,1)S(1)} %fusion.20), channel_id=1, source_target_pairs={{0,2},{1,3},{2,0},{3,1},{4,6},{5,7},{6,4},{7,5},{8,10},{9,11},{10,... | collective-permute-start | bytes 110600 | tf_op jit(solution)/shard_map/ppermute | solution.py:512
